TPU v7x, 32 devices: a whole 2x2x4 slice. The times are simulated.
32 devices in a mesh: section: 4 (over x, core), expert: 8 (over z, y).
Axes of the slice: x: 2, y: 2, z: 4, core: 2. Of those that a mesh axis runs over, the one named last changes fastest.
Arguments:
- hidden_in: bfloat16 [4, 32, 4096], P('section', 'expert'), may hold values from -4 to 4
- attn_gain: bfloat16 [4, 4096], P('section'), may hold values from 0.5 to 2
- w_query: bfloat16 [4, 4096, 4096], P('section', None, 'expert'), may hold values from -0.09375 to 0.09375
- w_out: bfloat16 [4, 4096, 4096], P('section', None, 'expert'), may hold values from -0.09375 to 0.09375
- key_cache: bfloat16 [4, 3, 32, 64, 4, 128], P('section', None, 'expert'), may hold values from -2 to 2
- value_cache: bfloat16 [4, 3, 32, 64, 4, 128], P('section', None, 'expert'), may hold values from -6 to 6
- lengths: int32 [4, 3, 32], P('section', None, 'expert'), may hold values from 1 to 64, 1024 in all within a row
- ffn_gain: bfloat16 [4, 4096], P('section'), may hold values from 0.5 to 2
- w_gate: bfloat16 [4, 8, 4096, 384], P('section', 'expert'), may hold values from -0.09375 to 0.09375
- w_up: bfloat16 [4, 8, 4096, 384], P('section', 'expert'), may hold values from -0.09375 to 0.09375
- w_down: bfloat16 [4, 8, 384, 4096], P('section', 'expert'), may hold values from -0.21875 to 0.21875
- routes: int32 [4, 3, 32, 2], P('section', None, 'expert'), may hold values from 0 to 3, all different within a row; in each aligned block of 4 rows (0 to 3, 4 to 7, ..., all dimensions but the last counted through in order) at most 4 rows name the same one
- gates: float32 [4, 3, 32, 2], P('section', None, 'expert'), may hold values from 0.1 to 1
Outputs:
- out: bfloat16 [4, 32, 4096], P('section', 'expert')
Inputs may be any that keep to these rules, and one draw needn't show every extreme that they name: `routes`: each row names 2 different experts of the 4; among the 4 rows that one index of the expert axis holds at one section and step, an expert is named by at most 4 rows.
All inputs are finite; a program needn't handle non-finite values. No bound on the sum of `lengths` on one device may be relied on, other than what follows from the above.
Results may differ from a plain program's by a relative error of at most 0.04.
Values may be sent and summed in bfloat16 or wider, within the bound.
No kernel may reach another device: no remote copies, remote signals or barrier semaphores. Data moves between devices by JAX's collectives and lax.ppermute only.
A program may use at most 64 MiB of HBM per device.

v0:
```python
import jax
import jax.numpy as jnp
from jax import lax
from jax.sharding import PartitionSpec as P

STEPS = 3


def passed_along(array, axis, by):
    length = lax.axis_size(axis)
    return lax.ppermute(array, axis, [(i, (i + by) % length) for i in range(length)])


def rms_scaled(values):
    return values * lax.rsqrt(jnp.mean(values * values, axis=-1, keepdims=True) + 1e-06)


def expert_half(slot_block, gate_w, up_w, down_w):
    leading = slot_block.shape[:-1]
    flat_rows = slot_block.reshape(-1, slot_block.shape[-1])
    gate_val = jnp.dot(flat_rows, gate_w, preferred_element_type=jnp.float32)
    up_val = jnp.dot(flat_rows, up_w, preferred_element_type=jnp.float32)
    active = (jax.nn.silu(gate_val) * up_val).astype(jnp.bfloat16)
    result = jnp.dot(active, down_w, preferred_element_type=jnp.float32).astype(jnp.bfloat16)
    return result.reshape(leading + (down_w.shape[1],))


def route_tables(route_ids, gate_vals, experts, capacity):
    row_count, top_count = route_ids.shape
    route_hits = (
        route_ids[:, :, None] == jnp.arange(experts, dtype=jnp.int32)[None, None, :]
    ).astype(jnp.int32)
    flat_hits = route_hits.reshape(row_count * top_count, experts)
    earlier = jnp.cumsum(flat_hits, axis=0) - flat_hits
    slot_ids = jnp.sum(earlier * flat_hits, axis=1)
    places = route_ids.reshape(-1) * capacity + slot_ids
    slot_table = (
        jnp.arange(experts * capacity, dtype=jnp.int32)[:, None] == places[None, :]
    ).astype(jnp.float32)
    slot_table = slot_table.reshape(experts * capacity, row_count, top_count)
    shares = gate_vals / jnp.sum(gate_vals, axis=-1, keepdims=True)
    picker = jnp.sum(slot_table, axis=-1).astype(jnp.bfloat16)
    weigher = jnp.sum(slot_table * shares[None, :, :], axis=-1).T
    return (picker, weigher)


def body(
    hidden_in,
    attn_gain,
    w_query,
    w_out,
    key_cache,
    value_cache,
    lengths,
    ffn_gain,
    w_gate,
    w_up,
    w_down,
    routes,
    gates,
):
    devices = lax.axis_size("expert")
    experts = devices // 2
    row_count = hidden_in.shape[1]
    model_width = hidden_in.shape[2]
    head_dim = key_cache.shape[-1]
    kv_heads = key_cache.shape[-2]
    cache_len = key_cache.shape[-3]
    query_w = w_query[0]
    out_w = w_out[0]
    local_heads = query_w.shape[1] // head_dim
    all_heads = local_heads * devices
    group_size = all_heads // kv_heads
    gate_w = w_gate[0, 0]
    up_w = w_up[0, 0]
    down_w = w_down[0, 0]
    gain_attn = attn_gain[0].astype(jnp.float32)
    gain_ffn = ffn_gain[0].astype(jnp.float32)
    hidden_state = hidden_in[0]
    result = hidden_state
    for layer_step in range(STEPS):
        state32 = hidden_state.astype(jnp.float32)
        normed = (rms_scaled(state32) * gain_attn).astype(jnp.bfloat16)
        project_piece_rows = lax.all_gather(normed, "expert", axis=0, tiled=True)
        raw_query = jnp.dot(project_piece_rows, query_w, preferred_element_type=jnp.float32)
        heads_view = raw_query.reshape(project_piece_rows.shape[0], local_heads, head_dim)
        gathered_q = (
            rms_scaled(heads_view)
            .astype(jnp.bfloat16)
            .reshape(project_piece_rows.shape[0], local_heads * head_dim)
        )
        queries = lax.all_to_all(gathered_q, "expert", split_axis=0, concat_axis=1, tiled=True)
        queries = queries.reshape(row_count, kv_heads, group_size, head_dim)
        scores = jnp.einsum(
            "rkgd,rpkd->rkgp", queries, key_cache[0, layer_step], preferred_element_type=jnp.float32
        ) * head_dim ** (-0.5)
        in_cache = jnp.arange(cache_len, dtype=jnp.int32)[None, :] < lengths[0, layer_step][:, None]
        exp_scores = jnp.where(in_cache[:, None, None, :], jnp.exp(scores), 0.0)
        weights = (exp_scores / jnp.sum(exp_scores, axis=-1, keepdims=True)).astype(jnp.bfloat16)
        context = jnp.einsum(
            "rkgp,rpkd->rkgd",
            weights,
            value_cache[0, layer_step],
            preferred_element_type=jnp.float32,
        )
        context = context.astype(jnp.bfloat16).reshape(row_count, all_heads * head_dim)
        out_cols = jnp.dot(
            lax.all_gather(context, "expert", axis=0, tiled=True),
            out_w,
            preferred_element_type=jnp.float32,
        )
        attended = lax.all_to_all(
            out_cols.astype(jnp.bfloat16), "expert", split_axis=0, concat_axis=1, tiled=True
        ).astype(out_cols.dtype)
        middle = state32 + attended
        ffn_in = (rms_scaled(middle) * gain_ffn).astype(jnp.bfloat16)
        picker, weigher = route_tables(
            routes[0, layer_step], gates[0, layer_step], experts, row_count
        )
        packed = jnp.dot(picker, ffn_in, preferred_element_type=jnp.float32).astype(jnp.bfloat16)
        outgoing = jnp.repeat(packed.reshape(experts, row_count, model_width), 2, axis=0)
        half_out = expert_half(
            lax.all_to_all(outgoing, "expert", split_axis=0, concat_axis=0, tiled=True),
            gate_w,
            up_w,
            down_w,
        )
        returned = lax.all_to_all(half_out, "expert", split_axis=0, concat_axis=0, tiled=True)
        paired_out = jnp.sum(
            returned.astype(jnp.float32).reshape(experts, 2, row_count, model_width), axis=1
        ).astype(jnp.bfloat16)
        combined = lax.optimization_barrier(paired_out).astype(jnp.float32)
        expert_sum = jnp.dot(
            weigher,
            combined.reshape(experts * row_count, model_width),
            precision=lax.Precision.HIGHEST,
        )
        result = (middle + expert_sum).astype(jnp.bfloat16)
        if layer_step + 1 < STEPS:
            hidden_state = passed_along(result, "section", 1)
    return result[None]


def solution(mesh):
    return jax.shard_map(
        body,
        mesh=mesh,
        in_specs=(
            P("section", "expert", None),
            P("section", None),
            P("section", None, "expert"),
            P("section", None, "expert"),
            P("section", None, "expert", None, None, None),
            P("section", None, "expert", None, None, None),
            P("section", None, "expert"),
            P("section", None),
            P("section", "expert", None, None),
            P("section", "expert", None, None),
            P("section", "expert", None, None),
            P("section", None, "expert", None),
            P("section", None, "expert", None),
        ),
        out_specs=P("section", "expert", None),
        check_vma=False,
    )
```

profile of v0, /device:TPU:0, one launch (start us, length us, event | category | flops | bytes accessed | tf_op | source)
XLA Modules:
  0.0 412.2 jit_solution(2094439423284562569)
XLA Ops:
  0.0 6.6 %copy.114 = bf16[512,4096]{1,0:T(8,128)(2,1)} copy(bf16[512,4096]{0,1:T(8,128)(2,1)} %bitcast.174) | data formatting | bytes 8388608 | tf_op jit(solution)/shard_map/dot_general | solution.py:85
  6.9 34.5 %all-gather = bf16[8,4,4096]{2,1,0:T(4,128)(2,1)} all-gather(bf16[1,4,4096]{2,1,0:T(4,128)(2,1)S(1)} %fusion.88), channel_id=1, replica_groups=mesh['section'=4,'expert'=8] {'expert'}, dimensions={0}, use_global_device_ids=true | all-gather | bytes 294912 | tf_op jit(solution)/shard_map/all_gather | solution.py:84
  41.4 1.0 reshape.425
  42.4 3.6 multiply_reduce_fusion.5
  46.9 5.5 %all-to-all-start = ((bf16[8,4,512]{2,1,0:T(4,128)(2,1)}), bf16[8,4,512]{2,1,0:T(4,128)(2,1)S(1)}, u32[]{:S(2)}, u32[]{:S(2)}) async-start(bf16[8,4,512]{2,1,0:T(4,128)(2,1)} %all_to_all.84), calls=%async_computation | async-start | bytes 65536 | tf_op jit(solution)/shard_map/all_to_all | solution.py:92
  54.1 2.2 fusion.118
  56.9 2.2 fusion.119
  59.8 0.9 fusion.28
  60.7 1.3 convolution_convert_fusion.8
  62.0 33.3 %all-gather.1 = bf16[8,4,4096]{2,1,0:T(4,128)(2,1)} all-gather(bf16[1,4,4096]{2,1,0:T(4,128)(2,1)S(1)} %reshape.412), channel_id=1, replica_groups=mesh['section'=4,'expert'=8] {'expert'}, dimensions={0}, use_global_device_ids=true | all-gather | bytes 294912 | tf_op jit(solution)/shard_map/all_gather | solution.py:108
  95.3 1.0 reshape.413
  96.3 3.0 fusion.40
  99.3 0.7 all_to_all.87
  100.0 5.4 %all-to-all-start.1 = ((bf16[8,4,512]{2,1,0:T(4,128)(2,1)}), bf16[8,4,512]{2,1,0:T(4,128)(2,1)S(1)}, u32[]{:S(2)}, u32[]{:S(2)}) async-start(bf16[8,4,512]{2,1,0:T(4,128)(2,1)} %all_to_all.87), calls=%async_computation.1 | async-start | bytes 65536 | tf_op jit(solution)/shard_map/all_to_all | solution.py:112
  105.5 6.6 %all-to-all-done.1 = bf16[8,4,512]{2,1,0:T(4,128)(2,1)S(1)} async-done(((bf16[8,4,512]{2,1,0:T(4,128)(2,1)}), bf16[8,4,512]{2,1,0:T(4,128)(2,1)S(1)}, u32[]{:S(2)}, u32[]{:S(2)}) %all-to-all-start.1) | async-done | bytes 32800 | tf_op jit(solution)/shard_map/all_to_all | solution.py:112
  112.7 11.3 %all_to_all.117 = bf16[8,4,4096]{2,1,0:T(4,128)(2,1)} all-to-all(bf16[8,4,4096]{2,1,0:T(4,128)(2,1)S(1)} %bitcast.175), channel_id=1, replica_groups=mesh['section'=4,'expert'=8] {'expert'}, dimensions={0} | all-to-all | bytes 524288 | tf_op jit(solution)/shard_map/all_to_all | solution.py:123
  124.0 1.0 reshape.381
  125.0 3.1 fusion.23
  128.1 4.0 convolution_convert_fusion.2
  132.1 1.1 reshape.382
  133.2 10.8 %all_to_all.118 = bf16[8,4,4096]{2,1,0:T(4,128)(2,1)S(1)} all-to-all(bf16[8,4,4096]{2,1,0:T(4,128)(2,1)S(1)} %reshape.382), channel_id=1, replica_groups=mesh['section'=4,'expert'=8] {'expert'}, dimensions={0} | all-to-all | bytes 524288 | tf_op jit(solution)/shard_map/all_to_all | solution.py:128
  144.5 3.3 collective-permute-done
  148.0 32.8 %all-gather.2 = bf16[8,4,4096]{2,1,0:T(4,128)(2,1)} all-gather(bf16[1,4,4096]{2,1,0:T(4,128)(2,1)S(1)} %fusion.90), channel_id=1, replica_groups=mesh['section'=4,'expert'=8] {'expert'}, dimensions={0}, use_global_device_ids=true | all-gather | bytes 294912 | tf_op jit(solution)/shard_map/all_gather | solution.py:84
  180.8 1.0 reshape.426
  181.9 3.6 multiply_reduce_fusion.3
  185.6 0.6 all_to_all.91
  186.3 3.3 all-to-all-start.4
  189.6 1.3 iota_compare_fusion.4
  190.9 5.3 %all-to-all-done.4 = bf16[8,4,512]{2,1,0:T(4,128)(2,1)S(1)} async-done(((bf16[8,4,512]{2,1,0:T(4,128)(2,1)}), bf16[8,4,512]{2,1,0:T(4,128)(2,1)S(1)}, u32[]{:S(2)}, u32[]{:S(2)}) %all-to-all-start.4) | async-done | bytes 32800 | tf_op jit(solution)/shard_map/all_to_all | solution.py:92
  196.3 1.2 fusion.29
  197.5 1.2 convolution_convert_fusion.7
  198.7 33.0 %all-gather.3 = bf16[8,4,4096]{2,1,0:T(4,128)(2,1)} all-gather(bf16[1,4,4096]{2,1,0:T(4,128)(2,1)S(1)} %reshape.416), channel_id=1, replica_groups=mesh['section'=4,'expert'=8] {'expert'}, dimensions={0}, use_global_device_ids=true | all-gather | bytes 294912 | tf_op jit(solution)/shard_map/all_gather | solution.py:108
  231.7 1.0 reshape.417
  232.7 3.0 fusion.43
  235.7 0.7 all_to_all.94
  236.4 3.3 all-to-all-start.5
  239.8 6.5 %all-to-all-done.5 = bf16[8,4,512]{2,1,0:T(4,128)(2,1)S(1)} async-done(((bf16[8,4,512]{2,1,0:T(4,128)(2,1)}), bf16[8,4,512]{2,1,0:T(4,128)(2,1)S(1)}, u32[]{:S(2)}, u32[]{:S(2)}) %all-to-all-start.5) | async-done | bytes 32800 | tf_op jit(solution)/shard_map/all_to_all | solution.py:112
  246.9 11.4 %all_to_all.119 = bf16[8,4,4096]{2,1,0:T(4,128)(2,1)} all-to-all(bf16[8,4,4096]{2,1,0:T(4,128)(2,1)S(1)} %bitcast.176), channel_id=1, replica_groups=mesh['section'=4,'expert'=8] {'expert'}, dimensions={0} | all-to-all | bytes 524288 | tf_op jit(solution)/shard_map/all_to_all | solution.py:123
  258.3 1.0 reshape.390
  259.3 3.1 fusion.21
  262.4 4.0 convolution_convert_fusion.1
  266.4 1.1 reshape.391
  267.5 10.8 %all_to_all.120 = bf16[8,4,4096]{2,1,0:T(4,128)(2,1)S(1)} all-to-all(bf16[8,4,4096]{2,1,0:T(4,128)(2,1)S(1)} %reshape.391), channel_id=1, replica_groups=mesh['section'=4,'expert'=8] {'expert'}, dimensions={0} | all-to-all | bytes 524288 | tf_op jit(solution)/shard_map/all_to_all | solution.py:128
  278.7 3.3 collective-permute-done.1
  282.3 32.7 %all-gather.4 = bf16[8,4,4096]{2,1,0:T(4,128)(2,1)} all-gather(bf16[1,4,4096]{2,1,0:T(4,128)(2,1)S(1)} %fusion.89), channel_id=1, replica_groups=mesh['section'=4,'expert'=8] {'expert'}, dimensions={0}, use_global_device_ids=true | all-gather | bytes 294912 | tf_op jit(solution)/shard_map/all_gather | solution.py:84
  315.1 1.0 reshape.427
  316.1 3.6 multiply_reduce_fusion.1
  319.9 9.4 %all_to_all.121 = bf16[8,4,512]{2,1,0:T(4,128)(2,1)S(1)} all-to-all(bf16[8,4,512]{2,1,0:T(4,128)(2,1)S(1)} %all_to_all.98), channel_id=1, replica_groups=mesh['section'=4,'expert'=8] {'expert'}, dimensions={0} | all-to-all | bytes 65536 | tf_op jit(solution)/shard_map/all_to_all | solution.py:92
  329.3 1.2 fusion.30
  330.5 1.2 convolution_convert_fusion.6
  331.8 32.9 %all-gather.5 = bf16[8,4,4096]{2,1,0:T(4,128)(2,1)} all-gather(bf16[1,4,4096]{2,1,0:T(4,128)(2,1)S(1)} %reshape.420), channel_id=1, replica_groups=mesh['section'=4,'expert'=8] {'expert'}, dimensions={0}, use_global_device_ids=true | all-gather | bytes 294912 | tf_op jit(solution)/shard_map/all_gather | solution.py:108
  364.7 1.0 reshape.421
  365.7 3.0 fusion.46
  368.7 0.7 all_to_all.101
  369.3 3.3 all-to-all-start.9
  372.7 0.7 convert_reduce_fusion
  373.3 6.0 %all-to-all-done.9 = bf16[8,4,512]{2,1,0:T(4,128)(2,1)S(1)} async-done(((bf16[8,4,512]{2,1,0:T(4,128)(2,1)}), bf16[8,4,512]{2,1,0:T(4,128)(2,1)S(1)}, u32[]{:S(2)}, u32[]{:S(2)}) %all-to-all-start.9) | async-done | bytes 32800 | tf_op jit(solution)/shard_map/all_to_all | solution.py:112
  379.9 11.4 %all_to_all.122 = bf16[8,4,4096]{2,1,0:T(4,128)(2,1)} all-to-all(bf16[8,4,4096]{2,1,0:T(4,128)(2,1)S(1)} %bitcast.177), channel_id=1, replica_groups=mesh['section'=4,'expert'=8] {'expert'}, dimensions={0} | all-to-all | bytes 524288 | tf_op jit(solution)/shard_map/all_to_all | solution.py:123
  391.3 1.0 reshape.399
  392.3 2.4 fusion.19
  394.7 4.0 convolution_convert_fusion
  398.7 1.1 reshape.400
  399.8 10.8 %all_to_all.123 = bf16[8,4,4096]{2,1,0:T(4,128)(2,1)S(1)} all-to-all(bf16[8,4,4096]{2,1,0:T(4,128)(2,1)S(1)} %reshape.400), channel_id=1, replica_groups=mesh['section'=4,'expert'=8] {'expert'}, dimensions={0} | all-to-all | bytes 524288 | tf_op jit(solution)/shard_map/all_to_all | solution.py:128
  410.8 1.5 fusion.3
  (107 shorter events, 7.8 us)
Async XLA Ops:
  0.0 128.1 %copy-start = (bf16[1,1,384,4096]{3,2,1,0:T(8,128)(2,1)S(1)}, bf16[1,1,384,4096]{3,2,1,0:T(8,128)(2,1)}, u32[]{:S(2)}) copy-start(bf16[1,1,384,4096]{3,2,1,0:T(8,128)(2,1)} %param.23) | copy-start | bytes 9437188
  0.0 6.6 %copy-start.2 = (bf16[1,4096]{1,0:T(2,128)(2,1)S(1)}, bf16[1,4096]{1,0:T(2,128)(2,1)}, u32[]{:S(2)}) copy-start(bf16[1,4096]{1,0:T(2,128)(2,1)} %param.14) | copy-start | bytes 24580
  0.0 6.6 %copy-start.1 = (bf16[1,4,4096]{2,1,0:T(4,128)(2,1)S(1)}, bf16[1,4,4096]{2,1,0:T(4,128)(2,1)}, u32[]{:S(2)}) copy-start(bf16[1,4,4096]{2,1,0:T(4,128)(2,1)} %param.13) | copy-start | bytes 98308
  6.6 45.8 %copy-start.4 = (s32[1,3,4,2]{2,3,1,0:T(2,128)S(1)}, s32[1,3,4,2]{2,3,1,0:T(2,128)}, u32[]{:S(2)}) copy-start(s32[1,3,4,2]{2,3,1,0:T(2,128)} %param.24) | copy-start | bytes 292
  6.6 47.5 %copy-start.5 = (f32[1,3,4,2]{2,3,1,0:T(2,128)S(1)}, f32[1,3,4,2]{2,3,1,0:T(2,128)}, u32[]{:S(2)}) copy-start(f32[1,3,4,2]{2,3,1,0:T(2,128)} %param.25) | copy-start | bytes 292
  42.4 13.9 %copy-start.8 = (s32[1,3,4]{2,0,1:T(1,128)S(1)}, s32[1,3,4]{2,0,1:T(1,128)}, u32[]{:S(2)}) copy-start(s32[1,3,4]{2,0,1:T(1,128)} %param.19) | copy-start | bytes 148
  46.9 12.9 %all-to-all-start = ((bf16[8,4,512]{2,1,0:T(4,128)(2,1)}), bf16[8,4,512]{2,1,0:T(4,128)(2,1)S(1)}, u32[]{:S(2)}, u32[]{:S(2)}) async-start(bf16[8,4,512]{2,1,0:T(4,128)(2,1)} %all_to_all.84), calls=%async_computation | async-start | bytes 65536 | tf_op jit(solution)/shard_map/all_to_all | solution.py:92
  59.8 45.7 %copy-start.3 = (bf16[1,4096]{1,0:T(2,128)(2,1)S(1)}, bf16[1,4096]{1,0:T(2,128)(2,1)}, u32[]{:S(2)}) copy-start(bf16[1,4096]{1,0:T(2,128)(2,1)} %param.20) | copy-start | bytes 24580
  100.0 12.1 %all-to-all-start.1 = ((bf16[8,4,512]{2,1,0:T(4,128)(2,1)}), bf16[8,4,512]{2,1,0:T(4,128)(2,1)S(1)}, u32[]{:S(2)}, u32[]{:S(2)}) async-start(bf16[8,4,512]{2,1,0:T(4,128)(2,1)} %all_to_all.87), calls=%async_computation.1 | async-start | bytes 65536 | tf_op jit(solution)/shard_map/all_to_all | solution.py:112
  144.4 3.4 collective-permute-start
  186.3 10.0 %all-to-all-start.4 = ((bf16[8,4,512]{2,1,0:T(4,128)(2,1)}), bf16[8,4,512]{2,1,0:T(4,128)(2,1)S(1)}, u32[]{:S(2)}, u32[]{:S(2)}) async-start(bf16[8,4,512]{2,1,0:T(4,128)(2,1)} %all_to_all.91), calls=%async_computation.4 | async-start | bytes 65536 | tf_op jit(solution)/shard_map/all_to_all | solution.py:92
  196.3 43.4 %copy-start.6 = (f32[4,2]{0,1:T(2,128)S(1)}, f32[4,2]{0,1:T(2,128)}, u32[]{:S(2)}) copy-start(f32[4,2]{0,1:T(2,128)} %get-tuple-element.22) | copy-start | bytes 100
  236.4 10.0 %all-to-all-start.5 = ((bf16[8,4,512]{2,1,0:T(4,128)(2,1)}), bf16[8,4,512]{2,1,0:T(4,128)(2,1)S(1)}, u32[]{:S(2)}, u32[]{:S(2)}) async-start(bf16[8,4,512]{2,1,0:T(4,128)(2,1)} %all_to_all.94), calls=%async_computation.5 | async-start | bytes 65536 | tf_op jit(solution)/shard_map/all_to_all | solution.py:112
  278.5 50.8 %copy-start.7 = (pred[4,64]{1,0:T(4,128)(4,1)S(1)}, pred[4,64]{1,0:T(4,128)(4,1)}, u32[]{:S(2)}) copy-start(pred[4,64]{1,0:T(4,128)(4,1)} %get-tuple-element.38) | copy-start | bytes 772
  278.7 3.4 collective-permute-start.1
  369.3 10.0 %all-to-all-start.9 = ((bf16[8,4,512]{2,1,0:T(4,128)(2,1)}), bf16[8,4,512]{2,1,0:T(4,128)(2,1)S(1)}, u32[]{:S(2)}, u32[]{:S(2)}) async-start(bf16[8,4,512]{2,1,0:T(4,128)(2,1)} %all_to_all.101), calls=%async_computation.9 | async-start | bytes 65536 | tf_op jit(solution)/shard_map/all_to_all | solution.py:112
where the time goes:
time: 417 us; the launch traced here: 412 us
  blocking collectives  275 us (66%)
  matrix products  50.1 us (12%)
  waiting for transfers between devices  31.1 us (7%)
  local copies, waits for them, and re-layouts  28.9 us (7%)
  starting transfers between devices  21.1 us (5%)
  other arithmetic  5.42 us (1%)
    all_gather x3, blocking collectives, body(): project_piece_rows = lax.all_gather(normed, 'expert', axis=0, tiled=True)  100 us
    all_gather x3, blocking collectives, body(): lax.all_gather(context, 'expert', axis=0, tiled=True)  99.2 us
    all_to_all x3, blocking collectives, body(): lax.all_to_all(outgoing, 'expert', split_axis=0, concat_axis=0, tiled=True)  34.1 us
    all_to_all x3, blocking collectives, body(): lax.all_to_all(half_out, 'expert', split_axis=0, concat_axis=0, tiled=True)  32.4 us
    all_to_all x3, waiting for transfers between devices, body(): lax.all_to_all(out_cols.astype(jnp.bfloat16), 'expert', split_axis=0, con...  19.1 us
    all_to_all x3, starting transfers between devices, body(): lax.all_to_all(out_cols.astype(jnp.bfloat16), 'expert', split_axis=0, con...  12.1 us
    dot_general x3, matrix products, expert_half(): jnp.dot(active, down_w, preferred_element_type=jnp.float32)  12.1 us
    dot_general x3, matrix products, body(): jnp.dot(project_piece_rows, query_w, preferred_element_type=jnp.float32)  10.9 us
  transfers between devices with their start and end apart: 7, of which 6 were waited for; matrix products, arithmetic and copies ran while one was open for 2% of the time, Pallas kernels for 0%

commit v1 on v0

v1 whole, which is shorter than its diff:
```python
import jax
import jax.numpy as jnp
from jax import lax
from jax.sharding import PartitionSpec as P

STEPS = 3


def passed_along(array, axis, by):
    length = lax.axis_size(axis)
    return lax.ppermute(array, axis, [(i, (i + by) % length) for i in range(length)])


def everyones(array):
    devices = lax.axis_size("expert")
    copies = jnp.broadcast_to(array[None], (devices,) + array.shape)
    return lax.all_to_all(copies, "expert", split_axis=0, concat_axis=0, tiled=True)


def rms_scaled(values):
    return values * lax.rsqrt(jnp.mean(values * values, axis=-1, keepdims=True) + 1e-06)


def coefficients(route_ids, gate_vals, experts):
    shares = gate_vals / jnp.sum(gate_vals, axis=-1, keepdims=True)
    chosen = route_ids[:, :, None] == jnp.arange(experts, dtype=jnp.int32)[None, None, :]
    return jnp.sum(jnp.where(chosen, shares[:, :, None], 0.0), axis=1)


def body(
    hidden_in,
    attn_gain,
    w_query,
    w_out,
    key_cache,
    value_cache,
    lengths,
    ffn_gain,
    w_gate,
    w_up,
    w_down,
    routes,
    gates,
):
    devices = lax.axis_size("expert")
    me = lax.axis_index("expert")
    experts = devices // 2
    row_count = hidden_in.shape[1]
    all_rows = row_count * devices
    model_width = hidden_in.shape[2]
    head_dim = key_cache.shape[-1]
    kv_heads = key_cache.shape[-2]
    cache_len = key_cache.shape[-3]
    query_w = w_query[0]
    out_w = w_out[0]
    local_heads = query_w.shape[1] // head_dim
    all_heads = local_heads * devices
    group_size = all_heads // kv_heads
    gate_w = w_gate[0, 0]
    up_w = w_up[0, 0]
    down_w = w_down[0, 0]
    gain_attn = attn_gain[0].astype(jnp.float32)
    gain_ffn = ffn_gain[0].astype(jnp.float32)
    hidden_state = hidden_in[0]
    for layer_step in range(STEPS):
        states = everyones(hidden_state).reshape(all_rows, model_width)
        states32 = states.astype(jnp.float32)
        normed = (rms_scaled(states32) * gain_attn).astype(jnp.bfloat16)
        raw_query = lax.optimization_barrier(
            jnp.dot(normed, query_w, preferred_element_type=jnp.float32)
        )
        heads_view = raw_query.reshape(all_rows, local_heads, head_dim)
        own_q = rms_scaled(heads_view).astype(jnp.bfloat16).reshape(all_rows, local_heads * head_dim)
        queries = lax.all_to_all(own_q, "expert", split_axis=0, concat_axis=1, tiled=True)
        queries = queries.reshape(row_count, kv_heads, group_size, head_dim)
        scores = jnp.einsum(
            "rkgd,rpkd->rkgp", queries, key_cache[0, layer_step], preferred_element_type=jnp.float32
        ) * head_dim ** (-0.5)
        in_cache = jnp.arange(cache_len, dtype=jnp.int32)[None, :] < lengths[0, layer_step][:, None]
        exp_scores = jnp.where(in_cache[:, None, None, :], jnp.exp(scores), 0.0)
        weights = (exp_scores / jnp.sum(exp_scores, axis=-1, keepdims=True)).astype(jnp.bfloat16)
        context = jnp.einsum(
            "rkgp,rpkd->rkgd",
            weights,
            value_cache[0, layer_step],
            preferred_element_type=jnp.float32,
        )
        context = context.astype(jnp.bfloat16).reshape(row_count, all_heads * head_dim)
        out_cols = jnp.dot(
            everyones(context).reshape(all_rows, all_heads * head_dim),
            out_w,
            preferred_element_type=jnp.float32,
        ).astype(jnp.bfloat16)
        attended = everyones(out_cols).transpose(1, 0, 2).reshape(all_rows, model_width)
        middle = states32 + attended.astype(jnp.float32)
        ffn_in = (rms_scaled(middle) * gain_ffn).astype(jnp.bfloat16)
        gate_val = jnp.dot(ffn_in, gate_w, preferred_element_type=jnp.float32)
        up_val = jnp.dot(ffn_in, up_w, preferred_element_type=jnp.float32)
        active = (jax.nn.silu(gate_val) * up_val).astype(jnp.bfloat16)
        half_out = jnp.dot(active, down_w, preferred_element_type=jnp.float32).astype(jnp.bfloat16)
        returned = lax.all_to_all(half_out, "expert", split_axis=0, concat_axis=0, tiled=True)
        paired_out = jnp.sum(
            returned.astype(jnp.float32).reshape(experts, 2, row_count, model_width), axis=1
        ).astype(jnp.bfloat16)
        coeffs = coefficients(routes[0, layer_step], gates[0, layer_step], experts)
        combined = lax.optimization_barrier(paired_out).astype(jnp.float32)
        expert_sum = jnp.sum(coeffs.T[:, :, None] * combined, axis=0)
        own_middle = lax.dynamic_slice_in_dim(middle, me * row_count, row_count, 0)
        result = (own_middle + expert_sum).astype(jnp.bfloat16)
        if layer_step + 1 < STEPS:
            hidden_state = passed_along(result, "section", 1)
    return result[None]


def solution(mesh):
    return jax.shard_map(
        body,
        mesh=mesh,
        in_specs=(
            P("section", "expert", None),
            P("section", None),
            P("section", None, "expert"),
            P("section", None, "expert"),
            P("section", None, "expert", None, None, None),
            P("section", None, "expert", None, None, None),
            P("section", None, "expert"),
            P("section", None),
            P("section", "expert", None, None),
            P("section", "expert", None, None),
            P("section", "expert", None, None),
            P("section", None, "expert", None),
            P("section", None, "expert", None),
        ),
        out_specs=P("section", "expert", None),
        check_vma=False,
    )
```

time: 417 us -> 298 us (0.71)
  blocking collectives: 275 us -> 87.5 us
  other arithmetic: 5.42 us -> 31.4 us
  local copies, waits for them, and re-layouts: 28.9 us -> 53 us
  waiting for transfers between devices: 31.1 us -> 44.9 us
  starting transfers between devices: 21.1 us -> 30.6 us
    all_gather x6 -> x0, blocking collectives: 199 us -> none  [the longest x3 100 us: body(): project_piece_rows = lax.all_gather(normed, 'expert', axis=0, tiled=True)]
    convert_element_type x3 -> x18, local copies, waits for them, and re-layouts: 0.06 us -> 28.5 us  [the longest x9 15.6 us: body(): middle = states32 + attended.astype(jnp.float32)]
    all_to_all x5 -> x7, waiting for transfers between devices: 24.4 us -> 38.3 us  [the longest x3 15.4 us: body(): lax.all_to_all(half_out, 'expert', split_axis=0, concat_axis=0, tiled=True)]
    all_to_all x7 -> x8, blocking collectives: 75.9 us -> 87.5 us  [the longest x7 77.7 us: everyones(): lax.all_to_all(copies, 'expert', split_axis=0, concat_axis=0, tiled=True)]
    convert_element_type x9 -> x11, other arithmetic: 0.3 us -> 10.7 us  [the longest x3 5.92 us: body(): ffn_in = (rms_scaled(middle) * gain_ffn).astype(jnp.bfloat16)]
    all_to_all x5 -> x7, starting transfers between devices: 21 us -> 30.5 us  [the longest x3 12.1 us: body(): lax.all_to_all(half_out, 'expert', split_axis=0, concat_axis=0, tiled=True)]
    dot_general x1 -> x0, local copies, waits for them, and re-layouts: 6.56 us -> none  [body(): jnp.dot(project_piece_rows, query_w, preferred_element_type=jnp.float32)]
    reduce_sum x6 -> x9, other arithmetic: 0.89 us -> 7.4 us  [rms_scaled(): jnp.mean(values * values, axis=-1, keepdims=True) + 1e-06]
  transfers between devices with their start and end apart: 7 -> 9, of which waited for: 6 -> 9; matrix products, arithmetic and copies ran while one was open for 2% -> 6% of each run, Pallas kernels for 0% -> 0%
where the time goes in v1:
time: 298 us; the launch traced here: 295 us
  blocking collectives  87.5 us (29%)
  local copies, waits for them, and re-layouts  53 us (18%)
  matrix products  47 us (16%)
  waiting for transfers between devices  44.9 us (15%)
  other arithmetic  31.4 us (11%)
  starting transfers between devices  30.6 us (10%)
    all_to_all x7, blocking collectives, everyones(): lax.all_to_all(copies, 'expert', split_axis=0, concat_axis=0, tiled=True)  77.7 us
    convert_element_type x9, local copies, waits for them, and re-layouts, body(): middle = states32 + attended.astype(jnp.float32)  15.6 us
    all_to_all x3, waiting for transfers between devices, body(): lax.all_to_all(half_out, 'expert', split_axis=0, concat_axis=0, tiled=True)  15.4 us
    dot_general x3, matrix products, body(): jnp.dot(active, down_w, preferred_element_type=jnp.float32)  12.4 us
    all_to_all x3, starting transfers between devices, body(): lax.all_to_all(half_out, 'expert', split_axis=0, concat_axis=0, tiled=True)  12.1 us
    all_to_all x2, waiting for transfers between devices, body(): lax.all_to_all(own_q, 'expert', split_axis=0, concat_axis=1, tiled=True)  12.1 us
    all_to_all x2, starting transfers between devices, everyones(): lax.all_to_all(copies, 'expert', split_axis=0, concat_axis=0, tiled=True)  11.3 us
    all_to_all x2, waiting for transfers between devices, everyones(): lax.all_to_all(copies, 'expert', split_axis=0, concat_axis=0, tiled=True)  10.8 us
  transfers between devices with their start and end apart: 9, of which 9 were waited for; matrix products, arithmetic and copies ran while one was open for 6% of the time, Pallas kernels for 0%

profile of v1, /device:TPU:0, one launch (start us, length us, event | category | flops | bytes accessed | tf_op | source)
XLA Modules:
  0.0 294.9 jit_solution(7240882575211964411)
XLA Ops:
  0.0 1.7 broadcast_in_dim.77
  1.7 7.3 %all-to-all-start = ((bf16[8,4,4096]{2,1,0:T(4,128)(2,1)}), bf16[8,4,4096]{2,1,0:T(4,128)(2,1)S(1)}, u32[]{:S(2)}, u32[]{:S(2)}) async-start(bf16[8,4,4096]{2,1,0:T(4,128)(2,1)} %broadcast_in_dim.77), calls=%async_computation | async-start | bytes 524288 | tf_op jit(solution)/shard_map/all_to_all | solution.py:17
  9.0 2.2 fusion.110
  13.1 2.2 fusion.109
  15.3 2.6 all-to-all-done
  19.0 1.7 convert_element_type.224
  20.8 3.1 %fusion.10 = f32[32,512]{1,0:T(8,128)S(1)} fusion(bf16[32,4096]{1,0:T(8,128)(2,1)} %convert_element_type.224, bf16[1,4096,512]{2,1,0:T(8,128)(2,1)} %param.15), kind=kOutput, calls=%fused_computation.13 | convolution fusion | flops 134217728 | bytes 4521984 | tf_op jit(solution)/shard_map/dot_general | solution.py:70
  27.7 3.6 %all-to-all-start.1 = ((bf16[8,4,512]{2,1,0:T(4,128)(2,1)}), bf16[8,4,512]{2,1,0:T(4,128)(2,1)S(1)}, u32[]{:S(2)}, u32[]{:S(2)}) async-start(bf16[8,4,512]{2,1,0:T(4,128)(2,1)} %all_to_all.88), calls=%async_computation.1 | async-start | bytes 65536 | tf_op jit(solution)/shard_map/all_to_all | solution.py:74
  31.3 6.6 %all-to-all-done.1 = bf16[8,4,512]{2,1,0:T(4,128)(2,1)S(1)} async-done(((bf16[8,4,512]{2,1,0:T(4,128)(2,1)}), bf16[8,4,512]{2,1,0:T(4,128)(2,1)S(1)}, u32[]{:S(2)}, u32[]{:S(2)}) %all-to-all-start.1) | async-done | bytes 32800 | tf_op jit(solution)/shard_map/all_to_all | solution.py:74
  38.0 1.8 fusion.30
  41.2 11.3 %all_to_all.129 = bf16[8,4,4096]{2,1,0:T(4,128)(2,1)} all-to-all(bf16[8,4,4096]{2,1,0:T(4,128)(2,1)S(1)} %broadcast_in_dim.81), channel_id=1, replica_groups=mesh['section'=4,'expert'=8] {'expert'}, dimensions={0} | all-to-all | bytes 524288 | tf_op jit(solution)/shard_map/all_to_all | solution.py:17
  52.5 1.7 reshape.416
  54.2 3.1 %fusion.42 = bf16[32,512]{1,0:T(8,128)(2,1)S(1)} fusion(bf16[32,4096]{1,0:T(8,128)(2,1)} %reshape.416, bf16[1,4096,512]{2,1,0:T(8,128)(2,1)} %param.16), kind=kOutput, calls=%fused_computation.45 | convolution fusion | flops 134234112 | bytes 4489216 | tf_op jit(solution)/shard_map/dot_general | solution.py:89
  58.0 4.0 %all-to-all-start.3 = ((bf16[8,32,512]{2,1,0:T(8,128)(2,1)}), bf16[8,32,512]{2,1,0:T(8,128)(2,1)}, u32[]{:S(2)}, u32[]{:S(2)}) async-start(bf16[8,32,512]{2,1,0:T(8,128)(2,1)} %broadcast_in_dim.82), calls=%async_computation.3 | async-start | bytes 524288 | tf_op jit(solution)/shard_map/all_to_all | solution.py:17
  62.1 8.2 %all-to-all-done.3 = bf16[8,32,512]{2,1,0:T(8,128)(2,1)} async-done(((bf16[8,32,512]{2,1,0:T(8,128)(2,1)}), bf16[8,32,512]{2,1,0:T(8,128)(2,1)}, u32[]{:S(2)}, u32[]{:S(2)}) %all-to-all-start.3) | async-done | bytes 262176 | tf_op jit(solution)/shard_map/all_to_all | solution.py:17
  70.3 1.8 convert_bitcast_fusion.4
  73.3 2.2 reshape.424
  76.8 2.0 multiply_convert_fusion.4
  78.7 1.7 convert_element_type.235
  80.5 2.5 fusion.25
  83.0 4.1 %convolution_convert_fusion.2 = bf16[32,4096]{1,0:T(8,128)(2,1)} fusion(bf16[1,1,384,4096]{3,2,1,0:T(8,128)(2,1)S(1)} %copy-done, bf16[32,4096]{1,0:T(8,128)(2,1)} %convert_element_type.235, bf16[1,1,4096,384]{3,2,1,0:T(8,128)(2,1)} %param.22, f32[32,384]{1,0:T(8,128)S(1)} %fusion.25), kind=kOutput, calls=%fused_computation.2 | convolution fusion | flops 201531392 | bytes 6864896 | tf_op jit(solution)/shard_map/dot_general | solution.py:100
  87.2 1.8 all_to_all.93
  88.9 4.0 %all-to-all-start.4 = ((bf16[8,4,4096]{2,1,0:T(4,128)(2,1)}), bf16[8,4,4096]{2,1,0:T(4,128)(2,1)}, u32[]{:S(2)}, u32[]{:S(2)}) async-start(bf16[8,4,4096]{2,1,0:T(4,128)(2,1)} %all_to_all.93), calls=%async_computation.4 | async-start | bytes 524288 | tf_op jit(solution)/shard_map/all_to_all | solution.py:101
  94.1 1.9 copy.98
  96.0 5.2 %all-to-all-done.4 = bf16[8,4,4096]{2,1,0:T(4,128)(2,1)} async-done(((bf16[8,4,4096]{2,1,0:T(4,128)(2,1)}), bf16[8,4,4096]{2,1,0:T(4,128)(2,1)}, u32[]{:S(2)}, u32[]{:S(2)}) %all-to-all-start.4) | async-done | bytes 262176 | tf_op jit(solution)/shard_map/all_to_all | solution.py:101
  103.6 3.3 %collective-permute-done = bf16[4,4096]{1,0:T(4,128)(2,1)S(1)} collective-permute-done((bf16[4,4096]{1,0:T(4,128)(2,1)S(1)}, bf16[4,4096]{1,0:T(4,128)(2,1)S(1)}, u32[]{:S(2)}, u32[]{:S(2)}) %collective-permute-start) | collective-permute-done | bytes 32800 | tf_op jit(solution)/shard_map/ppermute | solution.py:11
  107.0 11.2 %all_to_all.130 = bf16[8,4,4096]{2,1,0:T(4,128)(2,1)S(1)} all-to-all(bf16[8,4,4096]{2,1,0:T(4,128)(2,1)S(1)} %broadcast_in_dim.154), channel_id=1, replica_groups=mesh['section'=4,'expert'=8] {'expert'}, dimensions={0} | all-to-all | bytes 524288 | tf_op jit(solution)/shard_map/all_to_all | solution.py:17
  119.3 1.7 convert_element_type.244
  121.0 3.1 %fusion.8 = f32[32,512]{1,0:T(8,128)S(1)} fusion(bf16[32,4096]{1,0:T(8,128)(2,1)} %convert_element_type.244, bf16[1,4096,512]{2,1,0:T(8,128)(2,1)} %param.15), kind=kOutput, calls=%fused_computation.11 | convolution fusion | flops 134217728 | bytes 4521984 | tf_op jit(solution)/shard_map/dot_general | solution.py:70
  128.0 3.5 %all-to-all-start.6 = ((bf16[8,4,512]{2,1,0:T(4,128)(2,1)}), bf16[8,4,512]{2,1,0:T(4,128)(2,1)S(1)}, u32[]{:S(2)}, u32[]{:S(2)}) async-start(bf16[8,4,512]{2,1,0:T(4,128)(2,1)} %all_to_all.97), calls=%async_computation.6 | async-start | bytes 65536 | tf_op jit(solution)/shard_map/all_to_all | solution.py:74
  132.6 5.5 %all-to-all-done.6 = bf16[8,4,512]{2,1,0:T(4,128)(2,1)S(1)} async-done(((bf16[8,4,512]{2,1,0:T(4,128)(2,1)}), bf16[8,4,512]{2,1,0:T(4,128)(2,1)S(1)}, u32[]{:S(2)}, u32[]{:S(2)}) %all-to-all-start.6) | async-done | bytes 32800 | tf_op jit(solution)/shard_map/all_to_all | solution.py:74
  138.2 1.8 fusion.31
  141.4 11.3 %all_to_all.131 = bf16[8,4,4096]{2,1,0:T(4,128)(2,1)} all-to-all(bf16[8,4,4096]{2,1,0:T(4,128)(2,1)S(1)} %broadcast_in_dim.157), channel_id=1, replica_groups=mesh['section'=4,'expert'=8] {'expert'}, dimensions={0} | all-to-all | bytes 524288 | tf_op jit(solution)/shard_map/all_to_all | solution.py:17
  152.7 1.7 reshape.418
  154.4 3.1 %fusion.45 = bf16[32,512]{1,0:T(8,128)(2,1)S(1)} fusion(bf16[32,4096]{1,0:T(8,128)(2,1)} %reshape.418, bf16[1,4096,512]{2,1,0:T(8,128)(2,1)} %param.16), kind=kOutput, calls=%fused_computation.46 | convolution fusion | flops 134234112 | bytes 4489216 | tf_op jit(solution)/shard_map/dot_general | solution.py:89
  157.5 10.9 %all_to_all.132 = bf16[8,32,512]{2,1,0:T(8,128)(2,1)S(1)} all-to-all(bf16[8,32,512]{2,1,0:T(8,128)(2,1)S(1)} %broadcast_in_dim.158), channel_id=1, replica_groups=mesh['section'=4,'expert'=8] {'expert'}, dimensions={0} | all-to-all | bytes 524288 | tf_op jit(solution)/shard_map/all_to_all | solution.py:17
  170.4 2.2 reshape.428
  173.9 2.0 multiply_convert_fusion.2
  175.9 1.7 convert_element_type.255
  177.6 2.5 fusion.23
  180.1 4.1 %convolution_convert_fusion.1 = bf16[32,4096]{1,0:T(8,128)(2,1)} fusion(bf16[1,1,384,4096]{3,2,1,0:T(8,128)(2,1)S(1)} %copy-done, bf16[32,4096]{1,0:T(8,128)(2,1)} %convert_element_type.255, bf16[1,1,4096,384]{3,2,1,0:T(8,128)(2,1)} %param.22, f32[32,384]{1,0:T(8,128)S(1)} %fusion.23), kind=kOutput, calls=%fused_computation.1 | convolution fusion | flops 201531392 | bytes 6864896 | tf_op jit(solution)/shard_map/dot_general | solution.py:100
  184.2 1.8 all_to_all.102
  186.0 4.0 %all-to-all-start.9 = ((bf16[8,4,4096]{2,1,0:T(4,128)(2,1)}), bf16[8,4,4096]{2,1,0:T(4,128)(2,1)}, u32[]{:S(2)}, u32[]{:S(2)}) async-start(bf16[8,4,4096]{2,1,0:T(4,128)(2,1)} %all_to_all.102), calls=%async_computation.9 | async-start | bytes 524288 | tf_op jit(solution)/shard_map/all_to_all | solution.py:101
  191.7 1.9 copy.99
  193.6 4.7 %all-to-all-done.9 = bf16[8,4,4096]{2,1,0:T(4,128)(2,1)} async-done(((bf16[8,4,4096]{2,1,0:T(4,128)(2,1)}), bf16[8,4,4096]{2,1,0:T(4,128)(2,1)}, u32[]{:S(2)}, u32[]{:S(2)}) %all-to-all-start.9) | async-done | bytes 262176 | tf_op jit(solution)/shard_map/all_to_all | solution.py:101
  200.7 3.3 %collective-permute-done.1 = bf16[4,4096]{1,0:T(4,128)(2,1)S(1)} collective-permute-done((bf16[4,4096]{1,0:T(4,128)(2,1)S(1)}, bf16[4,4096]{1,0:T(4,128)(2,1)S(1)}, u32[]{:S(2)}, u32[]{:S(2)}) %collective-permute-start.1) | collective-permute-done | bytes 32800 | tf_op jit(solution)/shard_map/ppermute | solution.py:11
  204.1 10.9 %all_to_all.133 = bf16[8,4,4096]{2,1,0:T(4,128)(2,1)S(1)} all-to-all(bf16[8,4,4096]{2,1,0:T(4,128)(2,1)S(1)} %broadcast_in_dim.160), channel_id=1, replica_groups=mesh['section'=4,'expert'=8] {'expert'}, dimensions={0} | all-to-all | bytes 524288 | tf_op jit(solution)/shard_map/all_to_all | solution.py:17
  216.1 1.7 convert_element_type.264
  217.8 3.1 %fusion.6 = f32[32,512]{1,0:T(8,128)S(1)} fusion(bf16[32,4096]{1,0:T(8,128)(2,1)} %convert_element_type.264, bf16[1,4096,512]{2,1,0:T(8,128)(2,1)} %param.15), kind=kOutput, calls=%fused_computation.9 | convolution fusion | flops 134217728 | bytes 4521984 | tf_op jit(solution)/shard_map/dot_general | solution.py:70
  222.7 9.8 %all_to_all.134 = bf16[8,4,512]{2,1,0:T(4,128)(2,1)S(1)} all-to-all(bf16[8,4,512]{2,1,0:T(4,128)(2,1)S(1)} %all_to_all.106), channel_id=1, replica_groups=mesh['section'=4,'expert'=8] {'expert'}, dimensions={0} | all-to-all | bytes 65536 | tf_op jit(solution)/shard_map/all_to_all | solution.py:74
  235.0 11.3 %all_to_all.135 = bf16[8,4,4096]{2,1,0:T(4,128)(2,1)} all-to-all(bf16[8,4,4096]{2,1,0:T(4,128)(2,1)S(1)} %broadcast_in_dim.163), channel_id=1, replica_groups=mesh['section'=4,'expert'=8] {'expert'}, dimensions={0} | all-to-all | bytes 524288 | tf_op jit(solution)/shard_map/all_to_all | solution.py:17
  246.3 1.7 reshape.420
  248.0 3.1 %fusion.48 = bf16[32,512]{1,0:T(8,128)(2,1)S(1)} fusion(bf16[32,4096]{1,0:T(8,128)(2,1)} %reshape.420, bf16[1,4096,512]{2,1,0:T(8,128)(2,1)} %param.16), kind=kOutput, calls=%fused_computation.47 | convolution fusion | flops 134234112 | bytes 4489216 | tf_op jit(solution)/shard_map/dot_general | solution.py:89
  251.1 10.9 %all_to_all.136 = bf16[8,32,512]{2,1,0:T(8,128)(2,1)S(1)} all-to-all(bf16[8,32,512]{2,1,0:T(8,128)(2,1)S(1)} %broadcast_in_dim.164), channel_id=1, replica_groups=mesh['section'=4,'expert'=8] {'expert'}, dimensions={0} | all-to-all | bytes 524288 | tf_op jit(solution)/shard_map/all_to_all | solution.py:17
  264.0 2.2 reshape.431
  267.5 2.0 multiply_convert_fusion
  269.5 1.7 convert_element_type.275
  271.2 2.5 fusion.21
  273.8 4.1 %convolution_convert_fusion = bf16[32,4096]{1,0:T(8,128)(2,1)} fusion(bf16[1,1,384,4096]{3,2,1,0:T(8,128)(2,1)S(1)} %copy-done, bf16[32,4096]{1,0:T(8,128)(2,1)} %convert_element_type.275, bf16[1,1,4096,384]{3,2,1,0:T(8,128)(2,1)} %param.22, f32[32,384]{1,0:T(8,128)S(1)} %fusion.21), kind=kOutput, calls=%fused_computation | convolution fusion | flops 201531392 | bytes 6864896 | tf_op jit(solution)/shard_map/dot_general | solution.py:100
  277.9 1.8 all_to_all.111
  279.6 4.0 %all-to-all-start.14 = ((bf16[8,4,4096]{2,1,0:T(4,128)(2,1)}), bf16[8,4,4096]{2,1,0:T(4,128)(2,1)}, u32[]{:S(2)}, u32[]{:S(2)}) async-start(bf16[8,4,4096]{2,1,0:T(4,128)(2,1)} %all_to_all.111), calls=%async_computation.14 | async-start | bytes 524288 | tf_op jit(solution)/shard_map/all_to_all | solution.py:101
  284.7 1.9 copy.100
  286.5 5.4 %all-to-all-done.14 = bf16[8,4,4096]{2,1,0:T(4,128)(2,1)} async-done(((bf16[8,4,4096]{2,1,0:T(4,128)(2,1)}), bf16[8,4,4096]{2,1,0:T(4,128)(2,1)}, u32[]{:S(2)}, u32[]{:S(2)}) %all-to-all-start.14) | async-done | bytes 262176 | tf_op jit(solution)/shard_map/all_to_all | solution.py:101
  293.2 1.6 fusion.93
  (98 shorter events, 41.0 us)
Async XLA Ops:
  0.0 83.0 %copy-start = (bf16[1,1,384,4096]{3,2,1,0:T(8,128)(2,1)S(1)}, bf16[1,1,384,4096]{3,2,1,0:T(8,128)(2,1)}, u32[]{:S(2)}) copy-start(bf16[1,1,384,4096]{3,2,1,0:T(8,128)(2,1)} %param.23) | copy-start | bytes 9437188
  1.7 16.2 %all-to-all-start = ((bf16[8,4,4096]{2,1,0:T(4,128)(2,1)}), bf16[8,4,4096]{2,1,0:T(4,128)(2,1)S(1)}, u32[]{:S(2)}, u32[]{:S(2)}) async-start(bf16[8,4,4096]{2,1,0:T(4,128)(2,1)} %broadcast_in_dim.77), calls=%async_computation | async-start | bytes 524288 | tf_op jit(solution)/shard_map/all_to_all | solution.py:17
  27.7 10.3 %all-to-all-start.1 = ((bf16[8,4,512]{2,1,0:T(4,128)(2,1)}), bf16[8,4,512]{2,1,0:T(4,128)(2,1)S(1)}, u32[]{:S(2)}, u32[]{:S(2)}) async-start(bf16[8,4,512]{2,1,0:T(4,128)(2,1)} %all_to_all.88), calls=%async_computation.1 | async-start | bytes 65536 | tf_op jit(solution)/shard_map/all_to_all | solution.py:74
  41.2 20.9 %copy-start.1 = (bf16[1,4096]{1,0:T(2,128)(2,1)S(1)}, bf16[1,4096]{1,0:T(2,128)(2,1)}, u32[]{:S(2)}) copy-start(bf16[1,4096]{1,0:T(2,128)(2,1)} %param.20) | copy-start | bytes 24580
  58.0 12.3 %all-to-all-start.3 = ((bf16[8,32,512]{2,1,0:T(8,128)(2,1)}), bf16[8,32,512]{2,1,0:T(8,128)(2,1)}, u32[]{:S(2)}, u32[]{:S(2)}) async-start(bf16[8,32,512]{2,1,0:T(8,128)(2,1)} %broadcast_in_dim.82), calls=%async_computation.3 | async-start | bytes 524288 | tf_op jit(solution)/shard_map/all_to_all | solution.py:17
  83.0 10.0 %copy-start.4 = (s32[1,3,4,2]{2,3,1,0:T(2,128)S(1)}, s32[1,3,4,2]{2,3,1,0:T(2,128)}, u32[]{:S(2)}) copy-start(s32[1,3,4,2]{2,3,1,0:T(2,128)} %param.24) | copy-start | bytes 292
  83.0 10.0 %copy-start.2 = (f32[1,3,4,2]{2,3,1,0:T(2,128)S(1)}, f32[1,3,4,2]{2,3,1,0:T(2,128)}, u32[]{:S(2)}) copy-start(f32[1,3,4,2]{2,3,1,0:T(2,128)} %param.25) | copy-start | bytes 292
  88.9 12.3 %all-to-all-start.4 = ((bf16[8,4,4096]{2,1,0:T(4,128)(2,1)}), bf16[8,4,4096]{2,1,0:T(4,128)(2,1)}, u32[]{:S(2)}, u32[]{:S(2)}) async-start(bf16[8,4,4096]{2,1,0:T(4,128)(2,1)} %all_to_all.93), calls=%async_computation.4 | async-start | bytes 524288 | tf_op jit(solution)/shard_map/all_to_all | solution.py:101
  103.5 3.4 %collective-permute-start = (bf16[4,4096]{1,0:T(4,128)(2,1)S(1)}, bf16[4,4096]{1,0:T(4,128)(2,1)S(1)}, u32[]{:S(2)}, u32[]{:S(2)}) collective-permute-start(bf16[4,4096]{1,0:T(4,128)(2,1)S(1)} %fusion.77), channel_id=1, source_target_pairs={{0,8},{8,16},{16,24},{24,0},{1,9},{9,17},{17,25},{25,1},{2,10},{10... | collective-permute-start | bytes 98312 | tf_op jit(solution)/shard_map/ppermute | solution.py:11
  128.0 10.1 %all-to-all-start.6 = ((bf16[8,4,512]{2,1,0:T(4,128)(2,1)}), bf16[8,4,512]{2,1,0:T(4,128)(2,1)S(1)}, u32[]{:S(2)}, u32[]{:S(2)}) async-start(bf16[8,4,512]{2,1,0:T(4,128)(2,1)} %all_to_all.97), calls=%async_computation.6 | async-start | bytes 65536 | tf_op jit(solution)/shard_map/all_to_all | solution.py:74
  186.0 12.3 %all-to-all-start.9 = ((bf16[8,4,4096]{2,1,0:T(4,128)(2,1)}), bf16[8,4,4096]{2,1,0:T(4,128)(2,1)}, u32[]{:S(2)}, u32[]{:S(2)}) async-start(bf16[8,4,4096]{2,1,0:T(4,128)(2,1)} %all_to_all.102), calls=%async_computation.9 | async-start | bytes 524288 | tf_op jit(solution)/shard_map/all_to_all | solution.py:101
  200.6 3.4 %collective-permute-start.1 = (bf16[4,4096]{1,0:T(4,128)(2,1)S(1)}, bf16[4,4096]{1,0:T(4,128)(2,1)S(1)}, u32[]{:S(2)}, u32[]{:S(2)}) collective-permute-start(bf16[4,4096]{1,0:T(4,128)(2,1)S(1)} %fusion.75), channel_id=1, source_target_pairs={{0,8},{8,16},{16,24},{24,0},{1,9},{9,17},{17,25},{25,1},{2,10},{10... | collective-permute-start | bytes 98312 | tf_op jit(solution)/shard_map/ppermute | solution.py:11
  273.8 9.9 %copy-start.3 = (f32[4,4]{1,0:T(4,128)S(1)}, f32[4,4]{1,0:T(4,128)}, u32[]{:S(2)}) copy-start(f32[4,4]{1,0:T(4,128)} %get-tuple-element.31) | copy-start | bytes 196
  279.6 12.3 %all-to-all-start.14 = ((bf16[8,4,4096]{2,1,0:T(4,128)(2,1)}), bf16[8,4,4096]{2,1,0:T(4,128)(2,1)}, u32[]{:S(2)}, u32[]{:S(2)}) async-start(bf16[8,4,4096]{2,1,0:T(4,128)(2,1)} %all_to_all.111), calls=%async_computation.14 | async-start | bytes 524288 | tf_op jit(solution)/shard_map/all_to_all | solution.py:101

commit v2 on v1

v2 whole, which is shorter than its diff:
```python
import functools

import jax
import jax.numpy as jnp
from jax import lax
from jax.experimental import pallas as pl
from jax.experimental.pallas import tpu as pltpu
from jax.sharding import PartitionSpec as P

STEPS = 3
EPS = 1e-06
LIMIT = 32 * 1024 * 1024
F32 = jnp.float32
BF16 = jnp.bfloat16


def passed_along(array, axis, by):
    length = lax.axis_size(axis)
    return lax.ppermute(array, axis, [(i, (i + by) % length) for i in range(length)])


def swapped(blocks):
    return lax.all_to_all(blocks, "expert", split_axis=0, concat_axis=0, tiled=True)


def everyones(array):
    devices = lax.axis_size("expert")
    return swapped(jnp.broadcast_to(array[None], (devices,) + array.shape))


def coefficients(route_ids, gate_vals, experts):
    shares = gate_vals / jnp.sum(gate_vals, axis=-1, keepdims=True)
    chosen = route_ids[..., None] == jnp.arange(experts, dtype=jnp.int32)
    return jnp.sum(jnp.where(chosen, shares[..., None], 0.0), axis=-2)


def whole(memory_space=pltpu.VMEM):
    return pl.BlockSpec(memory_space=memory_space)


def call(kernel, out, operands, specs, scratch, name, cost):
    single = not isinstance(out, tuple)
    return pl.pallas_call(
        kernel,
        out_shape=out,
        in_specs=specs,
        out_specs=whole() if single else tuple(whole() for _ in out),
        scratch_shapes=scratch,
        compiler_params=pltpu.CompilerParams(vmem_limit_bytes=LIMIT),
        cost_estimate=pl.CostEstimate(flops=cost[0], bytes_accessed=cost[1], transcendentals=0),
        name=name,
    )(*operands)


def normalize(source, gain_ref, target):
    rows, width = source.shape
    block = 16
    gain = gain_ref[...].astype(F32)
    for at in range(0, rows, block):
        values = source[at:at + block, :]
        scale = lax.rsqrt(jnp.mean(values * values, axis=-1, keepdims=True) + EPS)
        target[at:at + block, :] = (source[at:at + block, :] * scale * gain).astype(BF16)


def matmul(left, right, chunk=1024):
    depth = left.shape[1]
    total = None
    for at in range(0, depth, chunk):
        part = jnp.dot(left[:, at:at + chunk], right[at:at + chunk, :], preferred_element_type=F32)
        total = part if total is None else total + part
    return total


def query_kernel(head_dim, x_ref, gain_ref, w_ref, q_ref, states, normed, spread):
    devices, own, _ = x_ref.shape
    rows = devices * own
    heads = w_ref.shape[1] // head_dim
    for i in range(devices):
        states[own * i:own * (i + 1), :] = x_ref[i].astype(F32)
    normalize(states, gain_ref, normed)
    query = matmul(normed, w_ref)
    for h in range(heads):
        one = query[:, head_dim * h:head_dim * (h + 1)]
        scale = lax.rsqrt(jnp.mean(one * one, axis=-1, keepdims=True) + EPS)
        spread[pl.ds(h, rows, stride=heads), :] = one * scale
    q_ref[...] = spread[...].astype(BF16)


def attention_kernel(step, own, local_heads, kv_heads, q_ref, k_ref, v_ref, len_ref, c_ref):
    count, head_dim = q_ref.shape
    places = k_ref.shape[0]
    heads = count // own
    group = heads // kv_heads
    cache = places // (own * kv_heads)
    target = lax.broadcasted_iota(jnp.int32, (count, count), 0)
    source = lax.broadcasted_iota(jnp.int32, (count, count), 1)
    row, head = target // heads, target % heads
    wanted = (head // local_heads) * (own * local_heads) + row * local_heads + head % local_heads
    order = (source == wanted).astype(F32).astype(BF16)
    q = jnp.dot(order, q_ref[...], preferred_element_type=F32).astype(BF16)
    scores = lax.dot_general(
        q, k_ref[...], (((1,), (1,)), ((), ())), preferred_element_type=F32
    ) * head_dim ** (-0.5)
    column = lax.broadcasted_iota(jnp.int32, (1, places), 1)
    of_row = column // (cache * kv_heads)
    position = (column // kv_heads) % cache
    length = jnp.zeros((1, places), jnp.int32)
    for r in range(own):
        length = jnp.where(of_row == r, len_ref[step, r], length)
    key_of = jnp.where(position < length, of_row * kv_heads + column % kv_heads, -1)
    line = lax.broadcasted_iota(jnp.int32, (count, 1), 0)
    key_for = (line // heads) * kv_heads + (line % heads) // group
    exps = jnp.where(key_of == key_for, jnp.exp(scores), 0.0)
    weights = (exps / jnp.sum(exps, axis=-1, keepdims=True)).astype(BF16)
    c_ref[...] = jnp.dot(weights, v_ref[...], preferred_element_type=F32).astype(BF16)


def out_kernel(heads, c_ref, w_ref, o_ref, wide, lines):
    rows = lines.shape[0]
    head_dim = c_ref.shape[1]
    wide[...] = c_ref[...].astype(F32)
    for h in range(heads):
        lines[:, head_dim * h:head_dim * (h + 1)] = wide[pl.ds(h, rows, stride=heads), :].astype(BF16)
    columns = matmul(lines, w_ref).astype(BF16)
    for i in range(o_ref.shape[0]):
        o_ref[i] = columns


def expert_kernel(me_ref, a_ref, x_ref, gain_ref, gate_ref, up_ref, down_ref, h_ref, m_ref, middle, normed):
    devices, own, width = x_ref.shape
    part = a_ref.shape[2]
    for i in range(devices):
        middle[own * i:own * (i + 1), :] = x_ref[i].astype(F32)
    for j in range(devices):
        at = slice(part * j, part * (j + 1))
        middle[:, at] = middle[:, at] + a_ref[j].astype(F32)
    normalize(middle, gain_ref, normed)
    gate = matmul(normed, gate_ref)
    up = matmul(normed, up_ref)
    active = (gate / (1.0 + jnp.exp(-gate)) * up).astype(BF16)
    chunk = 512
    for at in range(0, width, chunk):
        piece = jnp.dot(active, down_ref[:, at:at + chunk], preferred_element_type=F32)
        for i in range(devices):
            h_ref[i, :, at:at + chunk] = piece[own * i:own * (i + 1), :].astype(BF16)
    pairs = 8 // own
    me = me_ref[0]
    block = middle[pl.ds(pl.multiple_of((me // pairs) * 8, 8), 8), :]
    kept = block[0:own, :]
    for p in range(1, pairs):
        kept = jnp.where(me % pairs == p, block[own * p:own * (p + 1), :], kept)
    m_ref[...] = kept


def combine_kernel(r_ref, m_ref, coeff_ref, o_ref):
    total = m_ref[...]
    for e in range(r_ref.shape[0] // 2):
        pair = (r_ref[2 * e].astype(F32) + r_ref[2 * e + 1].astype(F32)).astype(BF16).astype(F32)
        total = total + coeff_ref[:, e:e + 1] * pair
    o_ref[...] = total.astype(BF16)


def body(
    hidden_in,
    attn_gain,
    w_query,
    w_out,
    key_cache,
    value_cache,
    lengths,
    ffn_gain,
    w_gate,
    w_up,
    w_down,
    routes,
    gates,
):
    devices = lax.axis_size("expert")
    me = lax.axis_index("expert").astype(jnp.int32).reshape(1)
    experts = devices // 2
    own, width = hidden_in.shape[1:]
    rows = own * devices
    cache_len, kv_heads, head_dim = key_cache.shape[3:]
    query_w, out_w = w_query[0], w_out[0]
    part = query_w.shape[1]
    local_heads = part // head_dim
    heads = local_heads * devices
    gate_w, up_w, down_w = w_gate[0, 0], w_up[0, 0], w_down[0, 0]
    hidden = gate_w.shape[1]
    places = own * cache_len * kv_heads
    keys = key_cache.reshape(STEPS, places, head_dim)
    values = value_cache.reshape(STEPS, places, head_dim)
    shares = coefficients(routes[0], gates[0], experts)
    state = hidden_in[0]
    smem = whole(pltpu.SMEM)
    for step in range(STEPS):
        states = everyones(state)
        own_q = call(
            functools.partial(query_kernel, head_dim),
            jax.ShapeDtypeStruct((rows * local_heads, head_dim), BF16),
            (states, attn_gain, query_w),
            [whole()] * 3,
            [
                pltpu.VMEM((rows, width), F32),
                pltpu.VMEM((rows, width), BF16),
                pltpu.VMEM((rows * local_heads, head_dim), F32),
            ],
            "query",
            (2 * rows * width * part, 2 * width * part),
        )
        queries = swapped(own_q.reshape(devices, own * local_heads, head_dim))
        of_step = pl.BlockSpec((None, places, head_dim), lambda i, step=step: (step, 0, 0))
        context = pl.pallas_call(
            functools.partial(attention_kernel, step, own, local_heads, kv_heads),
            grid=(1,),
            out_shape=jax.ShapeDtypeStruct((own * heads, head_dim), BF16),
            in_specs=[
                pl.BlockSpec((own * heads, head_dim), lambda i: (0, 0)),
                of_step,
                of_step,
                smem,
            ],
            out_specs=pl.BlockSpec((own * heads, head_dim), lambda i: (0, 0)),
            compiler_params=pltpu.CompilerParams(vmem_limit_bytes=LIMIT),
            cost_estimate=pl.CostEstimate(
                flops=4 * own * heads * places * head_dim,
                bytes_accessed=4 * places * head_dim,
                transcendentals=0,
            ),
            name="attention",
        )(queries.reshape(own * heads, head_dim), keys, values, lengths[0])
        contexts = everyones(context)
        columns = call(
            functools.partial(out_kernel, heads),
            jax.ShapeDtypeStruct((devices, rows, part), BF16),
            (contexts.reshape(rows * heads, head_dim), out_w),
            [whole()] * 2,
            [pltpu.VMEM((rows * heads, head_dim), F32), pltpu.VMEM((rows, heads * head_dim), BF16)],
            "attention_out",
            (2 * rows * width * part, 2 * width * part),
        )
        attended = swapped(columns)
        half_out, middle = call(
            expert_kernel,
            (
                jax.ShapeDtypeStruct((devices, own, width), BF16),
                jax.ShapeDtypeStruct((own, width), F32),
            ),
            (me, attended, states, ffn_gain, gate_w, up_w, down_w),
            [smem] + [whole()] * 6,
            [pltpu.VMEM((rows, width), F32), pltpu.VMEM((rows, width), BF16)],
            "experts",
            (6 * rows * width * hidden, 6 * width * hidden),
        )
        returned = swapped(half_out)
        state = call(
            combine_kernel,
            jax.ShapeDtypeStruct((own, width), BF16),
            (returned, middle, shares[step]),
            [whole()] * 3,
            [],
            "combine",
            (4 * rows * width, 4 * rows * width),
        )
        if step + 1 < STEPS:
            state = passed_along(state, "section", 1)
    return state[None]


def solution(mesh):
    return jax.shard_map(
        body,
        mesh=mesh,
        in_specs=(
            P("section", "expert", None),
            P("section", None),
            P("section", None, "expert"),
            P("section", None, "expert"),
            P("section", None, "expert", None, None, None),
            P("section", None, "expert", None, None, None),
            P("section", None, "expert"),
            P("section", None),
            P("section", "expert", None, None),
            P("section", "expert", None, None),
            P("section", "expert", None, None),
            P("section", None, "expert", None),
            P("section", None, "expert", None),
        ),
        out_specs=P("section", "expert", None),
        check_vma=False,
    )
```

time: 298 us -> 208 us (0.70)
  matrix products: 47 us -> 0 us
  blocking collectives: 87.5 us -> 133 us
  local copies, waits for them, and re-layouts: 53 us -> 14.8 us
  other arithmetic: 31.4 us -> 0.11 us
  starting transfers between devices: 30.6 us -> 11.1 us
  Pallas kernels: 0 us -> 17.6 us
  waiting for transfers between devices: 44.9 us -> 29.6 us
    dot_general x18 -> x0, matrix products: 47 us -> none  [the longest x3 12.4 us: body(): jnp.dot(active, down_w, preferred_element_type=jnp.float32)]
    all_to_all x8 -> x12, blocking collectives: 87.5 us -> 133 us  [swapped(): lax.all_to_all(blocks, 'expert', split_axis=0, concat_axis=0, tiled=True)]
    convert_element_type x18 -> x0, local copies, waits for them, and re-layouts: 28.5 us -> none  [the longest x9 15.6 us: body(): middle = states32 + attended.astype(jnp.float32)]
    all_to_all x7 -> x3, starting transfers between devices: 30.5 us -> 11 us  [swapped(): lax.all_to_all(blocks, 'expert', split_axis=0, concat_axis=0, tiled=True)]
    pallas_call x0 -> x15, Pallas kernels: none -> 17.6 us  [the longest x12 14 us: call(): pl.pallas_call(kernel, out_shape=out, in_specs=specs, out_specs=whole() i...]
    all_to_all x7 -> x3, waiting for transfers between devices: 38.3 us -> 22.9 us  [swapped(): lax.all_to_all(blocks, 'expert', split_axis=0, concat_axis=0, tiled=True)]
    unnamed x13 -> x47, local copies, waits for them, and re-layouts: 0.1 us -> 13.7 us
    reduce_sum x17 -> x1, other arithmetic: 12.1 us -> 0.08 us  [coefficients(): return jnp.sum(jnp.where(chosen, shares[..., None], 0.0), axis=-2)]
  transfers between devices with their start and end apart: 9 -> 5, of which waited for: 9 -> 5; matrix products, arithmetic and copies ran while one was open for 6% -> 0% of each run, Pallas kernels for 0% -> 0%
where the time goes in v2:
time: 208 us; the launch traced here: 207 us
  blocking collectives  133 us (64%)
  waiting for transfers between devices  29.6 us (14%)
  Pallas kernels  17.6 us (8%)
  local copies, waits for them, and re-layouts  14.8 us (7%)
  starting transfers between devices  11.1 us (5%)
    all_to_all x12, blocking collectives, swapped(): lax.all_to_all(blocks, 'expert', split_axis=0, concat_axis=0, tiled=True)  133 us
    all_to_all x3, waiting for transfers between devices, swapped(): lax.all_to_all(blocks, 'expert', split_axis=0, concat_axis=0, tiled=True)  22.9 us
    pallas_call x12, Pallas kernels, call(): pl.pallas_call(kernel, out_shape=out, in_specs=specs, out_specs=whole() i...  14 us
    unnamed x47, local copies, waits for them, and re-layouts  13.7 us
    all_to_all x3, starting transfers between devices, swapped(): lax.all_to_all(blocks, 'expert', split_axis=0, concat_axis=0, tiled=True)  11 us
    ppermute x2, waiting for transfers between devices, passed_along(): lax.ppermute(array, axis, [(i, (i + by) % length) for i in range(length)])  6.65 us
  transfers between devices with their start and end apart: 5, of which 5 were waited for; matrix products, arithmetic and copies ran while one was open for 0% of the time, Pallas kernels for 0%

profile of v2, /device:TPU:0, one launch (start us, length us, event | category | flops | bytes accessed | tf_op | source)
XLA Modules:
  0.0 206.9 jit_solution(5334859731848323181)
XLA Ops:
  0.0 0.9 broadcast_in_dim.29
  0.9 16.0 %all_to_all.75.x_ref = bf16[8,4,4096]{2,1,0:T(4,128)(2,1)S(1)} all-to-all(bf16[8,4,4096]{2,1,0:T(4,128)(2,1)S(1)} %broadcast_in_dim.29), channel_id=1, replica_groups=mesh['section'=4,'expert'=8] {'expert'}, dimensions={0} | all-to-all | bytes 524288 | tf_op jit(solution)/shard_map/all_to_all | solution.py:23
  16.9 2.2 %copy-done.2 = bf16[1,4096,512]{2,1,0:T(8,128)(2,1)S(1)} copy-done((bf16[1,4096,512]{2,1,0:T(8,128)(2,1)S(1)}, bf16[1,4096,512]{2,1,0:T(8,128)(2,1)}, u32[]{:S(2)}) %copy-start.2) | copy-done | bytes 4194328
  19.1 0.7 copy-done.17
  19.8 1.7 query.3
  21.5 3.6 %all-to-all-start.1 = ((bf16[8,16,128]{2,1,0:T(8,128)(2,1)}), bf16[8,16,128]{2,1,0:T(8,128)(2,1)S(1)}, u32[]{:S(2)}, u32[]{:S(2)}) async-start(bf16[8,16,128]{2,1,0:T(8,128)(2,1)} %bitcast.3), calls=%async_computation.1 | async-start | bytes 65536 | tf_op jit(solution)/shard_map/all_to_all | solution.py:23
  25.1 0.0 copy-done.22
  25.1 6.7 %all-to-all-done.1 = bf16[8,16,128]{2,1,0:T(8,128)(2,1)S(1)} async-done(((bf16[8,16,128]{2,1,0:T(8,128)(2,1)}), bf16[8,16,128]{2,1,0:T(8,128)(2,1)S(1)}, u32[]{:S(2)}, u32[]{:S(2)}) %all-to-all-start.1) | async-done | bytes 32800 | tf_op jit(solution)/shard_map/all_to_all | solution.py:23
  31.8 0.0 copy-done.10
  31.8 0.0 copy-done.12
  31.8 1.2 attention.3
  33.0 0.0 copy-start.20
  33.0 0.0 copy-start.19
  33.0 10.6 %all_to_all.76 = bf16[8,128,128]{2,1,0:T(8,128)(2,1)S(1)} all-to-all(bf16[8,128,128]{2,1,0:T(8,128)(2,1)S(1)} %broadcast_in_dim.30), channel_id=1, replica_groups=mesh['section'=4,'expert'=8] {'expert'}, dimensions={0} | all-to-all | bytes 524288 | tf_op jit(solution)/shard_map/all_to_all | solution.py:23
  43.7 2.2 %copy-done = bf16[1,4096,512]{2,1,0:T(8,128)(2,1)S(1)} copy-done((bf16[1,4096,512]{2,1,0:T(8,128)(2,1)S(1)}, bf16[1,4096,512]{2,1,0:T(8,128)(2,1)}, u32[]{:S(2)}) %copy-start) | copy-done | bytes 4194328
  45.9 0.8 attention_out.3
  46.7 0.0 copy-start.15
  46.7 0.7 copy-done.15
  47.4 4.0 %all-to-all-start.3 = ((bf16[8,32,512]{2,1,0:T(8,128)(2,1)}), bf16[8,32,512]{2,1,0:T(8,128)(2,1)}, u32[]{:S(2)}, u32[]{:S(2)}) async-start(bf16[8,32,512]{2,1,0:T(8,128)(2,1)} %copy-done.15), calls=%async_computation.3 | async-start | bytes 524288 | tf_op jit(solution)/shard_map/all_to_all | solution.py:23
  51.5 0.0 copy-done.20
  51.5 8.2 %all-to-all-done.3.a_ref = bf16[8,32,512]{2,1,0:T(8,128)(2,1)} async-done(((bf16[8,32,512]{2,1,0:T(8,128)(2,1)}), bf16[8,32,512]{2,1,0:T(8,128)(2,1)}, u32[]{:S(2)}, u32[]{:S(2)}) %all-to-all-start.3) | async-done | bytes 262176 | tf_op jit(solution)/shard_map/all_to_all | solution.py:23
  59.7 0.0 copy-done.19
  59.7 0.0 copy-done.5
  59.7 1.9 copy-done.6
  61.6 1.9 copy-done.8
  63.5 2.9 %experts.3 = (bf16[8,4,4096]{2,1,0:T(4,128)(2,1)S(1)}, f32[4,4096]{1,0:T(4,128)S(1)}) custom-call(s32[1]{0:T(128)} %bitcast.me_ref, bf16[8,32,512]{2,1,0:T(8,128)(2,1)} %all-to-all-done.3.a_ref, bf16[8,4,4096]{2,1,0:T(4,128)(2,1)S(1)} %all_to_all.75.x_ref, bf16[1,4096]{1,0:T(2,128)(2,1)S(1)} %copy-done.19, bf16[4096,384]{1,0:T(8,128)(2,1)S(1)} %bitcast.37, ...), custom_call_target="tpu_custom_call" | custom-call | flops 301989888 | bytes 9437184 | tf_op jit(solution)/shard_map/experts/pallas_call | solution.py:43
  66.3 0.0 copy-start.16
  66.4 0.7 copy-done.16
  67.1 3.4 %all-to-all-start.4 = ((bf16[8,4,4096]{2,1,0:T(4,128)(2,1)}), bf16[8,4,4096]{2,1,0:T(4,128)(2,1)S(1)}, u32[]{:S(2)}, u32[]{:S(2)}) async-start(bf16[8,4,4096]{2,1,0:T(4,128)(2,1)} %copy-done.16), calls=%async_computation.4 | async-start | bytes 524288 | tf_op jit(solution)/shard_map/all_to_all | solution.py:23
  70.5 0.1 select_reduce_fusion
  70.6 8.0 %all-to-all-done.4.r_ref = bf16[8,4,4096]{2,1,0:T(4,128)(2,1)S(1)} async-done(((bf16[8,4,4096]{2,1,0:T(4,128)(2,1)}), bf16[8,4,4096]{2,1,0:T(4,128)(2,1)S(1)}, u32[]{:S(2)}, u32[]{:S(2)}) %all-to-all-start.4) | async-done | bytes 262176 | tf_op jit(solution)/shard_map/all_to_all | solution.py:23
  78.6 0.1 combine.3
  78.8 0.1 collective-permute-start
  78.8 3.3 %collective-permute-done = bf16[4,4096]{1,0:T(4,128)(2,1)S(1)} collective-permute-done((bf16[4,4096]{1,0:T(4,128)(2,1)S(1)}, bf16[4,4096]{1,0:T(4,128)(2,1)S(1)}, u32[]{:S(2)}, u32[]{:S(2)}) %collective-permute-start) | collective-permute-done | bytes 32800 | tf_op jit(solution)/shard_map/ppermute | solution.py:19
  82.2 0.1 broadcast_in_dim.33
  82.2 11.2 %all_to_all.77.x_ref = bf16[8,4,4096]{2,1,0:T(4,128)(2,1)S(1)} all-to-all(bf16[8,4,4096]{2,1,0:T(4,128)(2,1)S(1)} %broadcast_in_dim.33), channel_id=1, replica_groups=mesh['section'=4,'expert'=8] {'expert'}, dimensions={0} | all-to-all | bytes 524288 | tf_op jit(solution)/shard_map/all_to_all | solution.py:23
  93.4 0.0 copy-done.18
  93.4 2.2 %copy-done.3 = bf16[1,4096,512]{2,1,0:T(8,128)(2,1)S(1)} copy-done((bf16[1,4096,512]{2,1,0:T(8,128)(2,1)S(1)}, bf16[1,4096,512]{2,1,0:T(8,128)(2,1)}, u32[]{:S(2)}) %copy-start.3) | copy-done | bytes 4194328
  95.6 1.1 query.4
  96.7 10.1 %all_to_all.78 = bf16[8,16,128]{2,1,0:T(8,128)(2,1)S(1)} all-to-all(bf16[8,16,128]{2,1,0:T(8,128)(2,1)S(1)} %bitcast.55), channel_id=1, replica_groups=mesh['section'=4,'expert'=8] {'expert'}, dimensions={0} | all-to-all | bytes 65536 | tf_op jit(solution)/shard_map/all_to_all | solution.py:23
  106.8 1.1 copy-done.13
  107.9 1.2 attention.4
  109.1 0.0 copy-start.7
  109.2 10.9 %all_to_all.79 = bf16[8,128,128]{2,1,0:T(8,128)(2,1)S(1)} all-to-all(bf16[8,128,128]{2,1,0:T(8,128)(2,1)S(1)} %broadcast_in_dim.34), channel_id=1, replica_groups=mesh['section'=4,'expert'=8] {'expert'}, dimensions={0} | all-to-all | bytes 524288 | tf_op jit(solution)/shard_map/all_to_all | solution.py:23
  120.1 0.8 attention_out.4
  120.9 10.9 %all_to_all.80.a_ref = bf16[8,32,512]{2,1,0:T(8,128)(2,1)S(1)} all-to-all(bf16[8,32,512]{2,1,0:T(8,128)(2,1)S(1)} %attention_out.4), channel_id=1, replica_groups=mesh['section'=4,'expert'=8] {'expert'}, dimensions={0} | all-to-all | bytes 524288 | tf_op jit(solution)/shard_map/all_to_all | solution.py:23
  131.8 0.0 copy-done.7
  131.8 1.9 experts.4
  133.7 11.0 %all_to_all.81.r_ref = bf16[8,4,4096]{2,1,0:T(4,128)(2,1)S(1)} all-to-all(bf16[8,4,4096]{2,1,0:T(4,128)(2,1)S(1)} %get-tuple-element.13), channel_id=1, replica_groups=mesh['section'=4,'expert'=8] {'expert'}, dimensions={0} | all-to-all | bytes 524288 | tf_op jit(solution)/shard_map/all_to_all | solution.py:23
  144.8 0.1 combine.4
  144.9 0.1 collective-permute-start.1
  145.0 3.3 %collective-permute-done.1 = bf16[4,4096]{1,0:T(4,128)(2,1)S(1)} collective-permute-done((bf16[4,4096]{1,0:T(4,128)(2,1)S(1)}, bf16[4,4096]{1,0:T(4,128)(2,1)S(1)}, u32[]{:S(2)}, u32[]{:S(2)}) %collective-permute-start.1) | collective-permute-done | bytes 32800 | tf_op jit(solution)/shard_map/ppermute | solution.py:19
  148.3 0.1 broadcast_in_dim.62
  148.4 10.9 %all_to_all.82.x_ref = bf16[8,4,4096]{2,1,0:T(4,128)(2,1)S(1)} all-to-all(bf16[8,4,4096]{2,1,0:T(4,128)(2,1)S(1)} %broadcast_in_dim.62), channel_id=1, replica_groups=mesh['section'=4,'expert'=8] {'expert'}, dimensions={0} | all-to-all | bytes 524288 | tf_op jit(solution)/shard_map/all_to_all | solution.py:23
  159.3 1.1 query.5
  160.4 9.4 %all_to_all.83 = bf16[8,16,128]{2,1,0:T(8,128)(2,1)S(1)} all-to-all(bf16[8,16,128]{2,1,0:T(8,128)(2,1)S(1)} %bitcast.56), channel_id=1, replica_groups=mesh['section'=4,'expert'=8] {'expert'}, dimensions={0} | all-to-all | bytes 65536 | tf_op jit(solution)/shard_map/all_to_all | solution.py:23
  169.7 0.0 copy-done.14
  169.7 1.2 attention.5
  171.0 10.6 %all_to_all.84 = bf16[8,128,128]{2,1,0:T(8,128)(2,1)S(1)} all-to-all(bf16[8,128,128]{2,1,0:T(8,128)(2,1)S(1)} %broadcast_in_dim.63), channel_id=1, replica_groups=mesh['section'=4,'expert'=8] {'expert'}, dimensions={0} | all-to-all | bytes 524288 | tf_op jit(solution)/shard_map/all_to_all | solution.py:23
  181.6 0.8 attention_out.5
  182.4 10.9 %all_to_all.85.a_ref = bf16[8,32,512]{2,1,0:T(8,128)(2,1)S(1)} all-to-all(bf16[8,32,512]{2,1,0:T(8,128)(2,1)S(1)} %attention_out.5), channel_id=1, replica_groups=mesh['section'=4,'expert'=8] {'expert'}, dimensions={0} | all-to-all | bytes 524288 | tf_op jit(solution)/shard_map/all_to_all | solution.py:23
  193.3 1.9 experts.5
  195.3 10.9 %all_to_all.86.r_ref = bf16[8,4,4096]{2,1,0:T(4,128)(2,1)S(1)} all-to-all(bf16[8,4,4096]{2,1,0:T(4,128)(2,1)S(1)} %get-tuple-element.15), channel_id=1, replica_groups=mesh['section'=4,'expert'=8] {'expert'}, dimensions={0} | all-to-all | bytes 524288 | tf_op jit(solution)/shard_map/all_to_all | solution.py:23
  206.2 0.7 combine.5
  (30 shorter events, 0.2 us)
Async XLA Ops:
  0.0 25.1 %copy-start.22 = (s32[1,3,4]{2,0,1:T(1,128)S(1)}, s32[1,3,4]{2,0,1:T(1,128)}, u32[]{:S(2)}) copy-start(s32[1,3,4]{2,0,1:T(1,128)} %param.19) | copy-start | bytes 148
  0.0 31.8 %copy-start.10 = (bf16[1,3,4,64,4,128]{5,4,3,2,1,0:T(4,128)(2,1)S(1)}, bf16[1,3,4,64,4,128]{5,4,3,2,1,0:T(4,128)(2,1)}, u32[]{:S(2)}) copy-start(bf16[1,3,4,64,4,128]{5,4,3,2,1,0:T(4,128)(2,1)} %param.17) | copy-start | bytes 2359300
  16.9 2.2 %copy-start.2 = (bf16[1,4096,512]{2,1,0:T(8,128)(2,1)S(1)}, bf16[1,4096,512]{2,1,0:T(8,128)(2,1)}, u32[]{:S(2)}) copy-start(bf16[1,4096,512]{2,1,0:T(8,128)(2,1)} %param.15) | copy-start | bytes 12582916
  19.1 0.7 copy-start.17
  19.8 12.0 %copy-start.12 = (bf16[1,3,4,64,4,128]{5,4,3,2,1,0:T(4,128)(2,1)S(1)}, bf16[1,3,4,64,4,128]{5,4,3,2,1,0:T(4,128)(2,1)}, u32[]{:S(2)}) copy-start(bf16[1,3,4,64,4,128]{5,4,3,2,1,0:T(4,128)(2,1)} %param.18) | copy-start | bytes 2359300
  21.5 10.3 %all-to-all-start.1 = ((bf16[8,16,128]{2,1,0:T(8,128)(2,1)}), bf16[8,16,128]{2,1,0:T(8,128)(2,1)S(1)}, u32[]{:S(2)}, u32[]{:S(2)}) async-start(bf16[8,16,128]{2,1,0:T(8,128)(2,1)} %bitcast.3), calls=%async_computation.1 | async-start | bytes 65536 | tf_op jit(solution)/shard_map/all_to_all | solution.py:23
  33.0 18.5 %copy-start.20 = (f32[1,3,4,2]{2,3,1,0:T(2,128)S(1)}, f32[1,3,4,2]{2,3,1,0:T(2,128)}, u32[]{:S(2)}) copy-start(f32[1,3,4,2]{2,3,1,0:T(2,128)} %param.25) | copy-start | bytes 292
  33.0 26.7 %copy-start.19 = (bf16[1,4096]{1,0:T(2,128)(2,1)S(1)}, bf16[1,4096]{1,0:T(2,128)(2,1)}, u32[]{:S(2)}) copy-start(bf16[1,4096]{1,0:T(2,128)(2,1)} %gain_ref.11) | copy-start | bytes 24580
  43.7 2.2 %copy-start = (bf16[1,4096,512]{2,1,0:T(8,128)(2,1)S(1)}, bf16[1,4096,512]{2,1,0:T(8,128)(2,1)}, u32[]{:S(2)}) copy-start(bf16[1,4096,512]{2,1,0:T(8,128)(2,1)} %param.16) | copy-start | bytes 12582916
  45.9 13.8 %copy-start.5 = (bf16[1,1,4096,384]{3,2,1,0:T(8,128)(2,1)S(1)}, bf16[1,1,4096,384]{3,2,1,0:T(8,128)(2,1)}, u32[]{:S(2)}) copy-start(bf16[1,1,4096,384]{3,2,1,0:T(8,128)(2,1)} %param.21) | copy-start | bytes 9437188
  46.7 0.7 copy-start.15
  47.4 12.3 %all-to-all-start.3 = ((bf16[8,32,512]{2,1,0:T(8,128)(2,1)}), bf16[8,32,512]{2,1,0:T(8,128)(2,1)}, u32[]{:S(2)}, u32[]{:S(2)}) async-start(bf16[8,32,512]{2,1,0:T(8,128)(2,1)} %copy-done.15), calls=%async_computation.3 | async-start | bytes 524288 | tf_op jit(solution)/shard_map/all_to_all | solution.py:23
  59.7 1.9 copy-start.6
  61.6 1.9 copy-start.8
  63.5 7.0 %copy-start.21 = (s32[1,3,4,2]{2,3,1,0:T(2,128)S(1)}, s32[1,3,4,2]{2,3,1,0:T(2,128)}, u32[]{:S(2)}) copy-start(s32[1,3,4,2]{2,3,1,0:T(2,128)} %param.24) | copy-start | bytes 292
  63.5 29.9 %copy-start.18 = (bf16[1,4096]{1,0:T(2,128)(2,1)S(1)}, bf16[1,4096]{1,0:T(2,128)(2,1)}, u32[]{:S(2)}) copy-start(bf16[1,4096]{1,0:T(2,128)(2,1)} %gain_ref.10) | copy-start | bytes 24580
  66.3 0.7 copy-start.16
  67.1 11.6 %all-to-all-start.4 = ((bf16[8,4,4096]{2,1,0:T(4,128)(2,1)}), bf16[8,4,4096]{2,1,0:T(4,128)(2,1)S(1)}, u32[]{:S(2)}, u32[]{:S(2)}) async-start(bf16[8,4,4096]{2,1,0:T(4,128)(2,1)} %copy-done.16), calls=%async_computation.4 | async-start | bytes 524288 | tf_op jit(solution)/shard_map/all_to_all | solution.py:23
  78.6 28.1 %copy-start.11 = (bf16[1,3,4,64,4,128]{5,4,3,2,1,0:T(4,128)(2,1)S(1)}, bf16[1,3,4,64,4,128]{5,4,3,2,1,0:T(4,128)(2,1)}, u32[]{:S(2)}) copy-start(bf16[1,3,4,64,4,128]{5,4,3,2,1,0:T(4,128)(2,1)} %param.17) | copy-start | bytes 2359300
  78.8 3.4 %collective-permute-start = (bf16[4,4096]{1,0:T(4,128)(2,1)S(1)}, bf16[4,4096]{1,0:T(4,128)(2,1)S(1)}, u32[]{:S(2)}, u32[]{:S(2)}) collective-permute-start(bf16[4,4096]{1,0:T(4,128)(2,1)S(1)} %combine.3), channel_id=1, source_target_pairs={{0,8},{8,16},{16,24},{24,0},{1,9},{9,17},{17,25},{25,1},{2,10},{10... | collective-permute-start | bytes 98312 | tf_op jit(solution)/shard_map/ppermute | solution.py:19
  93.4 2.2 %copy-start.3 = (bf16[1,4096,512]{2,1,0:T(8,128)(2,1)S(1)}, bf16[1,4096,512]{2,1,0:T(8,128)(2,1)}, u32[]{:S(2)}) copy-start(bf16[1,4096,512]{2,1,0:T(8,128)(2,1)} %param.15) | copy-start | bytes 12582916
  95.6 24.5 %copy-start.1 = (bf16[1,4096,512]{2,1,0:T(8,128)(2,1)S(1)}, bf16[1,4096,512]{2,1,0:T(8,128)(2,1)}, u32[]{:S(2)}) copy-start(bf16[1,4096,512]{2,1,0:T(8,128)(2,1)} %param.16) | copy-start | bytes 12582916
  106.7 1.1 copy-start.13
  107.9 23.9 %copy-start.9 = (bf16[1,1,384,4096]{3,2,1,0:T(8,128)(2,1)S(1)}, bf16[1,1,384,4096]{3,2,1,0:T(8,128)(2,1)}, u32[]{:S(2)}) copy-start(bf16[1,1,384,4096]{3,2,1,0:T(8,128)(2,1)} %param.23) | copy-start | bytes 9437188
  109.1 22.7 %copy-start.7 = (bf16[1,1,4096,384]{3,2,1,0:T(8,128)(2,1)S(1)}, bf16[1,1,4096,384]{3,2,1,0:T(8,128)(2,1)}, u32[]{:S(2)}) copy-start(bf16[1,1,4096,384]{3,2,1,0:T(8,128)(2,1)} %param.22) | copy-start | bytes 9437188
  131.8 27.5 %copy-start.4 = (bf16[1,4096,512]{2,1,0:T(8,128)(2,1)S(1)}, bf16[1,4096,512]{2,1,0:T(8,128)(2,1)}, u32[]{:S(2)}) copy-start(bf16[1,4096,512]{2,1,0:T(8,128)(2,1)} %param.15) | copy-start | bytes 12582916
  133.7 36.0 %copy-start.14 = (bf16[1,3,4,64,4,128]{5,4,3,2,1,0:T(4,128)(2,1)S(1)}, bf16[1,3,4,64,4,128]{5,4,3,2,1,0:T(4,128)(2,1)}, u32[]{:S(2)}) copy-start(bf16[1,3,4,64,4,128]{5,4,3,2,1,0:T(4,128)(2,1)} %param.18) | copy-start | bytes 2359300
  144.9 3.4 %collective-permute-start.1 = (bf16[4,4096]{1,0:T(4,128)(2,1)S(1)}, bf16[4,4096]{1,0:T(4,128)(2,1)S(1)}, u32[]{:S(2)}, u32[]{:S(2)}) collective-permute-start(bf16[4,4096]{1,0:T(4,128)(2,1)S(1)} %combine.4), channel_id=1, source_target_pairs={{0,8},{8,16},{16,24},{24,0},{1,9},{9,17},{17,25},{25,1},{2,10},{10... | collective-permute-start | bytes 98312 | tf_op jit(solution)/shard_map/ppermute | solution.py:19

commit v3 on v2

--- a/solution.py
+++ b/solution.py
@@ -9,7 +9,8 @@
 
 STEPS = 3
 EPS = 1e-06
-LIMIT = 32 * 1024 * 1024
+LIMIT = 24 * 1024 * 1024
+EXCHANGE = 20 * 1000 * 1000 * 1000
 F32 = jnp.float32
 BF16 = jnp.bfloat16
 
@@ -26,12 +27,6 @@
 def everyones(array):
     devices = lax.axis_size("expert")
     return swapped(jnp.broadcast_to(array[None], (devices,) + array.shape))
-
-
-def coefficients(route_ids, gate_vals, experts):
-    shares = gate_vals / jnp.sum(gate_vals, axis=-1, keepdims=True)
-    chosen = route_ids[..., None] == jnp.arange(experts, dtype=jnp.int32)
-    return jnp.sum(jnp.where(chosen, shares[..., None], 0.0), axis=-2)
 
 
 def whole(memory_space=pltpu.VMEM):
@@ -47,7 +42,7 @@
         out_specs=whole() if single else tuple(whole() for _ in out),
         scratch_shapes=scratch,
         compiler_params=pltpu.CompilerParams(vmem_limit_bytes=LIMIT),
-        cost_estimate=pl.CostEstimate(flops=cost[0], bytes_accessed=cost[1], transcendentals=0),
+        cost_estimate=pl.CostEstimate(flops=cost[0] + EXCHANGE, bytes_accessed=cost[1], transcendentals=0),
         name=name,
     )(*operands)
 
@@ -69,6 +64,11 @@
         part = jnp.dot(left[:, at:at + chunk], right[at:at + chunk, :], preferred_element_type=F32)
         total = part if total is None else total + part
     return total
+
+
+def spread_kernel(x_ref, o_ref):
+    for i in range(o_ref.shape[0]):
+        o_ref[i] = x_ref[...]
 
 
 def query_kernel(head_dim, x_ref, gain_ref, w_ref, q_ref, states, normed, spread):
@@ -106,7 +106,7 @@
     position = (column // kv_heads) % cache
     length = jnp.zeros((1, places), jnp.int32)
     for r in range(own):
-        length = jnp.where(of_row == r, len_ref[step, r], length)
+        length = jnp.where(of_row == r, len_ref[step, 0, r], length)
     key_of = jnp.where(position < length, of_row * kv_heads + column % kv_heads, -1)
     line = lax.broadcasted_iota(jnp.int32, (count, 1), 0)
     key_for = (line // heads) * kv_heads + (line % heads) // group
@@ -152,11 +152,18 @@
     m_ref[...] = kept
 
 
-def combine_kernel(r_ref, m_ref, coeff_ref, o_ref):
+def combine_kernel(step, r_ref, m_ref, routes_ref, gates_ref, o_ref):
+    own = m_ref.shape[0]
+    routes, gates = routes_ref[step], gates_ref[step]
+    shares = gates / jnp.sum(gates, axis=0, keepdims=True)
+    line = lax.broadcasted_iota(jnp.int32, (own, own), 0)
+    column = lax.broadcasted_iota(jnp.int32, (own, own), 1)
     total = m_ref[...]
     for e in range(r_ref.shape[0] // 2):
         pair = (r_ref[2 * e].astype(F32) + r_ref[2 * e + 1].astype(F32)).astype(BF16).astype(F32)
-        total = total + coeff_ref[:, e:e + 1] * pair
+        coeff = jnp.sum(jnp.where(routes == e, shares, 0.0), axis=0, keepdims=True)
+        coeff = jnp.sum(jnp.where(line == column, coeff, 0.0), axis=1, keepdims=True)
+        total = total + coeff * pair
     o_ref[...] = total.astype(BF16)
 
 
@@ -177,7 +184,6 @@
 ):
     devices = lax.axis_size("expert")
     me = lax.axis_index("expert").astype(jnp.int32).reshape(1)
-    experts = devices // 2
     own, width = hidden_in.shape[1:]
     rows = own * devices
     cache_len, kv_heads, head_dim = key_cache.shape[3:]
@@ -190,11 +196,23 @@
     places = own * cache_len * kv_heads
     keys = key_cache.reshape(STEPS, places, head_dim)
     values = value_cache.reshape(STEPS, places, head_dim)
-    shares = coefficients(routes[0], gates[0], experts)
-    state = hidden_in[0]
+    routes, gates = routes[0].transpose(0, 2, 1), gates[0].transpose(0, 2, 1)
+    lengths = lengths.reshape(STEPS, 1, own)
+    copies = call(
+        spread_kernel,
+        jax.ShapeDtypeStruct((devices, own, width), BF16),
+        (hidden_in[0],),
+        [whole()],
+        [],
+        "spread",
+        (0, 2 * rows * width),
+    )
+    me, copies = lax.optimization_barrier((me, copies))
     smem = whole(pltpu.SMEM)
     for step in range(STEPS):
-        states = everyones(state)
+        if step:
+            copies = jnp.broadcast_to(state[None], (devices, own, width))
+        states = swapped(copies)
         own_q = call(
             functools.partial(query_kernel, head_dim),
             jax.ShapeDtypeStruct((rows * local_heads, head_dim), BF16),
@@ -223,12 +241,12 @@
             out_specs=pl.BlockSpec((own * heads, head_dim), lambda i: (0, 0)),
             compiler_params=pltpu.CompilerParams(vmem_limit_bytes=LIMIT),
             cost_estimate=pl.CostEstimate(
-                flops=4 * own * heads * places * head_dim,
+                flops=4 * own * heads * places * head_dim + EXCHANGE,
                 bytes_accessed=4 * places * head_dim,
                 transcendentals=0,
             ),
             name="attention",
-        )(queries.reshape(own * heads, head_dim), keys, values, lengths[0])
+        )(queries.reshape(own * heads, head_dim), keys, values, lengths)
         contexts = everyones(context)
         columns = call(
             functools.partial(out_kernel, heads),
@@ -254,10 +272,10 @@
         )
         returned = swapped(half_out)
         state = call(
-            combine_kernel,
+            functools.partial(combine_kernel, step),
             jax.ShapeDtypeStruct((own, width), BF16),
-            (returned, middle, shares[step]),
-            [whole()] * 3,
+            (returned, middle, routes, gates),
+            [whole()] * 4,
             [],
             "combine",
             (4 * rows * width, 4 * rows * width),

time: 208 us -> 190 us (0.913)
  blocking collectives: 133 us -> 165 us
  waiting for transfers between devices: 29.6 us -> 6.65 us
  local copies, waits for them, and re-layouts: 14.8 us -> 1.06 us
  starting transfers between devices: 11.1 us -> 0.11 us
    all_to_all x12 -> x15, blocking collectives: 133 us -> 165 us  [swapped(): lax.all_to_all(blocks, 'expert', split_axis=0, concat_axis=0, tiled=True)]
    all_to_all x3 -> x0, waiting for transfers between devices: 22.9 us -> none  [swapped(): lax.all_to_all(blocks, 'expert', split_axis=0, concat_axis=0, tiled=True)]
    unnamed x47 -> x26, local copies, waits for them, and re-layouts: 13.7 us -> 0.81 us
    all_to_all x3 -> x0, starting transfers between devices: 11 us -> none  [swapped(): lax.all_to_all(blocks, 'expert', split_axis=0, concat_axis=0, tiled=True)]
    pallas_call x12 -> x13, Pallas kernels: 14 us -> 12.9 us  [call(): pl.pallas_call(kernel, out_shape=out, in_specs=specs, out_specs=whole() i...]
  transfers between devices with their start and end apart: 5 -> 2, of which waited for: 5 -> 2; matrix products, arithmetic and copies ran while one was open for 0% -> 0% of each run, Pallas kernels for 0% -> 0%
where the time goes in v3:
time: 190 us
  blocking collectives  165 us (87%)
  Pallas kernels  16.4 us (9%)
  waiting for transfers between devices  6.65 us (4%)
    all_to_all x15, blocking collectives, swapped(): lax.all_to_all(blocks, 'expert', split_axis=0, concat_axis=0, tiled=True)  165 us
    pallas_call x13, Pallas kernels, call(): pl.pallas_call(kernel, out_shape=out, in_specs=specs, out_specs=whole() i...  12.9 us
    ppermute x2, waiting for transfers between devices, passed_along(): lax.ppermute(array, axis, [(i, (i + by) % length) for i in range(length)])  6.65 us
  transfers between devices with their start and end apart: 2, of which 2 were waited for; matrix products, arithmetic and copies ran while one was open for 0% of the time, Pallas kernels for 0%

profile of v3, /device:TPU:0, one launch (start us, length us, event | category | flops | bytes accessed | tf_op | source)
XLA Modules:
  0.0 189.8 jit_solution(14380045183450823546)
XLA Ops:
  0.0 0.0 copy-start.7
  0.0 0.8 copy-done.7
  0.8 0.0 copy-start
  0.8 0.0 copy-start.8
  0.8 16.3 %all_to_all.75.x_ref = bf16[8,4,4096]{2,1,0:T(4,128)(2,1)S(1)} all-to-all(bf16[8,4,4096]{2,1,0:T(4,128)(2,1)S(1)} %spread.1), channel_id=1, replica_groups=mesh['section'=4,'expert'=8] {'expert'}, dimensions={0} | all-to-all | bytes 524288 | tf_op jit(solution)/shard_map/all_to_all | solution.py:24
  17.0 0.0 copy-done
  17.0 0.0 copy-done.8
  17.0 0.0 copy-start.5
  17.1 0.0 copy-start.6
  17.1 0.0 copy-start.12
  17.1 1.1 query.3
  18.2 10.1 %all_to_all.76 = bf16[8,16,128]{2,1,0:T(8,128)(2,1)S(1)} all-to-all(bf16[8,16,128]{2,1,0:T(8,128)(2,1)S(1)} %bitcast.32), channel_id=1, replica_groups=mesh['section'=4,'expert'=8] {'expert'}, dimensions={0} | all-to-all | bytes 65536 | tf_op jit(solution)/shard_map/all_to_all | solution.py:24
  28.2 0.0 copy-done.5
  28.2 0.0 copy-done.6
  28.2 0.0 copy-done.12
  28.2 0.0 copy-start.1
  28.3 1.2 attention.3
  29.5 10.8 %all_to_all.77 = bf16[8,128,128]{2,1,0:T(8,128)(2,1)S(1)} all-to-all(bf16[8,128,128]{2,1,0:T(8,128)(2,1)S(1)} %broadcast_in_dim.12), channel_id=1, replica_groups=mesh['section'=4,'expert'=8] {'expert'}, dimensions={0} | all-to-all | bytes 524288 | tf_op jit(solution)/shard_map/all_to_all | solution.py:24
  40.3 0.0 copy-done.1
  40.3 0.0 copy-start.2
  40.3 0.0 copy-start.3
  40.3 0.0 copy-start.4
  40.3 0.0 copy-start.9
  40.3 0.9 attention_out.3
  41.2 11.2 %all_to_all.78.a_ref = bf16[8,32,512]{2,1,0:T(8,128)(2,1)S(1)} all-to-all(bf16[8,32,512]{2,1,0:T(8,128)(2,1)S(1)} %attention_out.3), channel_id=1, replica_groups=mesh['section'=4,'expert'=8] {'expert'}, dimensions={0} | all-to-all | bytes 524288 | tf_op jit(solution)/shard_map/all_to_all | solution.py:24
  52.3 0.0 copy-done.2
  52.3 0.0 copy-done.3
  52.3 0.0 copy-done.4
  52.3 0.0 copy-done.9
  52.4 0.0 copy-start.10
  52.4 0.0 copy-start.11
  52.4 2.0 %experts.3 = (bf16[8,4,4096]{2,1,0:T(4,128)(2,1)S(1)}, f32[4,4096]{1,0:T(4,128)S(1)}) custom-call(s32[1]{0:T(128)} %bitcast.me_ref, bf16[8,32,512]{2,1,0:T(8,128)(2,1)S(1)} %all_to_all.78.a_ref, bf16[8,4,4096]{2,1,0:T(4,128)(2,1)S(1)} %all_to_all.75.x_ref, bf16[1,4096]{1,0:T(2,128)(2,1)S(1)} %copy-done.9, bf16[4096,384]{1,0:T(8,128)(2,1)S(1)} %bitcast.41, ...), custom_call_target="tpu_custom_call" | custom-call | flops 20301989888 | bytes 9437184 | tf_op jit(solution)/shard_map/experts/pallas_call | solution.py:38
  54.3 10.9 %all_to_all.79.r_ref = bf16[8,4,4096]{2,1,0:T(4,128)(2,1)S(1)} all-to-all(bf16[8,4,4096]{2,1,0:T(4,128)(2,1)S(1)} %get-tuple-element.15), channel_id=1, replica_groups=mesh['section'=4,'expert'=8] {'expert'}, dimensions={0} | all-to-all | bytes 524288 | tf_op jit(solution)/shard_map/all_to_all | solution.py:24
  65.2 0.0 copy-done.10
  65.3 0.0 copy-done.11
  65.3 0.1 combine.3
  65.4 0.1 collective-permute-start
  65.5 3.3 %collective-permute-done = bf16[4,4096]{1,0:T(4,128)(2,1)S(1)} collective-permute-done((bf16[4,4096]{1,0:T(4,128)(2,1)S(1)}, bf16[4,4096]{1,0:T(4,128)(2,1)S(1)}, u32[]{:S(2)}, u32[]{:S(2)}) %collective-permute-start) | collective-permute-done | bytes 32800 | tf_op jit(solution)/shard_map/ppermute | solution.py:20
  68.8 0.1 broadcast_in_dim.13
  68.9 11.1 %all_to_all.80.x_ref = bf16[8,4,4096]{2,1,0:T(4,128)(2,1)S(1)} all-to-all(bf16[8,4,4096]{2,1,0:T(4,128)(2,1)S(1)} %broadcast_in_dim.13), channel_id=1, replica_groups=mesh['section'=4,'expert'=8] {'expert'}, dimensions={0} | all-to-all | bytes 524288 | tf_op jit(solution)/shard_map/all_to_all | solution.py:24
  80.0 1.1 query.4
  81.0 9.9 %all_to_all.81 = bf16[8,16,128]{2,1,0:T(8,128)(2,1)S(1)} all-to-all(bf16[8,16,128]{2,1,0:T(8,128)(2,1)S(1)} %bitcast.33), channel_id=1, replica_groups=mesh['section'=4,'expert'=8] {'expert'}, dimensions={0} | all-to-all | bytes 65536 | tf_op jit(solution)/shard_map/all_to_all | solution.py:24
  91.0 1.2 attention.4
  92.2 10.6 %all_to_all.82 = bf16[8,128,128]{2,1,0:T(8,128)(2,1)S(1)} all-to-all(bf16[8,128,128]{2,1,0:T(8,128)(2,1)S(1)} %broadcast_in_dim.14), channel_id=1, replica_groups=mesh['section'=4,'expert'=8] {'expert'}, dimensions={0} | all-to-all | bytes 524288 | tf_op jit(solution)/shard_map/all_to_all | solution.py:24
  102.8 0.9 attention_out.4
  103.7 10.9 %all_to_all.83.a_ref = bf16[8,32,512]{2,1,0:T(8,128)(2,1)S(1)} all-to-all(bf16[8,32,512]{2,1,0:T(8,128)(2,1)S(1)} %attention_out.4), channel_id=1, replica_groups=mesh['section'=4,'expert'=8] {'expert'}, dimensions={0} | all-to-all | bytes 524288 | tf_op jit(solution)/shard_map/all_to_all | solution.py:24
  114.6 2.0 %experts.4 = (bf16[8,4,4096]{2,1,0:T(4,128)(2,1)S(1)}, f32[4,4096]{1,0:T(4,128)S(1)}) custom-call(s32[1]{0:T(128)} %bitcast.me_ref, bf16[8,32,512]{2,1,0:T(8,128)(2,1)S(1)} %all_to_all.83.a_ref, bf16[8,4,4096]{2,1,0:T(4,128)(2,1)S(1)} %all_to_all.80.x_ref, bf16[1,4096]{1,0:T(2,128)(2,1)S(1)} %copy-done.9, bf16[4096,384]{1,0:T(8,128)(2,1)S(1)} %bitcast.42, ...), custom_call_target="tpu_custom_call" | custom-call | flops 20301989888 | bytes 9437184 | tf_op jit(solution)/shard_map/experts/pallas_call | solution.py:38
  116.6 10.9 %all_to_all.84.r_ref = bf16[8,4,4096]{2,1,0:T(4,128)(2,1)S(1)} all-to-all(bf16[8,4,4096]{2,1,0:T(4,128)(2,1)S(1)} %get-tuple-element.17), channel_id=1, replica_groups=mesh['section'=4,'expert'=8] {'expert'}, dimensions={0} | all-to-all | bytes 524288 | tf_op jit(solution)/shard_map/all_to_all | solution.py:24
  127.5 0.1 combine.4
  127.6 0.1 collective-permute-start.1
  127.7 3.3 %collective-permute-done.1 = bf16[4,4096]{1,0:T(4,128)(2,1)S(1)} collective-permute-done((bf16[4,4096]{1,0:T(4,128)(2,1)S(1)}, bf16[4,4096]{1,0:T(4,128)(2,1)S(1)}, u32[]{:S(2)}, u32[]{:S(2)}) %collective-permute-start.1) | collective-permute-done | bytes 32800 | tf_op jit(solution)/shard_map/ppermute | solution.py:20
  131.0 0.1 broadcast_in_dim.15
  131.1 10.9 %all_to_all.85.x_ref = bf16[8,4,4096]{2,1,0:T(4,128)(2,1)S(1)} all-to-all(bf16[8,4,4096]{2,1,0:T(4,128)(2,1)S(1)} %broadcast_in_dim.15), channel_id=1, replica_groups=mesh['section'=4,'expert'=8] {'expert'}, dimensions={0} | all-to-all | bytes 524288 | tf_op jit(solution)/shard_map/all_to_all | solution.py:24
  142.0 1.1 query.5
  143.1 9.4 %all_to_all.86 = bf16[8,16,128]{2,1,0:T(8,128)(2,1)S(1)} all-to-all(bf16[8,16,128]{2,1,0:T(8,128)(2,1)S(1)} %bitcast.34), channel_id=1, replica_groups=mesh['section'=4,'expert'=8] {'expert'}, dimensions={0} | all-to-all | bytes 65536 | tf_op jit(solution)/shard_map/all_to_all | solution.py:24
  152.5 1.2 attention.5
  153.7 10.6 %all_to_all.87 = bf16[8,128,128]{2,1,0:T(8,128)(2,1)S(1)} all-to-all(bf16[8,128,128]{2,1,0:T(8,128)(2,1)S(1)} %broadcast_in_dim.16), channel_id=1, replica_groups=mesh['section'=4,'expert'=8] {'expert'}, dimensions={0} | all-to-all | bytes 524288 | tf_op jit(solution)/shard_map/all_to_all | solution.py:24
  164.4 0.9 attention_out.5
  165.3 10.9 %all_to_all.88.a_ref = bf16[8,32,512]{2,1,0:T(8,128)(2,1)S(1)} all-to-all(bf16[8,32,512]{2,1,0:T(8,128)(2,1)S(1)} %attention_out.5), channel_id=1, replica_groups=mesh['section'=4,'expert'=8] {'expert'}, dimensions={0} | all-to-all | bytes 524288 | tf_op jit(solution)/shard_map/all_to_all | solution.py:24
  176.2 2.0 %experts.5 = (bf16[8,4,4096]{2,1,0:T(4,128)(2,1)S(1)}, f32[4,4096]{1,0:T(4,128)S(1)}) custom-call(s32[1]{0:T(128)} %bitcast.me_ref, bf16[8,32,512]{2,1,0:T(8,128)(2,1)S(1)} %all_to_all.88.a_ref, bf16[8,4,4096]{2,1,0:T(4,128)(2,1)S(1)} %all_to_all.85.x_ref, bf16[1,4096]{1,0:T(2,128)(2,1)S(1)} %copy-done.9, bf16[4096,384]{1,0:T(8,128)(2,1)S(1)} %bitcast.43, ...), custom_call_target="tpu_custom_call" | custom-call | flops 20301989888 | bytes 9437184 | tf_op jit(solution)/shard_map/experts/pallas_call | solution.py:38
  178.1 10.9 %all_to_all.89.r_ref = bf16[8,4,4096]{2,1,0:T(4,128)(2,1)S(1)} all-to-all(bf16[8,4,4096]{2,1,0:T(4,128)(2,1)S(1)} %get-tuple-element.19), channel_id=1, replica_groups=mesh['section'=4,'expert'=8] {'expert'}, dimensions={0} | all-to-all | bytes 524288 | tf_op jit(solution)/shard_map/all_to_all | solution.py:24
  189.0 0.8 combine.5
  (4 shorter events, 0.1 us)
Async XLA Ops:
  0.0 0.8 copy-start.7
  0.8 16.3 %copy-start = (bf16[1,4096,512]{2,1,0:T(8,128)(2,1)S(1)}, bf16[1,4096,512]{2,1,0:T(8,128)(2,1)}, u32[]{:S(2)}) copy-start(bf16[1,4096,512]{2,1,0:T(8,128)(2,1)} %param.15) | copy-start | bytes 12582916
  0.8 16.3 %copy-start.8 = (bf16[1,4096]{1,0:T(2,128)(2,1)S(1)}, bf16[1,4096]{1,0:T(2,128)(2,1)}, u32[]{:S(2)}) copy-start(bf16[1,4096]{1,0:T(2,128)(2,1)} %gain_ref.10) | copy-start | bytes 24580
  17.0 11.2 %copy-start.5 = (bf16[1,3,4,64,4,128]{5,4,3,2,1,0:T(4,128)(2,1)S(1)}, bf16[1,3,4,64,4,128]{5,4,3,2,1,0:T(4,128)(2,1)}, u32[]{:S(2)}) copy-start(bf16[1,3,4,64,4,128]{5,4,3,2,1,0:T(4,128)(2,1)} %param.17) | copy-start | bytes 2359300
  17.1 11.2 %copy-start.6 = (bf16[1,3,4,64,4,128]{5,4,3,2,1,0:T(4,128)(2,1)S(1)}, bf16[1,3,4,64,4,128]{5,4,3,2,1,0:T(4,128)(2,1)}, u32[]{:S(2)}) copy-start(bf16[1,3,4,64,4,128]{5,4,3,2,1,0:T(4,128)(2,1)} %param.18) | copy-start | bytes 2359300
  17.1 11.2 %copy-start.12 = (s32[1,3,4]{2,0,1:T(1,128)S(1)}, s32[1,3,4]{2,0,1:T(1,128)}, u32[]{:S(2)}) copy-start(s32[1,3,4]{2,0,1:T(1,128)} %param.19) | copy-start | bytes 148
  28.2 12.0 %copy-start.1 = (bf16[1,4096,512]{2,1,0:T(8,128)(2,1)S(1)}, bf16[1,4096,512]{2,1,0:T(8,128)(2,1)}, u32[]{:S(2)}) copy-start(bf16[1,4096,512]{2,1,0:T(8,128)(2,1)} %param.16) | copy-start | bytes 12582916
  40.3 12.1 %copy-start.2 = (bf16[1,1,4096,384]{3,2,1,0:T(8,128)(2,1)S(1)}, bf16[1,1,4096,384]{3,2,1,0:T(8,128)(2,1)}, u32[]{:S(2)}) copy-start(bf16[1,1,4096,384]{3,2,1,0:T(8,128)(2,1)} %param.21) | copy-start | bytes 9437188
  40.3 12.1 %copy-start.3 = (bf16[1,1,4096,384]{3,2,1,0:T(8,128)(2,1)S(1)}, bf16[1,1,4096,384]{3,2,1,0:T(8,128)(2,1)}, u32[]{:S(2)}) copy-start(bf16[1,1,4096,384]{3,2,1,0:T(8,128)(2,1)} %param.22) | copy-start | bytes 9437188
  40.3 12.1 %copy-start.4 = (bf16[1,1,384,4096]{3,2,1,0:T(8,128)(2,1)S(1)}, bf16[1,1,384,4096]{3,2,1,0:T(8,128)(2,1)}, u32[]{:S(2)}) copy-start(bf16[1,1,384,4096]{3,2,1,0:T(8,128)(2,1)} %param.23) | copy-start | bytes 9437188
  40.3 12.1 %copy-start.9 = (bf16[1,4096]{1,0:T(2,128)(2,1)S(1)}, bf16[1,4096]{1,0:T(2,128)(2,1)}, u32[]{:S(2)}) copy-start(bf16[1,4096]{1,0:T(2,128)(2,1)} %gain_ref.11) | copy-start | bytes 24580
  52.4 12.9 %copy-start.10 = (s32[1,3,4,2]{2,3,1,0:T(2,128)S(1)}, s32[1,3,4,2]{2,3,1,0:T(2,128)}, u32[]{:S(2)}) copy-start(s32[1,3,4,2]{2,3,1,0:T(2,128)} %param.24) | copy-start | bytes 292
  52.4 12.9 %copy-start.11 = (f32[1,3,4,2]{2,3,1,0:T(2,128)S(1)}, f32[1,3,4,2]{2,3,1,0:T(2,128)}, u32[]{:S(2)}) copy-start(f32[1,3,4,2]{2,3,1,0:T(2,128)} %param.25) | copy-start | bytes 292
  65.4 3.4 %collective-permute-start = (bf16[4,4096]{1,0:T(4,128)(2,1)S(1)}, bf16[4,4096]{1,0:T(4,128)(2,1)S(1)}, u32[]{:S(2)}, u32[]{:S(2)}) collective-permute-start(bf16[4,4096]{1,0:T(4,128)(2,1)S(1)} %combine.3), channel_id=1, source_target_pairs={{0,8},{8,16},{16,24},{24,0},{1,9},{9,17},{17,25},{25,1},{2,10},{10... | collective-permute-start | bytes 98312 | tf_op jit(solution)/shard_map/ppermute | solution.py:20
  127.6 3.4 %collective-permute-start.1 = (bf16[4,4096]{1,0:T(4,128)(2,1)S(1)}, bf16[4,4096]{1,0:T(4,128)(2,1)S(1)}, u32[]{:S(2)}, u32[]{:S(2)}) collective-permute-start(bf16[4,4096]{1,0:T(4,128)(2,1)S(1)} %combine.4), channel_id=1, source_target_pairs={{0,8},{8,16},{16,24},{24,0},{1,9},{9,17},{17,25},{25,1},{2,10},{10... | collective-permute-start | bytes 98312 | tf_op jit(solution)/shard_map/ppermute | solution.py:20

commit v4 on v3

--- a/solution.py
+++ b/solution.py
@@ -15,9 +15,23 @@
 BF16 = jnp.bfloat16
 
 
-def passed_along(array, axis, by):
-    length = lax.axis_size(axis)
-    return lax.ppermute(array, axis, [(i, (i + by) % length) for i in range(length)])
+def shifted(array, mask, sections=0):
+    stages, devices = lax.axis_size("section"), lax.axis_size("expert")
+    pairs = [
+        (s * devices + e, (s + sections) % stages * devices + (e ^ mask))
+        for s in range(stages)
+        for e in range(devices)
+    ]
+    return lax.ppermute(array, ("section", "expert"), pairs)
+
+
+def from_last_section(state):
+    devices = lax.axis_size("expert")
+    pieces = 1
+    while pieces * pieces < devices:
+        pieces *= 2
+    first = jnp.stack([shifted(state, h * pieces, 1) for h in range(devices // pieces)])
+    return [first] + [shifted(first, l) for l in range(1, pieces)]
 
 
 def swapped(blocks):
@@ -69,6 +83,15 @@
 def spread_kernel(x_ref, o_ref):
     for i in range(o_ref.shape[0]):
         o_ref[i] = x_ref[...]
+
+
+def order_kernel(head_dim, count, me_ref, *refs):
+    pieces, (gain_ref, w_ref, q_ref, x_ref, *scratch) = refs[:count], refs[count:]
+    me = me_ref[0]
+    for l, piece in enumerate(pieces):
+        for h in range(piece.shape[0]):
+            x_ref[me ^ (l + h * count)] = piece[h]
+    query_kernel(head_dim, x_ref, gain_ref, w_ref, q_ref, *scratch)
 
 
 def query_kernel(head_dim, x_ref, gain_ref, w_ref, q_ref, states, normed, spread):
@@ -88,7 +111,7 @@
 
 def attention_kernel(step, own, local_heads, kv_heads, q_ref, k_ref, v_ref, len_ref, c_ref):
     count, head_dim = q_ref.shape
-    places = k_ref.shape[0]
+    places = k_ref.shape[1]
     heads = count // own
     group = heads // kv_heads
     cache = places // (own * kv_heads)
@@ -99,7 +122,7 @@
     order = (source == wanted).astype(F32).astype(BF16)
     q = jnp.dot(order, q_ref[...], preferred_element_type=F32).astype(BF16)
     scores = lax.dot_general(
-        q, k_ref[...], (((1,), (1,)), ((), ())), preferred_element_type=F32
+        q, k_ref[step], (((1,), (1,)), ((), ())), preferred_element_type=F32
     ) * head_dim ** (-0.5)
     column = lax.broadcasted_iota(jnp.int32, (1, places), 1)
     of_row = column // (cache * kv_heads)
@@ -112,7 +135,7 @@
     key_for = (line // heads) * kv_heads + (line % heads) // group
     exps = jnp.where(key_of == key_for, jnp.exp(scores), 0.0)
     weights = (exps / jnp.sum(exps, axis=-1, keepdims=True)).astype(BF16)
-    c_ref[...] = jnp.dot(weights, v_ref[...], preferred_element_type=F32).astype(BF16)
+    c_ref[...] = jnp.dot(weights, v_ref[step], preferred_element_type=F32).astype(BF16)
 
 
 def out_kernel(heads, c_ref, w_ref, o_ref, wide, lines):
@@ -210,43 +233,47 @@
     me, copies = lax.optimization_barrier((me, copies))
     smem = whole(pltpu.SMEM)
     for step in range(STEPS):
-        if step:
-            copies = jnp.broadcast_to(state[None], (devices, own, width))
-        states = swapped(copies)
-        own_q = call(
-            functools.partial(query_kernel, head_dim),
-            jax.ShapeDtypeStruct((rows * local_heads, head_dim), BF16),
-            (states, attn_gain, query_w),
-            [whole()] * 3,
-            [
-                pltpu.VMEM((rows, width), F32),
-                pltpu.VMEM((rows, width), BF16),
-                pltpu.VMEM((rows * local_heads, head_dim), F32),
-            ],
-            "query",
-            (2 * rows * width * part, 2 * width * part),
+        scratch = [
+            pltpu.VMEM((rows, width), F32),
+            pltpu.VMEM((rows, width), BF16),
+            pltpu.VMEM((rows * local_heads, head_dim), F32),
+        ]
+        q_shape = jax.ShapeDtypeStruct((rows * local_heads, head_dim), BF16)
+        x_shape = jax.ShapeDtypeStruct((devices, own, width), BF16)
+        cost = (2 * rows * width * part, 2 * width * part)
+        if step == 0:
+            states = swapped(copies)
+            own_q = call(
+                functools.partial(query_kernel, head_dim),
+                q_shape,
+                (states, attn_gain, query_w),
+                [whole()] * 3,
+                scratch,
+                "query",
+                cost,
+            )
+        else:
+            pieces = from_last_section(state)
+            count = len(pieces)
+            own_q, states = call(
+                functools.partial(order_kernel, head_dim, count),
+                (q_shape, x_shape),
+                (me, *pieces, attn_gain, query_w),
+                [smem] + [whole()] * (count + 2),
+                scratch,
+                "order_query",
+                cost,
+            )
+        queries = swapped(own_q.reshape(devices, own * local_heads, head_dim))
+        context = call(
+            functools.partial(attention_kernel, step, own, local_heads, kv_heads),
+            jax.ShapeDtypeStruct((own * heads, head_dim), BF16),
+            (queries.reshape(own * heads, head_dim), keys, values, lengths),
+            [whole()] * 3 + [smem],
+            [],
+            "attention",
+            (4 * own * heads * places * head_dim, 4 * places * head_dim),
         )
-        queries = swapped(own_q.reshape(devices, own * local_heads, head_dim))
-        of_step = pl.BlockSpec((None, places, head_dim), lambda i, step=step: (step, 0, 0))
-        context = pl.pallas_call(
-            functools.partial(attention_kernel, step, own, local_heads, kv_heads),
-            grid=(1,),
-            out_shape=jax.ShapeDtypeStruct((own * heads, head_dim), BF16),
-            in_specs=[
-                pl.BlockSpec((own * heads, head_dim), lambda i: (0, 0)),
-                of_step,
-                of_step,
-                smem,
-            ],
-            out_specs=pl.BlockSpec((own * heads, head_dim), lambda i: (0, 0)),
-            compiler_params=pltpu.CompilerParams(vmem_limit_bytes=LIMIT),
-            cost_estimate=pl.CostEstimate(
-                flops=4 * own * heads * places * head_dim + EXCHANGE,
-                bytes_accessed=4 * places * head_dim,
-                transcendentals=0,
-            ),
-            name="attention",
-        )(queries.reshape(own * heads, head_dim), keys, values, lengths)
         contexts = everyones(context)
         columns = call(
             functools.partial(out_kernel, heads),
@@ -280,8 +307,6 @@
             "combine",
             (4 * rows * width, 4 * rows * width),
         )
-        if step + 1 < STEPS:
-            state = passed_along(state, "section", 1)
     return state[None]
 
 

time: 190 us -> 185 us (0.974)
  blocking collectives: 165 us -> 144 us
  starting transfers between devices: 0.11 us -> 10.1 us
  waiting for transfers between devices: 6.65 us -> 12.1 us
    all_to_all x15 -> x13, blocking collectives: 165 us -> 144 us  [swapped(): lax.all_to_all(blocks, 'expert', split_axis=0, concat_axis=0, tiled=True)]
    ppermute x2 -> x10, starting transfers between devices: 0.11 us -> 10.1 us  [shifted(): return lax.ppermute(array, ('section', 'expert'), pairs)]
    ppermute x2 -> x10, waiting for transfers between devices: 6.65 us -> 12.1 us  [shifted(): return lax.ppermute(array, ('section', 'expert'), pairs)]
    pallas_call x13 -> x16, Pallas kernels: 12.9 us -> 16.4 us  [call(): pl.pallas_call(kernel, out_shape=out, in_specs=specs, out_specs=whole() i...]
    pallas_call x3 -> x0, Pallas kernels: 3.55 us -> none  [body(): pl.pallas_call(functools.partial(attention_kernel, step, own, local_heads...]
  transfers between devices with their start and end apart: 2 -> 10, of which waited for: 2 -> 6; matrix products, arithmetic and copies ran while one was open for 0% -> 0% of each run, Pallas kernels for 0% -> 0%
where the time goes in v4:
time: 185 us; the launch traced here: 184 us
  blocking collectives  144 us (78%)
  Pallas kernels  16.4 us (9%)
  waiting for transfers between devices  12.1 us (7%)
  starting transfers between devices  10.1 us (5%)
    all_to_all x13, blocking collectives, swapped(): lax.all_to_all(blocks, 'expert', split_axis=0, concat_axis=0, tiled=True)  144 us
    pallas_call x16, Pallas kernels, call(): pl.pallas_call(kernel, out_shape=out, in_specs=specs, out_specs=whole() i...  16.4 us
    ppermute x10, waiting for transfers between devices, shifted(): return lax.ppermute(array, ('section', 'expert'), pairs)  12.1 us
    ppermute x10, starting transfers between devices, shifted(): return lax.ppermute(array, ('section', 'expert'), pairs)  10.1 us
  transfers between devices with their start and end apart: 10, of which 6 were waited for; matrix products, arithmetic and copies ran while one was open for 0% of the time, Pallas kernels for 0%

profile of v4, /device:TPU:0, one launch (start us, length us, event | category | flops | bytes accessed | tf_op | source)
XLA Modules:
  0.0 184.0 jit_solution(13464159494906838355)
XLA Ops:
  0.0 0.8 copy-done.7
  0.8 16.3 %all_to_all.65.x_ref = bf16[8,4,4096]{2,1,0:T(4,128)(2,1)S(1)} all-to-all(bf16[8,4,4096]{2,1,0:T(4,128)(2,1)S(1)} %spread.1), channel_id=1, replica_groups=mesh['section'=4,'expert'=8] {'expert'}, dimensions={0} | all-to-all | bytes 524288 | tf_op jit(solution)/shard_map/all_to_all | solution.py:38
  17.0 0.0 copy-done
  17.0 0.0 copy-done.8
  17.1 0.0 copy-start.12
  17.1 1.1 query.1
  18.2 10.1 %all_to_all.66 = bf16[8,16,128]{2,1,0:T(8,128)(2,1)S(1)} all-to-all(bf16[8,16,128]{2,1,0:T(8,128)(2,1)S(1)} %bitcast.38), channel_id=1, replica_groups=mesh['section'=4,'expert'=8] {'expert'}, dimensions={0} | all-to-all | bytes 65536 | tf_op jit(solution)/shard_map/all_to_all | solution.py:38
  28.2 0.0 copy-done.5
  28.2 0.0 copy-done.6
  28.2 0.0 copy-done.12
  28.2 0.0 copy-start.1
  28.3 1.2 attention.3
  29.5 10.8 %all_to_all.67 = bf16[8,128,128]{2,1,0:T(8,128)(2,1)S(1)} all-to-all(bf16[8,128,128]{2,1,0:T(8,128)(2,1)S(1)} %broadcast_in_dim.8), channel_id=1, replica_groups=mesh['section'=4,'expert'=8] {'expert'}, dimensions={0} | all-to-all | bytes 524288 | tf_op jit(solution)/shard_map/all_to_all | solution.py:38
  40.3 0.0 copy-done.1
  40.3 0.0 copy-start.9
  40.3 0.9 attention_out.3
  41.2 11.2 %all_to_all.68.a_ref = bf16[8,32,512]{2,1,0:T(8,128)(2,1)S(1)} all-to-all(bf16[8,32,512]{2,1,0:T(8,128)(2,1)S(1)} %attention_out.3), channel_id=1, replica_groups=mesh['section'=4,'expert'=8] {'expert'}, dimensions={0} | all-to-all | bytes 524288 | tf_op jit(solution)/shard_map/all_to_all | solution.py:38
  52.3 0.0 copy-done.2
  52.3 0.0 copy-done.4
  52.3 0.0 copy-done.9
  52.4 0.0 copy-start.10
  52.4 0.0 copy-start.11
  52.4 2.0 %experts.3 = (bf16[8,4,4096]{2,1,0:T(4,128)(2,1)S(1)}, f32[4,4096]{1,0:T(4,128)S(1)}) custom-call(s32[1]{0:T(128)} %bitcast.me_ref, bf16[8,32,512]{2,1,0:T(8,128)(2,1)S(1)} %all_to_all.68.a_ref, bf16[8,4,4096]{2,1,0:T(4,128)(2,1)S(1)} %all_to_all.65.x_ref, bf16[1,4096]{1,0:T(2,128)(2,1)S(1)} %copy-done.9, bf16[4096,384]{1,0:T(8,128)(2,1)S(1)} %bitcast.45, ...), custom_call_target="tpu_custom_call" | custom-call | flops 20301989888 | bytes 9437184 | tf_op jit(solution)/shard_map/experts/pallas_call | solution.py:52
  54.3 10.9 %all_to_all.69.r_ref = bf16[8,4,4096]{2,1,0:T(4,128)(2,1)S(1)} all-to-all(bf16[8,4,4096]{2,1,0:T(4,128)(2,1)S(1)} %get-tuple-element.19), channel_id=1, replica_groups=mesh['section'=4,'expert'=8] {'expert'}, dimensions={0} | all-to-all | bytes 524288 | tf_op jit(solution)/shard_map/all_to_all | solution.py:38
  65.3 0.0 copy-done.11
  65.3 0.1 combine.3
  65.4 0.1 collective-permute-start.1
  65.5 1.5 collective-permute-start
  66.9 3.7 %collective-permute-done.1 = bf16[4,4096]{1,0:T(4,128)(2,1)S(1)} collective-permute-done((bf16[4,4096]{1,0:T(4,128)(2,1)S(1)}, bf16[4,4096]{1,0:T(4,128)(2,1)S(1)}, u32[]{:S(2)}, u32[]{:S(2)}) %collective-permute-start.1) | collective-permute-done | bytes 32800 | tf_op jit(solution)/shard_map/ppermute | solution.py:25
  70.6 0.0 collective-permute-done
  70.6 1.0 collective-permute-start.4
  71.6 0.6 collective-permute-start.3
  72.3 1.9 %collective-permute-start.2 = (bf16[2,4,4096]{2,1,0:T(4,128)(2,1)S(1)}, bf16[2,4,4096]{2,1,0:T(4,128)(2,1)S(1)}, u32[]{:S(2)}, u32[]{:S(2)}) collective-permute-start(bf16[2,4,4096]{2,1,0:T(4,128)(2,1)S(1)} %pad_maximum_fusion.refs_0_), channel_id=1, source_target_pairs={{0,1},{1,0},{2,3},{3,2},{4,5},{5,4},{6,7},{7,6},{8,9},{9,8},{10,11... | collective-permute-start | bytes 196616 | tf_op jit(solution)/shard_map/ppermute | solution.py:25
  74.2 1.7 collective-permute-done.4.refs_3_
  75.9 0.0 collective-permute-done.3.refs_2_
  75.9 0.7 collective-permute-done.2.refs_1_
  76.6 1.1 order_query.2
  77.7 10.1 %all_to_all.70 = bf16[8,16,128]{2,1,0:T(8,128)(2,1)S(1)} all-to-all(bf16[8,16,128]{2,1,0:T(8,128)(2,1)S(1)} %bitcast.33), channel_id=1, replica_groups=mesh['section'=4,'expert'=8] {'expert'}, dimensions={0} | all-to-all | bytes 65536 | tf_op jit(solution)/shard_map/all_to_all | solution.py:38
  87.8 1.2 attention.4
  89.0 10.6 %all_to_all.71 = bf16[8,128,128]{2,1,0:T(8,128)(2,1)S(1)} all-to-all(bf16[8,128,128]{2,1,0:T(8,128)(2,1)S(1)} %broadcast_in_dim.9), channel_id=1, replica_groups=mesh['section'=4,'expert'=8] {'expert'}, dimensions={0} | all-to-all | bytes 524288 | tf_op jit(solution)/shard_map/all_to_all | solution.py:38
  99.6 0.9 attention_out.4
  100.5 10.9 %all_to_all.72.a_ref = bf16[8,32,512]{2,1,0:T(8,128)(2,1)S(1)} all-to-all(bf16[8,32,512]{2,1,0:T(8,128)(2,1)S(1)} %attention_out.4), channel_id=1, replica_groups=mesh['section'=4,'expert'=8] {'expert'}, dimensions={0} | all-to-all | bytes 524288 | tf_op jit(solution)/shard_map/all_to_all | solution.py:38
  111.4 2.0 %experts.4 = (bf16[8,4,4096]{2,1,0:T(4,128)(2,1)S(1)}, f32[4,4096]{1,0:T(4,128)S(1)}) custom-call(s32[1]{0:T(128)} %bitcast.me_ref, bf16[8,32,512]{2,1,0:T(8,128)(2,1)S(1)} %all_to_all.72.a_ref, bf16[8,4,4096]{2,1,0:T(4,128)(2,1)S(1)} %get-tuple-element.22.x_ref, bf16[1,4096]{1,0:T(2,128)(2,1)S(1)} %copy-done.9, bf16[4096,384]{1,0:T(8,128)(2,1)S(1)} %bitcast.46, ...), custom_call_target="tpu_custom_call" | custom-call | flops 20301989888 | bytes 9437184 | tf_op jit(solution)/shard_map/experts/pallas_call | solution.py:52
  113.4 10.9 %all_to_all.73.r_ref = bf16[8,4,4096]{2,1,0:T(4,128)(2,1)S(1)} all-to-all(bf16[8,4,4096]{2,1,0:T(4,128)(2,1)S(1)} %get-tuple-element.23), channel_id=1, replica_groups=mesh['section'=4,'expert'=8] {'expert'}, dimensions={0} | all-to-all | bytes 524288 | tf_op jit(solution)/shard_map/all_to_all | solution.py:38
  124.3 0.1 combine.4
  124.4 0.1 collective-permute-start.6
  124.5 1.4 collective-permute-start.5
  125.9 3.7 %collective-permute-done.6 = bf16[4,4096]{1,0:T(4,128)(2,1)S(1)} collective-permute-done((bf16[4,4096]{1,0:T(4,128)(2,1)S(1)}, bf16[4,4096]{1,0:T(4,128)(2,1)S(1)}, u32[]{:S(2)}, u32[]{:S(2)}) %collective-permute-start.6) | collective-permute-done | bytes 32800 | tf_op jit(solution)/shard_map/ppermute | solution.py:25
  129.6 0.0 collective-permute-done.5
  129.7 1.0 collective-permute-start.9
  130.7 0.6 collective-permute-start.8
  131.2 2.0 %collective-permute-start.7 = (bf16[2,4,4096]{2,1,0:T(4,128)(2,1)S(1)}, bf16[2,4,4096]{2,1,0:T(4,128)(2,1)S(1)}, u32[]{:S(2)}, u32[]{:S(2)}) collective-permute-start(bf16[2,4,4096]{2,1,0:T(4,128)(2,1)S(1)} %pad_maximum_fusion.1.refs_0_), channel_id=1, source_target_pairs={{0,1},{1,0},{2,3},{3,2},{4,5},{5,4},{6,7},{7,6},{8,9},{9,8},{10,11... | collective-permute-start | bytes 196616 | tf_op jit(solution)/shard_map/ppermute | solution.py:25
  133.2 1.7 collective-permute-done.9.refs_3_
  134.9 0.0 collective-permute-done.8.refs_2_
  134.9 0.7 collective-permute-done.7.refs_1_
  135.6 1.1 order_query.3
  136.7 10.0 %all_to_all.74 = bf16[8,16,128]{2,1,0:T(8,128)(2,1)S(1)} all-to-all(bf16[8,16,128]{2,1,0:T(8,128)(2,1)S(1)} %bitcast.34), channel_id=1, replica_groups=mesh['section'=4,'expert'=8] {'expert'}, dimensions={0} | all-to-all | bytes 65536 | tf_op jit(solution)/shard_map/all_to_all | solution.py:38
  146.7 1.2 attention.5
  148.0 10.6 %all_to_all.75 = bf16[8,128,128]{2,1,0:T(8,128)(2,1)S(1)} all-to-all(bf16[8,128,128]{2,1,0:T(8,128)(2,1)S(1)} %broadcast_in_dim.10), channel_id=1, replica_groups=mesh['section'=4,'expert'=8] {'expert'}, dimensions={0} | all-to-all | bytes 524288 | tf_op jit(solution)/shard_map/all_to_all | solution.py:38
  158.6 0.9 attention_out.5
  159.5 10.9 %all_to_all.76.a_ref = bf16[8,32,512]{2,1,0:T(8,128)(2,1)S(1)} all-to-all(bf16[8,32,512]{2,1,0:T(8,128)(2,1)S(1)} %attention_out.5), channel_id=1, replica_groups=mesh['section'=4,'expert'=8] {'expert'}, dimensions={0} | all-to-all | bytes 524288 | tf_op jit(solution)/shard_map/all_to_all | solution.py:38
  170.4 2.0 %experts.5 = (bf16[8,4,4096]{2,1,0:T(4,128)(2,1)S(1)}, f32[4,4096]{1,0:T(4,128)S(1)}) custom-call(s32[1]{0:T(128)} %bitcast.me_ref, bf16[8,32,512]{2,1,0:T(8,128)(2,1)S(1)} %all_to_all.76.a_ref, bf16[8,4,4096]{2,1,0:T(4,128)(2,1)S(1)} %get-tuple-element.26.x_ref, bf16[1,4096]{1,0:T(2,128)(2,1)S(1)} %copy-done.9, bf16[4096,384]{1,0:T(8,128)(2,1)S(1)} %bitcast.47, ...), custom_call_target="tpu_custom_call" | custom-call | flops 20301989888 | bytes 9437184 | tf_op jit(solution)/shard_map/experts/pallas_call | solution.py:52
  172.4 10.9 %all_to_all.77.r_ref = bf16[8,4,4096]{2,1,0:T(4,128)(2,1)S(1)} all-to-all(bf16[8,4,4096]{2,1,0:T(4,128)(2,1)S(1)} %get-tuple-element.27), channel_id=1, replica_groups=mesh['section'=4,'expert'=8] {'expert'}, dimensions={0} | all-to-all | bytes 524288 | tf_op jit(solution)/shard_map/all_to_all | solution.py:38
  183.3 0.8 combine.5
  (16 shorter events, 0.2 us)
Async XLA Ops:
  0.0 0.8 copy-start.7
  0.8 16.3 %copy-start = (bf16[1,4096,512]{2,1,0:T(8,128)(2,1)S(1)}, bf16[1,4096,512]{2,1,0:T(8,128)(2,1)}, u32[]{:S(2)}) copy-start(bf16[1,4096,512]{2,1,0:T(8,128)(2,1)} %param.15) | copy-start | bytes 12582916
  0.8 16.3 %copy-start.8 = (bf16[1,4096]{1,0:T(2,128)(2,1)S(1)}, bf16[1,4096]{1,0:T(2,128)(2,1)}, u32[]{:S(2)}) copy-start(bf16[1,4096]{1,0:T(2,128)(2,1)} %refs_4_.3) | copy-start | bytes 24580
  17.0 11.2 %copy-start.5 = (bf16[1,3,4,64,4,128]{5,4,3,2,1,0:T(4,128)(2,1)S(1)}, bf16[1,3,4,64,4,128]{5,4,3,2,1,0:T(4,128)(2,1)}, u32[]{:S(2)}) copy-start(bf16[1,3,4,64,4,128]{5,4,3,2,1,0:T(4,128)(2,1)} %param.17) | copy-start | bytes 2359300
  17.1 11.2 %copy-start.6 = (bf16[1,3,4,64,4,128]{5,4,3,2,1,0:T(4,128)(2,1)S(1)}, bf16[1,3,4,64,4,128]{5,4,3,2,1,0:T(4,128)(2,1)}, u32[]{:S(2)}) copy-start(bf16[1,3,4,64,4,128]{5,4,3,2,1,0:T(4,128)(2,1)} %param.18) | copy-start | bytes 2359300
  17.1 11.2 %copy-start.12 = (s32[1,3,4]{2,0,1:T(1,128)S(1)}, s32[1,3,4]{2,0,1:T(1,128)}, u32[]{:S(2)}) copy-start(s32[1,3,4]{2,0,1:T(1,128)} %param.19) | copy-start | bytes 148
  28.2 12.0 %copy-start.1 = (bf16[1,4096,512]{2,1,0:T(8,128)(2,1)S(1)}, bf16[1,4096,512]{2,1,0:T(8,128)(2,1)}, u32[]{:S(2)}) copy-start(bf16[1,4096,512]{2,1,0:T(8,128)(2,1)} %param.16) | copy-start | bytes 12582916
  40.3 12.1 %copy-start.2 = (bf16[1,1,4096,384]{3,2,1,0:T(8,128)(2,1)S(1)}, bf16[1,1,4096,384]{3,2,1,0:T(8,128)(2,1)}, u32[]{:S(2)}) copy-start(bf16[1,1,4096,384]{3,2,1,0:T(8,128)(2,1)} %param.21) | copy-start | bytes 9437188
  40.3 12.1 %copy-start.3 = (bf16[1,1,4096,384]{3,2,1,0:T(8,128)(2,1)S(1)}, bf16[1,1,4096,384]{3,2,1,0:T(8,128)(2,1)}, u32[]{:S(2)}) copy-start(bf16[1,1,4096,384]{3,2,1,0:T(8,128)(2,1)} %param.22) | copy-start | bytes 9437188
  40.3 12.1 %copy-start.4 = (bf16[1,1,384,4096]{3,2,1,0:T(8,128)(2,1)S(1)}, bf16[1,1,384,4096]{3,2,1,0:T(8,128)(2,1)}, u32[]{:S(2)}) copy-start(bf16[1,1,384,4096]{3,2,1,0:T(8,128)(2,1)} %param.23) | copy-start | bytes 9437188
  40.3 12.1 %copy-start.9 = (bf16[1,4096]{1,0:T(2,128)(2,1)S(1)}, bf16[1,4096]{1,0:T(2,128)(2,1)}, u32[]{:S(2)}) copy-start(bf16[1,4096]{1,0:T(2,128)(2,1)} %gain_ref.7) | copy-start | bytes 24580
  52.4 12.9 %copy-start.10 = (s32[1,3,4,2]{2,3,1,0:T(2,128)S(1)}, s32[1,3,4,2]{2,3,1,0:T(2,128)}, u32[]{:S(2)}) copy-start(s32[1,3,4,2]{2,3,1,0:T(2,128)} %param.24) | copy-start | bytes 292
  52.4 12.9 %copy-start.11 = (f32[1,3,4,2]{2,3,1,0:T(2,128)S(1)}, f32[1,3,4,2]{2,3,1,0:T(2,128)}, u32[]{:S(2)}) copy-start(f32[1,3,4,2]{2,3,1,0:T(2,128)} %param.25) | copy-start | bytes 292
  65.4 5.2 %collective-permute-start.1 = (bf16[4,4096]{1,0:T(4,128)(2,1)S(1)}, bf16[4,4096]{1,0:T(4,128)(2,1)S(1)}, u32[]{:S(2)}, u32[]{:S(2)}) collective-permute-start(bf16[4,4096]{1,0:T(4,128)(2,1)S(1)} %combine.3), channel_id=1, source_target_pairs={{0,12},{1,13},{2,14},{3,15},{4,8},{5,9},{6,10},{7,11},{8,20},{9,21... | collective-permute-start | bytes 98312 | tf_op jit(solution)/shard_map/ppermute | solution.py:25
  65.5 5.1 %collective-permute-start = (bf16[4,4096]{1,0:T(4,128)(2,1)S(1)}, bf16[4,4096]{1,0:T(4,128)(2,1)S(1)}, u32[]{:S(2)}, u32[]{:S(2)}) collective-permute-start(bf16[4,4096]{1,0:T(4,128)(2,1)S(1)} %combine.3), channel_id=1, source_target_pairs={{0,8},{1,9},{2,10},{3,11},{4,12},{5,13},{6,14},{7,15},{8,16},{9,17... | collective-permute-start | bytes 98312 | tf_op jit(solution)/shard_map/ppermute | solution.py:25
  70.6 5.2 %collective-permute-start.4 = (bf16[2,4,4096]{2,1,0:T(4,128)(2,1)S(1)}, bf16[2,4,4096]{2,1,0:T(4,128)(2,1)S(1)}, u32[]{:S(2)}, u32[]{:S(2)}) collective-permute-start(bf16[2,4,4096]{2,1,0:T(4,128)(2,1)S(1)} %pad_maximum_fusion.refs_0_), channel_id=1, source_target_pairs={{0,3},{1,2},{2,1},{3,0},{4,7},{5,6},{6,5},{7,4},{8,11},{9,10},{10,... | collective-permute-start | bytes 196616 | tf_op jit(solution)/shard_map/ppermute | solution.py:25
  71.6 4.3 %collective-permute-start.3 = (bf16[2,4,4096]{2,1,0:T(4,128)(2,1)S(1)}, bf16[2,4,4096]{2,1,0:T(4,128)(2,1)S(1)}, u32[]{:S(2)}, u32[]{:S(2)}) collective-permute-start(bf16[2,4,4096]{2,1,0:T(4,128)(2,1)S(1)} %pad_maximum_fusion.refs_0_), channel_id=1, source_target_pairs={{0,2},{1,3},{2,0},{3,1},{4,6},{5,7},{6,4},{7,5},{8,10},{9,11},{10,... | collective-permute-start | bytes 196616 | tf_op jit(solution)/shard_map/ppermute | solution.py:25
  72.3 4.3 %collective-permute-start.2 = (bf16[2,4,4096]{2,1,0:T(4,128)(2,1)S(1)}, bf16[2,4,4096]{2,1,0:T(4,128)(2,1)S(1)}, u32[]{:S(2)}, u32[]{:S(2)}) collective-permute-start(bf16[2,4,4096]{2,1,0:T(4,128)(2,1)S(1)} %pad_maximum_fusion.refs_0_), channel_id=1, source_target_pairs={{0,1},{1,0},{2,3},{3,2},{4,5},{5,4},{6,7},{7,6},{8,9},{9,8},{10,11... | collective-permute-start | bytes 196616 | tf_op jit(solution)/shard_map/ppermute | solution.py:25
  124.4 5.2 %collective-permute-start.6 = (bf16[4,4096]{1,0:T(4,128)(2,1)S(1)}, bf16[4,4096]{1,0:T(4,128)(2,1)S(1)}, u32[]{:S(2)}, u32[]{:S(2)}) collective-permute-start(bf16[4,4096]{1,0:T(4,128)(2,1)S(1)} %combine.4), channel_id=1, source_target_pairs={{0,12},{1,13},{2,14},{3,15},{4,8},{5,9},{6,10},{7,11},{8,20},{9,21... | collective-permute-start | bytes 98312 | tf_op jit(solution)/shard_map/ppermute | solution.py:25
  124.5 5.1 %collective-permute-start.5 = (bf16[4,4096]{1,0:T(4,128)(2,1)S(1)}, bf16[4,4096]{1,0:T(4,128)(2,1)S(1)}, u32[]{:S(2)}, u32[]{:S(2)}) collective-permute-start(bf16[4,4096]{1,0:T(4,128)(2,1)S(1)} %combine.4), channel_id=1, source_target_pairs={{0,8},{1,9},{2,10},{3,11},{4,12},{5,13},{6,14},{7,15},{8,16},{9,17... | collective-permute-start | bytes 98312 | tf_op jit(solution)/shard_map/ppermute | solution.py:25
  129.7 5.2 %collective-permute-start.9 = (bf16[2,4,4096]{2,1,0:T(4,128)(2,1)S(1)}, bf16[2,4,4096]{2,1,0:T(4,128)(2,1)S(1)}, u32[]{:S(2)}, u32[]{:S(2)}) collective-permute-start(bf16[2,4,4096]{2,1,0:T(4,128)(2,1)S(1)} %pad_maximum_fusion.1.refs_0_), channel_id=1, source_target_pairs={{0,3},{1,2},{2,1},{3,0},{4,7},{5,6},{6,5},{7,4},{8,11},{9,10},{10,... | collective-permute-start | bytes 196616 | tf_op jit(solution)/shard_map/ppermute | solution.py:25
  130.7 4.3 %collective-permute-start.8 = (bf16[2,4,4096]{2,1,0:T(4,128)(2,1)S(1)}, bf16[2,4,4096]{2,1,0:T(4,128)(2,1)S(1)}, u32[]{:S(2)}, u32[]{:S(2)}) collective-permute-start(bf16[2,4,4096]{2,1,0:T(4,128)(2,1)S(1)} %pad_maximum_fusion.1.refs_0_), channel_id=1, source_target_pairs={{0,2},{1,3},{2,0},{3,1},{4,6},{5,7},{6,4},{7,5},{8,10},{9,11},{10,... | collective-permute-start | bytes 196616 | tf_op jit(solution)/shard_map/ppermute | solution.py:25
  131.2 4.4 %collective-permute-start.7 = (bf16[2,4,4096]{2,1,0:T(4,128)(2,1)S(1)}, bf16[2,4,4096]{2,1,0:T(4,128)(2,1)S(1)}, u32[]{:S(2)}, u32[]{:S(2)}) collective-permute-start(bf16[2,4,4096]{2,1,0:T(4,128)(2,1)S(1)} %pad_maximum_fusion.1.refs_0_), channel_id=1, source_target_pairs={{0,1},{1,0},{2,3},{3,2},{4,5},{5,4},{6,7},{7,6},{8,9},{9,8},{10,11... | collective-permute-start | bytes 196616 | tf_op jit(solution)/shard_map/ppermute | solution.py:25

commit v5 on v4

v5 whole, which is shorter than its diff:
```python
import functools
import math

import jax
import jax.numpy as jnp
import numpy as np
from jax import lax
from jax.experimental import pallas as pl
from jax.experimental.pallas import tpu as pltpu
from jax.sharding import PartitionSpec as P

STEPS = 3
EPS = 1e-06
LIMIT = 24 * 1024 * 1024
EXCHANGE = 20 * 1000 * 1000 * 1000
LANES = 128
EXTRA = 16
LOG2E = math.log2(math.e)
F32 = jnp.float32
BF16 = jnp.bfloat16


def shifted(array, mask, sections=0):
    stages, devices = lax.axis_size("section"), lax.axis_size("expert")
    pairs = [
        (s * devices + e, (s + sections) % stages * devices + (e ^ mask))
        for s in range(stages)
        for e in range(devices)
    ]
    return lax.ppermute(array, ("section", "expert"), pairs)


def split(devices):
    low = 1
    while low * low < devices:
        low *= 2
    return low, devices // low


def swapped(blocks):
    return lax.all_to_all(blocks, "expert", split_axis=0, concat_axis=0, tiled=True)


def everyones(array):
    devices = lax.axis_size("expert")
    return swapped(jnp.broadcast_to(array[None], (devices,) + array.shape))


def whole(memory_space=pltpu.VMEM):
    return pl.BlockSpec(memory_space=memory_space)


def call(kernel, out, operands, specs, scratch, name, cost):
    single = not isinstance(out, tuple)
    return pl.pallas_call(
        kernel,
        out_shape=out,
        in_specs=specs,
        out_specs=whole() if single else tuple(whole() for _ in out),
        scratch_shapes=scratch,
        compiler_params=pltpu.CompilerParams(vmem_limit_bytes=LIMIT),
        cost_estimate=pl.CostEstimate(flops=cost[0] + EXCHANGE, bytes_accessed=cost[1], transcendentals=0),
        name=name,
    )(*operands)


def normalize(source, gain_ref, target):
    rows, width = source.shape
    block = 16
    gain = gain_ref[...].astype(F32)
    for at in range(0, rows, block):
        values = source[at:at + block, :]
        scale = lax.rsqrt(jnp.mean(values * values, axis=-1, keepdims=True) + EPS)
        target[at:at + block, :] = (source[at:at + block, :] * scale * gain).astype(BF16)


def matmul(left, right, chunk=1024):
    depth = left.shape[1]
    total = None
    for at in range(0, depth, chunk):
        part = jnp.dot(left[:, at:at + chunk], right[at:at + chunk, :], preferred_element_type=F32)
        total = part if total is None else total + part
    return total


def spread_kernel(x_ref, o_ref):
    for i in range(o_ref.shape[0]):
        o_ref[i] = x_ref[...]


def coded_shares(routes_ref, gates_ref, experts):
    own = routes_ref.shape[2]
    lane = lax.broadcasted_iota(jnp.int32, (EXTRA, LANES), 1)
    row = lax.broadcasted_iota(jnp.int32, (EXTRA, LANES), 0)
    line = lax.broadcasted_iota(jnp.int32, (EXTRA, own), 0)
    column = lax.broadcasted_iota(jnp.int32, (EXTRA, own), 1)
    here = (line == column) | (line == column + own) | (line == column + 2 * own)
    shares = jnp.zeros((EXTRA, LANES), F32)
    for step in range(STEPS):
        routes, gates = routes_ref[step], gates_ref[step]
        parts = gates / jnp.sum(gates, axis=0, keepdims=True)
        for e in range(experts):
            share = jnp.sum(jnp.where(routes == e, parts, 0.0), axis=0, keepdims=True)
            share = jnp.sum(jnp.where(here, share, 0.0), axis=1, keepdims=True)
            shares = jnp.where(lane == step * experts + e, share, shares)
    first = shares.astype(BF16).astype(F32)
    second = (shares - first).astype(BF16).astype(F32)
    return jnp.where(row < own, first, jnp.where(row < 2 * own, second, shares - first - second)).astype(BF16)


def first_kernel(head_dim, x_ref, gain_ref, w_ref, routes_ref, gates_ref, q_ref, states, normed, spread):
    query_kernel(head_dim, x_ref, gain_ref, w_ref, None, states, normed, spread)
    devices = q_ref.shape[0]
    count = spread.shape[0] // devices
    coded = coded_shares(routes_ref, gates_ref, devices // 2)
    for i in range(devices):
        q_ref[i, :EXTRA, :] = coded
        q_ref[i, EXTRA:, :] = spread[count * i:count * (i + 1), :].astype(BF16)


def order_kernel(head_dim, low, me_ref, *refs):
    pieces, (gain_ref, w_ref, q_ref, x_ref, *scratch) = refs[:low], refs[low:]
    me = me_ref[0]
    for l, piece in enumerate(pieces):
        for h in range(piece.shape[0]):
            x_ref[me ^ (l + h * low)] = piece[h]
    query_kernel(head_dim, x_ref, gain_ref, w_ref, q_ref, *scratch)


def query_kernel(head_dim, x_ref, gain_ref, w_ref, q_ref, states, normed, spread):
    devices, own, _ = x_ref.shape
    width = w_ref.shape[0]
    rows = devices * own
    heads = w_ref.shape[1] // head_dim
    for i in range(devices):
        states[own * i:own * (i + 1), :] = x_ref[i, :, :width].astype(F32)
    normalize(states, gain_ref, normed)
    query = matmul(normed, w_ref)
    for h in range(heads):
        one = query[:, head_dim * h:head_dim * (h + 1)]
        scale = lax.rsqrt(jnp.mean(one * one, axis=-1, keepdims=True) + EPS)
        spread[pl.ds(h, rows, stride=heads), :] = one * scale
    if q_ref is not None:
        q_ref[...] = spread[...].astype(BF16)


def first_attention_kernel(own, pick_ref, q_ref, *refs):
    *rest, share_ref = refs
    share_ref[...] = jnp.dot(pick_ref[...], q_ref[...], preferred_element_type=F32)
    attention_kernel(0, own, q_ref, *rest)


def attention_kernel(step, own, q_ref, k_ref, v_ref, len_ref, order_ref, line_ref, column_ref, c_ref):
    head_dim = q_ref.shape[1]
    q = jnp.dot(order_ref[...], q_ref[...], preferred_element_type=F32).astype(BF16)
    scores = lax.dot_general(q, k_ref[step], (((1,), (1,)), ((), ())), preferred_element_type=F32)
    key_of, position, of_row = column_ref[0:1, :], column_ref[1:2, :], column_ref[2:3, :]
    length = jnp.zeros(of_row.shape, jnp.int32)
    for r in range(own):
        length = jnp.where(of_row == r, len_ref[step, 0, r], length)
    key_of = jnp.where(position < length, key_of, -1)
    exps = jnp.where(key_of == line_ref[...], jnp.exp2(scores * (head_dim ** (-0.5) * LOG2E)), 0.0)
    scale = 1.0 / jnp.sum(exps, axis=-1, keepdims=True)
    context = jnp.dot(exps.astype(BF16), v_ref[step], preferred_element_type=F32)
    c_ref[...] = (context * scale).astype(BF16)


def attention_tables(own, heads, local_heads, kv_heads, cache_len):
    group = heads // kv_heads
    row, head = np.divmod(np.arange(own * heads), heads)
    sender, place = head // local_heads, row * local_heads + head % local_heads
    devices, count = heads // local_heads, own * local_heads
    order = np.zeros((own * heads, own * heads), np.float32)
    order[np.arange(own * heads), sender * count + place] = 1.0
    first_order = np.zeros((own * heads, devices * (EXTRA + count)), np.float32)
    first_order[np.arange(own * heads), sender * (EXTRA + count) + EXTRA + place] = 1.0
    pick = np.zeros((devices * own, devices * (EXTRA + count)), np.float32)
    for part in range(3):
        for r in range(own):
            pick[np.arange(devices) * own + r, np.arange(devices) * (EXTRA + count) + part * own + r] = 1.0
    line = (row * kv_heads + head // group).astype(np.int32)[:, None]
    place = np.arange(own * cache_len * kv_heads)
    of_row, position, kv = place // (cache_len * kv_heads), place // kv_heads % cache_len, place % kv_heads
    column = np.zeros((8, place.size), np.int32)
    column[:3] = of_row * kv_heads + kv, position, of_row
    asis = jnp.asarray(line), jnp.asarray(column)
    return (jnp.asarray(order, BF16), *asis), (jnp.asarray(first_order, BF16), *asis), jnp.asarray(pick, BF16)


def out_kernel(heads, c_ref, w_ref, o_ref, wide, lines):
    rows = lines.shape[0]
    head_dim = c_ref.shape[1]
    wide[...] = c_ref[...].astype(F32)
    for h in range(heads):
        lines[:, head_dim * h:head_dim * (h + 1)] = wide[pl.ds(h, rows, stride=heads), :].astype(BF16)
    columns = matmul(lines, w_ref).astype(BF16)
    for i in range(o_ref.shape[0]):
        o_ref[i] = columns


def expert_kernel(step, me_ref, a_ref, x_ref, gain_ref, gate_ref, up_ref, down_ref, share_ref, h_ref, m_ref, middle, normed):
    devices, own, _ = x_ref.shape
    part = a_ref.shape[2]
    width = part * devices
    me = me_ref[0]
    for i in range(devices):
        middle[own * i:own * (i + 1), :] = x_ref[i, :, :width].astype(F32)
    for j in range(devices):
        at = slice(part * j, part * (j + 1))
        middle[:, at] = middle[:, at] + a_ref[j].astype(F32)
    normalize(middle, gain_ref, normed)
    gate = matmul(normed, gate_ref)
    up = matmul(normed, up_ref)
    lane = lax.broadcasted_iota(jnp.int32, share_ref.shape, 1)
    mine = lane == step * (devices // 2) + me // 2
    share = jnp.sum(jnp.where(mine, share_ref[...], 0.0), axis=1, keepdims=True)
    active = (gate / (1.0 + jnp.exp(-gate)) * up * share).astype(BF16)
    chunk = 512
    for at in range(0, width, chunk):
        piece = jnp.dot(active, down_ref[:, at:at + chunk], preferred_element_type=F32)
        for i in range(devices):
            h_ref[i, :, at:at + chunk] = piece[own * i:own * (i + 1), :].astype(BF16)
    pairs = 8 // own
    block = middle[pl.ds(pl.multiple_of((me // pairs) * 8, 8), 8), :]
    kept = block[0:own, :]
    for p in range(1, pairs):
        kept = jnp.where(me % pairs == p, block[own * p:own * (p + 1), :], kept)
    m_ref[...] = kept


def sending_kernel(step, low, me_ref, *refs):
    pieces, (m_ref, middle, normed, rows) = refs[7:7 + low], refs[7 + low:]
    expert_kernel(step, me_ref, *refs[:7], rows, m_ref, middle, normed)
    me = me_ref[0]
    for l, piece in enumerate(pieces):
        for h in range(piece.shape[0]):
            piece[h] = rows[me ^ (l + h * low)]


def partial_kernel(m_ref, *refs):
    pieces, t_ref = refs[:-1], refs[-1]
    for h in range(t_ref.shape[0]):
        total = m_ref[...] if h == 0 else jnp.zeros(m_ref.shape, F32)
        for piece in pieces:
            total = total + piece[h].astype(F32)
        t_ref[h] = total.astype(BF16)


def join_kernel(*refs):
    parts, x_ref = refs[:-1], refs[-1]
    for g in range(len(parts)):
        total = parts[0][g].astype(F32)
        for h in range(1, len(parts)):
            total = total + parts[h][h ^ g].astype(F32)
        x_ref[g] = total.astype(BF16)


def combine_kernel(r_ref, m_ref, o_ref):
    total = m_ref[...]
    for i in range(r_ref.shape[0]):
        total = total + r_ref[i].astype(F32)
    o_ref[...] = total.astype(BF16)


def body(
    hidden_in,
    attn_gain,
    w_query,
    w_out,
    key_cache,
    value_cache,
    lengths,
    ffn_gain,
    w_gate,
    w_up,
    w_down,
    routes,
    gates,
):
    devices = lax.axis_size("expert")
    me = lax.axis_index("expert").astype(jnp.int32).reshape(1)
    own, width = hidden_in.shape[1:]
    rows = own * devices
    cache_len, kv_heads, head_dim = key_cache.shape[3:]
    query_w, out_w = w_query[0], w_out[0]
    part = query_w.shape[1]
    local_heads = part // head_dim
    heads = local_heads * devices
    gate_w, up_w, down_w = w_gate[0, 0], w_up[0, 0], w_down[0, 0]
    hidden = gate_w.shape[1]
    places = own * cache_len * kv_heads
    keys = key_cache.reshape(STEPS, places, head_dim)
    values = value_cache.reshape(STEPS, places, head_dim)
    routes, gates = routes[0].transpose(0, 2, 1), gates[0].transpose(0, 2, 1)
    lengths = lengths.reshape(STEPS, 1, own)
    tables, first_tables, pick = attention_tables(own, heads, local_heads, kv_heads, cache_len)
    low, high = split(devices)
    smem = whole(pltpu.SMEM)
    q_shape = jax.ShapeDtypeStruct((rows * local_heads, head_dim), BF16)
    x_shape = jax.ShapeDtypeStruct((devices, own, width), BF16)
    m_shape = jax.ShapeDtypeStruct((own, width), F32)
    slots = jax.ShapeDtypeStruct((high, own, width), BF16)
    copies = call(
        spread_kernel,
        x_shape,
        (hidden_in[0],),
        [whole()],
        [],
        "spread",
        (0, 2 * rows * width),
    )
    me, copies = lax.optimization_barrier((me, copies))
    for step in range(STEPS):
        scratch = [
            pltpu.VMEM((rows, width), F32),
            pltpu.VMEM((rows, width), BF16),
            pltpu.VMEM((rows * local_heads, head_dim), F32),
        ]
        cost = (2 * rows * width * part, 2 * width * part)
        if step == 0:
            states = swapped(copies)
            own_q = call(
                functools.partial(first_kernel, head_dim),
                jax.ShapeDtypeStruct((devices, EXTRA + own * local_heads, head_dim), BF16),
                (states, attn_gain, query_w, routes, gates),
                [whole()] * 5,
                scratch,
                "first_query",
                cost,
            )
        else:
            pieces = [state] + [shifted(state, l) for l in range(1, low)]
            own_q, states = call(
                functools.partial(order_kernel, head_dim, low),
                (q_shape, x_shape),
                (me, *pieces, attn_gain, query_w),
                [smem] + [whole()] * (low + 2),
                scratch,
                "order_query",
                cost,
            )
        c_shape = jax.ShapeDtypeStruct((own * heads, head_dim), BF16)
        cost = (4 * own * heads * places * head_dim, 4 * places * head_dim)
        queries = swapped(own_q.reshape(devices, -1, head_dim)).reshape(-1, head_dim)
        if step == 0:
            context, shares = call(
                functools.partial(first_attention_kernel, own),
                (c_shape, jax.ShapeDtypeStruct((rows, LANES), F32)),
                (pick, queries, keys, values, lengths, *first_tables),
                [whole()] * 4 + [smem] + [whole()] * 3,
                [],
                "first_attention",
                cost,
            )
        else:
            context = call(
                functools.partial(attention_kernel, step, own),
                c_shape,
                (queries, keys, values, lengths, *tables),
                [whole()] * 3 + [smem] + [whole()] * 3,
                [],
                "attention",
                cost,
            )
        contexts = everyones(context)
        columns = call(
            functools.partial(out_kernel, heads),
            jax.ShapeDtypeStruct((devices, rows, part), BF16),
            (contexts.reshape(rows * heads, head_dim), out_w),
            [whole()] * 2,
            [pltpu.VMEM((rows * heads, head_dim), F32), pltpu.VMEM((rows, heads * head_dim), BF16)],
            "attention_out",
            (2 * rows * width * part, 2 * width * part),
        )
        attended = swapped(columns)
        operands = (me, attended, states, ffn_gain, gate_w, up_w, down_w, shares)
        specs = [smem] + [whole()] * 7
        scratch = [pltpu.VMEM((rows, width), F32), pltpu.VMEM((rows, width), BF16)]
        cost = (6 * rows * width * hidden, 6 * width * hidden)
        if step + 1 == STEPS:
            half_out, middle = call(
                functools.partial(expert_kernel, step), (x_shape, m_shape), operands, specs, scratch, "experts", cost
            )
            state = call(
                combine_kernel,
                jax.ShapeDtypeStruct((own, width), BF16),
                (swapped(half_out), middle),
                [whole()] * 2,
                [],
                "combine",
                (rows * width, 4 * rows * width),
            )
        else:
            *pieces, middle = call(
                functools.partial(sending_kernel, step, low),
                (slots,) * low + (m_shape,),
                operands,
                specs,
                scratch + [pltpu.VMEM((devices, own, width), BF16)],
                "experts_sending",
                cost,
            )
            pieces = [pieces[0]] + [shifted(pieces[l], l) for l in range(1, low)]
            part_sums = call(
                partial_kernel, slots, (middle, *pieces), [whole()] * (low + 1), [], "partial",
                (rows * width, 4 * rows * width),
            )
            parts = [shifted(part_sums, h * low, 1) for h in range(high)]
            state = call(
                join_kernel, slots, tuple(parts), [whole()] * high, [], "join", (rows * width, 4 * rows * width)
            )
    return state[None]


def solution(mesh):
    return jax.shard_map(
        body,
        mesh=mesh,
        in_specs=(
            P("section", "expert", None),
            P("section", None),
            P("section", None, "expert"),
            P("section", None, "expert"),
            P("section", None, "expert", None, None, None),
            P("section", None, "expert", None, None, None),
            P("section", None, "expert"),
            P("section", None),
            P("section", "expert", None, None),
            P("section", "expert", None, None),
            P("section", "expert", None, None),
            P("section", None, "expert", None),
            P("section", None, "expert", None),
        ),
        out_specs=P("section", "expert", None),
        check_vma=False,
    )
```

time: 185 us -> 180 us (0.973)
  blocking collectives: 144 us -> 125 us
  waiting for transfers between devices: 12.1 us -> 21.2 us
  starting transfers between devices: 10.1 us -> 16.7 us
    all_to_all x13 -> x11, blocking collectives: 144 us -> 125 us  [swapped(): lax.all_to_all(blocks, 'expert', split_axis=0, concat_axis=0, tiled=True)]
    ppermute x10 -> x16, waiting for transfers between devices: 12.1 us -> 21.2 us  [shifted(): return lax.ppermute(array, ('section', 'expert'), pairs)]
    ppermute x10 -> x16, starting transfers between devices: 10.1 us -> 16.7 us  [shifted(): return lax.ppermute(array, ('section', 'expert'), pairs)]
    pallas_call x16 -> x18, Pallas kernels: 16.4 us -> 15.9 us  [call(): pl.pallas_call(kernel, out_shape=out, in_specs=specs, out_specs=whole() i...]
  transfers between devices with their start and end apart: 10 -> 16, of which waited for: 6 -> 14; matrix products, arithmetic and copies ran while one was open for 0% -> 0% of each run, Pallas kernels for 0% -> 0%
where the time goes in v5:
time: 180 us
  blocking collectives  125 us (69%)
  waiting for transfers between devices  21.2 us (12%)
  starting transfers between devices  16.7 us (9%)
  Pallas kernels  15.9 us (9%)
    all_to_all x11, blocking collectives, swapped(): lax.all_to_all(blocks, 'expert', split_axis=0, concat_axis=0, tiled=True)  125 us
    ppermute x16, waiting for transfers between devices, shifted(): return lax.ppermute(array, ('section', 'expert'), pairs)  21.2 us
    ppermute x16, starting transfers between devices, shifted(): return lax.ppermute(array, ('section', 'expert'), pairs)  16.7 us
    pallas_call x18, Pallas kernels, call(): pl.pallas_call(kernel, out_shape=out, in_specs=specs, out_specs=whole() i...  15.9 us
  transfers between devices with their start and end apart: 16, of which 14 were waited for; matrix products, arithmetic and copies ran while one was open for 0% of the time, Pallas kernels for 0%

profile of v5, /device:TPU:0, one launch (start us, length us, event | category | flops | bytes accessed | tf_op | source)
XLA Modules:
  0.0 179.8 jit_solution(10435135536969651340)
XLA Ops:
  0.0 0.8 copy-done.7
  0.8 16.3 %all_to_all.55.x_ref.refs_1_ = bf16[8,4,4096]{2,1,0:T(4,128)(2,1)S(1)} all-to-all(bf16[8,4,4096]{2,1,0:T(4,128)(2,1)S(1)} %spread.1), channel_id=1, replica_groups=mesh['section'=4,'expert'=8] {'expert'}, dimensions={0} | all-to-all | bytes 524288 | tf_op jit(solution)/shard_map/all_to_all | solution.py:41
  17.1 0.0 copy-start.12
  17.1 0.0 copy-start.13
  17.1 0.0 copy-start.14
  17.1 0.0 copy-start.15
  17.2 0.0 copy-start.17
  17.2 1.1 first_query.1
  18.3 10.3 %all_to_all.56 = bf16[8,32,128]{2,1,0:T(8,128)(2,1)S(1)} all-to-all(bf16[8,32,128]{2,1,0:T(8,128)(2,1)S(1)} %first_query.1), channel_id=1, replica_groups=mesh['section'=4,'expert'=8] {'expert'}, dimensions={0} | all-to-all | bytes 131072 | tf_op jit(solution)/shard_map/all_to_all | solution.py:41
  28.6 0.0 copy-start.1
  28.6 1.1 first_attention.1
  29.7 10.8 %all_to_all.57 = bf16[8,128,128]{2,1,0:T(8,128)(2,1)S(1)} all-to-all(bf16[8,128,128]{2,1,0:T(8,128)(2,1)S(1)} %broadcast_in_dim.8), channel_id=1, replica_groups=mesh['section'=4,'expert'=8] {'expert'}, dimensions={0} | all-to-all | bytes 524288 | tf_op jit(solution)/shard_map/all_to_all | solution.py:41
  40.5 0.9 attention_out.3
  41.4 11.2 %all_to_all.58.refs_0_ = bf16[8,32,512]{2,1,0:T(8,128)(2,1)S(1)} all-to-all(bf16[8,32,512]{2,1,0:T(8,128)(2,1)S(1)} %attention_out.3), channel_id=1, replica_groups=mesh['section'=4,'expert'=8] {'expert'}, dimensions={0} | all-to-all | bytes 524288 | tf_op jit(solution)/shard_map/all_to_all | solution.py:41
  52.6 2.0 %experts_sending.2 = (bf16[2,4,4096]{2,1,0:T(4,128)(2,1)S(1)}, bf16[2,4,4096]{2,1,0:T(4,128)(2,1)S(1)}, bf16[2,4,4096]{2,1,0:T(4,128)(2,1)S(1)}, bf16[2,4,4096]{2,1,0:T(4,128)(2,1)S(1)}, f32[4,4096]{1,0:T(4,128)S(1)}) custom-call(s32[1]{0:T(128)} %bitcast.me_ref, bf16[8,32,512]{2,1,0:T(8,128)(2,1)S(1)} %all_to_all.58.refs_0_, ...), custom_call_target="tpu_custom_call" | custom-call | flops 20301989888 | bytes 9437184 | tf_op jit(solution)/shard_map/experts_sending/pallas_call | solution.py:55
  54.6 0.1 collective-permute-start
  54.7 1.5 collective-permute-start.1
  56.1 2.0 %collective-permute-start.2 = (bf16[2,4,4096]{2,1,0:T(4,128)(2,1)S(1)}, bf16[2,4,4096]{2,1,0:T(4,128)(2,1)S(1)}, u32[]{:S(2)}, u32[]{:S(2)}) collective-permute-start(bf16[2,4,4096]{2,1,0:T(4,128)(2,1)S(1)} %get-tuple-element.33), channel_id=1, source_target_pairs={{0,3},{1,2},{2,1},{3,0},{4,7},{5,6},{6,5},{7,4},{8,11},{9,10},{10,... | collective-permute-start | bytes 196616 | tf_op jit(solution)/shard_map/ppermute | solution.py:30
  58.1 0.8 collective-permute-done.refs_1_
  58.9 0.1 collective-permute-done.1.refs_2_
  59.0 2.3 %collective-permute-done.2.refs_3_ = bf16[2,4,4096]{2,1,0:T(4,128)(2,1)S(1)} collective-permute-done((bf16[2,4,4096]{2,1,0:T(4,128)(2,1)S(1)}, bf16[2,4,4096]{2,1,0:T(4,128)(2,1)S(1)}, u32[]{:S(2)}, u32[]{:S(2)}) %collective-permute-start.2) | collective-permute-done | bytes 65568 | tf_op jit(solution)/shard_map/ppermute | solution.py:30
  61.3 0.1 partial.2
  61.4 0.1 collective-permute-start.4
  61.4 2.3 %collective-permute-start.3 = (bf16[2,4,4096]{2,1,0:T(4,128)(2,1)S(1)}, bf16[2,4,4096]{2,1,0:T(4,128)(2,1)S(1)}, u32[]{:S(2)}, u32[]{:S(2)}) collective-permute-start(bf16[2,4,4096]{2,1,0:T(4,128)(2,1)S(1)} %partial.2), channel_id=1, source_target_pairs={{0,8},{1,9},{2,10},{3,11},{4,12},{5,13},{6,14},{7,15},{8,16},{9,17... | collective-permute-start | bytes 196616 | tf_op jit(solution)/shard_map/ppermute | solution.py:30
  63.7 3.9 %collective-permute-done.4.refs_1_ = bf16[2,4,4096]{2,1,0:T(4,128)(2,1)S(1)} collective-permute-done((bf16[2,4,4096]{2,1,0:T(4,128)(2,1)S(1)}, bf16[2,4,4096]{2,1,0:T(4,128)(2,1)S(1)}, u32[]{:S(2)}, u32[]{:S(2)}) %collective-permute-start.4) | collective-permute-done | bytes 65568 | tf_op jit(solution)/shard_map/ppermute | solution.py:30
  67.6 0.0 copy-start.16
  67.6 1.4 collective-permute-start.7
  69.0 0.4 collective-permute-start.6
  69.4 1.8 collective-permute-start.5
  71.2 1.7 collective-permute-done.7.refs_3_
  72.9 0.4 collective-permute-done.6.refs_2_
  73.3 0.4 collective-permute-done.5.refs_1_
  73.7 1.1 order_query.2
  74.8 11.0 %all_to_all.59 = bf16[8,16,128]{2,1,0:T(8,128)(2,1)S(1)} all-to-all(bf16[8,16,128]{2,1,0:T(8,128)(2,1)S(1)} %bitcast.29), channel_id=1, replica_groups=mesh['section'=4,'expert'=8] {'expert'}, dimensions={0} | all-to-all | bytes 65536 | tf_op jit(solution)/shard_map/all_to_all | solution.py:41
  85.9 1.1 attention.2
  87.0 10.6 %all_to_all.60 = bf16[8,128,128]{2,1,0:T(8,128)(2,1)S(1)} all-to-all(bf16[8,128,128]{2,1,0:T(8,128)(2,1)S(1)} %broadcast_in_dim.9), channel_id=1, replica_groups=mesh['section'=4,'expert'=8] {'expert'}, dimensions={0} | all-to-all | bytes 524288 | tf_op jit(solution)/shard_map/all_to_all | solution.py:41
  97.6 0.9 attention_out.4
  98.5 12.3 %all_to_all.61.refs_0_ = bf16[8,32,512]{2,1,0:T(8,128)(2,1)S(1)} all-to-all(bf16[8,32,512]{2,1,0:T(8,128)(2,1)S(1)} %attention_out.4), channel_id=1, replica_groups=mesh['section'=4,'expert'=8] {'expert'}, dimensions={0} | all-to-all | bytes 524288 | tf_op jit(solution)/shard_map/all_to_all | solution.py:41
  110.8 2.0 %experts_sending.3 = (bf16[2,4,4096]{2,1,0:T(4,128)(2,1)S(1)}, bf16[2,4,4096]{2,1,0:T(4,128)(2,1)S(1)}, bf16[2,4,4096]{2,1,0:T(4,128)(2,1)S(1)}, bf16[2,4,4096]{2,1,0:T(4,128)(2,1)S(1)}, f32[4,4096]{1,0:T(4,128)S(1)}) custom-call(s32[1]{0:T(128)} %bitcast.me_ref, bf16[8,32,512]{2,1,0:T(8,128)(2,1)S(1)} %all_to_all.61.refs_0_, ...), custom_call_target="tpu_custom_call" | custom-call | flops 20301989888 | bytes 9437184 | tf_op jit(solution)/shard_map/experts_sending/pallas_call | solution.py:55
  112.8 0.1 collective-permute-start.8
  112.9 1.5 collective-permute-start.9
  114.3 2.0 %collective-permute-start.10 = (bf16[2,4,4096]{2,1,0:T(4,128)(2,1)S(1)}, bf16[2,4,4096]{2,1,0:T(4,128)(2,1)S(1)}, u32[]{:S(2)}, u32[]{:S(2)}) collective-permute-start(bf16[2,4,4096]{2,1,0:T(4,128)(2,1)S(1)} %get-tuple-element.40), channel_id=1, source_target_pairs={{0,3},{1,2},{2,1},{3,0},{4,7},{5,6},{6,5},{7,4},{8,11},{9,10},{10,... | collective-permute-start | bytes 196616 | tf_op jit(solution)/shard_map/ppermute | solution.py:30
  116.3 0.8 collective-permute-done.8.refs_1_
  117.1 0.1 collective-permute-done.9.refs_2_
  117.2 2.3 %collective-permute-done.10.refs_3_ = bf16[2,4,4096]{2,1,0:T(4,128)(2,1)S(1)} collective-permute-done((bf16[2,4,4096]{2,1,0:T(4,128)(2,1)S(1)}, bf16[2,4,4096]{2,1,0:T(4,128)(2,1)S(1)}, u32[]{:S(2)}, u32[]{:S(2)}) %collective-permute-start.10) | collective-permute-done | bytes 65568 | tf_op jit(solution)/shard_map/ppermute | solution.py:30
  119.5 0.1 partial.3
  119.6 0.1 collective-permute-start.12
  119.6 0.1 collective-permute-start.11
  119.7 6.2 %collective-permute-done.12.refs_1_ = bf16[2,4,4096]{2,1,0:T(4,128)(2,1)S(1)} collective-permute-done((bf16[2,4,4096]{2,1,0:T(4,128)(2,1)S(1)}, bf16[2,4,4096]{2,1,0:T(4,128)(2,1)S(1)}, u32[]{:S(2)}, u32[]{:S(2)}) %collective-permute-start.12) | collective-permute-done | bytes 65568 | tf_op jit(solution)/shard_map/ppermute | solution.py:30
  125.9 1.3 collective-permute-start.15
  127.2 0.0 collective-permute-start.14
  127.2 2.2 %collective-permute-start.13 = (bf16[2,4,4096]{2,1,0:T(4,128)(2,1)S(1)}, bf16[2,4,4096]{2,1,0:T(4,128)(2,1)S(1)}, u32[]{:S(2)}, u32[]{:S(2)}) collective-permute-start(bf16[2,4,4096]{2,1,0:T(4,128)(2,1)S(1)} %join.3.refs_0_), channel_id=1, source_target_pairs={{0,1},{1,0},{2,3},{3,2},{4,5},{5,4},{6,7},{7,6},{8,9},{9,8},{10,11... | collective-permute-start | bytes 196616 | tf_op jit(solution)/shard_map/ppermute | solution.py:30
  129.4 1.7 collective-permute-done.15.refs_3_
  131.1 0.3 collective-permute-done.14.refs_2_
  131.5 0.3 collective-permute-done.13.refs_1_
  131.8 1.1 order_query.3
  132.9 9.8 %all_to_all.62 = bf16[8,16,128]{2,1,0:T(8,128)(2,1)S(1)} all-to-all(bf16[8,16,128]{2,1,0:T(8,128)(2,1)S(1)} %bitcast.30), channel_id=1, replica_groups=mesh['section'=4,'expert'=8] {'expert'}, dimensions={0} | all-to-all | bytes 65536 | tf_op jit(solution)/shard_map/all_to_all | solution.py:41
  142.8 1.1 attention.3
  143.9 10.6 %all_to_all.63 = bf16[8,128,128]{2,1,0:T(8,128)(2,1)S(1)} all-to-all(bf16[8,128,128]{2,1,0:T(8,128)(2,1)S(1)} %broadcast_in_dim.10), channel_id=1, replica_groups=mesh['section'=4,'expert'=8] {'expert'}, dimensions={0} | all-to-all | bytes 524288 | tf_op jit(solution)/shard_map/all_to_all | solution.py:41
  154.5 0.9 attention_out.5
  155.4 10.9 %all_to_all.64.a_ref = bf16[8,32,512]{2,1,0:T(8,128)(2,1)S(1)} all-to-all(bf16[8,32,512]{2,1,0:T(8,128)(2,1)S(1)} %attention_out.5), channel_id=1, replica_groups=mesh['section'=4,'expert'=8] {'expert'}, dimensions={0} | all-to-all | bytes 524288 | tf_op jit(solution)/shard_map/all_to_all | solution.py:41
  166.3 2.0 %experts.1 = (bf16[8,4,4096]{2,1,0:T(4,128)(2,1)S(1)}, f32[4,4096]{1,0:T(4,128)S(1)}) custom-call(s32[1]{0:T(128)} %bitcast.me_ref, bf16[8,32,512]{2,1,0:T(8,128)(2,1)S(1)} %all_to_all.64.a_ref, bf16[8,4,4096]{2,1,0:T(4,128)(2,1)S(1)} %get-tuple-element.42.x_ref, bf16[1,4096]{1,0:T(2,128)(2,1)S(1)} %copy-done.9, bf16[4096,384]{1,0:T(8,128)(2,1)S(1)} %bitcast.41, ...), custom_call_target="tpu_custom_call" | custom-call | flops 20301989888 | bytes 9437184 | tf_op jit(solution)/shard_map/experts/pallas_call | solution.py:55
  168.3 10.9 %all_to_all.65.r_ref = bf16[8,4,4096]{2,1,0:T(4,128)(2,1)S(1)} all-to-all(bf16[8,4,4096]{2,1,0:T(4,128)(2,1)S(1)} %get-tuple-element.43), channel_id=1, replica_groups=mesh['section'=4,'expert'=8] {'expert'}, dimensions={0} | all-to-all | bytes 524288 | tf_op jit(solution)/shard_map/all_to_all | solution.py:41
  179.2 0.7 combine.1
  (36 shorter events, 0.3 us)
Async XLA Ops:
  0.0 0.8 copy-start.7
  0.8 16.3 %copy-start = (bf16[1,4096,512]{2,1,0:T(8,128)(2,1)S(1)}, bf16[1,4096,512]{2,1,0:T(8,128)(2,1)}, u32[]{:S(2)}) copy-start(bf16[1,4096,512]{2,1,0:T(8,128)(2,1)} %param.20) | copy-start | bytes 12582916
  0.8 16.3 %copy-start.8 = (bf16[1,4096]{1,0:T(2,128)(2,1)S(1)}, bf16[1,4096]{1,0:T(2,128)(2,1)}, u32[]{:S(2)}) copy-start(bf16[1,4096]{1,0:T(2,128)(2,1)} %refs_4_.4) | copy-start | bytes 24580
  0.8 16.3 %copy-start.10 = (s32[1,3,4,2]{2,3,1,0:T(2,128)S(1)}, s32[1,3,4,2]{2,3,1,0:T(2,128)}, u32[]{:S(2)}) copy-start(s32[1,3,4,2]{2,3,1,0:T(2,128)} %param.29) | copy-start | bytes 292
  0.8 16.3 %copy-start.11 = (f32[1,3,4,2]{2,3,1,0:T(2,128)S(1)}, f32[1,3,4,2]{2,3,1,0:T(2,128)}, u32[]{:S(2)}) copy-start(f32[1,3,4,2]{2,3,1,0:T(2,128)} %param.30) | copy-start | bytes 292
  17.1 11.5 %copy-start.5 = (bf16[1,3,4,64,4,128]{5,4,3,2,1,0:T(4,128)(2,1)S(1)}, bf16[1,3,4,64,4,128]{5,4,3,2,1,0:T(4,128)(2,1)}, u32[]{:S(2)}) copy-start(bf16[1,3,4,64,4,128]{5,4,3,2,1,0:T(4,128)(2,1)} %param.22) | copy-start | bytes 2359300
  17.1 11.5 %copy-start.6 = (bf16[1,3,4,64,4,128]{5,4,3,2,1,0:T(4,128)(2,1)S(1)}, bf16[1,3,4,64,4,128]{5,4,3,2,1,0:T(4,128)(2,1)}, u32[]{:S(2)}) copy-start(bf16[1,3,4,64,4,128]{5,4,3,2,1,0:T(4,128)(2,1)} %param.23) | copy-start | bytes 2359300
  17.1 11.5 %copy-start.12 = (s32[1,3,4]{2,0,1:T(1,128)S(1)}, s32[1,3,4]{2,0,1:T(1,128)}, u32[]{:S(2)}) copy-start(s32[1,3,4]{2,0,1:T(1,128)} %param.24) | copy-start | bytes 148
  17.1 11.4 %copy-start.13 = (s32[128,1]{1,0:T(8,128)S(1)}, s32[128,1]{1,0:T(8,128)}, u32[]{:S(2)}) copy-start(s32[128,1]{1,0:T(8,128)} %constant.14.clone.refs_4_.line_ref) | copy-start | bytes 1540
  17.1 11.4 %copy-start.14 = (bf16[128,256]{1,0:T(8,128)(2,1)S(1)}, bf16[128,256]{1,0:T(8,128)(2,1)}, u32[]{:S(2)}) copy-start(bf16[128,256]{1,0:T(8,128)(2,1)} %constant.17.clone.refs_3_) | copy-start | bytes 196612
  17.1 11.4 %copy-start.15 = (s32[8,1024]{1,0:T(8,128)S(1)}, s32[8,1024]{1,0:T(8,128)}, u32[]{:S(2)}) copy-start(s32[8,1024]{1,0:T(8,128)} %constant.15.clone.refs_5_.column_ref) | copy-start | bytes 98308
  17.2 11.4 %copy-start.17 = (bf16[32,256]{1,0:T(8,128)(2,1)S(1)}, bf16[32,256]{1,0:T(8,128)(2,1)}, u32[]{:S(2)}) copy-start(bf16[32,256]{1,0:T(8,128)(2,1)} %constant.18.clone.pick_ref) | copy-start | bytes 49156
  28.6 11.9 %copy-start.1 = (bf16[1,4096,512]{2,1,0:T(8,128)(2,1)S(1)}, bf16[1,4096,512]{2,1,0:T(8,128)(2,1)}, u32[]{:S(2)}) copy-start(bf16[1,4096,512]{2,1,0:T(8,128)(2,1)} %param.21) | copy-start | bytes 12582916
  40.5 12.1 %copy-start.2 = (bf16[1,1,4096,384]{3,2,1,0:T(8,128)(2,1)S(1)}, bf16[1,1,4096,384]{3,2,1,0:T(8,128)(2,1)}, u32[]{:S(2)}) copy-start(bf16[1,1,4096,384]{3,2,1,0:T(8,128)(2,1)} %param.26) | copy-start | bytes 9437188
  40.5 12.1 %copy-start.3 = (bf16[1,1,4096,384]{3,2,1,0:T(8,128)(2,1)S(1)}, bf16[1,1,4096,384]{3,2,1,0:T(8,128)(2,1)}, u32[]{:S(2)}) copy-start(bf16[1,1,4096,384]{3,2,1,0:T(8,128)(2,1)} %param.27) | copy-start | bytes 9437188
  40.5 12.1 %copy-start.4 = (bf16[1,1,384,4096]{3,2,1,0:T(8,128)(2,1)S(1)}, bf16[1,1,384,4096]{3,2,1,0:T(8,128)(2,1)}, u32[]{:S(2)}) copy-start(bf16[1,1,384,4096]{3,2,1,0:T(8,128)(2,1)} %param.28) | copy-start | bytes 9437188
  40.5 12.1 %copy-start.9 = (bf16[1,4096]{1,0:T(2,128)(2,1)S(1)}, bf16[1,4096]{1,0:T(2,128)(2,1)}, u32[]{:S(2)}) copy-start(bf16[1,4096]{1,0:T(2,128)(2,1)} %gain_ref.3) | copy-start | bytes 24580
  54.6 4.3 %collective-permute-start = (bf16[2,4,4096]{2,1,0:T(4,128)(2,1)S(1)}, bf16[2,4,4096]{2,1,0:T(4,128)(2,1)S(1)}, u32[]{:S(2)}, u32[]{:S(2)}) collective-permute-start(bf16[2,4,4096]{2,1,0:T(4,128)(2,1)S(1)} %get-tuple-element.31), channel_id=1, source_target_pairs={{0,1},{1,0},{2,3},{3,2},{4,5},{5,4},{6,7},{7,6},{8,9},{9,8},{10,11... | collective-permute-start | bytes 196616 | tf_op jit(solution)/shard_map/ppermute | solution.py:30
  54.7 4.3 %collective-permute-start.1 = (bf16[2,4,4096]{2,1,0:T(4,128)(2,1)S(1)}, bf16[2,4,4096]{2,1,0:T(4,128)(2,1)S(1)}, u32[]{:S(2)}, u32[]{:S(2)}) collective-permute-start(bf16[2,4,4096]{2,1,0:T(4,128)(2,1)S(1)} %get-tuple-element.32), channel_id=1, source_target_pairs={{0,2},{1,3},{2,0},{3,1},{4,6},{5,7},{6,4},{7,5},{8,10},{9,11},{10,... | collective-permute-start | bytes 196616 | tf_op jit(solution)/shard_map/ppermute | solution.py:30
  56.1 5.2 %collective-permute-start.2 = (bf16[2,4,4096]{2,1,0:T(4,128)(2,1)S(1)}, bf16[2,4,4096]{2,1,0:T(4,128)(2,1)S(1)}, u32[]{:S(2)}, u32[]{:S(2)}) collective-permute-start(bf16[2,4,4096]{2,1,0:T(4,128)(2,1)S(1)} %get-tuple-element.33), channel_id=1, source_target_pairs={{0,3},{1,2},{2,1},{3,0},{4,7},{5,6},{6,5},{7,4},{8,11},{9,10},{10,... | collective-permute-start | bytes 196616 | tf_op jit(solution)/shard_map/ppermute | solution.py:30
  61.4 6.2 %collective-permute-start.4 = (bf16[2,4,4096]{2,1,0:T(4,128)(2,1)S(1)}, bf16[2,4,4096]{2,1,0:T(4,128)(2,1)S(1)}, u32[]{:S(2)}, u32[]{:S(2)}) collective-permute-start(bf16[2,4,4096]{2,1,0:T(4,128)(2,1)S(1)} %partial.2), channel_id=1, source_target_pairs={{0,12},{1,13},{2,14},{3,15},{4,8},{5,9},{6,10},{7,11},{8,20},{9,21... | collective-permute-start | bytes 196616 | tf_op jit(solution)/shard_map/ppermute | solution.py:30
  61.4 6.2 %collective-permute-start.3 = (bf16[2,4,4096]{2,1,0:T(4,128)(2,1)S(1)}, bf16[2,4,4096]{2,1,0:T(4,128)(2,1)S(1)}, u32[]{:S(2)}, u32[]{:S(2)}) collective-permute-start(bf16[2,4,4096]{2,1,0:T(4,128)(2,1)S(1)} %partial.2), channel_id=1, source_target_pairs={{0,8},{1,9},{2,10},{3,11},{4,12},{5,13},{6,14},{7,15},{8,16},{9,17... | collective-permute-start | bytes 196616 | tf_op jit(solution)/shard_map/ppermute | solution.py:30
  67.6 18.2 %copy-start.16 = (bf16[128,128]{1,0:T(8,128)(2,1)S(1)}, bf16[128,128]{1,0:T(8,128)(2,1)}, u32[]{:S(2)}) copy-start(bf16[128,128]{1,0:T(8,128)(2,1)} %constant.16.clone.order_ref) | copy-start | bytes 98308
  67.6 5.2 %collective-permute-start.7 = (bf16[2,4,4096]{2,1,0:T(4,128)(2,1)S(1)}, bf16[2,4,4096]{2,1,0:T(4,128)(2,1)S(1)}, u32[]{:S(2)}, u32[]{:S(2)}) collective-permute-start(bf16[2,4,4096]{2,1,0:T(4,128)(2,1)S(1)} %join.2.refs_0_), channel_id=1, source_target_pairs={{0,3},{1,2},{2,1},{3,0},{4,7},{5,6},{6,5},{7,4},{8,11},{9,10},{10,... | collective-permute-start | bytes 196616 | tf_op jit(solution)/shard_map/ppermute | solution.py:30
  69.0 4.3 %collective-permute-start.6 = (bf16[2,4,4096]{2,1,0:T(4,128)(2,1)S(1)}, bf16[2,4,4096]{2,1,0:T(4,128)(2,1)S(1)}, u32[]{:S(2)}, u32[]{:S(2)}) collective-permute-start(bf16[2,4,4096]{2,1,0:T(4,128)(2,1)S(1)} %join.2.refs_0_), channel_id=1, source_target_pairs={{0,2},{1,3},{2,0},{3,1},{4,6},{5,7},{6,4},{7,5},{8,10},{9,11},{10,... | collective-permute-start | bytes 196616 | tf_op jit(solution)/shard_map/ppermute | solution.py:30
  69.4 4.3 %collective-permute-start.5 = (bf16[2,4,4096]{2,1,0:T(4,128)(2,1)S(1)}, bf16[2,4,4096]{2,1,0:T(4,128)(2,1)S(1)}, u32[]{:S(2)}, u32[]{:S(2)}) collective-permute-start(bf16[2,4,4096]{2,1,0:T(4,128)(2,1)S(1)} %join.2.refs_0_), channel_id=1, source_target_pairs={{0,1},{1,0},{2,3},{3,2},{4,5},{5,4},{6,7},{7,6},{8,9},{9,8},{10,11... | collective-permute-start | bytes 196616 | tf_op jit(solution)/shard_map/ppermute | solution.py:30
  112.8 4.3 %collective-permute-start.8 = (bf16[2,4,4096]{2,1,0:T(4,128)(2,1)S(1)}, bf16[2,4,4096]{2,1,0:T(4,128)(2,1)S(1)}, u32[]{:S(2)}, u32[]{:S(2)}) collective-permute-start(bf16[2,4,4096]{2,1,0:T(4,128)(2,1)S(1)} %get-tuple-element.38), channel_id=1, source_target_pairs={{0,1},{1,0},{2,3},{3,2},{4,5},{5,4},{6,7},{7,6},{8,9},{9,8},{10,11... | collective-permute-start | bytes 196616 | tf_op jit(solution)/shard_map/ppermute | solution.py:30
  112.9 4.3 %collective-permute-start.9 = (bf16[2,4,4096]{2,1,0:T(4,128)(2,1)S(1)}, bf16[2,4,4096]{2,1,0:T(4,128)(2,1)S(1)}, u32[]{:S(2)}, u32[]{:S(2)}) collective-permute-start(bf16[2,4,4096]{2,1,0:T(4,128)(2,1)S(1)} %get-tuple-element.39), channel_id=1, source_target_pairs={{0,2},{1,3},{2,0},{3,1},{4,6},{5,7},{6,4},{7,5},{8,10},{9,11},{10,... | collective-permute-start | bytes 196616 | tf_op jit(solution)/shard_map/ppermute | solution.py:30
  114.3 5.2 %collective-permute-start.10 = (bf16[2,4,4096]{2,1,0:T(4,128)(2,1)S(1)}, bf16[2,4,4096]{2,1,0:T(4,128)(2,1)S(1)}, u32[]{:S(2)}, u32[]{:S(2)}) collective-permute-start(bf16[2,4,4096]{2,1,0:T(4,128)(2,1)S(1)} %get-tuple-element.40), channel_id=1, source_target_pairs={{0,3},{1,2},{2,1},{3,0},{4,7},{5,6},{6,5},{7,4},{8,11},{9,10},{10,... | collective-permute-start | bytes 196616 | tf_op jit(solution)/shard_map/ppermute | solution.py:30
  119.6 6.3 %collective-permute-start.12 = (bf16[2,4,4096]{2,1,0:T(4,128)(2,1)S(1)}, bf16[2,4,4096]{2,1,0:T(4,128)(2,1)S(1)}, u32[]{:S(2)}, u32[]{:S(2)}) collective-permute-start(bf16[2,4,4096]{2,1,0:T(4,128)(2,1)S(1)} %partial.3), channel_id=1, source_target_pairs={{0,12},{1,13},{2,14},{3,15},{4,8},{5,9},{6,10},{7,11},{8,20},{9,21... | collective-permute-start | bytes 196616 | tf_op jit(solution)/shard_map/ppermute | solution.py:30
  119.6 6.2 %collective-permute-start.11 = (bf16[2,4,4096]{2,1,0:T(4,128)(2,1)S(1)}, bf16[2,4,4096]{2,1,0:T(4,128)(2,1)S(1)}, u32[]{:S(2)}, u32[]{:S(2)}) collective-permute-start(bf16[2,4,4096]{2,1,0:T(4,128)(2,1)S(1)} %partial.3), channel_id=1, source_target_pairs={{0,8},{1,9},{2,10},{3,11},{4,12},{5,13},{6,14},{7,15},{8,16},{9,17... | collective-permute-start | bytes 196616 | tf_op jit(solution)/shard_map/ppermute | solution.py:30
  125.9 5.2 %collective-permute-start.15 = (bf16[2,4,4096]{2,1,0:T(4,128)(2,1)S(1)}, bf16[2,4,4096]{2,1,0:T(4,128)(2,1)S(1)}, u32[]{:S(2)}, u32[]{:S(2)}) collective-permute-start(bf16[2,4,4096]{2,1,0:T(4,128)(2,1)S(1)} %join.3.refs_0_), channel_id=1, source_target_pairs={{0,3},{1,2},{2,1},{3,0},{4,7},{5,6},{6,5},{7,4},{8,11},{9,10},{10,... | collective-permute-start | bytes 196616 | tf_op jit(solution)/shard_map/ppermute | solution.py:30
  127.2 4.3 %collective-permute-start.14 = (bf16[2,4,4096]{2,1,0:T(4,128)(2,1)S(1)}, bf16[2,4,4096]{2,1,0:T(4,128)(2,1)S(1)}, u32[]{:S(2)}, u32[]{:S(2)}) collective-permute-start(bf16[2,4,4096]{2,1,0:T(4,128)(2,1)S(1)} %join.3.refs_0_), channel_id=1, source_target_pairs={{0,2},{1,3},{2,0},{3,1},{4,6},{5,7},{6,4},{7,5},{8,10},{9,11},{10,... | collective-permute-start | bytes 196616 | tf_op jit(solution)/shard_map/ppermute | solution.py:30
  127.2 4.6 %collective-permute-start.13 = (bf16[2,4,4096]{2,1,0:T(4,128)(2,1)S(1)}, bf16[2,4,4096]{2,1,0:T(4,128)(2,1)S(1)}, u32[]{:S(2)}, u32[]{:S(2)}) collective-permute-start(bf16[2,4,4096]{2,1,0:T(4,128)(2,1)S(1)} %join.3.refs_0_), channel_id=1, source_target_pairs={{0,1},{1,0},{2,3},{3,2},{4,5},{5,4},{6,7},{7,6},{8,9},{9,8},{10,11... | collective-permute-start | bytes 196616 | tf_op jit(solution)/shard_map/ppermute | solution.py:30

commit v6 on v5

--- a/solution.py
+++ b/solution.py
@@ -64,23 +64,16 @@
     )(*operands)
 
 
-def normalize(source, gain_ref, target):
-    rows, width = source.shape
-    block = 16
-    gain = gain_ref[...].astype(F32)
-    for at in range(0, rows, block):
-        values = source[at:at + block, :]
-        scale = lax.rsqrt(jnp.mean(values * values, axis=-1, keepdims=True) + EPS)
-        target[at:at + block, :] = (source[at:at + block, :] * scale * gain).astype(BF16)
-
-
-def matmul(left, right, chunk=1024):
-    depth = left.shape[1]
-    total = None
-    for at in range(0, depth, chunk):
-        part = jnp.dot(left[:, at:at + chunk], right[at:at + chunk, :], preferred_element_type=F32)
-        total = part if total is None else total + part
-    return total
+def add_tiles(totals, left, right, depth, tile=128):
+    for at in range(0, right.shape[1], tile):
+        part = jnp.dot(left, right[depth, at:at + tile], preferred_element_type=F32)
+        totals[at] = totals[at] + part if at in totals else part
+
+
+def add_squares(totals, values):
+    for at in range(0, values.shape[1], 128):
+        totals = totals + values[:, at:at + 128] * values[:, at:at + 128]
+    return totals
 
 
 def spread_kernel(x_ref, o_ref):
@@ -108,8 +101,8 @@
     return jnp.where(row < own, first, jnp.where(row < 2 * own, second, shares - first - second)).astype(BF16)
 
 
-def first_kernel(head_dim, x_ref, gain_ref, w_ref, routes_ref, gates_ref, q_ref, states, normed, spread):
-    query_kernel(head_dim, x_ref, gain_ref, w_ref, None, states, normed, spread)
+def first_kernel(head_dim, x_ref, gain_ref, w_ref, routes_ref, gates_ref, q_ref, states, spread):
+    query_kernel(head_dim, x_ref, gain_ref, w_ref, None, states, spread)
     devices = q_ref.shape[0]
     count = spread.shape[0] // devices
     coded = coded_shares(routes_ref, gates_ref, devices // 2)
@@ -127,19 +120,24 @@
     query_kernel(head_dim, x_ref, gain_ref, w_ref, q_ref, *scratch)
 
 
-def query_kernel(head_dim, x_ref, gain_ref, w_ref, q_ref, states, normed, spread):
+def query_kernel(head_dim, x_ref, gain_ref, w_ref, q_ref, states, spread):
     devices, own, _ = x_ref.shape
-    width = w_ref.shape[0]
-    rows = devices * own
-    heads = w_ref.shape[1] // head_dim
-    for i in range(devices):
-        states[own * i:own * (i + 1), :] = x_ref[i, :, :width].astype(F32)
-    normalize(states, gain_ref, normed)
-    query = matmul(normed, w_ref)
+    rows, (width, columns) = devices * own, w_ref.shape
+    heads = columns // head_dim
+    chunk = 512
+    totals, squares = {}, jnp.zeros((rows, 128), F32)
+    for start in range(0, width, chunk):
+        at = slice(start, start + chunk)
+        for i in range(devices):
+            states[own * i:own * (i + 1), at] = x_ref[i, :, at].astype(F32)
+        values = states[:, at]
+        squares = add_squares(squares, values)
+        add_tiles(totals, (values * gain_ref[:, at].astype(F32)).astype(BF16), w_ref, at, head_dim)
+    scale = lax.rsqrt(jnp.sum(squares, axis=-1, keepdims=True) / width + EPS)
     for h in range(heads):
-        one = query[:, head_dim * h:head_dim * (h + 1)]
-        scale = lax.rsqrt(jnp.mean(one * one, axis=-1, keepdims=True) + EPS)
-        spread[pl.ds(h, rows, stride=heads), :] = one * scale
+        one = totals[head_dim * h] * scale
+        norm = lax.rsqrt(jnp.mean(one * one, axis=-1, keepdims=True) + EPS)
+        spread[pl.ds(h, rows, stride=heads), :] = one * norm
     if q_ref is not None:
         q_ref[...] = spread[...].astype(BF16)
 
@@ -193,33 +191,50 @@
     wide[...] = c_ref[...].astype(F32)
     for h in range(heads):
         lines[:, head_dim * h:head_dim * (h + 1)] = wide[pl.ds(h, rows, stride=heads), :].astype(BF16)
-    columns = matmul(lines, w_ref).astype(BF16)
+    chunk, total = 1024, None
+    for start in range(0, lines.shape[1], chunk):
+        at = slice(start, start + chunk)
+        part = jnp.dot(lines[:, at], w_ref[at, :], preferred_element_type=F32)
+        total = part if total is None else total + part
+    columns = total.astype(BF16)
     for i in range(o_ref.shape[0]):
         o_ref[i] = columns
 
 
-def expert_kernel(step, me_ref, a_ref, x_ref, gain_ref, gate_ref, up_ref, down_ref, share_ref, h_ref, m_ref, middle, normed):
+def expert_kernel(step, me_ref, a_ref, x_ref, gain_ref, gate_ref, up_ref, down_ref, share_ref, h_ref, m_ref, middle):
     devices, own, _ = x_ref.shape
     part = a_ref.shape[2]
     width = part * devices
     me = me_ref[0]
-    for i in range(devices):
-        middle[own * i:own * (i + 1), :] = x_ref[i, :, :width].astype(F32)
+    gates, ups, squares = {}, {}, jnp.zeros((devices * own, 128), F32)
     for j in range(devices):
         at = slice(part * j, part * (j + 1))
-        middle[:, at] = middle[:, at] + a_ref[j].astype(F32)
-    normalize(middle, gain_ref, normed)
-    gate = matmul(normed, gate_ref)
-    up = matmul(normed, up_ref)
+        for i in range(devices):
+            middle[own * i:own * (i + 1), at] = x_ref[i, :, at].astype(F32)
+        values = middle[:, at] + a_ref[j].astype(F32)
+        middle[:, at] = values
+        squares = add_squares(squares, values)
+        left = (values * gain_ref[:, at].astype(F32)).astype(BF16)
+        add_tiles(gates, left, gate_ref, at)
+        add_tiles(ups, left, up_ref, at)
+    scale = lax.rsqrt(jnp.sum(squares, axis=-1, keepdims=True) / width + EPS)
     lane = lax.broadcasted_iota(jnp.int32, share_ref.shape, 1)
     mine = lane == step * (devices // 2) + me // 2
     share = jnp.sum(jnp.where(mine, share_ref[...], 0.0), axis=1, keepdims=True)
-    active = (gate / (1.0 + jnp.exp(-gate)) * up * share).astype(BF16)
+    active = {}
+    for at in gates:
+        gate, up = gates[at] * scale, ups[at] * scale
+        active[at] = (gate / (1.0 + jnp.exp(-gate)) * up * share).astype(BF16)
     chunk = 512
-    for at in range(0, width, chunk):
-        piece = jnp.dot(active, down_ref[:, at:at + chunk], preferred_element_type=F32)
+    for start in range(0, width, chunk):
+        piece = None
+        for at, left in active.items():
+            term = jnp.dot(
+                left, down_ref[at:at + left.shape[1], start:start + chunk], preferred_element_type=F32
+            )
+            piece = term if piece is None else piece + term
         for i in range(devices):
-            h_ref[i, :, at:at + chunk] = piece[own * i:own * (i + 1), :].astype(BF16)
+            h_ref[i, :, start:start + chunk] = piece[own * i:own * (i + 1), :].astype(BF16)
     pairs = 8 // own
     block = middle[pl.ds(pl.multiple_of((me // pairs) * 8, 8), 8), :]
     kept = block[0:own, :]
@@ -229,8 +244,8 @@
 
 
 def sending_kernel(step, low, me_ref, *refs):
-    pieces, (m_ref, middle, normed, rows) = refs[7:7 + low], refs[7 + low:]
-    expert_kernel(step, me_ref, *refs[:7], rows, m_ref, middle, normed)
+    pieces, (m_ref, middle, rows) = refs[7:7 + low], refs[7 + low:]
+    expert_kernel(step, me_ref, *refs[:7], rows, m_ref, middle)
     me = me_ref[0]
     for l, piece in enumerate(pieces):
         for h in range(piece.shape[0]):
@@ -313,7 +328,6 @@
     for step in range(STEPS):
         scratch = [
             pltpu.VMEM((rows, width), F32),
-            pltpu.VMEM((rows, width), BF16),
             pltpu.VMEM((rows * local_heads, head_dim), F32),
         ]
         cost = (2 * rows * width * part, 2 * width * part)
@@ -375,7 +389,7 @@
         attended = swapped(columns)
         operands = (me, attended, states, ffn_gain, gate_w, up_w, down_w, shares)
         specs = [smem] + [whole()] * 7
-        scratch = [pltpu.VMEM((rows, width), F32), pltpu.VMEM((rows, width), BF16)]
+        scratch = [pltpu.VMEM((rows, width), F32)]
         cost = (6 * rows * width * hidden, 6 * width * hidden)
         if step + 1 == STEPS:
             half_out, middle = call(
@@ -400,7 +414,7 @@
                 "experts_sending",
                 cost,
             )
-            pieces = [pieces[0]] + [shifted(pieces[l], l) for l in range(1, low)]
+            pieces = [pieces[0]] + [shifted(pieces[l], l) for l in range(low - 1, 0, -1)]
             part_sums = call(
                 partial_kernel, slots, (middle, *pieces), [whole()] * (low + 1), [], "partial",
                 (rows * width, 4 * rows * width),

time: 180 us -> 178 us (0.989)
  Pallas kernels: 15.9 us -> 13.9 us
  blocking collectives: 125 us -> 123 us
    pallas_call x18, Pallas kernels: 15.9 us -> 13.9 us  [call(): pl.pallas_call(kernel, out_shape=out, in_specs=specs, out_specs=whole() i...]
  transfers between devices with their start and end apart: 16 -> 16, of which waited for: 14 -> 12; matrix products, arithmetic and copies ran while one was open for 0% -> 0% of each run, Pallas kernels for 0% -> 0%
where the time goes in v6:
time: 178 us; the launch traced here: 177 us
  blocking collectives  123 us (69%)
  waiting for transfers between devices  22.8 us (13%)
  starting transfers between devices  16.1 us (9%)
  Pallas kernels  13.9 us (8%)
    all_to_all x11, blocking collectives, swapped(): lax.all_to_all(blocks, 'expert', split_axis=0, concat_axis=0, tiled=True)  123 us
    ppermute x16, waiting for transfers between devices, shifted(): return lax.ppermute(array, ('section', 'expert'), pairs)  22.8 us
    ppermute x16, starting transfers between devices, shifted(): return lax.ppermute(array, ('section', 'expert'), pairs)  16.1 us
    pallas_call x18, Pallas kernels, call(): pl.pallas_call(kernel, out_shape=out, in_specs=specs, out_specs=whole() i...  13.9 us
  transfers between devices with their start and end apart: 16, of which 12 were waited for; matrix products, arithmetic and copies ran while one was open for 0% of the time, Pallas kernels for 0%

profile of v6, /device:TPU:0, one launch (start us, length us, event | category | flops | bytes accessed | tf_op | source)
XLA Modules:
  0.0 177.4 jit_solution(13183471708055103533)
XLA Ops:
  0.0 0.8 copy-done.7
  0.8 16.3 %all_to_all.55.x_ref.refs_1_ = bf16[8,4,4096]{2,1,0:T(4,128)(2,1)S(1)} all-to-all(bf16[8,4,4096]{2,1,0:T(4,128)(2,1)S(1)} %spread.1), channel_id=1, replica_groups=mesh['section'=4,'expert'=8] {'expert'}, dimensions={0} | all-to-all | bytes 524288 | tf_op jit(solution)/shard_map/all_to_all | solution.py:41
  17.1 0.0 copy-start.5
  17.1 0.0 copy-start.6
  17.1 0.0 copy-start.12
  17.1 0.0 copy-start.13
  17.1 0.0 copy-start.14
  17.1 0.0 copy-start.15
  17.2 0.0 copy-start.17
  17.2 0.8 first_query.1
  18.0 10.3 %all_to_all.56 = bf16[8,32,128]{2,1,0:T(8,128)(2,1)S(1)} all-to-all(bf16[8,32,128]{2,1,0:T(8,128)(2,1)S(1)} %first_query.1), channel_id=1, replica_groups=mesh['section'=4,'expert'=8] {'expert'}, dimensions={0} | all-to-all | bytes 131072 | tf_op jit(solution)/shard_map/all_to_all | solution.py:41
  28.3 0.0 copy-start.1
  28.4 1.1 first_attention.1
  29.5 10.8 %all_to_all.57 = bf16[8,128,128]{2,1,0:T(8,128)(2,1)S(1)} all-to-all(bf16[8,128,128]{2,1,0:T(8,128)(2,1)S(1)} %broadcast_in_dim.8), channel_id=1, replica_groups=mesh['section'=4,'expert'=8] {'expert'}, dimensions={0} | all-to-all | bytes 524288 | tf_op jit(solution)/shard_map/all_to_all | solution.py:41
  40.3 0.9 attention_out.3
  41.2 11.2 %all_to_all.58.refs_0_ = bf16[8,32,512]{2,1,0:T(8,128)(2,1)S(1)} all-to-all(bf16[8,32,512]{2,1,0:T(8,128)(2,1)S(1)} %attention_out.3), channel_id=1, replica_groups=mesh['section'=4,'expert'=8] {'expert'}, dimensions={0} | all-to-all | bytes 524288 | tf_op jit(solution)/shard_map/all_to_all | solution.py:41
  52.3 1.6 experts_sending.2
  53.9 1.0 collective-permute-start
  54.9 0.6 collective-permute-start.1
  55.4 2.0 %collective-permute-start.2 = (bf16[2,4,4096]{2,1,0:T(4,128)(2,1)S(1)}, bf16[2,4,4096]{2,1,0:T(4,128)(2,1)S(1)}, u32[]{:S(2)}, u32[]{:S(2)}) collective-permute-start(bf16[2,4,4096]{2,1,0:T(4,128)(2,1)S(1)} %get-tuple-element.33), channel_id=1, source_target_pairs={{0,1},{1,0},{2,3},{3,2},{4,5},{5,4},{6,7},{7,6},{8,9},{9,8},{10,11... | collective-permute-start | bytes 196616 | tf_op jit(solution)/shard_map/ppermute | solution.py:30
  57.5 1.7 collective-permute-done.refs_1_
  59.1 0.0 collective-permute-done.1.refs_2_
  59.2 0.7 collective-permute-done.2.refs_3_
  59.8 0.1 partial.2
  59.9 0.1 collective-permute-start.4
  60.0 1.6 collective-permute-start.3
  61.6 5.0 %collective-permute-done.4.refs_1_ = bf16[2,4,4096]{2,1,0:T(4,128)(2,1)S(1)} collective-permute-done((bf16[2,4,4096]{2,1,0:T(4,128)(2,1)S(1)}, bf16[2,4,4096]{2,1,0:T(4,128)(2,1)S(1)}, u32[]{:S(2)}, u32[]{:S(2)}) %collective-permute-start.4) | collective-permute-done | bytes 65568 | tf_op jit(solution)/shard_map/ppermute | solution.py:30
  66.6 0.0 copy-start.16
  66.6 0.3 collective-permute-start.7
  66.9 2.4 %collective-permute-start.6 = (bf16[2,4,4096]{2,1,0:T(4,128)(2,1)S(1)}, bf16[2,4,4096]{2,1,0:T(4,128)(2,1)S(1)}, u32[]{:S(2)}, u32[]{:S(2)}) collective-permute-start(bf16[2,4,4096]{2,1,0:T(4,128)(2,1)S(1)} %join.2.refs_0_), channel_id=1, source_target_pairs={{0,2},{1,3},{2,0},{3,1},{4,6},{5,7},{6,4},{7,5},{8,10},{9,11},{10,... | collective-permute-start | bytes 196616 | tf_op jit(solution)/shard_map/ppermute | solution.py:30
  69.3 0.9 collective-permute-start.5
  70.2 1.7 collective-permute-done.7.refs_3_
  71.9 0.3 collective-permute-done.6.refs_2_
  72.2 1.3 collective-permute-done.5.refs_1_
  73.5 0.9 order_query.2
  74.4 10.5 %all_to_all.59 = bf16[8,16,128]{2,1,0:T(8,128)(2,1)S(1)} all-to-all(bf16[8,16,128]{2,1,0:T(8,128)(2,1)S(1)} %bitcast.29), channel_id=1, replica_groups=mesh['section'=4,'expert'=8] {'expert'}, dimensions={0} | all-to-all | bytes 65536 | tf_op jit(solution)/shard_map/all_to_all | solution.py:41
  84.9 1.1 attention.2
  86.0 10.6 %all_to_all.60 = bf16[8,128,128]{2,1,0:T(8,128)(2,1)S(1)} all-to-all(bf16[8,128,128]{2,1,0:T(8,128)(2,1)S(1)} %broadcast_in_dim.9), channel_id=1, replica_groups=mesh['section'=4,'expert'=8] {'expert'}, dimensions={0} | all-to-all | bytes 524288 | tf_op jit(solution)/shard_map/all_to_all | solution.py:41
  96.6 0.9 attention_out.4
  97.5 12.3 %all_to_all.61.refs_0_ = bf16[8,32,512]{2,1,0:T(8,128)(2,1)S(1)} all-to-all(bf16[8,32,512]{2,1,0:T(8,128)(2,1)S(1)} %attention_out.4), channel_id=1, replica_groups=mesh['section'=4,'expert'=8] {'expert'}, dimensions={0} | all-to-all | bytes 524288 | tf_op jit(solution)/shard_map/all_to_all | solution.py:41
  109.8 1.6 experts_sending.3
  111.4 1.0 collective-permute-start.8
  112.3 2.6 %collective-permute-start.10 = (bf16[2,4,4096]{2,1,0:T(4,128)(2,1)S(1)}, bf16[2,4,4096]{2,1,0:T(4,128)(2,1)S(1)}, u32[]{:S(2)}, u32[]{:S(2)}) collective-permute-start(bf16[2,4,4096]{2,1,0:T(4,128)(2,1)S(1)} %get-tuple-element.40), channel_id=1, source_target_pairs={{0,1},{1,0},{2,3},{3,2},{4,5},{5,4},{6,7},{7,6},{8,9},{9,8},{10,11... | collective-permute-start | bytes 196616 | tf_op jit(solution)/shard_map/ppermute | solution.py:30
  114.9 1.7 collective-permute-done.8.refs_1_
  116.6 0.0 collective-permute-done.9.refs_2_
  116.6 0.7 collective-permute-done.10.refs_3_
  117.3 0.1 partial.3
  117.3 0.1 collective-permute-start.12
  117.4 0.1 collective-permute-start.11
  117.5 5.4 %collective-permute-done.12.refs_1_ = bf16[2,4,4096]{2,1,0:T(4,128)(2,1)S(1)} collective-permute-done((bf16[2,4,4096]{2,1,0:T(4,128)(2,1)S(1)}, bf16[2,4,4096]{2,1,0:T(4,128)(2,1)S(1)}, u32[]{:S(2)}, u32[]{:S(2)}) %collective-permute-start.12) | collective-permute-done | bytes 65568 | tf_op jit(solution)/shard_map/ppermute | solution.py:30
  122.9 1.4 collective-permute-start.15
  124.3 2.2 %collective-permute-start.14 = (bf16[2,4,4096]{2,1,0:T(4,128)(2,1)S(1)}, bf16[2,4,4096]{2,1,0:T(4,128)(2,1)S(1)}, u32[]{:S(2)}, u32[]{:S(2)}) collective-permute-start(bf16[2,4,4096]{2,1,0:T(4,128)(2,1)S(1)} %join.3.refs_0_), channel_id=1, source_target_pairs={{0,2},{1,3},{2,0},{3,1},{4,6},{5,7},{6,4},{7,5},{8,10},{9,11},{10,... | collective-permute-start | bytes 196616 | tf_op jit(solution)/shard_map/ppermute | solution.py:30
  126.5 1.7 collective-permute-done.15.refs_3_
  128.2 1.3 collective-permute-done.14.refs_2_
  129.5 1.3 collective-permute-done.13.refs_1_
  130.8 0.9 order_query.3
  131.7 9.1 %all_to_all.62 = bf16[8,16,128]{2,1,0:T(8,128)(2,1)S(1)} all-to-all(bf16[8,16,128]{2,1,0:T(8,128)(2,1)S(1)} %bitcast.30), channel_id=1, replica_groups=mesh['section'=4,'expert'=8] {'expert'}, dimensions={0} | all-to-all | bytes 65536 | tf_op jit(solution)/shard_map/all_to_all | solution.py:41
  140.7 1.1 attention.3
  141.8 10.6 %all_to_all.63 = bf16[8,128,128]{2,1,0:T(8,128)(2,1)S(1)} all-to-all(bf16[8,128,128]{2,1,0:T(8,128)(2,1)S(1)} %broadcast_in_dim.10), channel_id=1, replica_groups=mesh['section'=4,'expert'=8] {'expert'}, dimensions={0} | all-to-all | bytes 524288 | tf_op jit(solution)/shard_map/all_to_all | solution.py:41
  152.5 0.9 attention_out.5
  153.3 10.9 %all_to_all.64.a_ref = bf16[8,32,512]{2,1,0:T(8,128)(2,1)S(1)} all-to-all(bf16[8,32,512]{2,1,0:T(8,128)(2,1)S(1)} %attention_out.5), channel_id=1, replica_groups=mesh['section'=4,'expert'=8] {'expert'}, dimensions={0} | all-to-all | bytes 524288 | tf_op jit(solution)/shard_map/all_to_all | solution.py:41
  164.2 1.5 experts.1
  165.8 10.9 %all_to_all.65.r_ref = bf16[8,4,4096]{2,1,0:T(4,128)(2,1)S(1)} all-to-all(bf16[8,4,4096]{2,1,0:T(4,128)(2,1)S(1)} %get-tuple-element.43), channel_id=1, replica_groups=mesh['section'=4,'expert'=8] {'expert'}, dimensions={0} | all-to-all | bytes 524288 | tf_op jit(solution)/shard_map/all_to_all | solution.py:41
  176.7 0.7 combine.1
  (36 shorter events, 0.3 us)
Async XLA Ops:
  0.0 0.8 copy-start.7
  0.8 16.3 %copy-start = (bf16[1,4096,512]{2,1,0:T(8,128)(2,1)S(1)}, bf16[1,4096,512]{2,1,0:T(8,128)(2,1)}, u32[]{:S(2)}) copy-start(bf16[1,4096,512]{2,1,0:T(8,128)(2,1)} %param.20) | copy-start | bytes 12582916
  0.8 16.3 %copy-start.8 = (bf16[1,4096]{1,0:T(2,128)(2,1)S(1)}, bf16[1,4096]{1,0:T(2,128)(2,1)}, u32[]{:S(2)}) copy-start(bf16[1,4096]{1,0:T(2,128)(2,1)} %refs_4_.4) | copy-start | bytes 24580
  0.8 16.3 %copy-start.10 = (s32[1,3,4,2]{2,3,1,0:T(2,128)S(1)}, s32[1,3,4,2]{2,3,1,0:T(2,128)}, u32[]{:S(2)}) copy-start(s32[1,3,4,2]{2,3,1,0:T(2,128)} %param.29) | copy-start | bytes 292
  0.8 16.3 %copy-start.11 = (f32[1,3,4,2]{2,3,1,0:T(2,128)S(1)}, f32[1,3,4,2]{2,3,1,0:T(2,128)}, u32[]{:S(2)}) copy-start(f32[1,3,4,2]{2,3,1,0:T(2,128)} %param.30) | copy-start | bytes 292
  17.1 11.2 %copy-start.5 = (bf16[1,3,4,64,4,128]{5,4,3,2,1,0:T(4,128)(2,1)S(1)}, bf16[1,3,4,64,4,128]{5,4,3,2,1,0:T(4,128)(2,1)}, u32[]{:S(2)}) copy-start(bf16[1,3,4,64,4,128]{5,4,3,2,1,0:T(4,128)(2,1)} %param.22) | copy-start | bytes 2359300
  17.1 11.2 %copy-start.6 = (bf16[1,3,4,64,4,128]{5,4,3,2,1,0:T(4,128)(2,1)S(1)}, bf16[1,3,4,64,4,128]{5,4,3,2,1,0:T(4,128)(2,1)}, u32[]{:S(2)}) copy-start(bf16[1,3,4,64,4,128]{5,4,3,2,1,0:T(4,128)(2,1)} %param.23) | copy-start | bytes 2359300
  17.1 11.2 %copy-start.12 = (s32[1,3,4]{2,0,1:T(1,128)S(1)}, s32[1,3,4]{2,0,1:T(1,128)}, u32[]{:S(2)}) copy-start(s32[1,3,4]{2,0,1:T(1,128)} %param.24) | copy-start | bytes 148
  17.1 11.2 %copy-start.13 = (s32[128,1]{1,0:T(8,128)S(1)}, s32[128,1]{1,0:T(8,128)}, u32[]{:S(2)}) copy-start(s32[128,1]{1,0:T(8,128)} %constant.14.clone.refs_4_.line_ref) | copy-start | bytes 1540
  17.1 11.2 %copy-start.14 = (bf16[128,256]{1,0:T(8,128)(2,1)S(1)}, bf16[128,256]{1,0:T(8,128)(2,1)}, u32[]{:S(2)}) copy-start(bf16[128,256]{1,0:T(8,128)(2,1)} %constant.17.clone.refs_3_) | copy-start | bytes 196612
  17.1 11.2 %copy-start.15 = (s32[8,1024]{1,0:T(8,128)S(1)}, s32[8,1024]{1,0:T(8,128)}, u32[]{:S(2)}) copy-start(s32[8,1024]{1,0:T(8,128)} %constant.15.clone.refs_5_.column_ref) | copy-start | bytes 98308
  17.2 11.2 %copy-start.17 = (bf16[32,256]{1,0:T(8,128)(2,1)S(1)}, bf16[32,256]{1,0:T(8,128)(2,1)}, u32[]{:S(2)}) copy-start(bf16[32,256]{1,0:T(8,128)(2,1)} %constant.18.clone.pick_ref) | copy-start | bytes 49156
  28.3 11.9 %copy-start.1 = (bf16[1,4096,512]{2,1,0:T(8,128)(2,1)S(1)}, bf16[1,4096,512]{2,1,0:T(8,128)(2,1)}, u32[]{:S(2)}) copy-start(bf16[1,4096,512]{2,1,0:T(8,128)(2,1)} %param.21) | copy-start | bytes 12582916
  40.2 12.1 %copy-start.2 = (bf16[1,1,4096,384]{3,2,1,0:T(8,128)(2,1)S(1)}, bf16[1,1,4096,384]{3,2,1,0:T(8,128)(2,1)}, u32[]{:S(2)}) copy-start(bf16[1,1,4096,384]{3,2,1,0:T(8,128)(2,1)} %param.26) | copy-start | bytes 9437188
  40.2 12.1 %copy-start.3 = (bf16[1,1,4096,384]{3,2,1,0:T(8,128)(2,1)S(1)}, bf16[1,1,4096,384]{3,2,1,0:T(8,128)(2,1)}, u32[]{:S(2)}) copy-start(bf16[1,1,4096,384]{3,2,1,0:T(8,128)(2,1)} %param.27) | copy-start | bytes 9437188
  40.2 12.1 %copy-start.4 = (bf16[1,1,384,4096]{3,2,1,0:T(8,128)(2,1)S(1)}, bf16[1,1,384,4096]{3,2,1,0:T(8,128)(2,1)}, u32[]{:S(2)}) copy-start(bf16[1,1,384,4096]{3,2,1,0:T(8,128)(2,1)} %param.28) | copy-start | bytes 9437188
  40.2 12.1 %copy-start.9 = (bf16[1,4096]{1,0:T(2,128)(2,1)S(1)}, bf16[1,4096]{1,0:T(2,128)(2,1)}, u32[]{:S(2)}) copy-start(bf16[1,4096]{1,0:T(2,128)(2,1)} %gain_ref.3) | copy-start | bytes 24580
  53.9 5.2 %collective-permute-start = (bf16[2,4,4096]{2,1,0:T(4,128)(2,1)S(1)}, bf16[2,4,4096]{2,1,0:T(4,128)(2,1)S(1)}, u32[]{:S(2)}, u32[]{:S(2)}) collective-permute-start(bf16[2,4,4096]{2,1,0:T(4,128)(2,1)S(1)} %get-tuple-element.31), channel_id=1, source_target_pairs={{0,3},{1,2},{2,1},{3,0},{4,7},{5,6},{6,5},{7,4},{8,11},{9,10},{10,... | collective-permute-start | bytes 196616 | tf_op jit(solution)/shard_map/ppermute | solution.py:30
  54.9 4.3 %collective-permute-start.1 = (bf16[2,4,4096]{2,1,0:T(4,128)(2,1)S(1)}, bf16[2,4,4096]{2,1,0:T(4,128)(2,1)S(1)}, u32[]{:S(2)}, u32[]{:S(2)}) collective-permute-start(bf16[2,4,4096]{2,1,0:T(4,128)(2,1)S(1)} %get-tuple-element.32), channel_id=1, source_target_pairs={{0,2},{1,3},{2,0},{3,1},{4,6},{5,7},{6,4},{7,5},{8,10},{9,11},{10,... | collective-permute-start | bytes 196616 | tf_op jit(solution)/shard_map/ppermute | solution.py:30
  55.4 4.4 %collective-permute-start.2 = (bf16[2,4,4096]{2,1,0:T(4,128)(2,1)S(1)}, bf16[2,4,4096]{2,1,0:T(4,128)(2,1)S(1)}, u32[]{:S(2)}, u32[]{:S(2)}) collective-permute-start(bf16[2,4,4096]{2,1,0:T(4,128)(2,1)S(1)} %get-tuple-element.33), channel_id=1, source_target_pairs={{0,1},{1,0},{2,3},{3,2},{4,5},{5,4},{6,7},{7,6},{8,9},{9,8},{10,11... | collective-permute-start | bytes 196616 | tf_op jit(solution)/shard_map/ppermute | solution.py:30
  59.9 6.7 %collective-permute-start.4 = (bf16[2,4,4096]{2,1,0:T(4,128)(2,1)S(1)}, bf16[2,4,4096]{2,1,0:T(4,128)(2,1)S(1)}, u32[]{:S(2)}, u32[]{:S(2)}) collective-permute-start(bf16[2,4,4096]{2,1,0:T(4,128)(2,1)S(1)} %partial.2), channel_id=1, source_target_pairs={{0,12},{1,13},{2,14},{3,15},{4,8},{5,9},{6,10},{7,11},{8,20},{9,21... | collective-permute-start | bytes 196616 | tf_op jit(solution)/shard_map/ppermute | solution.py:30
  60.0 6.6 %collective-permute-start.3 = (bf16[2,4,4096]{2,1,0:T(4,128)(2,1)S(1)}, bf16[2,4,4096]{2,1,0:T(4,128)(2,1)S(1)}, u32[]{:S(2)}, u32[]{:S(2)}) collective-permute-start(bf16[2,4,4096]{2,1,0:T(4,128)(2,1)S(1)} %partial.2), channel_id=1, source_target_pairs={{0,8},{1,9},{2,10},{3,11},{4,12},{5,13},{6,14},{7,15},{8,16},{9,17... | collective-permute-start | bytes 196616 | tf_op jit(solution)/shard_map/ppermute | solution.py:30
  66.6 18.2 %copy-start.16 = (bf16[128,128]{1,0:T(8,128)(2,1)S(1)}, bf16[128,128]{1,0:T(8,128)(2,1)}, u32[]{:S(2)}) copy-start(bf16[128,128]{1,0:T(8,128)(2,1)} %constant.16.clone.order_ref) | copy-start | bytes 98308
  66.6 5.2 %collective-permute-start.7 = (bf16[2,4,4096]{2,1,0:T(4,128)(2,1)S(1)}, bf16[2,4,4096]{2,1,0:T(4,128)(2,1)S(1)}, u32[]{:S(2)}, u32[]{:S(2)}) collective-permute-start(bf16[2,4,4096]{2,1,0:T(4,128)(2,1)S(1)} %join.2.refs_0_), channel_id=1, source_target_pairs={{0,3},{1,2},{2,1},{3,0},{4,7},{5,6},{6,5},{7,4},{8,11},{9,10},{10,... | collective-permute-start | bytes 196616 | tf_op jit(solution)/shard_map/ppermute | solution.py:30
  66.9 5.3 %collective-permute-start.6 = (bf16[2,4,4096]{2,1,0:T(4,128)(2,1)S(1)}, bf16[2,4,4096]{2,1,0:T(4,128)(2,1)S(1)}, u32[]{:S(2)}, u32[]{:S(2)}) collective-permute-start(bf16[2,4,4096]{2,1,0:T(4,128)(2,1)S(1)} %join.2.refs_0_), channel_id=1, source_target_pairs={{0,2},{1,3},{2,0},{3,1},{4,6},{5,7},{6,4},{7,5},{8,10},{9,11},{10,... | collective-permute-start | bytes 196616 | tf_op jit(solution)/shard_map/ppermute | solution.py:30
  69.3 4.3 %collective-permute-start.5 = (bf16[2,4,4096]{2,1,0:T(4,128)(2,1)S(1)}, bf16[2,4,4096]{2,1,0:T(4,128)(2,1)S(1)}, u32[]{:S(2)}, u32[]{:S(2)}) collective-permute-start(bf16[2,4,4096]{2,1,0:T(4,128)(2,1)S(1)} %join.2.refs_0_), channel_id=1, source_target_pairs={{0,1},{1,0},{2,3},{3,2},{4,5},{5,4},{6,7},{7,6},{8,9},{9,8},{10,11... | collective-permute-start | bytes 196616 | tf_op jit(solution)/shard_map/ppermute | solution.py:30
  111.4 5.2 %collective-permute-start.8 = (bf16[2,4,4096]{2,1,0:T(4,128)(2,1)S(1)}, bf16[2,4,4096]{2,1,0:T(4,128)(2,1)S(1)}, u32[]{:S(2)}, u32[]{:S(2)}) collective-permute-start(bf16[2,4,4096]{2,1,0:T(4,128)(2,1)S(1)} %get-tuple-element.38), channel_id=1, source_target_pairs={{0,3},{1,2},{2,1},{3,0},{4,7},{5,6},{6,5},{7,4},{8,11},{9,10},{10,... | collective-permute-start | bytes 196616 | tf_op jit(solution)/shard_map/ppermute | solution.py:30
  112.3 4.3 %collective-permute-start.9 = (bf16[2,4,4096]{2,1,0:T(4,128)(2,1)S(1)}, bf16[2,4,4096]{2,1,0:T(4,128)(2,1)S(1)}, u32[]{:S(2)}, u32[]{:S(2)}) collective-permute-start(bf16[2,4,4096]{2,1,0:T(4,128)(2,1)S(1)} %get-tuple-element.39), channel_id=1, source_target_pairs={{0,2},{1,3},{2,0},{3,1},{4,6},{5,7},{6,4},{7,5},{8,10},{9,11},{10,... | collective-permute-start | bytes 196616 | tf_op jit(solution)/shard_map/ppermute | solution.py:30
  112.3 4.9 %collective-permute-start.10 = (bf16[2,4,4096]{2,1,0:T(4,128)(2,1)S(1)}, bf16[2,4,4096]{2,1,0:T(4,128)(2,1)S(1)}, u32[]{:S(2)}, u32[]{:S(2)}) collective-permute-start(bf16[2,4,4096]{2,1,0:T(4,128)(2,1)S(1)} %get-tuple-element.40), channel_id=1, source_target_pairs={{0,1},{1,0},{2,3},{3,2},{4,5},{5,4},{6,7},{7,6},{8,9},{9,8},{10,11... | collective-permute-start | bytes 196616 | tf_op jit(solution)/shard_map/ppermute | solution.py:30
  117.3 5.5 %collective-permute-start.12 = (bf16[2,4,4096]{2,1,0:T(4,128)(2,1)S(1)}, bf16[2,4,4096]{2,1,0:T(4,128)(2,1)S(1)}, u32[]{:S(2)}, u32[]{:S(2)}) collective-permute-start(bf16[2,4,4096]{2,1,0:T(4,128)(2,1)S(1)} %partial.3), channel_id=1, source_target_pairs={{0,12},{1,13},{2,14},{3,15},{4,8},{5,9},{6,10},{7,11},{8,20},{9,21... | collective-permute-start | bytes 196616 | tf_op jit(solution)/shard_map/ppermute | solution.py:30
  117.4 5.5 %collective-permute-start.11 = (bf16[2,4,4096]{2,1,0:T(4,128)(2,1)S(1)}, bf16[2,4,4096]{2,1,0:T(4,128)(2,1)S(1)}, u32[]{:S(2)}, u32[]{:S(2)}) collective-permute-start(bf16[2,4,4096]{2,1,0:T(4,128)(2,1)S(1)} %partial.3), channel_id=1, source_target_pairs={{0,8},{1,9},{2,10},{3,11},{4,12},{5,13},{6,14},{7,15},{8,16},{9,17... | collective-permute-start | bytes 196616 | tf_op jit(solution)/shard_map/ppermute | solution.py:30
  122.9 5.3 %collective-permute-start.15 = (bf16[2,4,4096]{2,1,0:T(4,128)(2,1)S(1)}, bf16[2,4,4096]{2,1,0:T(4,128)(2,1)S(1)}, u32[]{:S(2)}, u32[]{:S(2)}) collective-permute-start(bf16[2,4,4096]{2,1,0:T(4,128)(2,1)S(1)} %join.3.refs_0_), channel_id=1, source_target_pairs={{0,3},{1,2},{2,1},{3,0},{4,7},{5,6},{6,5},{7,4},{8,11},{9,10},{10,... | collective-permute-start | bytes 196616 | tf_op jit(solution)/shard_map/ppermute | solution.py:30
  124.3 5.1 %collective-permute-start.14 = (bf16[2,4,4096]{2,1,0:T(4,128)(2,1)S(1)}, bf16[2,4,4096]{2,1,0:T(4,128)(2,1)S(1)}, u32[]{:S(2)}, u32[]{:S(2)}) collective-permute-start(bf16[2,4,4096]{2,1,0:T(4,128)(2,1)S(1)} %join.3.refs_0_), channel_id=1, source_target_pairs={{0,2},{1,3},{2,0},{3,1},{4,6},{5,7},{6,4},{7,5},{8,10},{9,11},{10,... | collective-permute-start | bytes 196616 | tf_op jit(solution)/shard_map/ppermute | solution.py:30
  126.5 4.3 %collective-permute-start.13 = (bf16[2,4,4096]{2,1,0:T(4,128)(2,1)S(1)}, bf16[2,4,4096]{2,1,0:T(4,128)(2,1)S(1)}, u32[]{:S(2)}, u32[]{:S(2)}) collective-permute-start(bf16[2,4,4096]{2,1,0:T(4,128)(2,1)S(1)} %join.3.refs_0_), channel_id=1, source_target_pairs={{0,1},{1,0},{2,3},{3,2},{4,5},{5,4},{6,7},{7,6},{8,9},{9,8},{10,11... | collective-permute-start | bytes 196616 | tf_op jit(solution)/shard_map/ppermute | solution.py:30

commit v7 on v6

--- a/solution.py
+++ b/solution.py
@@ -112,12 +112,12 @@
 
 
 def order_kernel(head_dim, low, me_ref, *refs):
-    pieces, (gain_ref, w_ref, q_ref, x_ref, *scratch) = refs[:low], refs[low:]
+    pieces, (gain_ref, w_ref, q_ref, states, x_ref, spread) = refs[:low], refs[low:]
     me = me_ref[0]
     for l, piece in enumerate(pieces):
         for h in range(piece.shape[0]):
             x_ref[me ^ (l + h * low)] = piece[h]
-    query_kernel(head_dim, x_ref, gain_ref, w_ref, q_ref, *scratch)
+    query_kernel(head_dim, x_ref, gain_ref, w_ref, q_ref, states, spread)
 
 
 def query_kernel(head_dim, x_ref, gain_ref, w_ref, q_ref, states, spread):
@@ -143,24 +143,39 @@
 
 
 def first_attention_kernel(own, pick_ref, q_ref, *refs):
-    *rest, share_ref = refs
+    *rest, c_ref, share_ref, lines = refs
     share_ref[...] = jnp.dot(pick_ref[...], q_ref[...], preferred_element_type=F32)
-    attention_kernel(0, own, q_ref, *rest)
-
-
-def attention_kernel(step, own, q_ref, k_ref, v_ref, len_ref, order_ref, line_ref, column_ref, c_ref):
+    attention_kernel(0, own, q_ref, *rest, c_ref, lines)
+
+
+def attention_kernel(step, own, q_ref, k_ref, v_ref, len_ref, order_ref, line_ref, column_ref, c_ref, lines):
     head_dim = q_ref.shape[1]
+    heads = line_ref.shape[0]
+    span = column_ref.shape[1]
     q = jnp.dot(order_ref[...], q_ref[...], preferred_element_type=F32).astype(BF16)
-    scores = lax.dot_general(q, k_ref[step], (((1,), (1,)), ((), ())), preferred_element_type=F32)
-    key_of, position, of_row = column_ref[0:1, :], column_ref[1:2, :], column_ref[2:3, :]
-    length = jnp.zeros(of_row.shape, jnp.int32)
+    group_of, position = column_ref[0:1, :], column_ref[1:2, :]
+    same = group_of == line_ref[...]
+    ours = [slice(heads * r, heads * (r + 1)) for r in range(own)]
+    keys = [slice(span * r, span * (r + 1)) for r in range(own)]
+    scores = [
+        lax.dot_general(
+            q[ours[r], :], k_ref[step, keys[r], :], (((1,), (1,)), ((), ())), preferred_element_type=F32
+        )
+        for r in range(own)
+    ]
+    exps = [
+        jnp.where(
+            same & (position < len_ref[step, :, r:r + 1]), jnp.exp2(scores[r] * (head_dim ** (-0.5) * LOG2E)), 0.0
+        )
+        for r in range(own)
+    ]
+    contexts = [
+        jnp.dot(exps[r].astype(BF16), v_ref[step, keys[r], :], preferred_element_type=F32) for r in range(own)
+    ]
     for r in range(own):
-        length = jnp.where(of_row == r, len_ref[step, 0, r], length)
-    key_of = jnp.where(position < length, key_of, -1)
-    exps = jnp.where(key_of == line_ref[...], jnp.exp2(scores * (head_dim ** (-0.5) * LOG2E)), 0.0)
-    scale = 1.0 / jnp.sum(exps, axis=-1, keepdims=True)
-    context = jnp.dot(exps.astype(BF16), v_ref[step], preferred_element_type=F32)
-    c_ref[...] = (context * scale).astype(BF16)
+        lines[ours[r], :] = contexts[r] * (1.0 / jnp.sum(exps[r], axis=-1, keepdims=True))
+    for h in range(heads):
+        c_ref[:, head_dim * h:head_dim * (h + 1)] = lines[pl.ds(h, own, stride=heads), :].astype(BF16)
 
 
 def attention_tables(own, heads, local_heads, kv_heads, cache_len):
@@ -176,42 +191,37 @@
     for part in range(3):
         for r in range(own):
             pick[np.arange(devices) * own + r, np.arange(devices) * (EXTRA + count) + part * own + r] = 1.0
-    line = (row * kv_heads + head // group).astype(np.int32)[:, None]
-    place = np.arange(own * cache_len * kv_heads)
-    of_row, position, kv = place // (cache_len * kv_heads), place // kv_heads % cache_len, place % kv_heads
-    column = np.zeros((8, place.size), np.int32)
-    column[:3] = of_row * kv_heads + kv, position, of_row
+    line = (np.arange(heads) // group).astype(np.int32)[:, None]
+    position, kv = np.divmod(np.arange(cache_len * kv_heads), kv_heads)
+    column = np.zeros((8, cache_len * kv_heads), np.int32)
+    column[:2] = kv, position
     asis = jnp.asarray(line), jnp.asarray(column)
     return (jnp.asarray(order, BF16), *asis), (jnp.asarray(first_order, BF16), *asis), jnp.asarray(pick, BF16)
 
 
-def out_kernel(heads, c_ref, w_ref, o_ref, wide, lines):
-    rows = lines.shape[0]
-    head_dim = c_ref.shape[1]
-    wide[...] = c_ref[...].astype(F32)
-    for h in range(heads):
-        lines[:, head_dim * h:head_dim * (h + 1)] = wide[pl.ds(h, rows, stride=heads), :].astype(BF16)
-    chunk, total = 1024, None
-    for start in range(0, lines.shape[1], chunk):
+def out_kernel(c_ref, w_ref, o_ref, lines):
+    devices, own, width = c_ref.shape
+    chunk, total = 512, None
+    for start in range(0, width, chunk):
         at = slice(start, start + chunk)
-        part = jnp.dot(lines[:, at], w_ref[at, :], preferred_element_type=F32)
+        for i in range(devices):
+            lines[own * i:own * (i + 1), at] = c_ref[i, :, at].astype(F32)
+        part = jnp.dot(lines[:, at].astype(BF16), w_ref[at, :], preferred_element_type=F32)
         total = part if total is None else total + part
     columns = total.astype(BF16)
-    for i in range(o_ref.shape[0]):
+    for i in range(devices):
         o_ref[i] = columns
 
 
 def expert_kernel(step, me_ref, a_ref, x_ref, gain_ref, gate_ref, up_ref, down_ref, share_ref, h_ref, m_ref, middle):
-    devices, own, _ = x_ref.shape
+    devices, own, _ = h_ref.shape
     part = a_ref.shape[2]
     width = part * devices
     me = me_ref[0]
     gates, ups, squares = {}, {}, jnp.zeros((devices * own, 128), F32)
     for j in range(devices):
         at = slice(part * j, part * (j + 1))
-        for i in range(devices):
-            middle[own * i:own * (i + 1), at] = x_ref[i, :, at].astype(F32)
-        values = middle[:, at] + a_ref[j].astype(F32)
+        values = x_ref[:, at] + a_ref[j].astype(F32)
         middle[:, at] = values
         squares = add_squares(squares, values)
         left = (values * gain_ref[:, at].astype(F32)).astype(BF16)
@@ -313,6 +323,7 @@
     smem = whole(pltpu.SMEM)
     q_shape = jax.ShapeDtypeStruct((rows * local_heads, head_dim), BF16)
     x_shape = jax.ShapeDtypeStruct((devices, own, width), BF16)
+    states_shape = jax.ShapeDtypeStruct((rows, width), F32)
     m_shape = jax.ShapeDtypeStruct((own, width), F32)
     slots = jax.ShapeDtypeStruct((high, own, width), BF16)
     copies = call(
@@ -326,19 +337,15 @@
     )
     me, copies = lax.optimization_barrier((me, copies))
     for step in range(STEPS):
-        scratch = [
-            pltpu.VMEM((rows, width), F32),
-            pltpu.VMEM((rows * local_heads, head_dim), F32),
-        ]
+        spread = pltpu.VMEM((rows * local_heads, head_dim), F32)
         cost = (2 * rows * width * part, 2 * width * part)
         if step == 0:
-            states = swapped(copies)
-            own_q = call(
+            own_q, states = call(
                 functools.partial(first_kernel, head_dim),
-                jax.ShapeDtypeStruct((devices, EXTRA + own * local_heads, head_dim), BF16),
-                (states, attn_gain, query_w, routes, gates),
+                (jax.ShapeDtypeStruct((devices, EXTRA + own * local_heads, head_dim), BF16), states_shape),
+                (swapped(copies), attn_gain, query_w, routes, gates),
                 [whole()] * 5,
-                scratch,
+                [spread],
                 "first_query",
                 cost,
             )
@@ -346,14 +353,15 @@
             pieces = [state] + [shifted(state, l) for l in range(1, low)]
             own_q, states = call(
                 functools.partial(order_kernel, head_dim, low),
-                (q_shape, x_shape),
+                (q_shape, states_shape),
                 (me, *pieces, attn_gain, query_w),
                 [smem] + [whole()] * (low + 2),
-                scratch,
+                [pltpu.VMEM((devices, own, width), BF16), spread],
                 "order_query",
                 cost,
             )
-        c_shape = jax.ShapeDtypeStruct((own * heads, head_dim), BF16)
+        c_shape = jax.ShapeDtypeStruct((own, heads * head_dim), BF16)
+        by_row = [pltpu.VMEM((own * heads, head_dim), F32)]
         cost = (4 * own * heads * places * head_dim, 4 * places * head_dim)
         queries = swapped(own_q.reshape(devices, -1, head_dim)).reshape(-1, head_dim)
         if step == 0:
@@ -361,8 +369,8 @@
                 functools.partial(first_attention_kernel, own),
                 (c_shape, jax.ShapeDtypeStruct((rows, LANES), F32)),
                 (pick, queries, keys, values, lengths, *first_tables),
-                [whole()] * 4 + [smem] + [whole()] * 3,
-                [],
+                [whole()] * 8,
+                by_row,
                 "first_attention",
                 cost,
             )
@@ -371,18 +379,18 @@
                 functools.partial(attention_kernel, step, own),
                 c_shape,
                 (queries, keys, values, lengths, *tables),
-                [whole()] * 3 + [smem] + [whole()] * 3,
-                [],
+                [whole()] * 7,
+                by_row,
                 "attention",
                 cost,
             )
         contexts = everyones(context)
         columns = call(
-            functools.partial(out_kernel, heads),
+            out_kernel,
             jax.ShapeDtypeStruct((devices, rows, part), BF16),
-            (contexts.reshape(rows * heads, head_dim), out_w),
+            (contexts, out_w),
             [whole()] * 2,
-            [pltpu.VMEM((rows * heads, head_dim), F32), pltpu.VMEM((rows, heads * head_dim), BF16)],
+            [pltpu.VMEM((rows, heads * head_dim), F32)],
             "attention_out",
             (2 * rows * width * part, 2 * width * part),
         )

time: 178 us -> 176 us (0.989)
  Pallas kernels: 13.9 us -> 12 us
    pallas_call x18, Pallas kernels: 13.9 us -> 12 us  [call(): pl.pallas_call(kernel, out_shape=out, in_specs=specs, out_specs=whole() i...]
where the time goes in v7:
time: 176 us
  blocking collectives  123 us (70%)
  waiting for transfers between devices  22.7 us (13%)
  starting transfers between devices  16.1 us (9%)
  Pallas kernels  12 us (7%)
    all_to_all x11, blocking collectives, swapped(): lax.all_to_all(blocks, 'expert', split_axis=0, concat_axis=0, tiled=True)  123 us
    ppermute x16, waiting for transfers between devices, shifted(): return lax.ppermute(array, ('section', 'expert'), pairs)  22.7 us
    ppermute x16, starting transfers between devices, shifted(): return lax.ppermute(array, ('section', 'expert'), pairs)  16.1 us
    pallas_call x18, Pallas kernels, call(): pl.pallas_call(kernel, out_shape=out, in_specs=specs, out_specs=whole() i...  12 us
  transfers between devices with their start and end apart: 16, of which 12 were waited for; matrix products, arithmetic and copies ran while one was open for 0% of the time, Pallas kernels for 0%

profile of v7, /device:TPU:0, one launch (start us, length us, event | category | flops | bytes accessed | tf_op | source)
XLA Modules:
  0.0 175.6 jit_solution(17392286060091742904)
XLA Ops:
  0.0 0.8 copy-done.7
  0.8 16.3 %all_to_all.55.x_ref = bf16[8,4,4096]{2,1,0:T(4,128)(2,1)S(1)} all-to-all(bf16[8,4,4096]{2,1,0:T(4,128)(2,1)S(1)} %spread.1), channel_id=1, replica_groups=mesh['section'=4,'expert'=8] {'expert'}, dimensions={0} | all-to-all | bytes 524288 | tf_op jit(solution)/shard_map/all_to_all | solution.py:41
  17.1 0.0 copy-start.12
  17.1 0.0 copy-start.13
  17.1 0.0 copy-start.15
  17.1 0.0 copy-start.16
  17.2 0.0 copy-start.17
  17.2 0.9 first_query.1
  18.0 10.3 %all_to_all.56 = bf16[8,32,128]{2,1,0:T(8,128)(2,1)S(1)} all-to-all(bf16[8,32,128]{2,1,0:T(8,128)(2,1)S(1)} %get-tuple-element.29), channel_id=1, replica_groups=mesh['section'=4,'expert'=8] {'expert'}, dimensions={0} | all-to-all | bytes 131072 | tf_op jit(solution)/shard_map/all_to_all | solution.py:41
  28.4 0.5 first_attention.1
  28.8 0.1 broadcast_in_dim.8
  28.9 10.8 %all_to_all.57.c_ref = bf16[8,4,4096]{2,1,0:T(4,128)(2,1)S(1)} all-to-all(bf16[8,4,4096]{2,1,0:T(4,128)(2,1)S(1)} %broadcast_in_dim.8), channel_id=1, replica_groups=mesh['section'=4,'expert'=8] {'expert'}, dimensions={0} | all-to-all | bytes 524288 | tf_op jit(solution)/shard_map/all_to_all | solution.py:41
  39.7 0.9 attention_out.3
  40.6 11.2 %all_to_all.58.refs_0_ = bf16[8,32,512]{2,1,0:T(8,128)(2,1)S(1)} all-to-all(bf16[8,32,512]{2,1,0:T(8,128)(2,1)S(1)} %attention_out.3), channel_id=1, replica_groups=mesh['section'=4,'expert'=8] {'expert'}, dimensions={0} | all-to-all | bytes 524288 | tf_op jit(solution)/shard_map/all_to_all | solution.py:41
  51.8 1.5 experts_sending.2
  53.3 1.0 collective-permute-start
  54.3 0.6 collective-permute-start.1
  54.9 2.0 %collective-permute-start.2 = (bf16[2,4,4096]{2,1,0:T(4,128)(2,1)S(1)}, bf16[2,4,4096]{2,1,0:T(4,128)(2,1)S(1)}, u32[]{:S(2)}, u32[]{:S(2)}) collective-permute-start(bf16[2,4,4096]{2,1,0:T(4,128)(2,1)S(1)} %get-tuple-element.37), channel_id=1, source_target_pairs={{0,1},{1,0},{2,3},{3,2},{4,5},{5,4},{6,7},{7,6},{8,9},{9,8},{10,11... | collective-permute-start | bytes 196616 | tf_op jit(solution)/shard_map/ppermute | solution.py:30
  56.9 1.7 collective-permute-done.refs_1_
  58.6 0.0 collective-permute-done.1.refs_2_
  58.6 0.7 collective-permute-done.2.refs_3_
  59.3 0.1 partial.2
  59.3 0.1 collective-permute-start.4
  59.4 1.6 collective-permute-start.3
  61.0 5.0 %collective-permute-done.4.refs_1_ = bf16[2,4,4096]{2,1,0:T(4,128)(2,1)S(1)} collective-permute-done((bf16[2,4,4096]{2,1,0:T(4,128)(2,1)S(1)}, bf16[2,4,4096]{2,1,0:T(4,128)(2,1)S(1)}, u32[]{:S(2)}, u32[]{:S(2)}) %collective-permute-start.4) | collective-permute-done | bytes 65568 | tf_op jit(solution)/shard_map/ppermute | solution.py:30
  66.0 0.0 copy-start.14
  66.1 0.3 collective-permute-start.7
  66.3 2.4 %collective-permute-start.6 = (bf16[2,4,4096]{2,1,0:T(4,128)(2,1)S(1)}, bf16[2,4,4096]{2,1,0:T(4,128)(2,1)S(1)}, u32[]{:S(2)}, u32[]{:S(2)}) collective-permute-start(bf16[2,4,4096]{2,1,0:T(4,128)(2,1)S(1)} %join.2.refs_0_), channel_id=1, source_target_pairs={{0,2},{1,3},{2,0},{3,1},{4,6},{5,7},{6,4},{7,5},{8,10},{9,11},{10,... | collective-permute-start | bytes 196616 | tf_op jit(solution)/shard_map/ppermute | solution.py:30
  68.7 0.9 collective-permute-start.5
  69.6 1.7 collective-permute-done.7.refs_3_
  71.3 0.3 collective-permute-done.6.refs_2_
  71.6 1.3 collective-permute-done.5.refs_1_
  72.9 0.9 order_query.2
  73.8 10.5 %all_to_all.59 = bf16[8,16,128]{2,1,0:T(8,128)(2,1)S(1)} all-to-all(bf16[8,16,128]{2,1,0:T(8,128)(2,1)S(1)} %bitcast.23), channel_id=1, replica_groups=mesh['section'=4,'expert'=8] {'expert'}, dimensions={0} | all-to-all | bytes 65536 | tf_op jit(solution)/shard_map/all_to_all | solution.py:41
  84.3 0.5 attention.2
  84.7 0.1 broadcast_in_dim.9
  84.8 10.6 %all_to_all.60.c_ref = bf16[8,4,4096]{2,1,0:T(4,128)(2,1)S(1)} all-to-all(bf16[8,4,4096]{2,1,0:T(4,128)(2,1)S(1)} %broadcast_in_dim.9), channel_id=1, replica_groups=mesh['section'=4,'expert'=8] {'expert'}, dimensions={0} | all-to-all | bytes 524288 | tf_op jit(solution)/shard_map/all_to_all | solution.py:41
  95.5 0.9 attention_out.4
  96.3 12.3 %all_to_all.61.refs_0_ = bf16[8,32,512]{2,1,0:T(8,128)(2,1)S(1)} all-to-all(bf16[8,32,512]{2,1,0:T(8,128)(2,1)S(1)} %attention_out.4), channel_id=1, replica_groups=mesh['section'=4,'expert'=8] {'expert'}, dimensions={0} | all-to-all | bytes 524288 | tf_op jit(solution)/shard_map/all_to_all | solution.py:41
  108.6 1.5 experts_sending.3
  110.2 1.0 collective-permute-start.8
  111.2 2.6 %collective-permute-start.10 = (bf16[2,4,4096]{2,1,0:T(4,128)(2,1)S(1)}, bf16[2,4,4096]{2,1,0:T(4,128)(2,1)S(1)}, u32[]{:S(2)}, u32[]{:S(2)}) collective-permute-start(bf16[2,4,4096]{2,1,0:T(4,128)(2,1)S(1)} %get-tuple-element.44), channel_id=1, source_target_pairs={{0,1},{1,0},{2,3},{3,2},{4,5},{5,4},{6,7},{7,6},{8,9},{9,8},{10,11... | collective-permute-start | bytes 196616 | tf_op jit(solution)/shard_map/ppermute | solution.py:30
  113.7 1.7 collective-permute-done.8.refs_1_
  115.4 0.0 collective-permute-done.9.refs_2_
  115.4 0.7 collective-permute-done.10.refs_3_
  116.1 0.1 partial.3
  116.2 0.1 collective-permute-start.12
  116.2 0.1 collective-permute-start.11
  116.3 5.4 %collective-permute-done.12.refs_1_ = bf16[2,4,4096]{2,1,0:T(4,128)(2,1)S(1)} collective-permute-done((bf16[2,4,4096]{2,1,0:T(4,128)(2,1)S(1)}, bf16[2,4,4096]{2,1,0:T(4,128)(2,1)S(1)}, u32[]{:S(2)}, u32[]{:S(2)}) %collective-permute-start.12) | collective-permute-done | bytes 65568 | tf_op jit(solution)/shard_map/ppermute | solution.py:30
  121.8 1.4 collective-permute-start.15
  123.2 2.2 %collective-permute-start.14 = (bf16[2,4,4096]{2,1,0:T(4,128)(2,1)S(1)}, bf16[2,4,4096]{2,1,0:T(4,128)(2,1)S(1)}, u32[]{:S(2)}, u32[]{:S(2)}) collective-permute-start(bf16[2,4,4096]{2,1,0:T(4,128)(2,1)S(1)} %join.3.refs_0_), channel_id=1, source_target_pairs={{0,2},{1,3},{2,0},{3,1},{4,6},{5,7},{6,4},{7,5},{8,10},{9,11},{10,... | collective-permute-start | bytes 196616 | tf_op jit(solution)/shard_map/ppermute | solution.py:30
  125.4 1.7 collective-permute-done.15.refs_3_
  127.1 1.2 collective-permute-done.14.refs_2_
  128.3 1.3 collective-permute-done.13.refs_1_
  129.6 0.9 order_query.3
  130.5 9.1 %all_to_all.62 = bf16[8,16,128]{2,1,0:T(8,128)(2,1)S(1)} all-to-all(bf16[8,16,128]{2,1,0:T(8,128)(2,1)S(1)} %bitcast.24), channel_id=1, replica_groups=mesh['section'=4,'expert'=8] {'expert'}, dimensions={0} | all-to-all | bytes 65536 | tf_op jit(solution)/shard_map/all_to_all | solution.py:41
  139.5 0.5 attention.3
  140.0 0.1 broadcast_in_dim.10
  140.1 10.6 %all_to_all.63.c_ref = bf16[8,4,4096]{2,1,0:T(4,128)(2,1)S(1)} all-to-all(bf16[8,4,4096]{2,1,0:T(4,128)(2,1)S(1)} %broadcast_in_dim.10), channel_id=1, replica_groups=mesh['section'=4,'expert'=8] {'expert'}, dimensions={0} | all-to-all | bytes 524288 | tf_op jit(solution)/shard_map/all_to_all | solution.py:41
  150.7 0.9 attention_out.5
  151.6 10.9 %all_to_all.64.a_ref = bf16[8,32,512]{2,1,0:T(8,128)(2,1)S(1)} all-to-all(bf16[8,32,512]{2,1,0:T(8,128)(2,1)S(1)} %attention_out.5), channel_id=1, replica_groups=mesh['section'=4,'expert'=8] {'expert'}, dimensions={0} | all-to-all | bytes 524288 | tf_op jit(solution)/shard_map/all_to_all | solution.py:41
  162.5 1.5 experts.1
  164.0 10.9 %all_to_all.65.r_ref = bf16[8,4,4096]{2,1,0:T(4,128)(2,1)S(1)} all-to-all(bf16[8,4,4096]{2,1,0:T(4,128)(2,1)S(1)} %get-tuple-element.47), channel_id=1, replica_groups=mesh['section'=4,'expert'=8] {'expert'}, dimensions={0} | all-to-all | bytes 524288 | tf_op jit(solution)/shard_map/all_to_all | solution.py:41
  174.9 0.7 combine.1
  (36 shorter events, 0.2 us)
Async XLA Ops:
  0.0 0.8 copy-start.7
  0.8 16.3 %copy-start = (bf16[1,4096,512]{2,1,0:T(8,128)(2,1)S(1)}, bf16[1,4096,512]{2,1,0:T(8,128)(2,1)}, u32[]{:S(2)}) copy-start(bf16[1,4096,512]{2,1,0:T(8,128)(2,1)} %param.20) | copy-start | bytes 12582916
  0.8 16.3 %copy-start.8 = (bf16[1,4096]{1,0:T(2,128)(2,1)S(1)}, bf16[1,4096]{1,0:T(2,128)(2,1)}, u32[]{:S(2)}) copy-start(bf16[1,4096]{1,0:T(2,128)(2,1)} %refs_4_.4) | copy-start | bytes 24580
  0.8 16.3 %copy-start.10 = (s32[1,3,4,2]{2,3,1,0:T(2,128)S(1)}, s32[1,3,4,2]{2,3,1,0:T(2,128)}, u32[]{:S(2)}) copy-start(s32[1,3,4,2]{2,3,1,0:T(2,128)} %param.29) | copy-start | bytes 292
  0.8 16.3 %copy-start.11 = (f32[1,3,4,2]{2,3,1,0:T(2,128)S(1)}, f32[1,3,4,2]{2,3,1,0:T(2,128)}, u32[]{:S(2)}) copy-start(f32[1,3,4,2]{2,3,1,0:T(2,128)} %param.30) | copy-start | bytes 292
  17.1 11.2 %copy-start.5 = (bf16[1,3,4,64,4,128]{5,4,3,2,1,0:T(4,128)(2,1)S(1)}, bf16[1,3,4,64,4,128]{5,4,3,2,1,0:T(4,128)(2,1)}, u32[]{:S(2)}) copy-start(bf16[1,3,4,64,4,128]{5,4,3,2,1,0:T(4,128)(2,1)} %param.22) | copy-start | bytes 2359300
  17.1 11.2 %copy-start.6 = (bf16[1,3,4,64,4,128]{5,4,3,2,1,0:T(4,128)(2,1)S(1)}, bf16[1,3,4,64,4,128]{5,4,3,2,1,0:T(4,128)(2,1)}, u32[]{:S(2)}) copy-start(bf16[1,3,4,64,4,128]{5,4,3,2,1,0:T(4,128)(2,1)} %param.23) | copy-start | bytes 2359300
  17.1 11.2 %copy-start.12 = (s32[1,3,4]{2,0,1:T(1,128)S(1)}, s32[1,3,4]{2,0,1:T(1,128)}, u32[]{:S(2)}) copy-start(s32[1,3,4]{2,0,1:T(1,128)} %param.24) | copy-start | bytes 148
  17.1 11.2 %copy-start.13 = (bf16[128,256]{1,0:T(8,128)(2,1)S(1)}, bf16[128,256]{1,0:T(8,128)(2,1)}, u32[]{:S(2)}) copy-start(bf16[128,256]{1,0:T(8,128)(2,1)} %constant.17.clone.refs_3_) | copy-start | bytes 196612
  17.1 11.2 %copy-start.15 = (s32[32,1]{1,0:T(8,128)S(1)}, s32[32,1]{1,0:T(8,128)}, u32[]{:S(2)}) copy-start(s32[32,1]{1,0:T(8,128)} %constant.14.clone.refs_4_.line_ref) | copy-start | bytes 388
  17.1 11.2 %copy-start.16 = (bf16[32,256]{1,0:T(8,128)(2,1)S(1)}, bf16[32,256]{1,0:T(8,128)(2,1)}, u32[]{:S(2)}) copy-start(bf16[32,256]{1,0:T(8,128)(2,1)} %constant.18.clone.pick_ref) | copy-start | bytes 49156
  17.2 11.2 %copy-start.17 = (s32[8,256]{1,0:T(8,128)S(1)}, s32[8,256]{1,0:T(8,128)}, u32[]{:S(2)}) copy-start(s32[8,256]{1,0:T(8,128)} %constant.15.clone.refs_5_.column_ref) | copy-start | bytes 24580
  28.4 11.3 %copy-start.1 = (bf16[1,4096,512]{2,1,0:T(8,128)(2,1)S(1)}, bf16[1,4096,512]{2,1,0:T(8,128)(2,1)}, u32[]{:S(2)}) copy-start(bf16[1,4096,512]{2,1,0:T(8,128)(2,1)} %param.21) | copy-start | bytes 12582916
  39.7 12.1 %copy-start.2 = (bf16[1,1,4096,384]{3,2,1,0:T(8,128)(2,1)S(1)}, bf16[1,1,4096,384]{3,2,1,0:T(8,128)(2,1)}, u32[]{:S(2)}) copy-start(bf16[1,1,4096,384]{3,2,1,0:T(8,128)(2,1)} %param.26) | copy-start | bytes 9437188
  39.7 12.1 %copy-start.3 = (bf16[1,1,4096,384]{3,2,1,0:T(8,128)(2,1)S(1)}, bf16[1,1,4096,384]{3,2,1,0:T(8,128)(2,1)}, u32[]{:S(2)}) copy-start(bf16[1,1,4096,384]{3,2,1,0:T(8,128)(2,1)} %param.27) | copy-start | bytes 9437188
  39.7 12.1 %copy-start.4 = (bf16[1,1,384,4096]{3,2,1,0:T(8,128)(2,1)S(1)}, bf16[1,1,384,4096]{3,2,1,0:T(8,128)(2,1)}, u32[]{:S(2)}) copy-start(bf16[1,1,384,4096]{3,2,1,0:T(8,128)(2,1)} %param.28) | copy-start | bytes 9437188
  39.7 12.1 %copy-start.9 = (bf16[1,4096]{1,0:T(2,128)(2,1)S(1)}, bf16[1,4096]{1,0:T(2,128)(2,1)}, u32[]{:S(2)}) copy-start(bf16[1,4096]{1,0:T(2,128)(2,1)} %gain_ref.3) | copy-start | bytes 24580
  53.3 5.2 %collective-permute-start = (bf16[2,4,4096]{2,1,0:T(4,128)(2,1)S(1)}, bf16[2,4,4096]{2,1,0:T(4,128)(2,1)S(1)}, u32[]{:S(2)}, u32[]{:S(2)}) collective-permute-start(bf16[2,4,4096]{2,1,0:T(4,128)(2,1)S(1)} %get-tuple-element.35), channel_id=1, source_target_pairs={{0,3},{1,2},{2,1},{3,0},{4,7},{5,6},{6,5},{7,4},{8,11},{9,10},{10,... | collective-permute-start | bytes 196616 | tf_op jit(solution)/shard_map/ppermute | solution.py:30
  54.3 4.3 %collective-permute-start.1 = (bf16[2,4,4096]{2,1,0:T(4,128)(2,1)S(1)}, bf16[2,4,4096]{2,1,0:T(4,128)(2,1)S(1)}, u32[]{:S(2)}, u32[]{:S(2)}) collective-permute-start(bf16[2,4,4096]{2,1,0:T(4,128)(2,1)S(1)} %get-tuple-element.36), channel_id=1, source_target_pairs={{0,2},{1,3},{2,0},{3,1},{4,6},{5,7},{6,4},{7,5},{8,10},{9,11},{10,... | collective-permute-start | bytes 196616 | tf_op jit(solution)/shard_map/ppermute | solution.py:30
  54.9 4.4 %collective-permute-start.2 = (bf16[2,4,4096]{2,1,0:T(4,128)(2,1)S(1)}, bf16[2,4,4096]{2,1,0:T(4,128)(2,1)S(1)}, u32[]{:S(2)}, u32[]{:S(2)}) collective-permute-start(bf16[2,4,4096]{2,1,0:T(4,128)(2,1)S(1)} %get-tuple-element.37), channel_id=1, source_target_pairs={{0,1},{1,0},{2,3},{3,2},{4,5},{5,4},{6,7},{7,6},{8,9},{9,8},{10,11... | collective-permute-start | bytes 196616 | tf_op jit(solution)/shard_map/ppermute | solution.py:30
  59.3 6.7 %collective-permute-start.4 = (bf16[2,4,4096]{2,1,0:T(4,128)(2,1)S(1)}, bf16[2,4,4096]{2,1,0:T(4,128)(2,1)S(1)}, u32[]{:S(2)}, u32[]{:S(2)}) collective-permute-start(bf16[2,4,4096]{2,1,0:T(4,128)(2,1)S(1)} %partial.2), channel_id=1, source_target_pairs={{0,12},{1,13},{2,14},{3,15},{4,8},{5,9},{6,10},{7,11},{8,20},{9,21... | collective-permute-start | bytes 196616 | tf_op jit(solution)/shard_map/ppermute | solution.py:30
  59.4 6.6 %collective-permute-start.3 = (bf16[2,4,4096]{2,1,0:T(4,128)(2,1)S(1)}, bf16[2,4,4096]{2,1,0:T(4,128)(2,1)S(1)}, u32[]{:S(2)}, u32[]{:S(2)}) collective-permute-start(bf16[2,4,4096]{2,1,0:T(4,128)(2,1)S(1)} %partial.2), channel_id=1, source_target_pairs={{0,8},{1,9},{2,10},{3,11},{4,12},{5,13},{6,14},{7,15},{8,16},{9,17... | collective-permute-start | bytes 196616 | tf_op jit(solution)/shard_map/ppermute | solution.py:30
  66.0 18.2 %copy-start.14 = (bf16[128,128]{1,0:T(8,128)(2,1)S(1)}, bf16[128,128]{1,0:T(8,128)(2,1)}, u32[]{:S(2)}) copy-start(bf16[128,128]{1,0:T(8,128)(2,1)} %constant.16.clone.order_ref) | copy-start | bytes 98308
  66.1 5.2 %collective-permute-start.7 = (bf16[2,4,4096]{2,1,0:T(4,128)(2,1)S(1)}, bf16[2,4,4096]{2,1,0:T(4,128)(2,1)S(1)}, u32[]{:S(2)}, u32[]{:S(2)}) collective-permute-start(bf16[2,4,4096]{2,1,0:T(4,128)(2,1)S(1)} %join.2.refs_0_), channel_id=1, source_target_pairs={{0,3},{1,2},{2,1},{3,0},{4,7},{5,6},{6,5},{7,4},{8,11},{9,10},{10,... | collective-permute-start | bytes 196616 | tf_op jit(solution)/shard_map/ppermute | solution.py:30
  66.3 5.3 %collective-permute-start.6 = (bf16[2,4,4096]{2,1,0:T(4,128)(2,1)S(1)}, bf16[2,4,4096]{2,1,0:T(4,128)(2,1)S(1)}, u32[]{:S(2)}, u32[]{:S(2)}) collective-permute-start(bf16[2,4,4096]{2,1,0:T(4,128)(2,1)S(1)} %join.2.refs_0_), channel_id=1, source_target_pairs={{0,2},{1,3},{2,0},{3,1},{4,6},{5,7},{6,4},{7,5},{8,10},{9,11},{10,... | collective-permute-start | bytes 196616 | tf_op jit(solution)/shard_map/ppermute | solution.py:30
  68.7 4.3 %collective-permute-start.5 = (bf16[2,4,4096]{2,1,0:T(4,128)(2,1)S(1)}, bf16[2,4,4096]{2,1,0:T(4,128)(2,1)S(1)}, u32[]{:S(2)}, u32[]{:S(2)}) collective-permute-start(bf16[2,4,4096]{2,1,0:T(4,128)(2,1)S(1)} %join.2.refs_0_), channel_id=1, source_target_pairs={{0,1},{1,0},{2,3},{3,2},{4,5},{5,4},{6,7},{7,6},{8,9},{9,8},{10,11... | collective-permute-start | bytes 196616 | tf_op jit(solution)/shard_map/ppermute | solution.py:30
  110.2 5.2 %collective-permute-start.8 = (bf16[2,4,4096]{2,1,0:T(4,128)(2,1)S(1)}, bf16[2,4,4096]{2,1,0:T(4,128)(2,1)S(1)}, u32[]{:S(2)}, u32[]{:S(2)}) collective-permute-start(bf16[2,4,4096]{2,1,0:T(4,128)(2,1)S(1)} %get-tuple-element.42), channel_id=1, source_target_pairs={{0,3},{1,2},{2,1},{3,0},{4,7},{5,6},{6,5},{7,4},{8,11},{9,10},{10,... | collective-permute-start | bytes 196616 | tf_op jit(solution)/shard_map/ppermute | solution.py:30
  111.2 4.3 %collective-permute-start.9 = (bf16[2,4,4096]{2,1,0:T(4,128)(2,1)S(1)}, bf16[2,4,4096]{2,1,0:T(4,128)(2,1)S(1)}, u32[]{:S(2)}, u32[]{:S(2)}) collective-permute-start(bf16[2,4,4096]{2,1,0:T(4,128)(2,1)S(1)} %get-tuple-element.43), channel_id=1, source_target_pairs={{0,2},{1,3},{2,0},{3,1},{4,6},{5,7},{6,4},{7,5},{8,10},{9,11},{10,... | collective-permute-start | bytes 196616 | tf_op jit(solution)/shard_map/ppermute | solution.py:30
  111.2 4.9 %collective-permute-start.10 = (bf16[2,4,4096]{2,1,0:T(4,128)(2,1)S(1)}, bf16[2,4,4096]{2,1,0:T(4,128)(2,1)S(1)}, u32[]{:S(2)}, u32[]{:S(2)}) collective-permute-start(bf16[2,4,4096]{2,1,0:T(4,128)(2,1)S(1)} %get-tuple-element.44), channel_id=1, source_target_pairs={{0,1},{1,0},{2,3},{3,2},{4,5},{5,4},{6,7},{7,6},{8,9},{9,8},{10,11... | collective-permute-start | bytes 196616 | tf_op jit(solution)/shard_map/ppermute | solution.py:30
  116.2 5.5 %collective-permute-start.12 = (bf16[2,4,4096]{2,1,0:T(4,128)(2,1)S(1)}, bf16[2,4,4096]{2,1,0:T(4,128)(2,1)S(1)}, u32[]{:S(2)}, u32[]{:S(2)}) collective-permute-start(bf16[2,4,4096]{2,1,0:T(4,128)(2,1)S(1)} %partial.3), channel_id=1, source_target_pairs={{0,12},{1,13},{2,14},{3,15},{4,8},{5,9},{6,10},{7,11},{8,20},{9,21... | collective-permute-start | bytes 196616 | tf_op jit(solution)/shard_map/ppermute | solution.py:30
  116.2 5.5 %collective-permute-start.11 = (bf16[2,4,4096]{2,1,0:T(4,128)(2,1)S(1)}, bf16[2,4,4096]{2,1,0:T(4,128)(2,1)S(1)}, u32[]{:S(2)}, u32[]{:S(2)}) collective-permute-start(bf16[2,4,4096]{2,1,0:T(4,128)(2,1)S(1)} %partial.3), channel_id=1, source_target_pairs={{0,8},{1,9},{2,10},{3,11},{4,12},{5,13},{6,14},{7,15},{8,16},{9,17... | collective-permute-start | bytes 196616 | tf_op jit(solution)/shard_map/ppermute | solution.py:30
  121.8 5.3 %collective-permute-start.15 = (bf16[2,4,4096]{2,1,0:T(4,128)(2,1)S(1)}, bf16[2,4,4096]{2,1,0:T(4,128)(2,1)S(1)}, u32[]{:S(2)}, u32[]{:S(2)}) collective-permute-start(bf16[2,4,4096]{2,1,0:T(4,128)(2,1)S(1)} %join.3.refs_0_), channel_id=1, source_target_pairs={{0,3},{1,2},{2,1},{3,0},{4,7},{5,6},{6,5},{7,4},{8,11},{9,10},{10,... | collective-permute-start | bytes 196616 | tf_op jit(solution)/shard_map/ppermute | solution.py:30
  123.2 5.1 %collective-permute-start.14 = (bf16[2,4,4096]{2,1,0:T(4,128)(2,1)S(1)}, bf16[2,4,4096]{2,1,0:T(4,128)(2,1)S(1)}, u32[]{:S(2)}, u32[]{:S(2)}) collective-permute-start(bf16[2,4,4096]{2,1,0:T(4,128)(2,1)S(1)} %join.3.refs_0_), channel_id=1, source_target_pairs={{0,2},{1,3},{2,0},{3,1},{4,6},{5,7},{6,4},{7,5},{8,10},{9,11},{10,... | collective-permute-start | bytes 196616 | tf_op jit(solution)/shard_map/ppermute | solution.py:30
  125.3 4.3 %collective-permute-start.13 = (bf16[2,4,4096]{2,1,0:T(4,128)(2,1)S(1)}, bf16[2,4,4096]{2,1,0:T(4,128)(2,1)S(1)}, u32[]{:S(2)}, u32[]{:S(2)}) collective-permute-start(bf16[2,4,4096]{2,1,0:T(4,128)(2,1)S(1)} %join.3.refs_0_), channel_id=1, source_target_pairs={{0,1},{1,0},{2,3},{3,2},{4,5},{5,4},{6,7},{7,6},{8,9},{9,8},{10,11... | collective-permute-start | bytes 196616 | tf_op jit(solution)/shard_map/ppermute | solution.py:30

commit v8 on v7

--- a/solution.py
+++ b/solution.py
@@ -201,16 +201,16 @@
 
 def out_kernel(c_ref, w_ref, o_ref, lines):
     devices, own, width = c_ref.shape
-    chunk, total = 512, None
+    chunk, totals = 512, {}
     for start in range(0, width, chunk):
         at = slice(start, start + chunk)
         for i in range(devices):
             lines[own * i:own * (i + 1), at] = c_ref[i, :, at].astype(F32)
-        part = jnp.dot(lines[:, at].astype(BF16), w_ref[at, :], preferred_element_type=F32)
-        total = part if total is None else total + part
-    columns = total.astype(BF16)
-    for i in range(devices):
-        o_ref[i] = columns
+        add_tiles(totals, lines[:, at].astype(BF16), w_ref, at)
+    for at, total in totals.items():
+        columns = total.astype(BF16)
+        for i in range(devices):
+            o_ref[i, :, at:at + columns.shape[1]] = columns
 
 
 def expert_kernel(step, me_ref, a_ref, x_ref, gain_ref, gate_ref, up_ref, down_ref, share_ref, h_ref, m_ref, middle):

time: 176 us -> 176 us (level)
  no operation moved by 1% of the time
where the time goes in v8:
time: 176 us; the launch traced here: 175 us
  blocking collectives  123 us (70%)
  waiting for transfers between devices  22.8 us (13%)
  starting transfers between devices  16.1 us (9%)
  Pallas kernels  11.6 us (7%)
    all_to_all x11, blocking collectives, swapped(): lax.all_to_all(blocks, 'expert', split_axis=0, concat_axis=0, tiled=True)  123 us
    ppermute x16, waiting for transfers between devices, shifted(): return lax.ppermute(array, ('section', 'expert'), pairs)  22.8 us
    ppermute x16, starting transfers between devices, shifted(): return lax.ppermute(array, ('section', 'expert'), pairs)  16.1 us
    pallas_call x18, Pallas kernels, call(): pl.pallas_call(kernel, out_shape=out, in_specs=specs, out_specs=whole() i...  11.6 us
  transfers between devices with their start and end apart: 16, of which 12 were waited for; matrix products, arithmetic and copies ran while one was open for 0% of the time, Pallas kernels for 0%

profile of v8, /device:TPU:0, one launch (start us, length us, event | category | flops | bytes accessed | tf_op | source)
XLA Modules:
  0.0 175.2 jit_solution(17104281019759788591)
XLA Ops:
  0.0 0.8 copy-done.7
  0.8 16.3 %all_to_all.55.x_ref = bf16[8,4,4096]{2,1,0:T(4,128)(2,1)S(1)} all-to-all(bf16[8,4,4096]{2,1,0:T(4,128)(2,1)S(1)} %spread.1), channel_id=1, replica_groups=mesh['section'=4,'expert'=8] {'expert'}, dimensions={0} | all-to-all | bytes 524288 | tf_op jit(solution)/shard_map/all_to_all | solution.py:41
  17.1 0.0 copy-start.12
  17.1 0.0 copy-start.13
  17.1 0.0 copy-start.15
  17.1 0.0 copy-start.16
  17.2 0.0 copy-start.17
  17.2 0.9 first_query.1
  18.0 10.3 %all_to_all.56 = bf16[8,32,128]{2,1,0:T(8,128)(2,1)S(1)} all-to-all(bf16[8,32,128]{2,1,0:T(8,128)(2,1)S(1)} %get-tuple-element.29), channel_id=1, replica_groups=mesh['section'=4,'expert'=8] {'expert'}, dimensions={0} | all-to-all | bytes 131072 | tf_op jit(solution)/shard_map/all_to_all | solution.py:41
  28.4 0.5 first_attention.1
  28.8 0.1 broadcast_in_dim.8
  28.9 10.8 %all_to_all.57.c_ref = bf16[8,4,4096]{2,1,0:T(4,128)(2,1)S(1)} all-to-all(bf16[8,4,4096]{2,1,0:T(4,128)(2,1)S(1)} %broadcast_in_dim.8), channel_id=1, replica_groups=mesh['section'=4,'expert'=8] {'expert'}, dimensions={0} | all-to-all | bytes 524288 | tf_op jit(solution)/shard_map/all_to_all | solution.py:41
  39.7 0.7 attention_out.3
  40.5 11.2 %all_to_all.58.refs_0_ = bf16[8,32,512]{2,1,0:T(8,128)(2,1)S(1)} all-to-all(bf16[8,32,512]{2,1,0:T(8,128)(2,1)S(1)} %attention_out.3), channel_id=1, replica_groups=mesh['section'=4,'expert'=8] {'expert'}, dimensions={0} | all-to-all | bytes 524288 | tf_op jit(solution)/shard_map/all_to_all | solution.py:41
  51.6 1.5 experts_sending.2
  53.2 1.0 collective-permute-start
  54.2 0.6 collective-permute-start.1
  54.7 2.0 %collective-permute-start.2 = (bf16[2,4,4096]{2,1,0:T(4,128)(2,1)S(1)}, bf16[2,4,4096]{2,1,0:T(4,128)(2,1)S(1)}, u32[]{:S(2)}, u32[]{:S(2)}) collective-permute-start(bf16[2,4,4096]{2,1,0:T(4,128)(2,1)S(1)} %get-tuple-element.37), channel_id=1, source_target_pairs={{0,1},{1,0},{2,3},{3,2},{4,5},{5,4},{6,7},{7,6},{8,9},{9,8},{10,11... | collective-permute-start | bytes 196616 | tf_op jit(solution)/shard_map/ppermute | solution.py:30
  56.7 1.7 collective-permute-done.refs_1_
  58.4 0.0 collective-permute-done.1.refs_2_
  58.4 0.7 collective-permute-done.2.refs_3_
  59.1 0.1 partial.2
  59.2 0.1 collective-permute-start.4
  59.2 1.6 collective-permute-start.3
  60.9 5.0 %collective-permute-done.4.refs_1_ = bf16[2,4,4096]{2,1,0:T(4,128)(2,1)S(1)} collective-permute-done((bf16[2,4,4096]{2,1,0:T(4,128)(2,1)S(1)}, bf16[2,4,4096]{2,1,0:T(4,128)(2,1)S(1)}, u32[]{:S(2)}, u32[]{:S(2)}) %collective-permute-start.4) | collective-permute-done | bytes 65568 | tf_op jit(solution)/shard_map/ppermute | solution.py:30
  65.9 0.0 copy-start.14
  65.9 0.3 collective-permute-start.7
  66.2 2.4 %collective-permute-start.6 = (bf16[2,4,4096]{2,1,0:T(4,128)(2,1)S(1)}, bf16[2,4,4096]{2,1,0:T(4,128)(2,1)S(1)}, u32[]{:S(2)}, u32[]{:S(2)}) collective-permute-start(bf16[2,4,4096]{2,1,0:T(4,128)(2,1)S(1)} %join.2.refs_0_), channel_id=1, source_target_pairs={{0,2},{1,3},{2,0},{3,1},{4,6},{5,7},{6,4},{7,5},{8,10},{9,11},{10,... | collective-permute-start | bytes 196616 | tf_op jit(solution)/shard_map/ppermute | solution.py:30
  68.5 0.9 collective-permute-start.5
  69.5 1.7 collective-permute-done.7.refs_3_
  71.2 0.3 collective-permute-done.6.refs_2_
  71.5 1.3 collective-permute-done.5.refs_1_
  72.8 0.9 order_query.2
  73.7 10.5 %all_to_all.59 = bf16[8,16,128]{2,1,0:T(8,128)(2,1)S(1)} all-to-all(bf16[8,16,128]{2,1,0:T(8,128)(2,1)S(1)} %bitcast.23), channel_id=1, replica_groups=mesh['section'=4,'expert'=8] {'expert'}, dimensions={0} | all-to-all | bytes 65536 | tf_op jit(solution)/shard_map/all_to_all | solution.py:41
  84.2 0.5 attention.2
  84.6 0.1 broadcast_in_dim.9
  84.7 10.6 %all_to_all.60.c_ref = bf16[8,4,4096]{2,1,0:T(4,128)(2,1)S(1)} all-to-all(bf16[8,4,4096]{2,1,0:T(4,128)(2,1)S(1)} %broadcast_in_dim.9), channel_id=1, replica_groups=mesh['section'=4,'expert'=8] {'expert'}, dimensions={0} | all-to-all | bytes 524288 | tf_op jit(solution)/shard_map/all_to_all | solution.py:41
  95.3 0.7 attention_out.4
  96.1 12.3 %all_to_all.61.refs_0_ = bf16[8,32,512]{2,1,0:T(8,128)(2,1)S(1)} all-to-all(bf16[8,32,512]{2,1,0:T(8,128)(2,1)S(1)} %attention_out.4), channel_id=1, replica_groups=mesh['section'=4,'expert'=8] {'expert'}, dimensions={0} | all-to-all | bytes 524288 | tf_op jit(solution)/shard_map/all_to_all | solution.py:41
  108.4 1.5 experts_sending.3
  109.9 1.0 collective-permute-start.8
  110.9 2.6 %collective-permute-start.10 = (bf16[2,4,4096]{2,1,0:T(4,128)(2,1)S(1)}, bf16[2,4,4096]{2,1,0:T(4,128)(2,1)S(1)}, u32[]{:S(2)}, u32[]{:S(2)}) collective-permute-start(bf16[2,4,4096]{2,1,0:T(4,128)(2,1)S(1)} %get-tuple-element.44), channel_id=1, source_target_pairs={{0,1},{1,0},{2,3},{3,2},{4,5},{5,4},{6,7},{7,6},{8,9},{9,8},{10,11... | collective-permute-start | bytes 196616 | tf_op jit(solution)/shard_map/ppermute | solution.py:30
  113.5 1.7 collective-permute-done.8.refs_1_
  115.2 0.0 collective-permute-done.9.refs_2_
  115.2 0.7 collective-permute-done.10.refs_3_
  115.8 0.1 partial.3
  115.9 0.1 collective-permute-start.12
  116.0 0.1 collective-permute-start.11
  116.0 5.4 %collective-permute-done.12.refs_1_ = bf16[2,4,4096]{2,1,0:T(4,128)(2,1)S(1)} collective-permute-done((bf16[2,4,4096]{2,1,0:T(4,128)(2,1)S(1)}, bf16[2,4,4096]{2,1,0:T(4,128)(2,1)S(1)}, u32[]{:S(2)}, u32[]{:S(2)}) %collective-permute-start.12) | collective-permute-done | bytes 65568 | tf_op jit(solution)/shard_map/ppermute | solution.py:30
  121.5 1.4 collective-permute-start.15
  122.9 2.2 %collective-permute-start.14 = (bf16[2,4,4096]{2,1,0:T(4,128)(2,1)S(1)}, bf16[2,4,4096]{2,1,0:T(4,128)(2,1)S(1)}, u32[]{:S(2)}, u32[]{:S(2)}) collective-permute-start(bf16[2,4,4096]{2,1,0:T(4,128)(2,1)S(1)} %join.3.refs_0_), channel_id=1, source_target_pairs={{0,2},{1,3},{2,0},{3,1},{4,6},{5,7},{6,4},{7,5},{8,10},{9,11},{10,... | collective-permute-start | bytes 196616 | tf_op jit(solution)/shard_map/ppermute | solution.py:30
  125.1 1.7 collective-permute-done.15.refs_3_
  126.8 1.2 collective-permute-done.14.refs_2_
  128.0 1.3 collective-permute-done.13.refs_1_
  129.4 0.9 order_query.3
  130.2 9.1 %all_to_all.62 = bf16[8,16,128]{2,1,0:T(8,128)(2,1)S(1)} all-to-all(bf16[8,16,128]{2,1,0:T(8,128)(2,1)S(1)} %bitcast.24), channel_id=1, replica_groups=mesh['section'=4,'expert'=8] {'expert'}, dimensions={0} | all-to-all | bytes 65536 | tf_op jit(solution)/shard_map/all_to_all | solution.py:41
  139.3 0.5 attention.3
  139.7 0.1 broadcast_in_dim.10
  139.8 10.6 %all_to_all.63.c_ref = bf16[8,4,4096]{2,1,0:T(4,128)(2,1)S(1)} all-to-all(bf16[8,4,4096]{2,1,0:T(4,128)(2,1)S(1)} %broadcast_in_dim.10), channel_id=1, replica_groups=mesh['section'=4,'expert'=8] {'expert'}, dimensions={0} | all-to-all | bytes 524288 | tf_op jit(solution)/shard_map/all_to_all | solution.py:41
  150.5 0.7 attention_out.5
  151.2 10.9 %all_to_all.64.a_ref = bf16[8,32,512]{2,1,0:T(8,128)(2,1)S(1)} all-to-all(bf16[8,32,512]{2,1,0:T(8,128)(2,1)S(1)} %attention_out.5), channel_id=1, replica_groups=mesh['section'=4,'expert'=8] {'expert'}, dimensions={0} | all-to-all | bytes 524288 | tf_op jit(solution)/shard_map/all_to_all | solution.py:41
  162.1 1.5 experts.1
  163.6 10.9 %all_to_all.65.r_ref = bf16[8,4,4096]{2,1,0:T(4,128)(2,1)S(1)} all-to-all(bf16[8,4,4096]{2,1,0:T(4,128)(2,1)S(1)} %get-tuple-element.47), channel_id=1, replica_groups=mesh['section'=4,'expert'=8] {'expert'}, dimensions={0} | all-to-all | bytes 524288 | tf_op jit(solution)/shard_map/all_to_all | solution.py:41
  174.5 0.7 combine.1
  (36 shorter events, 0.2 us)
Async XLA Ops:
  0.0 0.8 copy-start.7
  0.8 16.3 %copy-start = (bf16[1,4096,512]{2,1,0:T(8,128)(2,1)S(1)}, bf16[1,4096,512]{2,1,0:T(8,128)(2,1)}, u32[]{:S(2)}) copy-start(bf16[1,4096,512]{2,1,0:T(8,128)(2,1)} %param.20) | copy-start | bytes 12582916
  0.8 16.3 %copy-start.8 = (bf16[1,4096]{1,0:T(2,128)(2,1)S(1)}, bf16[1,4096]{1,0:T(2,128)(2,1)}, u32[]{:S(2)}) copy-start(bf16[1,4096]{1,0:T(2,128)(2,1)} %refs_4_.4) | copy-start | bytes 24580
  0.8 16.3 %copy-start.10 = (s32[1,3,4,2]{2,3,1,0:T(2,128)S(1)}, s32[1,3,4,2]{2,3,1,0:T(2,128)}, u32[]{:S(2)}) copy-start(s32[1,3,4,2]{2,3,1,0:T(2,128)} %param.29) | copy-start | bytes 292
  0.8 16.3 %copy-start.11 = (f32[1,3,4,2]{2,3,1,0:T(2,128)S(1)}, f32[1,3,4,2]{2,3,1,0:T(2,128)}, u32[]{:S(2)}) copy-start(f32[1,3,4,2]{2,3,1,0:T(2,128)} %param.30) | copy-start | bytes 292
  17.1 11.2 %copy-start.5 = (bf16[1,3,4,64,4,128]{5,4,3,2,1,0:T(4,128)(2,1)S(1)}, bf16[1,3,4,64,4,128]{5,4,3,2,1,0:T(4,128)(2,1)}, u32[]{:S(2)}) copy-start(bf16[1,3,4,64,4,128]{5,4,3,2,1,0:T(4,128)(2,1)} %param.22) | copy-start | bytes 2359300
  17.1 11.2 %copy-start.6 = (bf16[1,3,4,64,4,128]{5,4,3,2,1,0:T(4,128)(2,1)S(1)}, bf16[1,3,4,64,4,128]{5,4,3,2,1,0:T(4,128)(2,1)}, u32[]{:S(2)}) copy-start(bf16[1,3,4,64,4,128]{5,4,3,2,1,0:T(4,128)(2,1)} %param.23) | copy-start | bytes 2359300
  17.1 11.2 %copy-start.12 = (s32[1,3,4]{2,0,1:T(1,128)S(1)}, s32[1,3,4]{2,0,1:T(1,128)}, u32[]{:S(2)}) copy-start(s32[1,3,4]{2,0,1:T(1,128)} %param.24) | copy-start | bytes 148
  17.1 11.2 %copy-start.13 = (bf16[128,256]{1,0:T(8,128)(2,1)S(1)}, bf16[128,256]{1,0:T(8,128)(2,1)}, u32[]{:S(2)}) copy-start(bf16[128,256]{1,0:T(8,128)(2,1)} %constant.17.clone.refs_3_) | copy-start | bytes 196612
  17.1 11.2 %copy-start.15 = (s32[32,1]{1,0:T(8,128)S(1)}, s32[32,1]{1,0:T(8,128)}, u32[]{:S(2)}) copy-start(s32[32,1]{1,0:T(8,128)} %constant.14.clone.refs_4_.line_ref) | copy-start | bytes 388
  17.1 11.2 %copy-start.16 = (bf16[32,256]{1,0:T(8,128)(2,1)S(1)}, bf16[32,256]{1,0:T(8,128)(2,1)}, u32[]{:S(2)}) copy-start(bf16[32,256]{1,0:T(8,128)(2,1)} %constant.18.clone.pick_ref) | copy-start | bytes 49156
  17.2 11.2 %copy-start.17 = (s32[8,256]{1,0:T(8,128)S(1)}, s32[8,256]{1,0:T(8,128)}, u32[]{:S(2)}) copy-start(s32[8,256]{1,0:T(8,128)} %constant.15.clone.refs_5_.column_ref) | copy-start | bytes 24580
  28.4 11.3 %copy-start.1 = (bf16[1,4096,512]{2,1,0:T(8,128)(2,1)S(1)}, bf16[1,4096,512]{2,1,0:T(8,128)(2,1)}, u32[]{:S(2)}) copy-start(bf16[1,4096,512]{2,1,0:T(8,128)(2,1)} %param.21) | copy-start | bytes 12582916
  39.7 11.9 %copy-start.2 = (bf16[1,1,4096,384]{3,2,1,0:T(8,128)(2,1)S(1)}, bf16[1,1,4096,384]{3,2,1,0:T(8,128)(2,1)}, u32[]{:S(2)}) copy-start(bf16[1,1,4096,384]{3,2,1,0:T(8,128)(2,1)} %param.26) | copy-start | bytes 9437188
  39.7 11.9 %copy-start.3 = (bf16[1,1,4096,384]{3,2,1,0:T(8,128)(2,1)S(1)}, bf16[1,1,4096,384]{3,2,1,0:T(8,128)(2,1)}, u32[]{:S(2)}) copy-start(bf16[1,1,4096,384]{3,2,1,0:T(8,128)(2,1)} %param.27) | copy-start | bytes 9437188
  39.7 11.9 %copy-start.4 = (bf16[1,1,384,4096]{3,2,1,0:T(8,128)(2,1)S(1)}, bf16[1,1,384,4096]{3,2,1,0:T(8,128)(2,1)}, u32[]{:S(2)}) copy-start(bf16[1,1,384,4096]{3,2,1,0:T(8,128)(2,1)} %param.28) | copy-start | bytes 9437188
  39.7 11.9 %copy-start.9 = (bf16[1,4096]{1,0:T(2,128)(2,1)S(1)}, bf16[1,4096]{1,0:T(2,128)(2,1)}, u32[]{:S(2)}) copy-start(bf16[1,4096]{1,0:T(2,128)(2,1)} %gain_ref.3) | copy-start | bytes 24580
  53.2 5.2 %collective-permute-start = (bf16[2,4,4096]{2,1,0:T(4,128)(2,1)S(1)}, bf16[2,4,4096]{2,1,0:T(4,128)(2,1)S(1)}, u32[]{:S(2)}, u32[]{:S(2)}) collective-permute-start(bf16[2,4,4096]{2,1,0:T(4,128)(2,1)S(1)} %get-tuple-element.35), channel_id=1, source_target_pairs={{0,3},{1,2},{2,1},{3,0},{4,7},{5,6},{6,5},{7,4},{8,11},{9,10},{10,... | collective-permute-start | bytes 196616 | tf_op jit(solution)/shard_map/ppermute | solution.py:30
  54.2 4.3 %collective-permute-start.1 = (bf16[2,4,4096]{2,1,0:T(4,128)(2,1)S(1)}, bf16[2,4,4096]{2,1,0:T(4,128)(2,1)S(1)}, u32[]{:S(2)}, u32[]{:S(2)}) collective-permute-start(bf16[2,4,4096]{2,1,0:T(4,128)(2,1)S(1)} %get-tuple-element.36), channel_id=1, source_target_pairs={{0,2},{1,3},{2,0},{3,1},{4,6},{5,7},{6,4},{7,5},{8,10},{9,11},{10,... | collective-permute-start | bytes 196616 | tf_op jit(solution)/shard_map/ppermute | solution.py:30
  54.7 4.4 %collective-permute-start.2 = (bf16[2,4,4096]{2,1,0:T(4,128)(2,1)S(1)}, bf16[2,4,4096]{2,1,0:T(4,128)(2,1)S(1)}, u32[]{:S(2)}, u32[]{:S(2)}) collective-permute-start(bf16[2,4,4096]{2,1,0:T(4,128)(2,1)S(1)} %get-tuple-element.37), channel_id=1, source_target_pairs={{0,1},{1,0},{2,3},{3,2},{4,5},{5,4},{6,7},{7,6},{8,9},{9,8},{10,11... | collective-permute-start | bytes 196616 | tf_op jit(solution)/shard_map/ppermute | solution.py:30
  59.2 6.7 %collective-permute-start.4 = (bf16[2,4,4096]{2,1,0:T(4,128)(2,1)S(1)}, bf16[2,4,4096]{2,1,0:T(4,128)(2,1)S(1)}, u32[]{:S(2)}, u32[]{:S(2)}) collective-permute-start(bf16[2,4,4096]{2,1,0:T(4,128)(2,1)S(1)} %partial.2), channel_id=1, source_target_pairs={{0,12},{1,13},{2,14},{3,15},{4,8},{5,9},{6,10},{7,11},{8,20},{9,21... | collective-permute-start | bytes 196616 | tf_op jit(solution)/shard_map/ppermute | solution.py:30
  59.2 6.6 %collective-permute-start.3 = (bf16[2,4,4096]{2,1,0:T(4,128)(2,1)S(1)}, bf16[2,4,4096]{2,1,0:T(4,128)(2,1)S(1)}, u32[]{:S(2)}, u32[]{:S(2)}) collective-permute-start(bf16[2,4,4096]{2,1,0:T(4,128)(2,1)S(1)} %partial.2), channel_id=1, source_target_pairs={{0,8},{1,9},{2,10},{3,11},{4,12},{5,13},{6,14},{7,15},{8,16},{9,17... | collective-permute-start | bytes 196616 | tf_op jit(solution)/shard_map/ppermute | solution.py:30
  65.9 18.2 %copy-start.14 = (bf16[128,128]{1,0:T(8,128)(2,1)S(1)}, bf16[128,128]{1,0:T(8,128)(2,1)}, u32[]{:S(2)}) copy-start(bf16[128,128]{1,0:T(8,128)(2,1)} %constant.16.clone.order_ref) | copy-start | bytes 98308
  65.9 5.2 %collective-permute-start.7 = (bf16[2,4,4096]{2,1,0:T(4,128)(2,1)S(1)}, bf16[2,4,4096]{2,1,0:T(4,128)(2,1)S(1)}, u32[]{:S(2)}, u32[]{:S(2)}) collective-permute-start(bf16[2,4,4096]{2,1,0:T(4,128)(2,1)S(1)} %join.2.refs_0_), channel_id=1, source_target_pairs={{0,3},{1,2},{2,1},{3,0},{4,7},{5,6},{6,5},{7,4},{8,11},{9,10},{10,... | collective-permute-start | bytes 196616 | tf_op jit(solution)/shard_map/ppermute | solution.py:30
  66.2 5.3 %collective-permute-start.6 = (bf16[2,4,4096]{2,1,0:T(4,128)(2,1)S(1)}, bf16[2,4,4096]{2,1,0:T(4,128)(2,1)S(1)}, u32[]{:S(2)}, u32[]{:S(2)}) collective-permute-start(bf16[2,4,4096]{2,1,0:T(4,128)(2,1)S(1)} %join.2.refs_0_), channel_id=1, source_target_pairs={{0,2},{1,3},{2,0},{3,1},{4,6},{5,7},{6,4},{7,5},{8,10},{9,11},{10,... | collective-permute-start | bytes 196616 | tf_op jit(solution)/shard_map/ppermute | solution.py:30
  68.5 4.3 %collective-permute-start.5 = (bf16[2,4,4096]{2,1,0:T(4,128)(2,1)S(1)}, bf16[2,4,4096]{2,1,0:T(4,128)(2,1)S(1)}, u32[]{:S(2)}, u32[]{:S(2)}) collective-permute-start(bf16[2,4,4096]{2,1,0:T(4,128)(2,1)S(1)} %join.2.refs_0_), channel_id=1, source_target_pairs={{0,1},{1,0},{2,3},{3,2},{4,5},{5,4},{6,7},{7,6},{8,9},{9,8},{10,11... | collective-permute-start | bytes 196616 | tf_op jit(solution)/shard_map/ppermute | solution.py:30
  109.9 5.2 %collective-permute-start.8 = (bf16[2,4,4096]{2,1,0:T(4,128)(2,1)S(1)}, bf16[2,4,4096]{2,1,0:T(4,128)(2,1)S(1)}, u32[]{:S(2)}, u32[]{:S(2)}) collective-permute-start(bf16[2,4,4096]{2,1,0:T(4,128)(2,1)S(1)} %get-tuple-element.42), channel_id=1, source_target_pairs={{0,3},{1,2},{2,1},{3,0},{4,7},{5,6},{6,5},{7,4},{8,11},{9,10},{10,... | collective-permute-start | bytes 196616 | tf_op jit(solution)/shard_map/ppermute | solution.py:30
  110.9 4.3 %collective-permute-start.9 = (bf16[2,4,4096]{2,1,0:T(4,128)(2,1)S(1)}, bf16[2,4,4096]{2,1,0:T(4,128)(2,1)S(1)}, u32[]{:S(2)}, u32[]{:S(2)}) collective-permute-start(bf16[2,4,4096]{2,1,0:T(4,128)(2,1)S(1)} %get-tuple-element.43), channel_id=1, source_target_pairs={{0,2},{1,3},{2,0},{3,1},{4,6},{5,7},{6,4},{7,5},{8,10},{9,11},{10,... | collective-permute-start | bytes 196616 | tf_op jit(solution)/shard_map/ppermute | solution.py:30
  110.9 4.9 %collective-permute-start.10 = (bf16[2,4,4096]{2,1,0:T(4,128)(2,1)S(1)}, bf16[2,4,4096]{2,1,0:T(4,128)(2,1)S(1)}, u32[]{:S(2)}, u32[]{:S(2)}) collective-permute-start(bf16[2,4,4096]{2,1,0:T(4,128)(2,1)S(1)} %get-tuple-element.44), channel_id=1, source_target_pairs={{0,1},{1,0},{2,3},{3,2},{4,5},{5,4},{6,7},{7,6},{8,9},{9,8},{10,11... | collective-permute-start | bytes 196616 | tf_op jit(solution)/shard_map/ppermute | solution.py:30
  115.9 5.5 %collective-permute-start.12 = (bf16[2,4,4096]{2,1,0:T(4,128)(2,1)S(1)}, bf16[2,4,4096]{2,1,0:T(4,128)(2,1)S(1)}, u32[]{:S(2)}, u32[]{:S(2)}) collective-permute-start(bf16[2,4,4096]{2,1,0:T(4,128)(2,1)S(1)} %partial.3), channel_id=1, source_target_pairs={{0,12},{1,13},{2,14},{3,15},{4,8},{5,9},{6,10},{7,11},{8,20},{9,21... | collective-permute-start | bytes 196616 | tf_op jit(solution)/shard_map/ppermute | solution.py:30
  116.0 5.5 %collective-permute-start.11 = (bf16[2,4,4096]{2,1,0:T(4,128)(2,1)S(1)}, bf16[2,4,4096]{2,1,0:T(4,128)(2,1)S(1)}, u32[]{:S(2)}, u32[]{:S(2)}) collective-permute-start(bf16[2,4,4096]{2,1,0:T(4,128)(2,1)S(1)} %partial.3), channel_id=1, source_target_pairs={{0,8},{1,9},{2,10},{3,11},{4,12},{5,13},{6,14},{7,15},{8,16},{9,17... | collective-permute-start | bytes 196616 | tf_op jit(solution)/shard_map/ppermute | solution.py:30
  121.5 5.3 %collective-permute-start.15 = (bf16[2,4,4096]{2,1,0:T(4,128)(2,1)S(1)}, bf16[2,4,4096]{2,1,0:T(4,128)(2,1)S(1)}, u32[]{:S(2)}, u32[]{:S(2)}) collective-permute-start(bf16[2,4,4096]{2,1,0:T(4,128)(2,1)S(1)} %join.3.refs_0_), channel_id=1, source_target_pairs={{0,3},{1,2},{2,1},{3,0},{4,7},{5,6},{6,5},{7,4},{8,11},{9,10},{10,... | collective-permute-start | bytes 196616 | tf_op jit(solution)/shard_map/ppermute | solution.py:30
  122.9 5.1 %collective-permute-start.14 = (bf16[2,4,4096]{2,1,0:T(4,128)(2,1)S(1)}, bf16[2,4,4096]{2,1,0:T(4,128)(2,1)S(1)}, u32[]{:S(2)}, u32[]{:S(2)}) collective-permute-start(bf16[2,4,4096]{2,1,0:T(4,128)(2,1)S(1)} %join.3.refs_0_), channel_id=1, source_target_pairs={{0,2},{1,3},{2,0},{3,1},{4,6},{5,7},{6,4},{7,5},{8,10},{9,11},{10,... | collective-permute-start | bytes 196616 | tf_op jit(solution)/shard_map/ppermute | solution.py:30
  125.1 4.3 %collective-permute-start.13 = (bf16[2,4,4096]{2,1,0:T(4,128)(2,1)S(1)}, bf16[2,4,4096]{2,1,0:T(4,128)(2,1)S(1)}, u32[]{:S(2)}, u32[]{:S(2)}) collective-permute-start(bf16[2,4,4096]{2,1,0:T(4,128)(2,1)S(1)} %join.3.refs_0_), channel_id=1, source_target_pairs={{0,1},{1,0},{2,3},{3,2},{4,5},{5,4},{6,7},{7,6},{8,9},{9,8},{10,11... | collective-permute-start | bytes 196616 | tf_op jit(solution)/shard_map/ppermute | solution.py:30

commit v9 on v8

--- a/solution.py
+++ b/solution.py
@@ -50,7 +50,7 @@
     return pl.BlockSpec(memory_space=memory_space)
 
 
-def call(kernel, out, operands, specs, scratch, name, cost):
+def call(kernel, out, operands, specs, scratch, name, cost, exchange=EXCHANGE):
     single = not isinstance(out, tuple)
     return pl.pallas_call(
         kernel,
@@ -59,7 +59,7 @@
         out_specs=whole() if single else tuple(whole() for _ in out),
         scratch_shapes=scratch,
         compiler_params=pltpu.CompilerParams(vmem_limit_bytes=LIMIT),
-        cost_estimate=pl.CostEstimate(flops=cost[0] + EXCHANGE, bytes_accessed=cost[1], transcendentals=0),
+        cost_estimate=pl.CostEstimate(flops=cost[0] + exchange, bytes_accessed=cost[1], transcendentals=0),
         name=name,
     )(*operands)
 
@@ -120,10 +120,9 @@
     query_kernel(head_dim, x_ref, gain_ref, w_ref, q_ref, states, spread)
 
 
-def query_kernel(head_dim, x_ref, gain_ref, w_ref, q_ref, states, spread):
+def head_queries(head_dim, x_ref, gain_ref, w_ref, states):
     devices, own, _ = x_ref.shape
     rows, (width, columns) = devices * own, w_ref.shape
-    heads = columns // head_dim
     chunk = 512
     totals, squares = {}, jnp.zeros((rows, 128), F32)
     for start in range(0, width, chunk):
@@ -134,12 +133,111 @@
         squares = add_squares(squares, values)
         add_tiles(totals, (values * gain_ref[:, at].astype(F32)).astype(BF16), w_ref, at, head_dim)
     scale = lax.rsqrt(jnp.sum(squares, axis=-1, keepdims=True) / width + EPS)
-    for h in range(heads):
+    queries = []
+    for h in range(columns // head_dim):
         one = totals[head_dim * h] * scale
-        norm = lax.rsqrt(jnp.mean(one * one, axis=-1, keepdims=True) + EPS)
-        spread[pl.ds(h, rows, stride=heads), :] = one * norm
+        queries.append(one * lax.rsqrt(jnp.mean(one * one, axis=-1, keepdims=True) + EPS))
+    return queries
+
+
+def query_kernel(head_dim, x_ref, gain_ref, w_ref, q_ref, states, spread):
+    queries = head_queries(head_dim, x_ref, gain_ref, w_ref, states)
+    for h, one in enumerate(queries):
+        spread[pl.ds(h, one.shape[0], stride=len(queries)), :] = one
     if q_ref is not None:
         q_ref[...] = spread[...].astype(BF16)
+
+
+def halves_kernel(head_dim, low, me_ref, *refs):
+    pieces, refs = refs[:low], refs[low:]
+    (gain_ref, w_ref), outs, (states, x_ref, spread) = refs[:2], refs[2:2 + low], refs[2 + low:]
+    me = me_ref[0]
+    for l, piece in enumerate(pieces):
+        for h in range(piece.shape[0]):
+            x_ref[me ^ (l + h * low)] = piece[h]
+    devices, own, _ = x_ref.shape
+    for h, one in enumerate(head_queries(head_dim, x_ref, gain_ref, w_ref, states)):
+        for i in range(devices):
+            spread[i, own * h:own * (h + 1), :] = one[own * i:own * (i + 1), :]
+    for l, out in enumerate(outs):
+        for g in range(out.shape[0]):
+            out[g] = spread[(me % low ^ l) + g * low].astype(BF16)
+
+
+def cache_kernel(own, kv_heads, me_ref, len_ref, k_ref, v_ref, *refs):
+    *blocks, wide = refs
+    half = kv_heads // 2
+    first = jnp.where(me_ref[0] >= kv_heads, 0, half)
+    span = k_ref.shape[1] // kv_heads
+    cache = span // own
+    line = lax.broadcasted_iota(jnp.int32, (EXTRA, LANES), 0)
+    place = lax.broadcasted_iota(jnp.int32, (EXTRA, LANES), 1) + line * LANES
+    for step, block in enumerate(blocks, 1):
+        at = 0
+        for ref in (k_ref, v_ref):
+            wide[...] = ref[step].astype(F32)
+            for j in range(half):
+                block[at:at + span, :] = wide[pl.ds(first + j, span, stride=kv_heads), :].astype(BF16)
+                at += span
+        valid = jnp.zeros((EXTRA, LANES), F32)
+        for r in range(own):
+            inside = (place >= r * cache) & (place < r * cache + len_ref[step, :, r:r + 1])
+            valid = jnp.where(inside, 1.0, valid)
+        block[at:, :] = valid.astype(BF16)
+
+
+def softmax_times(scores, valid, head_dim, values):
+    exps = jnp.where(valid, jnp.exp2(scores * (head_dim ** (-0.5) * LOG2E)), 0.0)
+    context = jnp.dot(exps.astype(BF16), values, preferred_element_type=F32)
+    return context * (1.0 / jnp.sum(exps, axis=-1, keepdims=True))
+
+
+def products(queries, keys):
+    return lax.dot_general(queries, keys, (((1,), (1,)), ((), ())), preferred_element_type=F32)
+
+
+def half_attention_kernel(step, own, kv_heads, me_ref, *refs):
+    low = len(refs) - 6
+    pieces, (k_ref, v_ref, len_ref, pair_ref, c_ref, q_ref) = refs[:low], refs[low:]
+    me = me_ref[0]
+    mine = jnp.where(me >= low, 1, 0)
+    half = kv_heads // 2
+    count, head_dim = pieces[0].shape[1:]
+    for l, piece in enumerate(pieces):
+        for g in range(2):
+            q_ref[g, me % low ^ l] = piece[g]
+    rows = low * count
+    span = k_ref.shape[1] // kv_heads
+    cache = span // own
+    q = q_ref[mine].reshape(rows, head_dim)
+    line = lax.broadcasted_iota(jnp.int32, (rows, 1), 0)
+    place = lax.broadcasted_iota(jnp.int32, (1, span * kv_heads), 1)
+    of_row = place // (cache * kv_heads)
+    length = jnp.zeros(place.shape, jnp.int32)
+    for r in range(own):
+        length = jnp.where(of_row == r, len_ref[step, :, r:r + 1], length)
+    key_of = jnp.where(place // kv_heads % cache < length, of_row * kv_heads + place % kv_heads, -1)
+    key_for = line % own * kv_heads + line // (rows // half) + half * mine
+    scores = products(q, k_ref[step])
+    other = q_ref[1 - mine].reshape(rows, head_dim)
+    part = rows // half
+    ends = pair_ref[2 * half * span:, :].astype(F32)
+    valid = jnp.concatenate([ends[g:g + 1, :] for g in range(span // LANES)], axis=1) > 0.0
+    line = lax.broadcasted_iota(jnp.int32, (part, 1), 0)
+    place = lax.broadcasted_iota(jnp.int32, (1, span), 1)
+    theirs = (line % own == place // cache) & valid
+    others = [products(other[part * j:part * (j + 1), :], pair_ref[span * j:span * (j + 1), :]) for j in range(half)]
+    own_context = softmax_times(scores, key_of == key_for, head_dim, v_ref[step])
+    contexts = [
+        softmax_times(others[j], theirs, head_dim, pair_ref[span * (half + j):span * (half + j + 1), :])
+        for j in range(half)
+    ]
+    heads = part // own
+    for h in range(rows // own):
+        at = slice(head_dim * h, head_dim * (h + 1))
+        c_ref[mine, :, at] = own_context[own * h:own * (h + 1), :].astype(BF16)
+        j, inside = h // heads, h % heads
+        c_ref[1 - mine, :, at] = contexts[j][own * inside:own * (inside + 1), :].astype(BF16)
 
 
 def first_attention_kernel(own, pick_ref, q_ref, *refs):
@@ -206,6 +304,22 @@
         at = slice(start, start + chunk)
         for i in range(devices):
             lines[own * i:own * (i + 1), at] = c_ref[i, :, at].astype(F32)
+        add_tiles(totals, lines[:, at].astype(BF16), w_ref, at)
+    for at, total in totals.items():
+        columns = total.astype(BF16)
+        for i in range(devices):
+            o_ref[i, :, at:at + columns.shape[1]] = columns
+
+
+def half_out_kernel(c_ref, w_ref, o_ref, lines):
+    devices, slots, own, part = c_ref.shape
+    low = devices // slots
+    chunk, totals = 512, {}
+    for start in range(0, slots * part, chunk):
+        at = slice(start, start + chunk)
+        half, inside = start // part, slice(start % part, start % part + chunk)
+        for i in range(devices):
+            lines[own * i:own * (i + 1), at] = c_ref[half * low + i % low, i // low, :, inside].astype(F32)
         add_tiles(totals, lines[:, at].astype(BF16), w_ref, at)
     for at, total in totals.items():
         columns = total.astype(BF16)
@@ -320,6 +434,7 @@
     lengths = lengths.reshape(STEPS, 1, own)
     tables, first_tables, pick = attention_tables(own, heads, local_heads, kv_heads, cache_len)
     low, high = split(devices)
+    by_half = high == 2 and devices == 2 * kv_heads
     smem = whole(pltpu.SMEM)
     q_shape = jax.ShapeDtypeStruct((rows * local_heads, head_dim), BF16)
     x_shape = jax.ShapeDtypeStruct((devices, own, width), BF16)
@@ -336,6 +451,19 @@
         (0, 2 * rows * width),
     )
     me, copies = lax.optimization_barrier((me, copies))
+    if by_half:
+        block = jax.ShapeDtypeStruct((2 * places // 2 + EXTRA, head_dim), BF16)
+        others = call(
+            functools.partial(cache_kernel, own, kv_heads),
+            (block,) * (STEPS - 1),
+            (me, lengths, keys, values),
+            [smem] + [whole()] * 3,
+            [pltpu.VMEM((places, head_dim), F32)],
+            "caches_of_other_half",
+            (places * head_dim, 8 * places * head_dim),
+            0,
+        )
+        others = [shifted(one, low) for one in others]
     for step in range(STEPS):
         spread = pltpu.VMEM((rows * local_heads, head_dim), F32)
         cost = (2 * rows * width * part, 2 * width * part)
@@ -351,42 +479,65 @@
             )
         else:
             pieces = [state] + [shifted(state, l) for l in range(1, low)]
-            own_q, states = call(
-                functools.partial(order_kernel, head_dim, low),
-                (q_shape, states_shape),
-                (me, *pieces, attn_gain, query_w),
-                [smem] + [whole()] * (low + 2),
-                [pltpu.VMEM((devices, own, width), BF16), spread],
-                "order_query",
+            if by_half:
+                *queries, states = call(
+                    functools.partial(halves_kernel, head_dim, low),
+                    (jax.ShapeDtypeStruct((2, own * local_heads, head_dim), BF16),) * low + (states_shape,),
+                    (me, *pieces, attn_gain, query_w),
+                    [smem] + [whole()] * (low + 2),
+                    [pltpu.VMEM((devices, own, width), BF16), pltpu.VMEM((devices, own * local_heads, head_dim), F32)],
+                    "queries_by_half",
+                    cost,
+                )
+                queries = [queries[0]] + [shifted(queries[l], l) for l in range(1, low)]
+            else:
+                own_q, states = call(
+                    functools.partial(order_kernel, head_dim, low),
+                    (q_shape, states_shape),
+                    (me, *pieces, attn_gain, query_w),
+                    [smem] + [whole()] * (low + 2),
+                    [pltpu.VMEM((devices, own, width), BF16), spread],
+                    "order_query",
+                    cost,
+                )
+        if step and by_half:
+            context = call(
+                functools.partial(half_attention_kernel, step, own, kv_heads),
+                jax.ShapeDtypeStruct((2, own, heads * head_dim // 2), BF16),
+                (me, *queries, keys, values, lengths, others[step - 1]),
+                [smem] + [whole()] * (low + 4),
+                [pltpu.VMEM((2, low, own * local_heads, head_dim), BF16)],
+                "half_attention",
                 cost,
             )
-        c_shape = jax.ShapeDtypeStruct((own, heads * head_dim), BF16)
-        by_row = [pltpu.VMEM((own * heads, head_dim), F32)]
-        cost = (4 * own * heads * places * head_dim, 4 * places * head_dim)
-        queries = swapped(own_q.reshape(devices, -1, head_dim)).reshape(-1, head_dim)
-        if step == 0:
-            context, shares = call(
-                functools.partial(first_attention_kernel, own),
-                (c_shape, jax.ShapeDtypeStruct((rows, LANES), F32)),
-                (pick, queries, keys, values, lengths, *first_tables),
-                [whole()] * 8,
-                by_row,
-                "first_attention",
-                cost,
-            )
         else:
-            context = call(
-                functools.partial(attention_kernel, step, own),
-                c_shape,
-                (queries, keys, values, lengths, *tables),
-                [whole()] * 7,
-                by_row,
-                "attention",
-                cost,
-            )
+            c_shape = jax.ShapeDtypeStruct((own, heads * head_dim), BF16)
+            by_row = [pltpu.VMEM((own * heads, head_dim), F32)]
+            cost = (4 * own * heads * places * head_dim, 4 * places * head_dim)
+            queries = swapped(own_q.reshape(devices, -1, head_dim)).reshape(-1, head_dim)
+            if step == 0:
+                context, shares = call(
+                    functools.partial(first_attention_kernel, own),
+                    (c_shape, jax.ShapeDtypeStruct((rows, LANES), F32)),
+                    (pick, queries, keys, values, lengths, *first_tables),
+                    [whole()] * 8,
+                    by_row,
+                    "first_attention",
+                    cost,
+                )
+            else:
+                context = call(
+                    functools.partial(attention_kernel, step, own),
+                    c_shape,
+                    (queries, keys, values, lengths, *tables),
+                    [whole()] * 7,
+                    by_row,
+                    "attention",
+                    cost,
+                )
         contexts = everyones(context)
         columns = call(
-            out_kernel,
+            half_out_kernel if step and by_half else out_kernel,
             jax.ShapeDtypeStruct((devices, rows, part), BF16),
             (contexts, out_w),
             [whole()] * 2,
@@ -428,6 +579,8 @@
                 (rows * width, 4 * rows * width),
             )
             parts = [shifted(part_sums, h * low, 1) for h in range(high)]
+            if by_half:
+                parts[0], others[step] = lax.optimization_barrier((parts[0], others[step]))
             state = call(
                 join_kernel, slots, tuple(parts), [whole()] * high, [], "join", (rows * width, 4 * rows * width)
             )

time: 176 us -> 174 us (0.989)
  blocking collectives: 123 us -> 105 us
  starting transfers between devices: 16.1 us -> 25 us
  waiting for transfers between devices: 22.8 us -> 31 us
    all_to_all x11 -> x9, blocking collectives: 123 us -> 105 us  [swapped(): lax.all_to_all(blocks, 'expert', split_axis=0, concat_axis=0, tiled=True)]
    ppermute x16 -> x24, starting transfers between devices: 16.1 us -> 25 us  [shifted(): return lax.ppermute(array, ('section', 'expert'), pairs)]
    ppermute x16 -> x24, waiting for transfers between devices: 22.8 us -> 31 us  [shifted(): return lax.ppermute(array, ('section', 'expert'), pairs)]
    pallas_call x18 -> x19, Pallas kernels: 11.6 us -> 11.5 us  [call(): pl.pallas_call(kernel, out_shape=out, in_specs=specs, out_specs=whole() i...]
  transfers between devices with their start and end apart: 16 -> 24, of which waited for: 12 -> 16; matrix products, arithmetic and copies ran while one was open for 0% -> 0% of each run, Pallas kernels for 0% -> 0%
where the time goes in v9:
time: 174 us
  blocking collectives  105 us (60%)
  waiting for transfers between devices  31 us (18%)
  starting transfers between devices  25 us (14%)
  Pallas kernels  11.5 us (7%)
    all_to_all x9, blocking collectives, swapped(): lax.all_to_all(blocks, 'expert', split_axis=0, concat_axis=0, tiled=True)  105 us
    ppermute x24, waiting for transfers between devices, shifted(): return lax.ppermute(array, ('section', 'expert'), pairs)  31 us
    ppermute x24, starting transfers between devices, shifted(): return lax.ppermute(array, ('section', 'expert'), pairs)  25 us
    pallas_call x19, Pallas kernels, call(): pl.pallas_call(kernel, out_shape=out, in_specs=specs, out_specs=whole() i...  11.5 us
  transfers between devices with their start and end apart: 24, of which 16 were waited for; matrix products, arithmetic and copies ran while one was open for 0% of the time, Pallas kernels for 0%

profile of v9, /device:TPU:0, one launch (start us, length us, event | category | flops | bytes accessed | tf_op | source)
XLA Modules:
  0.0 173.9 jit_solution(328731909673462245)
XLA Ops:
  0.0 0.8 copy-done.8
  0.8 16.3 %all_to_all.45.x_ref = bf16[8,4,4096]{2,1,0:T(4,128)(2,1)S(1)} all-to-all(bf16[8,4,4096]{2,1,0:T(4,128)(2,1)S(1)} %spread.1), channel_id=1, replica_groups=mesh['section'=4,'expert'=8] {'expert'}, dimensions={0} | all-to-all | bytes 524288 | tf_op jit(solution)/shard_map/all_to_all | solution.py:41
  17.2 0.8 first_query.1
  18.0 10.3 %all_to_all.46 = bf16[8,32,128]{2,1,0:T(8,128)(2,1)S(1)} all-to-all(bf16[8,32,128]{2,1,0:T(8,128)(2,1)S(1)} %get-tuple-element.41), channel_id=1, replica_groups=mesh['section'=4,'expert'=8] {'expert'}, dimensions={0} | all-to-all | bytes 131072 | tf_op jit(solution)/shard_map/all_to_all | solution.py:41
  28.4 0.5 first_attention.1
  28.8 0.1 broadcast_in_dim.8
  28.9 10.8 %all_to_all.47.c_ref = bf16[8,4,4096]{2,1,0:T(4,128)(2,1)S(1)} all-to-all(bf16[8,4,4096]{2,1,0:T(4,128)(2,1)S(1)} %broadcast_in_dim.8), channel_id=1, replica_groups=mesh['section'=4,'expert'=8] {'expert'}, dimensions={0} | all-to-all | bytes 524288 | tf_op jit(solution)/shard_map/all_to_all | solution.py:41
  39.7 0.7 attention_out.3
  40.4 11.2 %all_to_all.48.refs_0_ = bf16[8,32,512]{2,1,0:T(8,128)(2,1)S(1)} all-to-all(bf16[8,32,512]{2,1,0:T(8,128)(2,1)S(1)} %attention_out.3), channel_id=1, replica_groups=mesh['section'=4,'expert'=8] {'expert'}, dimensions={0} | all-to-all | bytes 524288 | tf_op jit(solution)/shard_map/all_to_all | solution.py:41
  51.6 1.5 experts_sending.2
  53.1 1.0 collective-permute-start
  54.1 0.6 collective-permute-start.1
  54.7 2.0 %collective-permute-start.2 = (bf16[2,4,4096]{2,1,0:T(4,128)(2,1)S(1)}, bf16[2,4,4096]{2,1,0:T(4,128)(2,1)S(1)}, u32[]{:S(2)}, u32[]{:S(2)}) collective-permute-start(bf16[2,4,4096]{2,1,0:T(4,128)(2,1)S(1)} %get-tuple-element.49), channel_id=1, source_target_pairs={{0,1},{1,0},{2,3},{3,2},{4,5},{5,4},{6,7},{7,6},{8,9},{9,8},{10,11... | collective-permute-start | bytes 196616 | tf_op jit(solution)/shard_map/ppermute | solution.py:30
  56.7 0.3 caches_of_other_half.1
  57.0 0.6 collective-permute-start.4
  57.6 1.3 collective-permute-done.refs_1_
  58.9 0.4 collective-permute-done.2.refs_3_
  59.3 0.1 collective-permute-start.3
  59.4 2.0 %collective-permute-start.5 = (bf16[2,4,4096]{2,1,0:T(4,128)(2,1)S(1)}, bf16[2,4,4096]{2,1,0:T(4,128)(2,1)S(1)}, u32[]{:S(2)}, u32[]{:S(2)}) collective-permute-start(bf16[2,4,4096]{2,1,0:T(4,128)(2,1)S(1)} %partial.2), channel_id=1, source_target_pairs={{0,12},{1,13},{2,14},{3,15},{4,8},{5,9},{6,10},{7,11},{8,20},{9,21... | collective-permute-start | bytes 196616 | tf_op jit(solution)/shard_map/ppermute | solution.py:30
  61.4 7.4 %collective-permute-done.4.refs_7_ = bf16[1040,128]{1,0:T(8,128)(2,1)S(1)} collective-permute-done((bf16[1040,128]{1,0:T(8,128)(2,1)S(1)}, bf16[1040,128]{1,0:T(8,128)(2,1)S(1)}, u32[]{:S(2)}, u32[]{:S(2)}) %collective-permute-start.4) | collective-permute-done | bytes 266272 | tf_op jit(solution)/shard_map/ppermute | solution.py:30
  68.8 0.1 collective-permute-start.8
  68.9 2.4 %collective-permute-start.7 = (bf16[2,4,4096]{2,1,0:T(4,128)(2,1)S(1)}, bf16[2,4,4096]{2,1,0:T(4,128)(2,1)S(1)}, u32[]{:S(2)}, u32[]{:S(2)}) collective-permute-start(bf16[2,4,4096]{2,1,0:T(4,128)(2,1)S(1)} %join.2.refs_0_), channel_id=1, source_target_pairs={{0,2},{1,3},{2,0},{3,1},{4,6},{5,7},{6,4},{7,5},{8,10},{9,11},{10,... | collective-permute-start | bytes 196616 | tf_op jit(solution)/shard_map/ppermute | solution.py:30
  71.3 1.1 collective-permute-start.6
  72.4 2.3 %collective-permute-done.8.refs_3_ = bf16[2,4,4096]{2,1,0:T(4,128)(2,1)S(1)} collective-permute-done((bf16[2,4,4096]{2,1,0:T(4,128)(2,1)S(1)}, bf16[2,4,4096]{2,1,0:T(4,128)(2,1)S(1)}, u32[]{:S(2)}, u32[]{:S(2)}) %collective-permute-start.8) | collective-permute-done | bytes 65568 | tf_op jit(solution)/shard_map/ppermute | solution.py:30
  74.6 0.1 collective-permute-done.7.refs_2_
  74.8 0.9 collective-permute-done.6.refs_1_
  75.7 0.8 queries_by_half.2
  76.5 1.1 collective-permute-start.9
  77.6 2.5 %collective-permute-start.11 = (bf16[2,16,128]{2,1,0:T(8,128)(2,1)S(1)}, bf16[2,16,128]{2,1,0:T(8,128)(2,1)S(1)}, u32[]{:S(2)}, u32[]{:S(2)}) collective-permute-start(bf16[2,16,128]{2,1,0:T(8,128)(2,1)S(1)} %get-tuple-element.55), channel_id=1, source_target_pairs={{0,3},{1,2},{2,1},{3,0},{4,7},{5,6},{6,5},{7,4},{8,11},{9,10},{10,... | collective-permute-start | bytes 24584 | tf_op jit(solution)/shard_map/ppermute | solution.py:30
  80.1 0.2 collective-permute-done.9.refs_1_
  80.2 1.0 collective-permute-done.10.refs_2_
  81.2 0.9 collective-permute-done.11.refs_3_
  82.1 0.4 half_attention.2
  82.5 0.1 broadcast_in_dim.9
  82.6 12.0 %all_to_all.49.c_ref = bf16[8,2,4,2048]{3,2,1,0:T(4,128)(2,1)S(1)} all-to-all(bf16[8,2,4,2048]{3,2,1,0:T(4,128)(2,1)S(1)} %broadcast_in_dim.9), channel_id=1, replica_groups=mesh['section'=4,'expert'=8] {'expert'}, dimensions={0} | all-to-all | bytes 524288 | tf_op jit(solution)/shard_map/all_to_all | solution.py:41
  94.6 0.7 attention_out.4
  95.3 10.9 %all_to_all.50.refs_0_ = bf16[8,32,512]{2,1,0:T(8,128)(2,1)S(1)} all-to-all(bf16[8,32,512]{2,1,0:T(8,128)(2,1)S(1)} %attention_out.4), channel_id=1, replica_groups=mesh['section'=4,'expert'=8] {'expert'}, dimensions={0} | all-to-all | bytes 524288 | tf_op jit(solution)/shard_map/all_to_all | solution.py:41
  106.2 1.5 experts_sending.3
  107.8 1.2 collective-permute-start.12
  108.9 0.4 collective-permute-start.13
  109.3 2.0 %collective-permute-start.14 = (bf16[2,4,4096]{2,1,0:T(4,128)(2,1)S(1)}, bf16[2,4,4096]{2,1,0:T(4,128)(2,1)S(1)}, u32[]{:S(2)}, u32[]{:S(2)}) collective-permute-start(bf16[2,4,4096]{2,1,0:T(4,128)(2,1)S(1)} %get-tuple-element.62), channel_id=1, source_target_pairs={{0,1},{1,0},{2,3},{3,2},{4,5},{5,4},{6,7},{7,6},{8,9},{9,8},{10,11... | collective-permute-start | bytes 196616 | tf_op jit(solution)/shard_map/ppermute | solution.py:30
  111.3 0.6 collective-permute-start.16
  111.9 3.2 %collective-permute-done.12.refs_1_ = bf16[2,4,4096]{2,1,0:T(4,128)(2,1)S(1)} collective-permute-done((bf16[2,4,4096]{2,1,0:T(4,128)(2,1)S(1)}, bf16[2,4,4096]{2,1,0:T(4,128)(2,1)S(1)}, u32[]{:S(2)}, u32[]{:S(2)}) %collective-permute-start.12) | collective-permute-done | bytes 65568 | tf_op jit(solution)/shard_map/ppermute | solution.py:30
  115.2 0.4 collective-permute-start.17
  115.7 7.9 %collective-permute-done.16.refs_7_ = bf16[1040,128]{1,0:T(8,128)(2,1)S(1)} collective-permute-done((bf16[1040,128]{1,0:T(8,128)(2,1)S(1)}, bf16[1040,128]{1,0:T(8,128)(2,1)S(1)}, u32[]{:S(2)}, u32[]{:S(2)}) %collective-permute-start.16) | collective-permute-done | bytes 266272 | tf_op jit(solution)/shard_map/ppermute | solution.py:30
  123.6 0.1 collective-permute-start.20
  123.7 2.3 %collective-permute-start.19 = (bf16[2,4,4096]{2,1,0:T(4,128)(2,1)S(1)}, bf16[2,4,4096]{2,1,0:T(4,128)(2,1)S(1)}, u32[]{:S(2)}, u32[]{:S(2)}) collective-permute-start(bf16[2,4,4096]{2,1,0:T(4,128)(2,1)S(1)} %join.3.refs_0_), channel_id=1, source_target_pairs={{0,2},{1,3},{2,0},{3,1},{4,6},{5,7},{6,4},{7,5},{8,10},{9,11},{10,... | collective-permute-start | bytes 196616 | tf_op jit(solution)/shard_map/ppermute | solution.py:30
  126.0 1.2 collective-permute-start.18
  127.2 2.3 %collective-permute-done.20.refs_3_ = bf16[2,4,4096]{2,1,0:T(4,128)(2,1)S(1)} collective-permute-done((bf16[2,4,4096]{2,1,0:T(4,128)(2,1)S(1)}, bf16[2,4,4096]{2,1,0:T(4,128)(2,1)S(1)}, u32[]{:S(2)}, u32[]{:S(2)}) %collective-permute-start.20) | collective-permute-done | bytes 65568 | tf_op jit(solution)/shard_map/ppermute | solution.py:30
  129.5 1.0 collective-permute-done.18.refs_1_
  130.5 0.8 queries_by_half.3
  131.4 1.0 collective-permute-start.21
  132.4 2.5 %collective-permute-start.23 = (bf16[2,16,128]{2,1,0:T(8,128)(2,1)S(1)}, bf16[2,16,128]{2,1,0:T(8,128)(2,1)S(1)}, u32[]{:S(2)}, u32[]{:S(2)}) collective-permute-start(bf16[2,16,128]{2,1,0:T(8,128)(2,1)S(1)} %get-tuple-element.68), channel_id=1, source_target_pairs={{0,3},{1,2},{2,1},{3,0},{4,7},{5,6},{6,5},{7,4},{8,11},{9,10},{10,... | collective-permute-start | bytes 24584 | tf_op jit(solution)/shard_map/ppermute | solution.py:30
  134.9 0.2 collective-permute-done.21.refs_1_
  135.1 1.0 collective-permute-done.22.refs_2_
  136.0 0.9 collective-permute-done.23.refs_3_
  136.9 0.4 half_attention.3
  137.3 0.1 broadcast_in_dim.10
  137.4 11.8 %all_to_all.51.c_ref = bf16[8,2,4,2048]{3,2,1,0:T(4,128)(2,1)S(1)} all-to-all(bf16[8,2,4,2048]{3,2,1,0:T(4,128)(2,1)S(1)} %broadcast_in_dim.10), channel_id=1, replica_groups=mesh['section'=4,'expert'=8] {'expert'}, dimensions={0} | all-to-all | bytes 524288 | tf_op jit(solution)/shard_map/all_to_all | solution.py:41
  149.3 0.7 attention_out.5
  150.0 10.9 %all_to_all.52.a_ref = bf16[8,32,512]{2,1,0:T(8,128)(2,1)S(1)} all-to-all(bf16[8,32,512]{2,1,0:T(8,128)(2,1)S(1)} %attention_out.5), channel_id=1, replica_groups=mesh['section'=4,'expert'=8] {'expert'}, dimensions={0} | all-to-all | bytes 524288 | tf_op jit(solution)/shard_map/all_to_all | solution.py:41
  160.9 1.5 experts.1
  162.4 10.9 %all_to_all.53.r_ref = bf16[8,4,4096]{2,1,0:T(4,128)(2,1)S(1)} all-to-all(bf16[8,4,4096]{2,1,0:T(4,128)(2,1)S(1)} %get-tuple-element.71), channel_id=1, replica_groups=mesh['section'=4,'expert'=8] {'expert'}, dimensions={0} | all-to-all | bytes 524288 | tf_op jit(solution)/shard_map/all_to_all | solution.py:41
  173.3 0.7 combine.1
  (49 shorter events, 0.4 us)
Async XLA Ops:
  0.0 0.8 copy-start.8
  0.8 16.3 %copy-start.3 = (bf16[1,4096,512]{2,1,0:T(8,128)(2,1)S(1)}, bf16[1,4096,512]{2,1,0:T(8,128)(2,1)}, u32[]{:S(2)}) copy-start(bf16[1,4096,512]{2,1,0:T(8,128)(2,1)} %param.19) | copy-start | bytes 12582916
  0.8 16.3 %copy-start.9 = (bf16[1,4096]{1,0:T(2,128)(2,1)S(1)}, bf16[1,4096]{1,0:T(2,128)(2,1)}, u32[]{:S(2)}) copy-start(bf16[1,4096]{1,0:T(2,128)(2,1)} %refs_4_.4) | copy-start | bytes 24580
  0.8 16.3 %copy-start.11 = (s32[1,3,4,2]{2,3,1,0:T(2,128)S(1)}, s32[1,3,4,2]{2,3,1,0:T(2,128)}, u32[]{:S(2)}) copy-start(s32[1,3,4,2]{2,3,1,0:T(2,128)} %param.28) | copy-start | bytes 292
  0.8 16.3 %copy-start.12 = (f32[1,3,4,2]{2,3,1,0:T(2,128)S(1)}, f32[1,3,4,2]{2,3,1,0:T(2,128)}, u32[]{:S(2)}) copy-start(f32[1,3,4,2]{2,3,1,0:T(2,128)} %param.29) | copy-start | bytes 292
  17.1 11.2 %copy-start = (bf16[1,3,4,64,4,128]{5,4,3,2,1,0:T(4,128)(2,1)S(1)}, bf16[1,3,4,64,4,128]{5,4,3,2,1,0:T(4,128)(2,1)}, u32[]{:S(2)}) copy-start(bf16[1,3,4,64,4,128]{5,4,3,2,1,0:T(4,128)(2,1)} %param.21) | copy-start | bytes 2359300
  17.1 11.2 %copy-start.1 = (bf16[1,3,4,64,4,128]{5,4,3,2,1,0:T(4,128)(2,1)S(1)}, bf16[1,3,4,64,4,128]{5,4,3,2,1,0:T(4,128)(2,1)}, u32[]{:S(2)}) copy-start(bf16[1,3,4,64,4,128]{5,4,3,2,1,0:T(4,128)(2,1)} %param.22) | copy-start | bytes 2359300
  17.1 11.2 %copy-start.2 = (s32[1,3,4]{2,0,1:T(1,128)S(1)}, s32[1,3,4]{2,0,1:T(1,128)}, u32[]{:S(2)}) copy-start(s32[1,3,4]{2,0,1:T(1,128)} %param.23) | copy-start | bytes 148
  17.1 11.2 %copy-start.13 = (bf16[128,256]{1,0:T(8,128)(2,1)S(1)}, bf16[128,256]{1,0:T(8,128)(2,1)}, u32[]{:S(2)}) copy-start(bf16[128,256]{1,0:T(8,128)(2,1)} %constant.14.clone.refs_3_) | copy-start | bytes 196612
  17.1 11.2 %copy-start.14 = (bf16[32,256]{1,0:T(8,128)(2,1)S(1)}, bf16[32,256]{1,0:T(8,128)(2,1)}, u32[]{:S(2)}) copy-start(bf16[32,256]{1,0:T(8,128)(2,1)} %constant.15.clone.pick_ref) | copy-start | bytes 49156
  17.1 11.2 %copy-start.15 = (s32[32,1]{1,0:T(8,128)S(1)}, s32[32,1]{1,0:T(8,128)}, u32[]{:S(2)}) copy-start(s32[32,1]{1,0:T(8,128)} %constant.12.clone.refs_4_) | copy-start | bytes 388
  17.2 11.2 %copy-start.16 = (s32[8,256]{1,0:T(8,128)S(1)}, s32[8,256]{1,0:T(8,128)}, u32[]{:S(2)}) copy-start(s32[8,256]{1,0:T(8,128)} %constant.13.clone.refs_5_) | copy-start | bytes 24580
  28.3 11.3 %copy-start.4 = (bf16[1,4096,512]{2,1,0:T(8,128)(2,1)S(1)}, bf16[1,4096,512]{2,1,0:T(8,128)(2,1)}, u32[]{:S(2)}) copy-start(bf16[1,4096,512]{2,1,0:T(8,128)(2,1)} %param.20) | copy-start | bytes 12582916
  39.7 11.9 %copy-start.5 = (bf16[1,1,4096,384]{3,2,1,0:T(8,128)(2,1)S(1)}, bf16[1,1,4096,384]{3,2,1,0:T(8,128)(2,1)}, u32[]{:S(2)}) copy-start(bf16[1,1,4096,384]{3,2,1,0:T(8,128)(2,1)} %param.25) | copy-start | bytes 9437188
  39.7 11.9 %copy-start.6 = (bf16[1,1,4096,384]{3,2,1,0:T(8,128)(2,1)S(1)}, bf16[1,1,4096,384]{3,2,1,0:T(8,128)(2,1)}, u32[]{:S(2)}) copy-start(bf16[1,1,4096,384]{3,2,1,0:T(8,128)(2,1)} %param.26) | copy-start | bytes 9437188
  39.7 11.9 %copy-start.7 = (bf16[1,1,384,4096]{3,2,1,0:T(8,128)(2,1)S(1)}, bf16[1,1,384,4096]{3,2,1,0:T(8,128)(2,1)}, u32[]{:S(2)}) copy-start(bf16[1,1,384,4096]{3,2,1,0:T(8,128)(2,1)} %param.27) | copy-start | bytes 9437188
  39.7 11.9 %copy-start.10 = (bf16[1,4096]{1,0:T(2,128)(2,1)S(1)}, bf16[1,4096]{1,0:T(2,128)(2,1)}, u32[]{:S(2)}) copy-start(bf16[1,4096]{1,0:T(2,128)(2,1)} %gain_ref.3) | copy-start | bytes 24580
  53.1 5.7 %collective-permute-start = (bf16[2,4,4096]{2,1,0:T(4,128)(2,1)S(1)}, bf16[2,4,4096]{2,1,0:T(4,128)(2,1)S(1)}, u32[]{:S(2)}, u32[]{:S(2)}) collective-permute-start(bf16[2,4,4096]{2,1,0:T(4,128)(2,1)S(1)} %get-tuple-element.47), channel_id=1, source_target_pairs={{0,3},{1,2},{2,1},{3,0},{4,7},{5,6},{6,5},{7,4},{8,11},{9,10},{10,... | collective-permute-start | bytes 196616 | tf_op jit(solution)/shard_map/ppermute | solution.py:30
  54.1 4.8 %collective-permute-start.1 = (bf16[2,4,4096]{2,1,0:T(4,128)(2,1)S(1)}, bf16[2,4,4096]{2,1,0:T(4,128)(2,1)S(1)}, u32[]{:S(2)}, u32[]{:S(2)}) collective-permute-start(bf16[2,4,4096]{2,1,0:T(4,128)(2,1)S(1)} %get-tuple-element.48), channel_id=1, source_target_pairs={{0,2},{1,3},{2,0},{3,1},{4,6},{5,7},{6,4},{7,5},{8,10},{9,11},{10,... | collective-permute-start | bytes 196616 | tf_op jit(solution)/shard_map/ppermute | solution.py:30
  54.7 4.6 %collective-permute-start.2 = (bf16[2,4,4096]{2,1,0:T(4,128)(2,1)S(1)}, bf16[2,4,4096]{2,1,0:T(4,128)(2,1)S(1)}, u32[]{:S(2)}, u32[]{:S(2)}) collective-permute-start(bf16[2,4,4096]{2,1,0:T(4,128)(2,1)S(1)} %get-tuple-element.49), channel_id=1, source_target_pairs={{0,1},{1,0},{2,3},{3,2},{4,5},{5,4},{6,7},{7,6},{8,9},{9,8},{10,11... | collective-permute-start | bytes 196616 | tf_op jit(solution)/shard_map/ppermute | solution.py:30
  57.0 11.8 %collective-permute-start.4 = (bf16[1040,128]{1,0:T(8,128)(2,1)S(1)}, bf16[1040,128]{1,0:T(8,128)(2,1)S(1)}, u32[]{:S(2)}, u32[]{:S(2)}) collective-permute-start(bf16[1040,128]{1,0:T(8,128)(2,1)S(1)} %get-tuple-element.50), channel_id=1, source_target_pairs={{0,4},{1,5},{2,6},{3,7},{4,0},{5,1},{6,2},{7,3},{8,12},{9,13},{10,... | collective-permute-start | bytes 798728 | tf_op jit(solution)/shard_map/ppermute | solution.py:30
  59.3 9.4 %collective-permute-start.3 = (bf16[2,4,4096]{2,1,0:T(4,128)(2,1)S(1)}, bf16[2,4,4096]{2,1,0:T(4,128)(2,1)S(1)}, u32[]{:S(2)}, u32[]{:S(2)}) collective-permute-start(bf16[2,4,4096]{2,1,0:T(4,128)(2,1)S(1)} %partial.2), channel_id=1, source_target_pairs={{0,8},{1,9},{2,10},{3,11},{4,12},{5,13},{6,14},{7,15},{8,16},{9,17... | collective-permute-start | bytes 196616 | tf_op jit(solution)/shard_map/ppermute | solution.py:30
  59.4 9.4 %collective-permute-start.5 = (bf16[2,4,4096]{2,1,0:T(4,128)(2,1)S(1)}, bf16[2,4,4096]{2,1,0:T(4,128)(2,1)S(1)}, u32[]{:S(2)}, u32[]{:S(2)}) collective-permute-start(bf16[2,4,4096]{2,1,0:T(4,128)(2,1)S(1)} %partial.2), channel_id=1, source_target_pairs={{0,12},{1,13},{2,14},{3,15},{4,8},{5,9},{6,10},{7,11},{8,20},{9,21... | collective-permute-start | bytes 196616 | tf_op jit(solution)/shard_map/ppermute | solution.py:30
  68.8 5.8 %collective-permute-start.8 = (bf16[2,4,4096]{2,1,0:T(4,128)(2,1)S(1)}, bf16[2,4,4096]{2,1,0:T(4,128)(2,1)S(1)}, u32[]{:S(2)}, u32[]{:S(2)}) collective-permute-start(bf16[2,4,4096]{2,1,0:T(4,128)(2,1)S(1)} %join.2.refs_0_), channel_id=1, source_target_pairs={{0,3},{1,2},{2,1},{3,0},{4,7},{5,6},{6,5},{7,4},{8,11},{9,10},{10,... | collective-permute-start | bytes 196616 | tf_op jit(solution)/shard_map/ppermute | solution.py:30
  68.9 5.9 %collective-permute-start.7 = (bf16[2,4,4096]{2,1,0:T(4,128)(2,1)S(1)}, bf16[2,4,4096]{2,1,0:T(4,128)(2,1)S(1)}, u32[]{:S(2)}, u32[]{:S(2)}) collective-permute-start(bf16[2,4,4096]{2,1,0:T(4,128)(2,1)S(1)} %join.2.refs_0_), channel_id=1, source_target_pairs={{0,2},{1,3},{2,0},{3,1},{4,6},{5,7},{6,4},{7,5},{8,10},{9,11},{10,... | collective-permute-start | bytes 196616 | tf_op jit(solution)/shard_map/ppermute | solution.py:30
  71.3 4.4 %collective-permute-start.6 = (bf16[2,4,4096]{2,1,0:T(4,128)(2,1)S(1)}, bf16[2,4,4096]{2,1,0:T(4,128)(2,1)S(1)}, u32[]{:S(2)}, u32[]{:S(2)}) collective-permute-start(bf16[2,4,4096]{2,1,0:T(4,128)(2,1)S(1)} %join.2.refs_0_), channel_id=1, source_target_pairs={{0,1},{1,0},{2,3},{3,2},{4,5},{5,4},{6,7},{7,6},{8,9},{9,8},{10,11... | collective-permute-start | bytes 196616 | tf_op jit(solution)/shard_map/ppermute | solution.py:30
  76.5 3.7 %collective-permute-start.9 = (bf16[2,16,128]{2,1,0:T(8,128)(2,1)S(1)}, bf16[2,16,128]{2,1,0:T(8,128)(2,1)S(1)}, u32[]{:S(2)}, u32[]{:S(2)}) collective-permute-start(bf16[2,16,128]{2,1,0:T(8,128)(2,1)S(1)} %get-tuple-element.53), channel_id=1, source_target_pairs={{0,1},{1,0},{2,3},{3,2},{4,5},{5,4},{6,7},{7,6},{8,9},{9,8},{10,11... | collective-permute-start | bytes 24584 | tf_op jit(solution)/shard_map/ppermute | solution.py:30
  77.6 3.7 %collective-permute-start.10 = (bf16[2,16,128]{2,1,0:T(8,128)(2,1)S(1)}, bf16[2,16,128]{2,1,0:T(8,128)(2,1)S(1)}, u32[]{:S(2)}, u32[]{:S(2)}) collective-permute-start(bf16[2,16,128]{2,1,0:T(8,128)(2,1)S(1)} %get-tuple-element.54), channel_id=1, source_target_pairs={{0,2},{1,3},{2,0},{3,1},{4,6},{5,7},{6,4},{7,5},{8,10},{9,11},{10,... | collective-permute-start | bytes 24584 | tf_op jit(solution)/shard_map/ppermute | solution.py:30
  77.6 4.5 %collective-permute-start.11 = (bf16[2,16,128]{2,1,0:T(8,128)(2,1)S(1)}, bf16[2,16,128]{2,1,0:T(8,128)(2,1)S(1)}, u32[]{:S(2)}, u32[]{:S(2)}) collective-permute-start(bf16[2,16,128]{2,1,0:T(8,128)(2,1)S(1)} %get-tuple-element.55), channel_id=1, source_target_pairs={{0,3},{1,2},{2,1},{3,0},{4,7},{5,6},{6,5},{7,4},{8,11},{9,10},{10,... | collective-permute-start | bytes 24584 | tf_op jit(solution)/shard_map/ppermute | solution.py:30
  107.8 7.3 %collective-permute-start.12 = (bf16[2,4,4096]{2,1,0:T(4,128)(2,1)S(1)}, bf16[2,4,4096]{2,1,0:T(4,128)(2,1)S(1)}, u32[]{:S(2)}, u32[]{:S(2)}) collective-permute-start(bf16[2,4,4096]{2,1,0:T(4,128)(2,1)S(1)} %get-tuple-element.60), channel_id=1, source_target_pairs={{0,3},{1,2},{2,1},{3,0},{4,7},{5,6},{6,5},{7,4},{8,11},{9,10},{10,... | collective-permute-start | bytes 196616 | tf_op jit(solution)/shard_map/ppermute | solution.py:30
  108.9 6.2 %collective-permute-start.13 = (bf16[2,4,4096]{2,1,0:T(4,128)(2,1)S(1)}, bf16[2,4,4096]{2,1,0:T(4,128)(2,1)S(1)}, u32[]{:S(2)}, u32[]{:S(2)}) collective-permute-start(bf16[2,4,4096]{2,1,0:T(4,128)(2,1)S(1)} %get-tuple-element.61), channel_id=1, source_target_pairs={{0,2},{1,3},{2,0},{3,1},{4,6},{5,7},{6,4},{7,5},{8,10},{9,11},{10,... | collective-permute-start | bytes 196616 | tf_op jit(solution)/shard_map/ppermute | solution.py:30
  109.3 5.8 %collective-permute-start.14 = (bf16[2,4,4096]{2,1,0:T(4,128)(2,1)S(1)}, bf16[2,4,4096]{2,1,0:T(4,128)(2,1)S(1)}, u32[]{:S(2)}, u32[]{:S(2)}) collective-permute-start(bf16[2,4,4096]{2,1,0:T(4,128)(2,1)S(1)} %get-tuple-element.62), channel_id=1, source_target_pairs={{0,1},{1,0},{2,3},{3,2},{4,5},{5,4},{6,7},{7,6},{8,9},{9,8},{10,11... | collective-permute-start | bytes 196616 | tf_op jit(solution)/shard_map/ppermute | solution.py:30
  111.3 12.3 %collective-permute-start.16 = (bf16[1040,128]{1,0:T(8,128)(2,1)S(1)}, bf16[1040,128]{1,0:T(8,128)(2,1)S(1)}, u32[]{:S(2)}, u32[]{:S(2)}) collective-permute-start(bf16[1040,128]{1,0:T(8,128)(2,1)S(1)} %get-tuple-element.63), channel_id=1, source_target_pairs={{0,4},{1,5},{2,6},{3,7},{4,0},{5,1},{6,2},{7,3},{8,12},{9,13},{10,... | collective-permute-start | bytes 798728 | tf_op jit(solution)/shard_map/ppermute | solution.py:30
  115.2 8.4 %collective-permute-start.15 = (bf16[2,4,4096]{2,1,0:T(4,128)(2,1)S(1)}, bf16[2,4,4096]{2,1,0:T(4,128)(2,1)S(1)}, u32[]{:S(2)}, u32[]{:S(2)}) collective-permute-start(bf16[2,4,4096]{2,1,0:T(4,128)(2,1)S(1)} %partial.3), channel_id=1, source_target_pairs={{0,8},{1,9},{2,10},{3,11},{4,12},{5,13},{6,14},{7,15},{8,16},{9,17... | collective-permute-start | bytes 196616 | tf_op jit(solution)/shard_map/ppermute | solution.py:30
  115.2 8.4 %collective-permute-start.17 = (bf16[2,4,4096]{2,1,0:T(4,128)(2,1)S(1)}, bf16[2,4,4096]{2,1,0:T(4,128)(2,1)S(1)}, u32[]{:S(2)}, u32[]{:S(2)}) collective-permute-start(bf16[2,4,4096]{2,1,0:T(4,128)(2,1)S(1)} %partial.3), channel_id=1, source_target_pairs={{0,12},{1,13},{2,14},{3,15},{4,8},{5,9},{6,10},{7,11},{8,20},{9,21... | collective-permute-start | bytes 196616 | tf_op jit(solution)/shard_map/ppermute | solution.py:30
  123.6 5.8 %collective-permute-start.20 = (bf16[2,4,4096]{2,1,0:T(4,128)(2,1)S(1)}, bf16[2,4,4096]{2,1,0:T(4,128)(2,1)S(1)}, u32[]{:S(2)}, u32[]{:S(2)}) collective-permute-start(bf16[2,4,4096]{2,1,0:T(4,128)(2,1)S(1)} %join.3.refs_0_), channel_id=1, source_target_pairs={{0,3},{1,2},{2,1},{3,0},{4,7},{5,6},{6,5},{7,4},{8,11},{9,10},{10,... | collective-permute-start | bytes 196616 | tf_op jit(solution)/shard_map/ppermute | solution.py:30
  123.7 5.8 %collective-permute-start.19 = (bf16[2,4,4096]{2,1,0:T(4,128)(2,1)S(1)}, bf16[2,4,4096]{2,1,0:T(4,128)(2,1)S(1)}, u32[]{:S(2)}, u32[]{:S(2)}) collective-permute-start(bf16[2,4,4096]{2,1,0:T(4,128)(2,1)S(1)} %join.3.refs_0_), channel_id=1, source_target_pairs={{0,2},{1,3},{2,0},{3,1},{4,6},{5,7},{6,4},{7,5},{8,10},{9,11},{10,... | collective-permute-start | bytes 196616 | tf_op jit(solution)/shard_map/ppermute | solution.py:30
  126.0 4.5 %collective-permute-start.18 = (bf16[2,4,4096]{2,1,0:T(4,128)(2,1)S(1)}, bf16[2,4,4096]{2,1,0:T(4,128)(2,1)S(1)}, u32[]{:S(2)}, u32[]{:S(2)}) collective-permute-start(bf16[2,4,4096]{2,1,0:T(4,128)(2,1)S(1)} %join.3.refs_0_), channel_id=1, source_target_pairs={{0,1},{1,0},{2,3},{3,2},{4,5},{5,4},{6,7},{7,6},{8,9},{9,8},{10,11... | collective-permute-start | bytes 196616 | tf_op jit(solution)/shard_map/ppermute | solution.py:30
  131.4 3.7 %collective-permute-start.21 = (bf16[2,16,128]{2,1,0:T(8,128)(2,1)S(1)}, bf16[2,16,128]{2,1,0:T(8,128)(2,1)S(1)}, u32[]{:S(2)}, u32[]{:S(2)}) collective-permute-start(bf16[2,16,128]{2,1,0:T(8,128)(2,1)S(1)} %get-tuple-element.66), channel_id=1, source_target_pairs={{0,1},{1,0},{2,3},{3,2},{4,5},{5,4},{6,7},{7,6},{8,9},{9,8},{10,11... | collective-permute-start | bytes 24584 | tf_op jit(solution)/shard_map/ppermute | solution.py:30
  132.4 3.7 %collective-permute-start.22 = (bf16[2,16,128]{2,1,0:T(8,128)(2,1)S(1)}, bf16[2,16,128]{2,1,0:T(8,128)(2,1)S(1)}, u32[]{:S(2)}, u32[]{:S(2)}) collective-permute-start(bf16[2,16,128]{2,1,0:T(8,128)(2,1)S(1)} %get-tuple-element.67), channel_id=1, source_target_pairs={{0,2},{1,3},{2,0},{3,1},{4,6},{5,7},{6,4},{7,5},{8,10},{9,11},{10,... | collective-permute-start | bytes 24584 | tf_op jit(solution)/shard_map/ppermute | solution.py:30
  132.4 4.5 %collective-permute-start.23 = (bf16[2,16,128]{2,1,0:T(8,128)(2,1)S(1)}, bf16[2,16,128]{2,1,0:T(8,128)(2,1)S(1)}, u32[]{:S(2)}, u32[]{:S(2)}) collective-permute-start(bf16[2,16,128]{2,1,0:T(8,128)(2,1)S(1)} %get-tuple-element.68), channel_id=1, source_target_pairs={{0,3},{1,2},{2,1},{3,0},{4,7},{5,6},{6,5},{7,4},{8,11},{9,10},{10,... | collective-permute-start | bytes 24584 | tf_op jit(solution)/shard_map/ppermute | solution.py:30

commit v10 on v9

--- a/solution.py
+++ b/solution.py
@@ -205,7 +205,7 @@
     count, head_dim = pieces[0].shape[1:]
     for l, piece in enumerate(pieces):
         for g in range(2):
-            q_ref[g, me % low ^ l] = piece[g]
+            q_ref[g, me % low ^ (low - l) % low] = piece[g]
     rows = low * count
     span = k_ref.shape[1] // kv_heads
     cache = span // own
@@ -488,8 +488,9 @@
                     [pltpu.VMEM((devices, own, width), BF16), pltpu.VMEM((devices, own * local_heads, head_dim), F32)],
                     "queries_by_half",
                     cost,
+                    0,
                 )
-                queries = [queries[0]] + [shifted(queries[l], l) for l in range(1, low)]
+                queries = [queries[0]] + [shifted(queries[l], l) for l in range(low - 1, 0, -1)]
             else:
                 own_q, states = call(
                     functools.partial(order_kernel, head_dim, low),
@@ -579,10 +580,8 @@
                 (rows * width, 4 * rows * width),
             )
             parts = [shifted(part_sums, h * low, 1) for h in range(high)]
-            if by_half:
-                parts[0], others[step] = lax.optimization_barrier((parts[0], others[step]))
             state = call(
-                join_kernel, slots, tuple(parts), [whole()] * high, [], "join", (rows * width, 4 * rows * width)
+                join_kernel, slots, tuple(parts), [whole()] * high, [], "join", (rows * width, 4 * rows * width), 0
             )
     return state[None]
 

time: 174 us -> 174 us (level)
  transfers between devices with their start and end apart: 24 -> 24, of which waited for: 16 -> 15; matrix products, arithmetic and copies ran while one was open for 0% -> 0% of each run, Pallas kernels for 0% -> 1%
where the time goes in v10:
time: 174 us; the launch traced here: 173 us
  blocking collectives  104 us (60%)
  waiting for transfers between devices  30 us (17%)
  starting transfers between devices  26.4 us (15%)
  Pallas kernels  11.6 us (7%)
    all_to_all x9, blocking collectives, swapped(): lax.all_to_all(blocks, 'expert', split_axis=0, concat_axis=0, tiled=True)  104 us
    ppermute x24, waiting for transfers between devices, shifted(): return lax.ppermute(array, ('section', 'expert'), pairs)  30 us
    ppermute x24, starting transfers between devices, shifted(): return lax.ppermute(array, ('section', 'expert'), pairs)  26.4 us
    pallas_call x19, Pallas kernels, call(): pl.pallas_call(kernel, out_shape=out, in_specs=specs, out_specs=whole() i...  11.6 us
  transfers between devices with their start and end apart: 24, of which 15 were waited for; matrix products, arithmetic and copies ran while one was open for 0% of the time, Pallas kernels for 1%

profile of v10, /device:TPU:0, one launch (start us, length us, event | category | flops | bytes accessed | tf_op | source)
XLA Modules:
  0.0 173.3 jit_solution(1335560938704932711)
XLA Ops:
  0.0 0.8 copy-done.9
  0.8 16.3 %all_to_all.45.x_ref = bf16[8,4,4096]{2,1,0:T(4,128)(2,1)S(1)} all-to-all(bf16[8,4,4096]{2,1,0:T(4,128)(2,1)S(1)} %spread.1), channel_id=1, replica_groups=mesh['section'=4,'expert'=8] {'expert'}, dimensions={0} | all-to-all | bytes 524288 | tf_op jit(solution)/shard_map/all_to_all | solution.py:41
  17.2 0.8 first_query.1
  18.0 10.3 %all_to_all.46 = bf16[8,32,128]{2,1,0:T(8,128)(2,1)S(1)} all-to-all(bf16[8,32,128]{2,1,0:T(8,128)(2,1)S(1)} %get-tuple-element.37), channel_id=1, replica_groups=mesh['section'=4,'expert'=8] {'expert'}, dimensions={0} | all-to-all | bytes 131072 | tf_op jit(solution)/shard_map/all_to_all | solution.py:41
  28.3 0.5 first_attention.1
  28.8 0.1 broadcast_in_dim.8
  28.9 10.8 %all_to_all.47.c_ref = bf16[8,4,4096]{2,1,0:T(4,128)(2,1)S(1)} all-to-all(bf16[8,4,4096]{2,1,0:T(4,128)(2,1)S(1)} %broadcast_in_dim.8), channel_id=1, replica_groups=mesh['section'=4,'expert'=8] {'expert'}, dimensions={0} | all-to-all | bytes 524288 | tf_op jit(solution)/shard_map/all_to_all | solution.py:41
  39.7 0.7 attention_out.3
  40.4 11.2 %all_to_all.48.refs_0_ = bf16[8,32,512]{2,1,0:T(8,128)(2,1)S(1)} all-to-all(bf16[8,32,512]{2,1,0:T(8,128)(2,1)S(1)} %attention_out.3), channel_id=1, replica_groups=mesh['section'=4,'expert'=8] {'expert'}, dimensions={0} | all-to-all | bytes 524288 | tf_op jit(solution)/shard_map/all_to_all | solution.py:41
  51.6 1.5 experts_sending.2
  53.1 1.0 collective-permute-start
  54.1 0.6 collective-permute-start.1
  54.7 2.0 %collective-permute-start.2 = (bf16[2,4,4096]{2,1,0:T(4,128)(2,1)S(1)}, bf16[2,4,4096]{2,1,0:T(4,128)(2,1)S(1)}, u32[]{:S(2)}, u32[]{:S(2)}) collective-permute-start(bf16[2,4,4096]{2,1,0:T(4,128)(2,1)S(1)} %get-tuple-element.45), channel_id=1, source_target_pairs={{0,1},{1,0},{2,3},{3,2},{4,5},{5,4},{6,7},{7,6},{8,9},{9,8},{10,11... | collective-permute-start | bytes 196616 | tf_op jit(solution)/shard_map/ppermute | solution.py:30
  56.7 0.3 caches_of_other_half.1
  56.9 0.6 collective-permute-start.11
  57.6 1.3 collective-permute-done.refs_1_
  58.9 0.4 collective-permute-done.2.refs_3_
  59.4 1.8 %collective-permute-start.3 = (bf16[2,4,4096]{2,1,0:T(4,128)(2,1)S(1)}, bf16[2,4,4096]{2,1,0:T(4,128)(2,1)S(1)}, u32[]{:S(2)}, u32[]{:S(2)}) collective-permute-start(bf16[2,4,4096]{2,1,0:T(4,128)(2,1)S(1)} %partial.2), channel_id=1, source_target_pairs={{0,8},{1,9},{2,10},{3,11},{4,12},{5,13},{6,14},{7,15},{8,16},{9,17... | collective-permute-start | bytes 196616 | tf_op jit(solution)/shard_map/ppermute | solution.py:30
  61.2 6.4 %collective-permute-done.4.refs_1_ = bf16[2,4,4096]{2,1,0:T(4,128)(2,1)S(1)} collective-permute-done((bf16[2,4,4096]{2,1,0:T(4,128)(2,1)S(1)}, bf16[2,4,4096]{2,1,0:T(4,128)(2,1)S(1)}, u32[]{:S(2)}, u32[]{:S(2)}) %collective-permute-start.4) | collective-permute-done | bytes 65568 | tf_op jit(solution)/shard_map/ppermute | solution.py:30
  67.6 0.7 collective-permute-start.7
  68.3 2.3 %collective-permute-start.6 = (bf16[2,4,4096]{2,1,0:T(4,128)(2,1)S(1)}, bf16[2,4,4096]{2,1,0:T(4,128)(2,1)S(1)}, u32[]{:S(2)}, u32[]{:S(2)}) collective-permute-start(bf16[2,4,4096]{2,1,0:T(4,128)(2,1)S(1)} %join.2.refs_0_), channel_id=1, source_target_pairs={{0,2},{1,3},{2,0},{3,1},{4,6},{5,7},{6,4},{7,5},{8,10},{9,11},{10,... | collective-permute-start | bytes 196616 | tf_op jit(solution)/shard_map/ppermute | solution.py:30
  70.7 0.5 collective-permute-start.5
  71.2 1.7 %collective-permute-done.7.refs_3_ = bf16[2,4,4096]{2,1,0:T(4,128)(2,1)S(1)} collective-permute-done((bf16[2,4,4096]{2,1,0:T(4,128)(2,1)S(1)}, bf16[2,4,4096]{2,1,0:T(4,128)(2,1)S(1)}, u32[]{:S(2)}, u32[]{:S(2)}) %collective-permute-start.7) | collective-permute-done | bytes 65568 | tf_op jit(solution)/shard_map/ppermute | solution.py:30
  72.9 1.8 %collective-permute-done.6.refs_2_ = bf16[2,4,4096]{2,1,0:T(4,128)(2,1)S(1)} collective-permute-done((bf16[2,4,4096]{2,1,0:T(4,128)(2,1)S(1)}, bf16[2,4,4096]{2,1,0:T(4,128)(2,1)S(1)}, u32[]{:S(2)}, u32[]{:S(2)}) %collective-permute-start.6) | collective-permute-done | bytes 65568 | tf_op jit(solution)/shard_map/ppermute | solution.py:30
  74.8 0.5 collective-permute-done.5.refs_1_
  75.2 0.9 queries_by_half.2
  76.1 0.3 collective-permute-start.8
  76.4 2.3 %collective-permute-start.9 = (bf16[2,16,128]{2,1,0:T(8,128)(2,1)S(1)}, bf16[2,16,128]{2,1,0:T(8,128)(2,1)S(1)}, u32[]{:S(2)}, u32[]{:S(2)}) collective-permute-start(bf16[2,16,128]{2,1,0:T(8,128)(2,1)S(1)} %get-tuple-element.48), channel_id=1, source_target_pairs={{0,2},{1,3},{2,0},{3,1},{4,6},{5,7},{6,4},{7,5},{8,10},{9,11},{10,... | collective-permute-start | bytes 24584 | tf_op jit(solution)/shard_map/ppermute | solution.py:30
  78.7 1.0 collective-permute-start.10
  79.7 1.1 collective-permute-done.8.refs_1_
  80.7 1.6 collective-permute-done.10.refs_3_
  82.3 0.4 half_attention.2
  82.7 0.1 broadcast_in_dim.9
  82.8 11.3 %all_to_all.49.c_ref = bf16[8,2,4,2048]{3,2,1,0:T(4,128)(2,1)S(1)} all-to-all(bf16[8,2,4,2048]{3,2,1,0:T(4,128)(2,1)S(1)} %broadcast_in_dim.9), channel_id=1, replica_groups=mesh['section'=4,'expert'=8] {'expert'}, dimensions={0} | all-to-all | bytes 524288 | tf_op jit(solution)/shard_map/all_to_all | solution.py:41
  94.1 0.7 attention_out.4
  94.8 10.9 %all_to_all.50.refs_0_ = bf16[8,32,512]{2,1,0:T(8,128)(2,1)S(1)} all-to-all(bf16[8,32,512]{2,1,0:T(8,128)(2,1)S(1)} %attention_out.4), channel_id=1, replica_groups=mesh['section'=4,'expert'=8] {'expert'}, dimensions={0} | all-to-all | bytes 524288 | tf_op jit(solution)/shard_map/all_to_all | solution.py:41
  105.7 1.5 experts_sending.3
  107.2 1.0 collective-permute-start.12
  108.2 0.6 collective-permute-start.13
  108.8 2.0 %collective-permute-start.14 = (bf16[2,4,4096]{2,1,0:T(4,128)(2,1)S(1)}, bf16[2,4,4096]{2,1,0:T(4,128)(2,1)S(1)}, u32[]{:S(2)}, u32[]{:S(2)}) collective-permute-start(bf16[2,4,4096]{2,1,0:T(4,128)(2,1)S(1)} %get-tuple-element.56), channel_id=1, source_target_pairs={{0,1},{1,0},{2,3},{3,2},{4,5},{5,4},{6,7},{7,6},{8,9},{9,8},{10,11... | collective-permute-start | bytes 196616 | tf_op jit(solution)/shard_map/ppermute | solution.py:30
  110.8 0.6 collective-permute-start.23
  111.4 1.7 collective-permute-done.12.refs_1_
  113.1 0.3 collective-permute-done.14.refs_3_
  113.5 2.0 %collective-permute-start.15 = (bf16[2,4,4096]{2,1,0:T(4,128)(2,1)S(1)}, bf16[2,4,4096]{2,1,0:T(4,128)(2,1)S(1)}, u32[]{:S(2)}, u32[]{:S(2)}) collective-permute-start(bf16[2,4,4096]{2,1,0:T(4,128)(2,1)S(1)} %partial.3), channel_id=1, source_target_pairs={{0,8},{1,9},{2,10},{3,11},{4,12},{5,13},{6,14},{7,15},{8,16},{9,17... | collective-permute-start | bytes 196616 | tf_op jit(solution)/shard_map/ppermute | solution.py:30
  115.5 7.3 %collective-permute-done.16.refs_1_ = bf16[2,4,4096]{2,1,0:T(4,128)(2,1)S(1)} collective-permute-done((bf16[2,4,4096]{2,1,0:T(4,128)(2,1)S(1)}, bf16[2,4,4096]{2,1,0:T(4,128)(2,1)S(1)}, u32[]{:S(2)}, u32[]{:S(2)}) %collective-permute-start.16) | collective-permute-done | bytes 65568 | tf_op jit(solution)/shard_map/ppermute | solution.py:30
  122.8 0.1 collective-permute-start.19
  122.9 2.1 %collective-permute-start.18 = (bf16[2,4,4096]{2,1,0:T(4,128)(2,1)S(1)}, bf16[2,4,4096]{2,1,0:T(4,128)(2,1)S(1)}, u32[]{:S(2)}, u32[]{:S(2)}) collective-permute-start(bf16[2,4,4096]{2,1,0:T(4,128)(2,1)S(1)} %join.3.refs_0_), channel_id=1, source_target_pairs={{0,2},{1,3},{2,0},{3,1},{4,6},{5,7},{6,4},{7,5},{8,10},{9,11},{10,... | collective-permute-start | bytes 196616 | tf_op jit(solution)/shard_map/ppermute | solution.py:30
  125.0 1.4 collective-permute-start.17
  126.3 2.3 %collective-permute-done.19.refs_3_ = bf16[2,4,4096]{2,1,0:T(4,128)(2,1)S(1)} collective-permute-done((bf16[2,4,4096]{2,1,0:T(4,128)(2,1)S(1)}, bf16[2,4,4096]{2,1,0:T(4,128)(2,1)S(1)}, u32[]{:S(2)}, u32[]{:S(2)}) %collective-permute-start.19) | collective-permute-done | bytes 65568 | tf_op jit(solution)/shard_map/ppermute | solution.py:30
  128.7 0.8 collective-permute-done.17.refs_1_
  129.5 0.9 queries_by_half.3
  130.4 0.6 collective-permute-start.20
  131.0 2.0 %collective-permute-start.21 = (bf16[2,16,128]{2,1,0:T(8,128)(2,1)S(1)}, bf16[2,16,128]{2,1,0:T(8,128)(2,1)S(1)}, u32[]{:S(2)}, u32[]{:S(2)}) collective-permute-start(bf16[2,16,128]{2,1,0:T(8,128)(2,1)S(1)} %get-tuple-element.59), channel_id=1, source_target_pairs={{0,2},{1,3},{2,0},{3,1},{4,6},{5,7},{6,4},{7,5},{8,10},{9,11},{10,... | collective-permute-start | bytes 24584 | tf_op jit(solution)/shard_map/ppermute | solution.py:30
  133.0 0.9 collective-permute-start.22
  133.9 1.1 collective-permute-done.20.refs_1_
  135.0 1.7 collective-permute-done.22.refs_3_
  136.7 0.4 half_attention.3
  137.0 0.1 broadcast_in_dim.10
  137.2 11.4 %all_to_all.51.c_ref = bf16[8,2,4,2048]{3,2,1,0:T(4,128)(2,1)S(1)} all-to-all(bf16[8,2,4,2048]{3,2,1,0:T(4,128)(2,1)S(1)} %broadcast_in_dim.10), channel_id=1, replica_groups=mesh['section'=4,'expert'=8] {'expert'}, dimensions={0} | all-to-all | bytes 524288 | tf_op jit(solution)/shard_map/all_to_all | solution.py:41
  148.6 0.7 attention_out.5
  149.3 10.9 %all_to_all.52.a_ref = bf16[8,32,512]{2,1,0:T(8,128)(2,1)S(1)} all-to-all(bf16[8,32,512]{2,1,0:T(8,128)(2,1)S(1)} %attention_out.5), channel_id=1, replica_groups=mesh['section'=4,'expert'=8] {'expert'}, dimensions={0} | all-to-all | bytes 524288 | tf_op jit(solution)/shard_map/all_to_all | solution.py:41
  160.2 1.5 experts.1
  161.7 10.9 %all_to_all.53.r_ref = bf16[8,4,4096]{2,1,0:T(4,128)(2,1)S(1)} all-to-all(bf16[8,4,4096]{2,1,0:T(4,128)(2,1)S(1)} %get-tuple-element.63), channel_id=1, replica_groups=mesh['section'=4,'expert'=8] {'expert'}, dimensions={0} | all-to-all | bytes 524288 | tf_op jit(solution)/shard_map/all_to_all | solution.py:41
  172.6 0.7 combine.1
  (49 shorter events, 0.4 us)
Async XLA Ops:
  0.0 0.8 copy-start.9
  0.8 16.3 %copy-start = (bf16[1,4096,512]{2,1,0:T(8,128)(2,1)S(1)}, bf16[1,4096,512]{2,1,0:T(8,128)(2,1)}, u32[]{:S(2)}) copy-start(bf16[1,4096,512]{2,1,0:T(8,128)(2,1)} %param.19) | copy-start | bytes 12582916
  0.8 16.3 %copy-start.3 = (bf16[1,4096]{1,0:T(2,128)(2,1)S(1)}, bf16[1,4096]{1,0:T(2,128)(2,1)}, u32[]{:S(2)}) copy-start(bf16[1,4096]{1,0:T(2,128)(2,1)} %refs_4_.4) | copy-start | bytes 24580
  0.8 16.3 %copy-start.11 = (s32[1,3,4,2]{2,3,1,0:T(2,128)S(1)}, s32[1,3,4,2]{2,3,1,0:T(2,128)}, u32[]{:S(2)}) copy-start(s32[1,3,4,2]{2,3,1,0:T(2,128)} %param.28) | copy-start | bytes 292
  0.8 16.3 %copy-start.12 = (f32[1,3,4,2]{2,3,1,0:T(2,128)S(1)}, f32[1,3,4,2]{2,3,1,0:T(2,128)}, u32[]{:S(2)}) copy-start(f32[1,3,4,2]{2,3,1,0:T(2,128)} %param.29) | copy-start | bytes 292
  17.1 11.2 %copy-start.1 = (bf16[1,3,4,64,4,128]{5,4,3,2,1,0:T(4,128)(2,1)S(1)}, bf16[1,3,4,64,4,128]{5,4,3,2,1,0:T(4,128)(2,1)}, u32[]{:S(2)}) copy-start(bf16[1,3,4,64,4,128]{5,4,3,2,1,0:T(4,128)(2,1)} %param.21) | copy-start | bytes 2359300
  17.1 11.2 %copy-start.2 = (bf16[1,3,4,64,4,128]{5,4,3,2,1,0:T(4,128)(2,1)S(1)}, bf16[1,3,4,64,4,128]{5,4,3,2,1,0:T(4,128)(2,1)}, u32[]{:S(2)}) copy-start(bf16[1,3,4,64,4,128]{5,4,3,2,1,0:T(4,128)(2,1)} %param.22) | copy-start | bytes 2359300
  17.1 11.2 %copy-start.4 = (s32[1,3,4]{2,0,1:T(1,128)S(1)}, s32[1,3,4]{2,0,1:T(1,128)}, u32[]{:S(2)}) copy-start(s32[1,3,4]{2,0,1:T(1,128)} %param.23) | copy-start | bytes 148
  17.1 11.2 %copy-start.13 = (bf16[128,256]{1,0:T(8,128)(2,1)S(1)}, bf16[128,256]{1,0:T(8,128)(2,1)}, u32[]{:S(2)}) copy-start(bf16[128,256]{1,0:T(8,128)(2,1)} %constant.14.clone.refs_3_) | copy-start | bytes 196612
  17.1 11.2 %copy-start.14 = (bf16[32,256]{1,0:T(8,128)(2,1)S(1)}, bf16[32,256]{1,0:T(8,128)(2,1)}, u32[]{:S(2)}) copy-start(bf16[32,256]{1,0:T(8,128)(2,1)} %constant.15.clone.pick_ref) | copy-start | bytes 49156
  17.1 11.2 %copy-start.15 = (s32[32,1]{1,0:T(8,128)S(1)}, s32[32,1]{1,0:T(8,128)}, u32[]{:S(2)}) copy-start(s32[32,1]{1,0:T(8,128)} %constant.12.clone.refs_4_) | copy-start | bytes 388
  17.2 11.2 %copy-start.16 = (s32[8,256]{1,0:T(8,128)S(1)}, s32[8,256]{1,0:T(8,128)}, u32[]{:S(2)}) copy-start(s32[8,256]{1,0:T(8,128)} %constant.13.clone.refs_5_) | copy-start | bytes 24580
  28.3 11.3 %copy-start.5 = (bf16[1,4096,512]{2,1,0:T(8,128)(2,1)S(1)}, bf16[1,4096,512]{2,1,0:T(8,128)(2,1)}, u32[]{:S(2)}) copy-start(bf16[1,4096,512]{2,1,0:T(8,128)(2,1)} %param.20) | copy-start | bytes 12582916
  39.7 11.9 %copy-start.6 = (bf16[1,1,4096,384]{3,2,1,0:T(8,128)(2,1)S(1)}, bf16[1,1,4096,384]{3,2,1,0:T(8,128)(2,1)}, u32[]{:S(2)}) copy-start(bf16[1,1,4096,384]{3,2,1,0:T(8,128)(2,1)} %param.25) | copy-start | bytes 9437188
  39.7 11.9 %copy-start.7 = (bf16[1,1,4096,384]{3,2,1,0:T(8,128)(2,1)S(1)}, bf16[1,1,4096,384]{3,2,1,0:T(8,128)(2,1)}, u32[]{:S(2)}) copy-start(bf16[1,1,4096,384]{3,2,1,0:T(8,128)(2,1)} %param.26) | copy-start | bytes 9437188
  39.7 11.9 %copy-start.8 = (bf16[1,1,384,4096]{3,2,1,0:T(8,128)(2,1)S(1)}, bf16[1,1,384,4096]{3,2,1,0:T(8,128)(2,1)}, u32[]{:S(2)}) copy-start(bf16[1,1,384,4096]{3,2,1,0:T(8,128)(2,1)} %param.27) | copy-start | bytes 9437188
  39.7 11.9 %copy-start.10 = (bf16[1,4096]{1,0:T(2,128)(2,1)S(1)}, bf16[1,4096]{1,0:T(2,128)(2,1)}, u32[]{:S(2)}) copy-start(bf16[1,4096]{1,0:T(2,128)(2,1)} %gain_ref.3) | copy-start | bytes 24580
  53.1 5.7 %collective-permute-start = (bf16[2,4,4096]{2,1,0:T(4,128)(2,1)S(1)}, bf16[2,4,4096]{2,1,0:T(4,128)(2,1)S(1)}, u32[]{:S(2)}, u32[]{:S(2)}) collective-permute-start(bf16[2,4,4096]{2,1,0:T(4,128)(2,1)S(1)} %get-tuple-element.43), channel_id=1, source_target_pairs={{0,3},{1,2},{2,1},{3,0},{4,7},{5,6},{6,5},{7,4},{8,11},{9,10},{10,... | collective-permute-start | bytes 196616 | tf_op jit(solution)/shard_map/ppermute | solution.py:30
  54.1 4.8 %collective-permute-start.1 = (bf16[2,4,4096]{2,1,0:T(4,128)(2,1)S(1)}, bf16[2,4,4096]{2,1,0:T(4,128)(2,1)S(1)}, u32[]{:S(2)}, u32[]{:S(2)}) collective-permute-start(bf16[2,4,4096]{2,1,0:T(4,128)(2,1)S(1)} %get-tuple-element.44), channel_id=1, source_target_pairs={{0,2},{1,3},{2,0},{3,1},{4,6},{5,7},{6,4},{7,5},{8,10},{9,11},{10,... | collective-permute-start | bytes 196616 | tf_op jit(solution)/shard_map/ppermute | solution.py:30
  54.7 4.6 %collective-permute-start.2 = (bf16[2,4,4096]{2,1,0:T(4,128)(2,1)S(1)}, bf16[2,4,4096]{2,1,0:T(4,128)(2,1)S(1)}, u32[]{:S(2)}, u32[]{:S(2)}) collective-permute-start(bf16[2,4,4096]{2,1,0:T(4,128)(2,1)S(1)} %get-tuple-element.45), channel_id=1, source_target_pairs={{0,1},{1,0},{2,3},{3,2},{4,5},{5,4},{6,7},{7,6},{8,9},{9,8},{10,11... | collective-permute-start | bytes 196616 | tf_op jit(solution)/shard_map/ppermute | solution.py:30
  56.9 22.7 %collective-permute-start.11 = (bf16[1040,128]{1,0:T(8,128)(2,1)S(1)}, bf16[1040,128]{1,0:T(8,128)(2,1)S(1)}, u32[]{:S(2)}, u32[]{:S(2)}) collective-permute-start(bf16[1040,128]{1,0:T(8,128)(2,1)S(1)} %get-tuple-element.50), channel_id=1, source_target_pairs={{0,4},{1,5},{2,6},{3,7},{4,0},{5,1},{6,2},{7,3},{8,12},{9,13},{10,... | collective-permute-start | bytes 798728 | tf_op jit(solution)/shard_map/ppermute | solution.py:30
  59.3 8.3 %collective-permute-start.4 = (bf16[2,4,4096]{2,1,0:T(4,128)(2,1)S(1)}, bf16[2,4,4096]{2,1,0:T(4,128)(2,1)S(1)}, u32[]{:S(2)}, u32[]{:S(2)}) collective-permute-start(bf16[2,4,4096]{2,1,0:T(4,128)(2,1)S(1)} %partial.2), channel_id=1, source_target_pairs={{0,12},{1,13},{2,14},{3,15},{4,8},{5,9},{6,10},{7,11},{8,20},{9,21... | collective-permute-start | bytes 196616 | tf_op jit(solution)/shard_map/ppermute | solution.py:30
  59.4 8.2 %collective-permute-start.3 = (bf16[2,4,4096]{2,1,0:T(4,128)(2,1)S(1)}, bf16[2,4,4096]{2,1,0:T(4,128)(2,1)S(1)}, u32[]{:S(2)}, u32[]{:S(2)}) collective-permute-start(bf16[2,4,4096]{2,1,0:T(4,128)(2,1)S(1)} %partial.2), channel_id=1, source_target_pairs={{0,8},{1,9},{2,10},{3,11},{4,12},{5,13},{6,14},{7,15},{8,16},{9,17... | collective-permute-start | bytes 196616 | tf_op jit(solution)/shard_map/ppermute | solution.py:30
  67.6 5.3 %collective-permute-start.7 = (bf16[2,4,4096]{2,1,0:T(4,128)(2,1)S(1)}, bf16[2,4,4096]{2,1,0:T(4,128)(2,1)S(1)}, u32[]{:S(2)}, u32[]{:S(2)}) collective-permute-start(bf16[2,4,4096]{2,1,0:T(4,128)(2,1)S(1)} %join.2.refs_0_), channel_id=1, source_target_pairs={{0,3},{1,2},{2,1},{3,0},{4,7},{5,6},{6,5},{7,4},{8,11},{9,10},{10,... | collective-permute-start | bytes 196616 | tf_op jit(solution)/shard_map/ppermute | solution.py:30
  68.3 6.4 %collective-permute-start.6 = (bf16[2,4,4096]{2,1,0:T(4,128)(2,1)S(1)}, bf16[2,4,4096]{2,1,0:T(4,128)(2,1)S(1)}, u32[]{:S(2)}, u32[]{:S(2)}) collective-permute-start(bf16[2,4,4096]{2,1,0:T(4,128)(2,1)S(1)} %join.2.refs_0_), channel_id=1, source_target_pairs={{0,2},{1,3},{2,0},{3,1},{4,6},{5,7},{6,4},{7,5},{8,10},{9,11},{10,... | collective-permute-start | bytes 196616 | tf_op jit(solution)/shard_map/ppermute | solution.py:30
  70.7 4.5 %collective-permute-start.5 = (bf16[2,4,4096]{2,1,0:T(4,128)(2,1)S(1)}, bf16[2,4,4096]{2,1,0:T(4,128)(2,1)S(1)}, u32[]{:S(2)}, u32[]{:S(2)}) collective-permute-start(bf16[2,4,4096]{2,1,0:T(4,128)(2,1)S(1)} %join.2.refs_0_), channel_id=1, source_target_pairs={{0,1},{1,0},{2,3},{3,2},{4,5},{5,4},{6,7},{7,6},{8,9},{9,8},{10,11... | collective-permute-start | bytes 196616 | tf_op jit(solution)/shard_map/ppermute | solution.py:30
  76.1 4.6 %collective-permute-start.8 = (bf16[2,16,128]{2,1,0:T(8,128)(2,1)S(1)}, bf16[2,16,128]{2,1,0:T(8,128)(2,1)S(1)}, u32[]{:S(2)}, u32[]{:S(2)}) collective-permute-start(bf16[2,16,128]{2,1,0:T(8,128)(2,1)S(1)} %get-tuple-element.47), channel_id=1, source_target_pairs={{0,3},{1,2},{2,1},{3,0},{4,7},{5,6},{6,5},{7,4},{8,11},{9,10},{10,... | collective-permute-start | bytes 24584 | tf_op jit(solution)/shard_map/ppermute | solution.py:30
  76.4 4.3 %collective-permute-start.9 = (bf16[2,16,128]{2,1,0:T(8,128)(2,1)S(1)}, bf16[2,16,128]{2,1,0:T(8,128)(2,1)S(1)}, u32[]{:S(2)}, u32[]{:S(2)}) collective-permute-start(bf16[2,16,128]{2,1,0:T(8,128)(2,1)S(1)} %get-tuple-element.48), channel_id=1, source_target_pairs={{0,2},{1,3},{2,0},{3,1},{4,6},{5,7},{6,4},{7,5},{8,10},{9,11},{10,... | collective-permute-start | bytes 24584 | tf_op jit(solution)/shard_map/ppermute | solution.py:30
  78.7 3.7 %collective-permute-start.10 = (bf16[2,16,128]{2,1,0:T(8,128)(2,1)S(1)}, bf16[2,16,128]{2,1,0:T(8,128)(2,1)S(1)}, u32[]{:S(2)}, u32[]{:S(2)}) collective-permute-start(bf16[2,16,128]{2,1,0:T(8,128)(2,1)S(1)} %get-tuple-element.49), channel_id=1, source_target_pairs={{0,1},{1,0},{2,3},{3,2},{4,5},{5,4},{6,7},{7,6},{8,9},{9,8},{10,11... | collective-permute-start | bytes 24584 | tf_op jit(solution)/shard_map/ppermute | solution.py:30
  107.2 5.8 %collective-permute-start.12 = (bf16[2,4,4096]{2,1,0:T(4,128)(2,1)S(1)}, bf16[2,4,4096]{2,1,0:T(4,128)(2,1)S(1)}, u32[]{:S(2)}, u32[]{:S(2)}) collective-permute-start(bf16[2,4,4096]{2,1,0:T(4,128)(2,1)S(1)} %get-tuple-element.54), channel_id=1, source_target_pairs={{0,3},{1,2},{2,1},{3,0},{4,7},{5,6},{6,5},{7,4},{8,11},{9,10},{10,... | collective-permute-start | bytes 196616 | tf_op jit(solution)/shard_map/ppermute | solution.py:30
  108.2 4.8 %collective-permute-start.13 = (bf16[2,4,4096]{2,1,0:T(4,128)(2,1)S(1)}, bf16[2,4,4096]{2,1,0:T(4,128)(2,1)S(1)}, u32[]{:S(2)}, u32[]{:S(2)}) collective-permute-start(bf16[2,4,4096]{2,1,0:T(4,128)(2,1)S(1)} %get-tuple-element.55), channel_id=1, source_target_pairs={{0,2},{1,3},{2,0},{3,1},{4,6},{5,7},{6,4},{7,5},{8,10},{9,11},{10,... | collective-permute-start | bytes 196616 | tf_op jit(solution)/shard_map/ppermute | solution.py:30
  108.8 4.6 %collective-permute-start.14 = (bf16[2,4,4096]{2,1,0:T(4,128)(2,1)S(1)}, bf16[2,4,4096]{2,1,0:T(4,128)(2,1)S(1)}, u32[]{:S(2)}, u32[]{:S(2)}) collective-permute-start(bf16[2,4,4096]{2,1,0:T(4,128)(2,1)S(1)} %get-tuple-element.56), channel_id=1, source_target_pairs={{0,1},{1,0},{2,3},{3,2},{4,5},{5,4},{6,7},{7,6},{8,9},{9,8},{10,11... | collective-permute-start | bytes 196616 | tf_op jit(solution)/shard_map/ppermute | solution.py:30
  110.8 23.1 %collective-permute-start.23 = (bf16[1040,128]{1,0:T(8,128)(2,1)S(1)}, bf16[1040,128]{1,0:T(8,128)(2,1)S(1)}, u32[]{:S(2)}, u32[]{:S(2)}) collective-permute-start(bf16[1040,128]{1,0:T(8,128)(2,1)S(1)} %get-tuple-element.61), channel_id=1, source_target_pairs={{0,4},{1,5},{2,6},{3,7},{4,0},{5,1},{6,2},{7,3},{8,12},{9,13},{10,... | collective-permute-start | bytes 798728 | tf_op jit(solution)/shard_map/ppermute | solution.py:30
  113.4 9.3 %collective-permute-start.16 = (bf16[2,4,4096]{2,1,0:T(4,128)(2,1)S(1)}, bf16[2,4,4096]{2,1,0:T(4,128)(2,1)S(1)}, u32[]{:S(2)}, u32[]{:S(2)}) collective-permute-start(bf16[2,4,4096]{2,1,0:T(4,128)(2,1)S(1)} %partial.3), channel_id=1, source_target_pairs={{0,12},{1,13},{2,14},{3,15},{4,8},{5,9},{6,10},{7,11},{8,20},{9,21... | collective-permute-start | bytes 196616 | tf_op jit(solution)/shard_map/ppermute | solution.py:30
  113.5 9.3 %collective-permute-start.15 = (bf16[2,4,4096]{2,1,0:T(4,128)(2,1)S(1)}, bf16[2,4,4096]{2,1,0:T(4,128)(2,1)S(1)}, u32[]{:S(2)}, u32[]{:S(2)}) collective-permute-start(bf16[2,4,4096]{2,1,0:T(4,128)(2,1)S(1)} %partial.3), channel_id=1, source_target_pairs={{0,8},{1,9},{2,10},{3,11},{4,12},{5,13},{6,14},{7,15},{8,16},{9,17... | collective-permute-start | bytes 196616 | tf_op jit(solution)/shard_map/ppermute | solution.py:30
  122.8 5.9 %collective-permute-start.19 = (bf16[2,4,4096]{2,1,0:T(4,128)(2,1)S(1)}, bf16[2,4,4096]{2,1,0:T(4,128)(2,1)S(1)}, u32[]{:S(2)}, u32[]{:S(2)}) collective-permute-start(bf16[2,4,4096]{2,1,0:T(4,128)(2,1)S(1)} %join.3.refs_0_), channel_id=1, source_target_pairs={{0,3},{1,2},{2,1},{3,0},{4,7},{5,6},{6,5},{7,4},{8,11},{9,10},{10,... | collective-permute-start | bytes 196616 | tf_op jit(solution)/shard_map/ppermute | solution.py:30
  122.9 5.8 %collective-permute-start.18 = (bf16[2,4,4096]{2,1,0:T(4,128)(2,1)S(1)}, bf16[2,4,4096]{2,1,0:T(4,128)(2,1)S(1)}, u32[]{:S(2)}, u32[]{:S(2)}) collective-permute-start(bf16[2,4,4096]{2,1,0:T(4,128)(2,1)S(1)} %join.3.refs_0_), channel_id=1, source_target_pairs={{0,2},{1,3},{2,0},{3,1},{4,6},{5,7},{6,4},{7,5},{8,10},{9,11},{10,... | collective-permute-start | bytes 196616 | tf_op jit(solution)/shard_map/ppermute | solution.py:30
  125.0 4.6 %collective-permute-start.17 = (bf16[2,4,4096]{2,1,0:T(4,128)(2,1)S(1)}, bf16[2,4,4096]{2,1,0:T(4,128)(2,1)S(1)}, u32[]{:S(2)}, u32[]{:S(2)}) collective-permute-start(bf16[2,4,4096]{2,1,0:T(4,128)(2,1)S(1)} %join.3.refs_0_), channel_id=1, source_target_pairs={{0,1},{1,0},{2,3},{3,2},{4,5},{5,4},{6,7},{7,6},{8,9},{9,8},{10,11... | collective-permute-start | bytes 196616 | tf_op jit(solution)/shard_map/ppermute | solution.py:30
  130.4 4.6 %collective-permute-start.20 = (bf16[2,16,128]{2,1,0:T(8,128)(2,1)S(1)}, bf16[2,16,128]{2,1,0:T(8,128)(2,1)S(1)}, u32[]{:S(2)}, u32[]{:S(2)}) collective-permute-start(bf16[2,16,128]{2,1,0:T(8,128)(2,1)S(1)} %get-tuple-element.58), channel_id=1, source_target_pairs={{0,3},{1,2},{2,1},{3,0},{4,7},{5,6},{6,5},{7,4},{8,11},{9,10},{10,... | collective-permute-start | bytes 24584 | tf_op jit(solution)/shard_map/ppermute | solution.py:30
  131.0 4.0 %collective-permute-start.21 = (bf16[2,16,128]{2,1,0:T(8,128)(2,1)S(1)}, bf16[2,16,128]{2,1,0:T(8,128)(2,1)S(1)}, u32[]{:S(2)}, u32[]{:S(2)}) collective-permute-start(bf16[2,16,128]{2,1,0:T(8,128)(2,1)S(1)} %get-tuple-element.59), channel_id=1, source_target_pairs={{0,2},{1,3},{2,0},{3,1},{4,6},{5,7},{6,4},{7,5},{8,10},{9,11},{10,... | collective-permute-start | bytes 24584 | tf_op jit(solution)/shard_map/ppermute | solution.py:30
  133.0 3.7 %collective-permute-start.22 = (bf16[2,16,128]{2,1,0:T(8,128)(2,1)S(1)}, bf16[2,16,128]{2,1,0:T(8,128)(2,1)S(1)}, u32[]{:S(2)}, u32[]{:S(2)}) collective-permute-start(bf16[2,16,128]{2,1,0:T(8,128)(2,1)S(1)} %get-tuple-element.60), channel_id=1, source_target_pairs={{0,1},{1,0},{2,3},{3,2},{4,5},{5,4},{6,7},{7,6},{8,9},{9,8},{10,11... | collective-permute-start | bytes 24584 | tf_op jit(solution)/shard_map/ppermute | solution.py:30

commit v11 on v10

--- a/solution.py
+++ b/solution.py
@@ -39,11 +39,6 @@
 
 def swapped(blocks):
     return lax.all_to_all(blocks, "expert", split_axis=0, concat_axis=0, tiled=True)
-
-
-def everyones(array):
-    devices = lax.axis_size("expert")
-    return swapped(jnp.broadcast_to(array[None], (devices,) + array.shape))
 
 
 def whole(memory_space=pltpu.VMEM):
@@ -235,9 +230,12 @@
     heads = part // own
     for h in range(rows // own):
         at = slice(head_dim * h, head_dim * (h + 1))
-        c_ref[mine, :, at] = own_context[own * h:own * (h + 1), :].astype(BF16)
         j, inside = h // heads, h % heads
-        c_ref[1 - mine, :, at] = contexts[j][own * inside:own * (inside + 1), :].astype(BF16)
+        one = own_context[own * h:own * (h + 1), :].astype(BF16)
+        two = contexts[j][own * inside:own * (inside + 1), :].astype(BF16)
+        for i in range(c_ref.shape[0]):
+            c_ref[i, mine, :, at] = one
+            c_ref[i, 1 - mine, :, at] = two
 
 
 def first_attention_kernel(own, pick_ref, q_ref, *refs):
@@ -273,7 +271,9 @@
     for r in range(own):
         lines[ours[r], :] = contexts[r] * (1.0 / jnp.sum(exps[r], axis=-1, keepdims=True))
     for h in range(heads):
-        c_ref[:, head_dim * h:head_dim * (h + 1)] = lines[pl.ds(h, own, stride=heads), :].astype(BF16)
+        piece = lines[pl.ds(h, own, stride=heads), :].astype(BF16)
+        for i in range(c_ref.shape[0]):
+            c_ref[i, :, head_dim * h:head_dim * (h + 1)] = piece
 
 
 def attention_tables(own, heads, local_heads, kv_heads, cache_len):
@@ -504,7 +504,7 @@
         if step and by_half:
             context = call(
                 functools.partial(half_attention_kernel, step, own, kv_heads),
-                jax.ShapeDtypeStruct((2, own, heads * head_dim // 2), BF16),
+                jax.ShapeDtypeStruct((devices, 2, own, heads * head_dim // 2), BF16),
                 (me, *queries, keys, values, lengths, others[step - 1]),
                 [smem] + [whole()] * (low + 4),
                 [pltpu.VMEM((2, low, own * local_heads, head_dim), BF16)],
@@ -512,7 +512,7 @@
                 cost,
             )
         else:
-            c_shape = jax.ShapeDtypeStruct((own, heads * head_dim), BF16)
+            c_shape = jax.ShapeDtypeStruct((devices, own, heads * head_dim), BF16)
             by_row = [pltpu.VMEM((own * heads, head_dim), F32)]
             cost = (4 * own * heads * places * head_dim, 4 * places * head_dim)
             queries = swapped(own_q.reshape(devices, -1, head_dim)).reshape(-1, head_dim)
@@ -536,7 +536,7 @@
                     "attention",
                     cost,
                 )
-        contexts = everyones(context)
+        contexts = swapped(context)
         columns = call(
             half_out_kernel if step and by_half else out_kernel,
             jax.ShapeDtypeStruct((devices, rows, part), BF16),

time: 174 us -> 174 us (level)
  no operation moved by 1% of the time
where the time goes in v11:
time: 174 us; the launch traced here: 173 us
  blocking collectives  104 us (60%)
  waiting for transfers between devices  30 us (17%)
  starting transfers between devices  26.4 us (15%)
  Pallas kernels  11.7 us (7%)
    all_to_all x9, blocking collectives, swapped(): lax.all_to_all(blocks, 'expert', split_axis=0, concat_axis=0, tiled=True)  104 us
    ppermute x24, waiting for transfers between devices, shifted(): return lax.ppermute(array, ('section', 'expert'), pairs)  30 us
    ppermute x24, starting transfers between devices, shifted(): return lax.ppermute(array, ('section', 'expert'), pairs)  26.4 us
    pallas_call x19, Pallas kernels, call(): pl.pallas_call(kernel, out_shape=out, in_specs=specs, out_specs=whole() i...  11.7 us
  transfers between devices with their start and end apart: 24, of which 15 were waited for; matrix products, arithmetic and copies ran while one was open for 0% of the time, Pallas kernels for 1%

profile of v11, /device:TPU:0, one launch (start us, length us, event | category | flops | bytes accessed | tf_op | source)
XLA Modules:
  0.0 173.1 jit_solution(7921623470777389812)
XLA Ops:
  0.0 0.8 copy-done.9
  0.8 16.3 %all_to_all.45.x_ref = bf16[8,4,4096]{2,1,0:T(4,128)(2,1)S(1)} all-to-all(bf16[8,4,4096]{2,1,0:T(4,128)(2,1)S(1)} %spread.1), channel_id=1, replica_groups=mesh['section'=4,'expert'=8] {'expert'}, dimensions={0} | all-to-all | bytes 524288 | tf_op jit(solution)/shard_map/all_to_all | solution.py:41
  17.2 0.8 first_query.1
  18.0 10.3 %all_to_all.46 = bf16[8,32,128]{2,1,0:T(8,128)(2,1)S(1)} all-to-all(bf16[8,32,128]{2,1,0:T(8,128)(2,1)S(1)} %get-tuple-element.37), channel_id=1, replica_groups=mesh['section'=4,'expert'=8] {'expert'}, dimensions={0} | all-to-all | bytes 131072 | tf_op jit(solution)/shard_map/all_to_all | solution.py:41
  28.3 0.5 first_attention.1
  28.9 10.8 %all_to_all.47.c_ref = bf16[8,4,4096]{2,1,0:T(4,128)(2,1)S(1)} all-to-all(bf16[8,4,4096]{2,1,0:T(4,128)(2,1)S(1)} %get-tuple-element.38), channel_id=1, replica_groups=mesh['section'=4,'expert'=8] {'expert'}, dimensions={0} | all-to-all | bytes 524288 | tf_op jit(solution)/shard_map/all_to_all | solution.py:41
  39.7 0.7 attention_out.3
  40.4 11.2 %all_to_all.48.refs_0_ = bf16[8,32,512]{2,1,0:T(8,128)(2,1)S(1)} all-to-all(bf16[8,32,512]{2,1,0:T(8,128)(2,1)S(1)} %attention_out.3), channel_id=1, replica_groups=mesh['section'=4,'expert'=8] {'expert'}, dimensions={0} | all-to-all | bytes 524288 | tf_op jit(solution)/shard_map/all_to_all | solution.py:41
  51.5 1.5 experts_sending.2
  53.1 1.0 collective-permute-start
  54.1 0.6 collective-permute-start.1
  54.6 2.0 %collective-permute-start.2 = (bf16[2,4,4096]{2,1,0:T(4,128)(2,1)S(1)}, bf16[2,4,4096]{2,1,0:T(4,128)(2,1)S(1)}, u32[]{:S(2)}, u32[]{:S(2)}) collective-permute-start(bf16[2,4,4096]{2,1,0:T(4,128)(2,1)S(1)} %get-tuple-element.45), channel_id=1, source_target_pairs={{0,1},{1,0},{2,3},{3,2},{4,5},{5,4},{6,7},{7,6},{8,9},{9,8},{10,11... | collective-permute-start | bytes 196616 | tf_op jit(solution)/shard_map/ppermute | solution.py:30
  56.6 0.3 caches_of_other_half.1
  56.9 0.6 collective-permute-start.11
  57.5 1.3 collective-permute-done.refs_1_
  58.8 0.4 collective-permute-done.2.refs_3_
  59.2 0.1 partial.2
  59.3 0.1 collective-permute-start.4
  59.3 1.8 %collective-permute-start.3 = (bf16[2,4,4096]{2,1,0:T(4,128)(2,1)S(1)}, bf16[2,4,4096]{2,1,0:T(4,128)(2,1)S(1)}, u32[]{:S(2)}, u32[]{:S(2)}) collective-permute-start(bf16[2,4,4096]{2,1,0:T(4,128)(2,1)S(1)} %partial.2), channel_id=1, source_target_pairs={{0,8},{1,9},{2,10},{3,11},{4,12},{5,13},{6,14},{7,15},{8,16},{9,17... | collective-permute-start | bytes 196616 | tf_op jit(solution)/shard_map/ppermute | solution.py:30
  61.1 6.4 %collective-permute-done.4.refs_1_ = bf16[2,4,4096]{2,1,0:T(4,128)(2,1)S(1)} collective-permute-done((bf16[2,4,4096]{2,1,0:T(4,128)(2,1)S(1)}, bf16[2,4,4096]{2,1,0:T(4,128)(2,1)S(1)}, u32[]{:S(2)}, u32[]{:S(2)}) %collective-permute-start.4) | collective-permute-done | bytes 65568 | tf_op jit(solution)/shard_map/ppermute | solution.py:30
  67.6 0.7 collective-permute-start.7
  68.3 2.4 %collective-permute-start.6 = (bf16[2,4,4096]{2,1,0:T(4,128)(2,1)S(1)}, bf16[2,4,4096]{2,1,0:T(4,128)(2,1)S(1)}, u32[]{:S(2)}, u32[]{:S(2)}) collective-permute-start(bf16[2,4,4096]{2,1,0:T(4,128)(2,1)S(1)} %join.2.refs_0_), channel_id=1, source_target_pairs={{0,2},{1,3},{2,0},{3,1},{4,6},{5,7},{6,4},{7,5},{8,10},{9,11},{10,... | collective-permute-start | bytes 196616 | tf_op jit(solution)/shard_map/ppermute | solution.py:30
  70.7 0.5 collective-permute-start.5
  71.2 1.7 %collective-permute-done.7.refs_3_ = bf16[2,4,4096]{2,1,0:T(4,128)(2,1)S(1)} collective-permute-done((bf16[2,4,4096]{2,1,0:T(4,128)(2,1)S(1)}, bf16[2,4,4096]{2,1,0:T(4,128)(2,1)S(1)}, u32[]{:S(2)}, u32[]{:S(2)}) %collective-permute-start.7) | collective-permute-done | bytes 65568 | tf_op jit(solution)/shard_map/ppermute | solution.py:30
  72.9 1.8 %collective-permute-done.6.refs_2_ = bf16[2,4,4096]{2,1,0:T(4,128)(2,1)S(1)} collective-permute-done((bf16[2,4,4096]{2,1,0:T(4,128)(2,1)S(1)}, bf16[2,4,4096]{2,1,0:T(4,128)(2,1)S(1)}, u32[]{:S(2)}, u32[]{:S(2)}) %collective-permute-start.6) | collective-permute-done | bytes 65568 | tf_op jit(solution)/shard_map/ppermute | solution.py:30
  74.7 0.5 collective-permute-done.5.refs_1_
  75.2 0.9 queries_by_half.2
  76.1 0.3 collective-permute-start.8
  76.4 2.2 %collective-permute-start.9 = (bf16[2,16,128]{2,1,0:T(8,128)(2,1)S(1)}, bf16[2,16,128]{2,1,0:T(8,128)(2,1)S(1)}, u32[]{:S(2)}, u32[]{:S(2)}) collective-permute-start(bf16[2,16,128]{2,1,0:T(8,128)(2,1)S(1)} %get-tuple-element.48), channel_id=1, source_target_pairs={{0,2},{1,3},{2,0},{3,1},{4,6},{5,7},{6,4},{7,5},{8,10},{9,11},{10,... | collective-permute-start | bytes 24584 | tf_op jit(solution)/shard_map/ppermute | solution.py:30
  78.6 1.0 collective-permute-start.10
  79.6 1.1 collective-permute-done.8.refs_1_
  80.7 1.6 collective-permute-done.10.refs_3_
  82.3 0.4 half_attention.2
  82.7 11.3 %all_to_all.49.c_ref = bf16[8,2,4,2048]{3,2,1,0:T(4,128)(2,1)S(1)} all-to-all(bf16[8,2,4,2048]{3,2,1,0:T(4,128)(2,1)S(1)} %half_attention.2), channel_id=1, replica_groups=mesh['section'=4,'expert'=8] {'expert'}, dimensions={0} | all-to-all | bytes 524288 | tf_op jit(solution)/shard_map/all_to_all | solution.py:41
  94.0 0.7 attention_out.4
  94.7 10.9 %all_to_all.50.refs_0_ = bf16[8,32,512]{2,1,0:T(8,128)(2,1)S(1)} all-to-all(bf16[8,32,512]{2,1,0:T(8,128)(2,1)S(1)} %attention_out.4), channel_id=1, replica_groups=mesh['section'=4,'expert'=8] {'expert'}, dimensions={0} | all-to-all | bytes 524288 | tf_op jit(solution)/shard_map/all_to_all | solution.py:41
  105.6 1.5 experts_sending.3
  107.1 1.0 collective-permute-start.12
  108.1 0.6 collective-permute-start.13
  108.7 2.0 %collective-permute-start.14 = (bf16[2,4,4096]{2,1,0:T(4,128)(2,1)S(1)}, bf16[2,4,4096]{2,1,0:T(4,128)(2,1)S(1)}, u32[]{:S(2)}, u32[]{:S(2)}) collective-permute-start(bf16[2,4,4096]{2,1,0:T(4,128)(2,1)S(1)} %get-tuple-element.56), channel_id=1, source_target_pairs={{0,1},{1,0},{2,3},{3,2},{4,5},{5,4},{6,7},{7,6},{8,9},{9,8},{10,11... | collective-permute-start | bytes 196616 | tf_op jit(solution)/shard_map/ppermute | solution.py:30
  110.7 0.6 collective-permute-start.23
  111.3 1.7 collective-permute-done.12.refs_1_
  113.0 0.3 collective-permute-done.14.refs_3_
  113.3 0.1 collective-permute-start.16
  113.4 2.0 %collective-permute-start.15 = (bf16[2,4,4096]{2,1,0:T(4,128)(2,1)S(1)}, bf16[2,4,4096]{2,1,0:T(4,128)(2,1)S(1)}, u32[]{:S(2)}, u32[]{:S(2)}) collective-permute-start(bf16[2,4,4096]{2,1,0:T(4,128)(2,1)S(1)} %partial.3), channel_id=1, source_target_pairs={{0,8},{1,9},{2,10},{3,11},{4,12},{5,13},{6,14},{7,15},{8,16},{9,17... | collective-permute-start | bytes 196616 | tf_op jit(solution)/shard_map/ppermute | solution.py:30
  115.4 7.3 %collective-permute-done.16.refs_1_ = bf16[2,4,4096]{2,1,0:T(4,128)(2,1)S(1)} collective-permute-done((bf16[2,4,4096]{2,1,0:T(4,128)(2,1)S(1)}, bf16[2,4,4096]{2,1,0:T(4,128)(2,1)S(1)}, u32[]{:S(2)}, u32[]{:S(2)}) %collective-permute-start.16) | collective-permute-done | bytes 65568 | tf_op jit(solution)/shard_map/ppermute | solution.py:30
  122.7 0.1 collective-permute-start.19
  122.8 2.1 %collective-permute-start.18 = (bf16[2,4,4096]{2,1,0:T(4,128)(2,1)S(1)}, bf16[2,4,4096]{2,1,0:T(4,128)(2,1)S(1)}, u32[]{:S(2)}, u32[]{:S(2)}) collective-permute-start(bf16[2,4,4096]{2,1,0:T(4,128)(2,1)S(1)} %join.3.refs_0_), channel_id=1, source_target_pairs={{0,2},{1,3},{2,0},{3,1},{4,6},{5,7},{6,4},{7,5},{8,10},{9,11},{10,... | collective-permute-start | bytes 196616 | tf_op jit(solution)/shard_map/ppermute | solution.py:30
  124.9 1.4 collective-permute-start.17
  126.3 2.3 %collective-permute-done.19.refs_3_ = bf16[2,4,4096]{2,1,0:T(4,128)(2,1)S(1)} collective-permute-done((bf16[2,4,4096]{2,1,0:T(4,128)(2,1)S(1)}, bf16[2,4,4096]{2,1,0:T(4,128)(2,1)S(1)}, u32[]{:S(2)}, u32[]{:S(2)}) %collective-permute-start.19) | collective-permute-done | bytes 65568 | tf_op jit(solution)/shard_map/ppermute | solution.py:30
  128.6 0.8 collective-permute-done.17.refs_1_
  129.4 0.9 queries_by_half.3
  130.3 0.6 collective-permute-start.20
  130.9 2.0 %collective-permute-start.21 = (bf16[2,16,128]{2,1,0:T(8,128)(2,1)S(1)}, bf16[2,16,128]{2,1,0:T(8,128)(2,1)S(1)}, u32[]{:S(2)}, u32[]{:S(2)}) collective-permute-start(bf16[2,16,128]{2,1,0:T(8,128)(2,1)S(1)} %get-tuple-element.59), channel_id=1, source_target_pairs={{0,2},{1,3},{2,0},{3,1},{4,6},{5,7},{6,4},{7,5},{8,10},{9,11},{10,... | collective-permute-start | bytes 24584 | tf_op jit(solution)/shard_map/ppermute | solution.py:30
  132.9 0.9 collective-permute-start.22
  133.8 1.1 collective-permute-done.20.refs_1_
  134.9 1.7 collective-permute-done.22.refs_3_
  136.6 0.4 half_attention.3
  137.0 11.4 %all_to_all.51.c_ref = bf16[8,2,4,2048]{3,2,1,0:T(4,128)(2,1)S(1)} all-to-all(bf16[8,2,4,2048]{3,2,1,0:T(4,128)(2,1)S(1)} %half_attention.3), channel_id=1, replica_groups=mesh['section'=4,'expert'=8] {'expert'}, dimensions={0} | all-to-all | bytes 524288 | tf_op jit(solution)/shard_map/all_to_all | solution.py:41
  148.4 0.7 attention_out.5
  149.1 10.9 %all_to_all.52.a_ref = bf16[8,32,512]{2,1,0:T(8,128)(2,1)S(1)} all-to-all(bf16[8,32,512]{2,1,0:T(8,128)(2,1)S(1)} %attention_out.5), channel_id=1, replica_groups=mesh['section'=4,'expert'=8] {'expert'}, dimensions={0} | all-to-all | bytes 524288 | tf_op jit(solution)/shard_map/all_to_all | solution.py:41
  160.0 1.5 experts.1
  161.5 10.9 %all_to_all.53.r_ref = bf16[8,4,4096]{2,1,0:T(4,128)(2,1)S(1)} all-to-all(bf16[8,4,4096]{2,1,0:T(4,128)(2,1)S(1)} %get-tuple-element.63), channel_id=1, replica_groups=mesh['section'=4,'expert'=8] {'expert'}, dimensions={0} | all-to-all | bytes 524288 | tf_op jit(solution)/shard_map/all_to_all | solution.py:41
  172.5 0.7 combine.1
  (46 shorter events, 0.2 us)
Async XLA Ops:
  0.0 0.8 copy-start.9
  0.8 16.3 %copy-start = (bf16[1,4096,512]{2,1,0:T(8,128)(2,1)S(1)}, bf16[1,4096,512]{2,1,0:T(8,128)(2,1)}, u32[]{:S(2)}) copy-start(bf16[1,4096,512]{2,1,0:T(8,128)(2,1)} %param.19) | copy-start | bytes 12582916
  0.8 16.3 %copy-start.3 = (bf16[1,4096]{1,0:T(2,128)(2,1)S(1)}, bf16[1,4096]{1,0:T(2,128)(2,1)}, u32[]{:S(2)}) copy-start(bf16[1,4096]{1,0:T(2,128)(2,1)} %refs_4_.4) | copy-start | bytes 24580
  0.8 16.3 %copy-start.11 = (s32[1,3,4,2]{2,3,1,0:T(2,128)S(1)}, s32[1,3,4,2]{2,3,1,0:T(2,128)}, u32[]{:S(2)}) copy-start(s32[1,3,4,2]{2,3,1,0:T(2,128)} %param.28) | copy-start | bytes 292
  0.8 16.3 %copy-start.12 = (f32[1,3,4,2]{2,3,1,0:T(2,128)S(1)}, f32[1,3,4,2]{2,3,1,0:T(2,128)}, u32[]{:S(2)}) copy-start(f32[1,3,4,2]{2,3,1,0:T(2,128)} %param.29) | copy-start | bytes 292
  17.1 11.2 %copy-start.1 = (bf16[1,3,4,64,4,128]{5,4,3,2,1,0:T(4,128)(2,1)S(1)}, bf16[1,3,4,64,4,128]{5,4,3,2,1,0:T(4,128)(2,1)}, u32[]{:S(2)}) copy-start(bf16[1,3,4,64,4,128]{5,4,3,2,1,0:T(4,128)(2,1)} %param.21) | copy-start | bytes 2359300
  17.1 11.2 %copy-start.2 = (bf16[1,3,4,64,4,128]{5,4,3,2,1,0:T(4,128)(2,1)S(1)}, bf16[1,3,4,64,4,128]{5,4,3,2,1,0:T(4,128)(2,1)}, u32[]{:S(2)}) copy-start(bf16[1,3,4,64,4,128]{5,4,3,2,1,0:T(4,128)(2,1)} %param.22) | copy-start | bytes 2359300
  17.1 11.2 %copy-start.4 = (s32[1,3,4]{2,0,1:T(1,128)S(1)}, s32[1,3,4]{2,0,1:T(1,128)}, u32[]{:S(2)}) copy-start(s32[1,3,4]{2,0,1:T(1,128)} %param.23) | copy-start | bytes 148
  17.1 11.2 %copy-start.13 = (bf16[128,256]{1,0:T(8,128)(2,1)S(1)}, bf16[128,256]{1,0:T(8,128)(2,1)}, u32[]{:S(2)}) copy-start(bf16[128,256]{1,0:T(8,128)(2,1)} %constant.14.clone.refs_3_) | copy-start | bytes 196612
  17.1 11.2 %copy-start.14 = (bf16[32,256]{1,0:T(8,128)(2,1)S(1)}, bf16[32,256]{1,0:T(8,128)(2,1)}, u32[]{:S(2)}) copy-start(bf16[32,256]{1,0:T(8,128)(2,1)} %constant.15.clone.pick_ref) | copy-start | bytes 49156
  17.1 11.2 %copy-start.15 = (s32[32,1]{1,0:T(8,128)S(1)}, s32[32,1]{1,0:T(8,128)}, u32[]{:S(2)}) copy-start(s32[32,1]{1,0:T(8,128)} %constant.12.clone.refs_4_) | copy-start | bytes 388
  17.2 11.2 %copy-start.16 = (s32[8,256]{1,0:T(8,128)S(1)}, s32[8,256]{1,0:T(8,128)}, u32[]{:S(2)}) copy-start(s32[8,256]{1,0:T(8,128)} %constant.13.clone.refs_5_) | copy-start | bytes 24580
  28.3 11.3 %copy-start.5 = (bf16[1,4096,512]{2,1,0:T(8,128)(2,1)S(1)}, bf16[1,4096,512]{2,1,0:T(8,128)(2,1)}, u32[]{:S(2)}) copy-start(bf16[1,4096,512]{2,1,0:T(8,128)(2,1)} %param.20) | copy-start | bytes 12582916
  39.6 11.9 %copy-start.6 = (bf16[1,1,4096,384]{3,2,1,0:T(8,128)(2,1)S(1)}, bf16[1,1,4096,384]{3,2,1,0:T(8,128)(2,1)}, u32[]{:S(2)}) copy-start(bf16[1,1,4096,384]{3,2,1,0:T(8,128)(2,1)} %param.25) | copy-start | bytes 9437188
  39.6 11.9 %copy-start.7 = (bf16[1,1,4096,384]{3,2,1,0:T(8,128)(2,1)S(1)}, bf16[1,1,4096,384]{3,2,1,0:T(8,128)(2,1)}, u32[]{:S(2)}) copy-start(bf16[1,1,4096,384]{3,2,1,0:T(8,128)(2,1)} %param.26) | copy-start | bytes 9437188
  39.6 11.9 %copy-start.8 = (bf16[1,1,384,4096]{3,2,1,0:T(8,128)(2,1)S(1)}, bf16[1,1,384,4096]{3,2,1,0:T(8,128)(2,1)}, u32[]{:S(2)}) copy-start(bf16[1,1,384,4096]{3,2,1,0:T(8,128)(2,1)} %param.27) | copy-start | bytes 9437188
  39.6 11.9 %copy-start.10 = (bf16[1,4096]{1,0:T(2,128)(2,1)S(1)}, bf16[1,4096]{1,0:T(2,128)(2,1)}, u32[]{:S(2)}) copy-start(bf16[1,4096]{1,0:T(2,128)(2,1)} %gain_ref.3) | copy-start | bytes 24580
  53.1 5.8 %collective-permute-start = (bf16[2,4,4096]{2,1,0:T(4,128)(2,1)S(1)}, bf16[2,4,4096]{2,1,0:T(4,128)(2,1)S(1)}, u32[]{:S(2)}, u32[]{:S(2)}) collective-permute-start(bf16[2,4,4096]{2,1,0:T(4,128)(2,1)S(1)} %get-tuple-element.43), channel_id=1, source_target_pairs={{0,3},{1,2},{2,1},{3,0},{4,7},{5,6},{6,5},{7,4},{8,11},{9,10},{10,... | collective-permute-start | bytes 196616 | tf_op jit(solution)/shard_map/ppermute | solution.py:30
  54.1 4.8 %collective-permute-start.1 = (bf16[2,4,4096]{2,1,0:T(4,128)(2,1)S(1)}, bf16[2,4,4096]{2,1,0:T(4,128)(2,1)S(1)}, u32[]{:S(2)}, u32[]{:S(2)}) collective-permute-start(bf16[2,4,4096]{2,1,0:T(4,128)(2,1)S(1)} %get-tuple-element.44), channel_id=1, source_target_pairs={{0,2},{1,3},{2,0},{3,1},{4,6},{5,7},{6,4},{7,5},{8,10},{9,11},{10,... | collective-permute-start | bytes 196616 | tf_op jit(solution)/shard_map/ppermute | solution.py:30
  54.6 4.6 %collective-permute-start.2 = (bf16[2,4,4096]{2,1,0:T(4,128)(2,1)S(1)}, bf16[2,4,4096]{2,1,0:T(4,128)(2,1)S(1)}, u32[]{:S(2)}, u32[]{:S(2)}) collective-permute-start(bf16[2,4,4096]{2,1,0:T(4,128)(2,1)S(1)} %get-tuple-element.45), channel_id=1, source_target_pairs={{0,1},{1,0},{2,3},{3,2},{4,5},{5,4},{6,7},{7,6},{8,9},{9,8},{10,11... | collective-permute-start | bytes 196616 | tf_op jit(solution)/shard_map/ppermute | solution.py:30
  56.9 22.7 %collective-permute-start.11 = (bf16[1040,128]{1,0:T(8,128)(2,1)S(1)}, bf16[1040,128]{1,0:T(8,128)(2,1)S(1)}, u32[]{:S(2)}, u32[]{:S(2)}) collective-permute-start(bf16[1040,128]{1,0:T(8,128)(2,1)S(1)} %get-tuple-element.50), channel_id=1, source_target_pairs={{0,4},{1,5},{2,6},{3,7},{4,0},{5,1},{6,2},{7,3},{8,12},{9,13},{10,... | collective-permute-start | bytes 798728 | tf_op jit(solution)/shard_map/ppermute | solution.py:30
  59.3 8.3 %collective-permute-start.4 = (bf16[2,4,4096]{2,1,0:T(4,128)(2,1)S(1)}, bf16[2,4,4096]{2,1,0:T(4,128)(2,1)S(1)}, u32[]{:S(2)}, u32[]{:S(2)}) collective-permute-start(bf16[2,4,4096]{2,1,0:T(4,128)(2,1)S(1)} %partial.2), channel_id=1, source_target_pairs={{0,12},{1,13},{2,14},{3,15},{4,8},{5,9},{6,10},{7,11},{8,20},{9,21... | collective-permute-start | bytes 196616 | tf_op jit(solution)/shard_map/ppermute | solution.py:30
  59.3 8.2 %collective-permute-start.3 = (bf16[2,4,4096]{2,1,0:T(4,128)(2,1)S(1)}, bf16[2,4,4096]{2,1,0:T(4,128)(2,1)S(1)}, u32[]{:S(2)}, u32[]{:S(2)}) collective-permute-start(bf16[2,4,4096]{2,1,0:T(4,128)(2,1)S(1)} %partial.2), channel_id=1, source_target_pairs={{0,8},{1,9},{2,10},{3,11},{4,12},{5,13},{6,14},{7,15},{8,16},{9,17... | collective-permute-start | bytes 196616 | tf_op jit(solution)/shard_map/ppermute | solution.py:30
  67.6 5.3 %collective-permute-start.7 = (bf16[2,4,4096]{2,1,0:T(4,128)(2,1)S(1)}, bf16[2,4,4096]{2,1,0:T(4,128)(2,1)S(1)}, u32[]{:S(2)}, u32[]{:S(2)}) collective-permute-start(bf16[2,4,4096]{2,1,0:T(4,128)(2,1)S(1)} %join.2.refs_0_), channel_id=1, source_target_pairs={{0,3},{1,2},{2,1},{3,0},{4,7},{5,6},{6,5},{7,4},{8,11},{9,10},{10,... | collective-permute-start | bytes 196616 | tf_op jit(solution)/shard_map/ppermute | solution.py:30
  68.3 6.4 %collective-permute-start.6 = (bf16[2,4,4096]{2,1,0:T(4,128)(2,1)S(1)}, bf16[2,4,4096]{2,1,0:T(4,128)(2,1)S(1)}, u32[]{:S(2)}, u32[]{:S(2)}) collective-permute-start(bf16[2,4,4096]{2,1,0:T(4,128)(2,1)S(1)} %join.2.refs_0_), channel_id=1, source_target_pairs={{0,2},{1,3},{2,0},{3,1},{4,6},{5,7},{6,4},{7,5},{8,10},{9,11},{10,... | collective-permute-start | bytes 196616 | tf_op jit(solution)/shard_map/ppermute | solution.py:30
  70.7 4.5 %collective-permute-start.5 = (bf16[2,4,4096]{2,1,0:T(4,128)(2,1)S(1)}, bf16[2,4,4096]{2,1,0:T(4,128)(2,1)S(1)}, u32[]{:S(2)}, u32[]{:S(2)}) collective-permute-start(bf16[2,4,4096]{2,1,0:T(4,128)(2,1)S(1)} %join.2.refs_0_), channel_id=1, source_target_pairs={{0,1},{1,0},{2,3},{3,2},{4,5},{5,4},{6,7},{7,6},{8,9},{9,8},{10,11... | collective-permute-start | bytes 196616 | tf_op jit(solution)/shard_map/ppermute | solution.py:30
  76.1 4.6 %collective-permute-start.8 = (bf16[2,16,128]{2,1,0:T(8,128)(2,1)S(1)}, bf16[2,16,128]{2,1,0:T(8,128)(2,1)S(1)}, u32[]{:S(2)}, u32[]{:S(2)}) collective-permute-start(bf16[2,16,128]{2,1,0:T(8,128)(2,1)S(1)} %get-tuple-element.47), channel_id=1, source_target_pairs={{0,3},{1,2},{2,1},{3,0},{4,7},{5,6},{6,5},{7,4},{8,11},{9,10},{10,... | collective-permute-start | bytes 24584 | tf_op jit(solution)/shard_map/ppermute | solution.py:30
  76.4 4.3 %collective-permute-start.9 = (bf16[2,16,128]{2,1,0:T(8,128)(2,1)S(1)}, bf16[2,16,128]{2,1,0:T(8,128)(2,1)S(1)}, u32[]{:S(2)}, u32[]{:S(2)}) collective-permute-start(bf16[2,16,128]{2,1,0:T(8,128)(2,1)S(1)} %get-tuple-element.48), channel_id=1, source_target_pairs={{0,2},{1,3},{2,0},{3,1},{4,6},{5,7},{6,4},{7,5},{8,10},{9,11},{10,... | collective-permute-start | bytes 24584 | tf_op jit(solution)/shard_map/ppermute | solution.py:30
  78.6 3.7 %collective-permute-start.10 = (bf16[2,16,128]{2,1,0:T(8,128)(2,1)S(1)}, bf16[2,16,128]{2,1,0:T(8,128)(2,1)S(1)}, u32[]{:S(2)}, u32[]{:S(2)}) collective-permute-start(bf16[2,16,128]{2,1,0:T(8,128)(2,1)S(1)} %get-tuple-element.49), channel_id=1, source_target_pairs={{0,1},{1,0},{2,3},{3,2},{4,5},{5,4},{6,7},{7,6},{8,9},{9,8},{10,11... | collective-permute-start | bytes 24584 | tf_op jit(solution)/shard_map/ppermute | solution.py:30
  107.1 5.8 %collective-permute-start.12 = (bf16[2,4,4096]{2,1,0:T(4,128)(2,1)S(1)}, bf16[2,4,4096]{2,1,0:T(4,128)(2,1)S(1)}, u32[]{:S(2)}, u32[]{:S(2)}) collective-permute-start(bf16[2,4,4096]{2,1,0:T(4,128)(2,1)S(1)} %get-tuple-element.54), channel_id=1, source_target_pairs={{0,3},{1,2},{2,1},{3,0},{4,7},{5,6},{6,5},{7,4},{8,11},{9,10},{10,... | collective-permute-start | bytes 196616 | tf_op jit(solution)/shard_map/ppermute | solution.py:30
  108.1 4.8 %collective-permute-start.13 = (bf16[2,4,4096]{2,1,0:T(4,128)(2,1)S(1)}, bf16[2,4,4096]{2,1,0:T(4,128)(2,1)S(1)}, u32[]{:S(2)}, u32[]{:S(2)}) collective-permute-start(bf16[2,4,4096]{2,1,0:T(4,128)(2,1)S(1)} %get-tuple-element.55), channel_id=1, source_target_pairs={{0,2},{1,3},{2,0},{3,1},{4,6},{5,7},{6,4},{7,5},{8,10},{9,11},{10,... | collective-permute-start | bytes 196616 | tf_op jit(solution)/shard_map/ppermute | solution.py:30
  108.7 4.6 %collective-permute-start.14 = (bf16[2,4,4096]{2,1,0:T(4,128)(2,1)S(1)}, bf16[2,4,4096]{2,1,0:T(4,128)(2,1)S(1)}, u32[]{:S(2)}, u32[]{:S(2)}) collective-permute-start(bf16[2,4,4096]{2,1,0:T(4,128)(2,1)S(1)} %get-tuple-element.56), channel_id=1, source_target_pairs={{0,1},{1,0},{2,3},{3,2},{4,5},{5,4},{6,7},{7,6},{8,9},{9,8},{10,11... | collective-permute-start | bytes 196616 | tf_op jit(solution)/shard_map/ppermute | solution.py:30
  110.7 23.1 %collective-permute-start.23 = (bf16[1040,128]{1,0:T(8,128)(2,1)S(1)}, bf16[1040,128]{1,0:T(8,128)(2,1)S(1)}, u32[]{:S(2)}, u32[]{:S(2)}) collective-permute-start(bf16[1040,128]{1,0:T(8,128)(2,1)S(1)} %get-tuple-element.61), channel_id=1, source_target_pairs={{0,4},{1,5},{2,6},{3,7},{4,0},{5,1},{6,2},{7,3},{8,12},{9,13},{10,... | collective-permute-start | bytes 798728 | tf_op jit(solution)/shard_map/ppermute | solution.py:30
  113.3 9.3 %collective-permute-start.16 = (bf16[2,4,4096]{2,1,0:T(4,128)(2,1)S(1)}, bf16[2,4,4096]{2,1,0:T(4,128)(2,1)S(1)}, u32[]{:S(2)}, u32[]{:S(2)}) collective-permute-start(bf16[2,4,4096]{2,1,0:T(4,128)(2,1)S(1)} %partial.3), channel_id=1, source_target_pairs={{0,12},{1,13},{2,14},{3,15},{4,8},{5,9},{6,10},{7,11},{8,20},{9,21... | collective-permute-start | bytes 196616 | tf_op jit(solution)/shard_map/ppermute | solution.py:30
  113.4 9.2 %collective-permute-start.15 = (bf16[2,4,4096]{2,1,0:T(4,128)(2,1)S(1)}, bf16[2,4,4096]{2,1,0:T(4,128)(2,1)S(1)}, u32[]{:S(2)}, u32[]{:S(2)}) collective-permute-start(bf16[2,4,4096]{2,1,0:T(4,128)(2,1)S(1)} %partial.3), channel_id=1, source_target_pairs={{0,8},{1,9},{2,10},{3,11},{4,12},{5,13},{6,14},{7,15},{8,16},{9,17... | collective-permute-start | bytes 196616 | tf_op jit(solution)/shard_map/ppermute | solution.py:30
  122.7 5.9 %collective-permute-start.19 = (bf16[2,4,4096]{2,1,0:T(4,128)(2,1)S(1)}, bf16[2,4,4096]{2,1,0:T(4,128)(2,1)S(1)}, u32[]{:S(2)}, u32[]{:S(2)}) collective-permute-start(bf16[2,4,4096]{2,1,0:T(4,128)(2,1)S(1)} %join.3.refs_0_), channel_id=1, source_target_pairs={{0,3},{1,2},{2,1},{3,0},{4,7},{5,6},{6,5},{7,4},{8,11},{9,10},{10,... | collective-permute-start | bytes 196616 | tf_op jit(solution)/shard_map/ppermute | solution.py:30
  122.8 5.8 %collective-permute-start.18 = (bf16[2,4,4096]{2,1,0:T(4,128)(2,1)S(1)}, bf16[2,4,4096]{2,1,0:T(4,128)(2,1)S(1)}, u32[]{:S(2)}, u32[]{:S(2)}) collective-permute-start(bf16[2,4,4096]{2,1,0:T(4,128)(2,1)S(1)} %join.3.refs_0_), channel_id=1, source_target_pairs={{0,2},{1,3},{2,0},{3,1},{4,6},{5,7},{6,4},{7,5},{8,10},{9,11},{10,... | collective-permute-start | bytes 196616 | tf_op jit(solution)/shard_map/ppermute | solution.py:30
  124.9 4.6 %collective-permute-start.17 = (bf16[2,4,4096]{2,1,0:T(4,128)(2,1)S(1)}, bf16[2,4,4096]{2,1,0:T(4,128)(2,1)S(1)}, u32[]{:S(2)}, u32[]{:S(2)}) collective-permute-start(bf16[2,4,4096]{2,1,0:T(4,128)(2,1)S(1)} %join.3.refs_0_), channel_id=1, source_target_pairs={{0,1},{1,0},{2,3},{3,2},{4,5},{5,4},{6,7},{7,6},{8,9},{9,8},{10,11... | collective-permute-start | bytes 196616 | tf_op jit(solution)/shard_map/ppermute | solution.py:30
  130.3 4.6 %collective-permute-start.20 = (bf16[2,16,128]{2,1,0:T(8,128)(2,1)S(1)}, bf16[2,16,128]{2,1,0:T(8,128)(2,1)S(1)}, u32[]{:S(2)}, u32[]{:S(2)}) collective-permute-start(bf16[2,16,128]{2,1,0:T(8,128)(2,1)S(1)} %get-tuple-element.58), channel_id=1, source_target_pairs={{0,3},{1,2},{2,1},{3,0},{4,7},{5,6},{6,5},{7,4},{8,11},{9,10},{10,... | collective-permute-start | bytes 24584 | tf_op jit(solution)/shard_map/ppermute | solution.py:30
  130.9 4.0 %collective-permute-start.21 = (bf16[2,16,128]{2,1,0:T(8,128)(2,1)S(1)}, bf16[2,16,128]{2,1,0:T(8,128)(2,1)S(1)}, u32[]{:S(2)}, u32[]{:S(2)}) collective-permute-start(bf16[2,16,128]{2,1,0:T(8,128)(2,1)S(1)} %get-tuple-element.59), channel_id=1, source_target_pairs={{0,2},{1,3},{2,0},{3,1},{4,6},{5,7},{6,4},{7,5},{8,10},{9,11},{10,... | collective-permute-start | bytes 24584 | tf_op jit(solution)/shard_map/ppermute | solution.py:30
  132.9 3.7 %collective-permute-start.22 = (bf16[2,16,128]{2,1,0:T(8,128)(2,1)S(1)}, bf16[2,16,128]{2,1,0:T(8,128)(2,1)S(1)}, u32[]{:S(2)}, u32[]{:S(2)}) collective-permute-start(bf16[2,16,128]{2,1,0:T(8,128)(2,1)S(1)} %get-tuple-element.60), channel_id=1, source_target_pairs={{0,1},{1,0},{2,3},{3,2},{4,5},{5,4},{6,7},{7,6},{8,9},{9,8},{10,11... | collective-permute-start | bytes 24584 | tf_op jit(solution)/shard_map/ppermute | solution.py:30
